TPU v7x, 32 devices: a whole 2x2x4 slice. The times are simulated.
32 devices in a mesh: depth: 2 (over y), row: 4 (over x, core), col: 4 (over z).
Axes of the slice: x: 2, y: 2, z: 4, core: 2. Of those that a mesh axis runs over, the one named last changes fastest.
Arguments:
- volume: bfloat16 [64, 64, 4096], P('depth', 'row', 'col'), may hold values from -6 to 6
- first_weight: bfloat16 [64, 864], replicated, may hold values from -0.21875 to 0.21875
- second_weight: bfloat16 [128, 1728], replicated, may hold values from -0.15625 to 0.15625
- cotangent: bfloat16 [16, 16, 4096], P('depth', 'row', 'col'), may hold values from -0.011962891 to 0.011962891
Outputs:
- first_grad: float32 [64, 864], replicated
- second_grad: float32 [128, 1728], replicated
All inputs are finite; a program needn't handle non-finite values.
Results may differ from a plain program's by a relative error of at most 0.0047.
Values may be sent and summed in bfloat16 or wider, within the bound.
No kernel may reach another device: no remote copies, remote signals or barrier semaphores. Data moves between devices by JAX's collectives and lax.ppermute only.
A program may use at most 128 MiB of HBM per device.

v0:
```python
import jax
import jax.numpy as jnp
from jax import lax
from jax.experimental import pallas as pl
from jax.experimental.pallas import tpu as pltpu
from jax.sharding import PartitionSpec as P

LANES = 128
SECOND_ROWS = 27 * 64
F32 = jnp.float32
BF16 = jnp.bfloat16


def pairs_on_line(count, kind):
    firsts = range(kind, count - 1, 2)
    swapped = [(i, i + 1) for i in firsts] + [(i + 1, i) for i in firsts]
    met = {i for i, j in swapped}
    return swapped + [(i, i) for i in range(count) if i not in met]


def add_up(*terms):
    terms = [term.astype(F32) for term in terms]
    while len(terms) > 1:
        terms = [terms[n] + terms[n + 1] for n in range(0, len(terms), 2)]
    return terms[0].astype(BF16)


def matmul(left, right):
    return lax.dot_general(left, right, (((1,), (0,)), ((), ())), preferred_element_type=F32)


def pack(flag_ref, vol_ref, cot_ref, dep_ref, row_a_ref, row_b_ref, edge_a_ref, edge_b_ref, col_a_ref, col_b_ref):
    first_plane, row_even, col_even = flag_ref[0] == 0, flag_ref[1] == 0, flag_ref[2] == 0
    row_inner, col_inner = flag_ref[3] != 0, flag_ref[4] != 0
    planes, high, width = vol_ref.shape
    cots = cot_ref.shape[0]

    def rows(block, a_ref, b_ref, n):
        low, top = block[:4], block[high - 4 :]
        a_ref[n] = jnp.where(row_even, top, low).astype(BF16)
        b_ref[n] = jnp.where(row_inner, jnp.where(row_even, low, top), 0.0).astype(BF16)

    def plane(d, carry):
        block = vol_ref[d].astype(F32)
        rows(block, row_a_ref, row_b_ref, d)
        left, right = block[:, :LANES], block[:, width - LANES :]
        col_a_ref[d] = jnp.where(col_even, right, left).astype(BF16)
        col_b_ref[d] = jnp.where(col_inner, jnp.where(col_even, left, right), 0.0).astype(BF16)
        return carry

    lax.fori_loop(0, planes, plane, 0)
    for q in range(4):
        block = jnp.where(first_plane, vol_ref[planes - 4 + q].astype(F32), vol_ref[q].astype(F32))
        dep_ref[q] = block.astype(BF16)
        rows(block, edge_a_ref, edge_b_ref, q)
    cot = cot_ref[...].astype(F32)
    dep_ref[4] = jnp.concatenate([cot[0]] * 4, axis=0).astype(BF16)
    edge_a_ref[4] = cot[0].astype(BF16)
    edge_b_ref[4] = jnp.where(row_inner, cot[0], 0.0).astype(BF16)
    for g in range(cots // 4):
        tops = jnp.concatenate([cot[4 * g + n, :1] for n in range(4)], axis=0)
        row_a_ref[planes + g] = tops.astype(BF16)
        row_b_ref[planes + g] = jnp.where(row_inner, tops, 0.0).astype(BF16)
        side = jnp.concatenate([cot[4 * g + n, :, :LANES] for n in range(4)], axis=0)
        col_a_ref[planes + g] = side.astype(BF16)
        col_b_ref[planes + g] = jnp.where(col_inner, side, 0.0).astype(BF16)


def pack_corners(flag_ref, dep_ref, row_a_ref, row_b_ref, edge_a_ref, edge_b_ref, col_a_ref, col_b_ref):
    row_even, col_even, col_inner = flag_ref[1] == 0, flag_ref[2] == 0, flag_ref[4] != 0
    width = dep_ref.shape[2]
    groups = row_a_ref.shape[0]
    planes = (groups * 16) // 17
    faces = (slice(0, LANES), slice(width - LANES, width))

    def store(n, left, right):
        col_a_ref[n] = jnp.where(col_even, right, left).astype(BF16)
        col_b_ref[n] = jnp.where(col_inner, jnp.where(col_even, left, right), 0.0).astype(BF16)

    def lower_upper(a_ref, b_ref, source, target):
        values = []
        for lanes in faces:
            a, b = a_ref[source, :, lanes].astype(F32), b_ref[source, :, lanes].astype(F32)
            values.append(jnp.concatenate([jnp.where(row_even, b, a), jnp.where(row_even, a, b)], axis=0))
        store(target, *values)

    def plane(d, carry):
        lower_upper(row_a_ref, row_b_ref, d, d)
        return carry

    lax.fori_loop(0, planes, plane, 0)
    for q in range(4):
        lower_upper(edge_a_ref, edge_b_ref, q, planes + q)
        left, right = [dep_ref[q, :, lanes].astype(F32) for lanes in faces]
        for n in range(2):
            store(planes + 4 + 2 * q + n, left[8 * n : 8 * n + 8], right[8 * n : 8 * n + 8])
    lanes = faces[0]
    tops = [
        jnp.where(row_even, row_a_ref[g, :, lanes].astype(F32), row_b_ref[g, :, lanes].astype(F32))
        for g in range(planes, groups)
    ]
    corner = jnp.where(row_even, edge_a_ref[4, :, lanes].astype(F32), edge_b_ref[4, :, lanes].astype(F32))
    own = dep_ref[4, :, lanes].astype(F32)[:4]
    for n, values in enumerate((jnp.concatenate(tops, axis=0), jnp.concatenate([own, corner], axis=0))):
        col_a_ref[planes + 12 + n] = values.astype(BF16)
        col_b_ref[planes + 12 + n] = jnp.where(col_inner, values, 0.0).astype(BF16)


def bands(first_ref, second_ref, w1_ref, w2_ref, w2b_ref):
    out_chan = first_ref.shape[0]
    first = first_ref[...].astype(F32)
    blank = jnp.zeros((out_chan, LANES), F32)
    for tap in range(9):
        rows = slice(tap * LANES, (tap + 1) * LANES)
        taps = first[:, tap * 96 : (tap + 1) * 96]
        main_even = jnp.concatenate([taps[:, 32:], blank[:, :64]], axis=1)
        main_odd = jnp.concatenate([blank[:, :32], taps], axis=1)
        prev_even = jnp.concatenate([blank[:, :96], taps[:, :32]], axis=1)
        w1_ref[rows] = jnp.concatenate([main_even, main_odd, prev_even, blank], axis=0).T.astype(BF16)
        main = second_ref[tap * 192 + 64 : (tap + 1) * 192, :]
        prev = jnp.concatenate([jnp.zeros((64, LANES), BF16), second_ref[tap * 192 : tap * 192 + 64, :]], axis=0)
        both = jnp.concatenate([main, prev], axis=1)
        w2_ref[rows] = both
        w2b_ref[tap] = both.astype(F32).T.astype(BF16)


def split_rows(stage, tiles, index, blocks):
    for m in blocks:
        rows = [stage[m, pl.ds(4 + s, 8, stride=4), :] for s in range(-1, 4)]
        for b in range(3):
            tiles[b, index, m] = jnp.concatenate([rows[b], rows[b + 2]], axis=0).astype(BF16)


def clear_stage(stage):
    stage[:, :, 0:8, :] = jnp.zeros(stage.shape[:2] + (8, LANES), F32)
    stage[:, :, 24:40, :] = jnp.zeros(stage.shape[:2] + (16, LANES), F32)


def ahead(even, a, b):
    return jnp.where(even, a.astype(F32), b.astype(F32))


def behind(even, a, b):
    return jnp.where(even, b.astype(F32), a.astype(F32))


def own_blocks(
    flag_ref, vol_ref, dep_ref, row_a_ref, row_b_ref, edge_a_ref, edge_b_ref, w1_ref, tiles, parts, stage
):
    first_plane, row_even = flag_ref[0] == 0, flag_ref[1] == 0
    planes = vol_ref.shape[0]
    blocks = vol_ref.shape[2] // LANES
    clear_stage(stage)

    def place(n, target, own, a, b, keep):
        def kept(values):
            return values if keep is None else jnp.where(keep, values, 0.0)

        for m in range(blocks):
            lanes = slice(m * LANES, (m + 1) * LANES)
            stage[n, m, 8:24, :] = kept(own(lanes).astype(F32))
            stage[n, m, 4:8, :] = kept(behind(row_even, a(lanes), b(lanes)))
            stage[n, m, 24:28, :] = kept(ahead(row_even, a(lanes), b(lanes)))
        split_rows(stage.at[n], tiles, target, range(blocks))

    def place_own(pair, carry):
        for n in range(2):
            d = 2 * pair + n
            place(
                n, d + 3, lambda lanes: vol_ref[d, :, lanes],
                lambda lanes: row_a_ref[d, :, lanes], lambda lanes: row_b_ref[d, :, lanes], None,
            )
        return carry

    def place_halo(target, q, keep):
        place(
            target % 2, target, lambda lanes: dep_ref[q, :, lanes],
            lambda lanes: edge_a_ref[q, :, lanes], lambda lanes: edge_b_ref[q, :, lanes], keep,
        )

    lax.fori_loop(0, planes // 2, place_own, 0)
    for q in range(3):
        place_halo(q, q + 1, jnp.logical_not(first_plane))
    for q in range(4):
        place_halo(planes + 3 + q, q, first_plane)
    tiles[:, planes + 7 :] = jnp.zeros((3, 2, blocks, 16, LANES), BF16)

    def product(pair, carry):
        taps = []
        for a in range(3):
            for b in range(3):
                both = [tiles[b, 4 * pair + 2 * n + a].reshape(blocks * 16, LANES) for n in range(2)]
                taps.append(jnp.concatenate(both, axis=0))
        found = matmul(jnp.concatenate(taps, axis=1), w1_ref[...])
        parts[pl.ds(2 * pair, 2)] = found.reshape(2, blocks, 16, 2 * LANES)
        return carry

    lax.fori_loop(0, planes // 4 + 2, product, 0)


def body(
    flag_ref, place_ref, tiles, parts, dep_ref, row_a_ref, row_b_ref, edge_a_ref, edge_b_ref,
    side_a_ref, side_b_ref, col_a_ref, col_b_ref, cot_ref, w1_ref, w2_ref, w2b_ref, keep_ref, give_ref,
    out_ref, stage, rim_tiles, rim_parts, slopes, hid, pairs, ups, deltas, shifted,
):
    first_plane, row_even, col_even = flag_ref[0] == 0, flag_ref[1] == 0, flag_ref[2] == 0
    planes = tiles.shape[1] - 9
    blocks = tiles.shape[2]
    half_planes = planes // 4
    hidden_planes = planes // 2 + 3

    clear_stage(stage)

    def place(n, target, source, side_a, side_b, keep):
        for m, choose in ((0, behind), (1, ahead)):
            corners = choose(col_even, col_a_ref[source], col_b_ref[source])
            own = choose(col_even, side_a, side_b)
            if keep is not None:
                corners, own = jnp.where(keep, corners, 0.0), jnp.where(keep, own, 0.0)
            stage[n, m, 4:8, :] = corners[:4]
            stage[n, m, 8:24, :] = own
            stage[n, m, 24:28, :] = corners[4:]
        split_rows(stage.at[n], rim_tiles, target, range(2))

    def place_own(group, carry):
        for n in range(4):
            d = 4 * group + n
            place(n, d + 3, d, side_a_ref[d], side_b_ref[d], None)
        return carry

    def place_halo(target, q, keep):
        start = planes + 4 + 2 * q
        side_a = jnp.concatenate([col_a_ref[start].astype(F32), col_a_ref[start + 1].astype(F32)], axis=0)
        side_b = jnp.concatenate([col_b_ref[start].astype(F32), col_b_ref[start + 1].astype(F32)], axis=0)
        place(target % 4, target, planes + q, side_a, side_b, keep)

    lax.fori_loop(0, planes // 4, place_own, 0)
    for q in range(3):
        place_halo(q, q + 1, jnp.logical_not(first_plane))
    for q in range(4):
        place_halo(planes + 3 + q, q, first_plane)

    taps = []
    for a in range(3):
        for b in range(3):
            rows = [rim_tiles[b, 2 * i + a].reshape(32, LANES) for i in range(hidden_planes)]
            taps.append(jnp.concatenate(rows, axis=0))
    found = matmul(jnp.concatenate(taps, axis=1), w1_ref[...])
    rim_parts[...] = found.reshape(hidden_planes, 2, 16, 2 * LANES)

    def conv_one(i, carry):
        main, prev = parts[i, :, :, :LANES], parts[i, :, :, LANES:]
        rim, rim_prev = rim_parts[i, :, :, :LANES], rim_parts[i, 0:1, :, LANES:]
        blank = jnp.zeros((1, 16, LANES), F32)
        pre = jnp.concatenate([rim[:1], main, rim[1:]], axis=0) + jnp.concatenate([blank, rim_prev, prev], axis=0)
        root = jnp.sqrt(pre * pre + 1.0)
        slopes[i] = 0.6 + 0.4 * pre / root
        hidden = (0.6 * pre + 0.4 * (root - 1.0)).astype(BF16).astype(F32)
        odd = hidden[:, 8:, :]
        hid[0, i] = pltpu.roll(odd, 1, 1)
        hid[1, i] = hidden[:, :8, :]
        hid[2, i] = odd
        return carry

    lax.fori_loop(0, hidden_planes, conv_one, 0)

    wide = (blocks + 2) * 16

    def pair(i, carry):
        for b in range(3):
            pairs[b, i] = jnp.concatenate([hid[b, i], hid[b, i + half_planes]], axis=1).astype(BF16)
        return carry

    lax.fori_loop(0, half_planes + 3, pair, 0)

    ups[...] = jnp.zeros_like(ups)
    for k in range(blocks):
        lanes = slice(k * LANES, (k + 1) * LANES)
        ups[0:half_planes, k, 1:5, :] = cot_ref[:, :, lanes].astype(F32)
        ups[half_planes, k, 1:5, :] = jnp.where(first_plane, dep_ref[4, 0:4, lanes].astype(F32), 0.0)
        for g in range(half_planes // 4):
            tops = ahead(row_even, row_a_ref[planes + g, :, lanes], row_b_ref[planes + g, :, lanes])
            for n in range(4):
                ups[4 * g + n, k, 5:6, :] = tops[n : n + 1]
        corner = ahead(row_even, edge_a_ref[4, :, lanes], edge_b_ref[4, :, lanes])[:1]
        ups[half_planes, k, 5:6, :] = jnp.where(first_plane, corner, 0.0)
    for g in range(half_planes // 4):
        side = ahead(col_even, side_a_ref[planes + g], side_b_ref[planes + g])
        for n in range(4):
            ups[4 * g + n, blocks, 1:5, :] = side[4 * n : 4 * n + 4]
    tops = ahead(col_even, col_a_ref[planes + 12], col_b_ref[planes + 12])
    for n in range(half_planes):
        ups[n, blocks, 5:6, :] = tops[n : n + 1]
    beyond = jnp.where(first_plane, ahead(col_even, col_a_ref[planes + 13], col_b_ref[planes + 13]), 0.0)
    ups[half_planes, blocks, 1:6, :] = beyond[:5]

    quarter = half_planes // 2

    def conv_two(t, carry):
        taps = [pairs[b, 2 * t + a].reshape(wide, LANES) for a in range(3) for b in range(3)]
        parts = matmul(jnp.concatenate(taps, axis=1), w2_ref[...]).reshape(blocks + 2, 16, 2 * LANES)
        pre = parts[1:, :, :LANES] + parts[:-1, :, LANES:]
        slope = 0.6 + 0.4 * pre / jnp.sqrt(pre * pre + 1.0)
        upstream = jnp.concatenate([ups[t], ups[t + quarter]], axis=1)
        delta = (upstream * slope).astype(BF16).astype(F32)
        moved = jnp.concatenate([pltpu.roll(delta[:, :8], 7, 1), pltpu.roll(delta[:, 8:], 7, 1)], axis=1)
        deltas[t] = delta
        shifted[t] = moved.astype(BF16)
        return carry

    lax.fori_loop(0, quarter + 1, conv_two, 0)

    sublane = lax.broadcasted_iota(jnp.int32, (1, 1, 16, 1), 2) % 8
    own_rows = jnp.logical_and(sublane >= 1, sublane <= 4)

    def with_next(values):
        values = values.T
        edge = jnp.zeros((LANES, values.shape[1] // blocks), values.dtype)
        here = jnp.concatenate([edge, values], axis=1)
        after = jnp.concatenate([values, edge], axis=1)
        return jnp.concatenate([here, after], axis=0)

    own_delta = [jnp.where(own_rows[0], deltas[t, 0:blocks], 0.0) for t in range(quarter)]
    left = with_next(jnp.stack(own_delta, axis=1).reshape(blocks * quarter * 16, LANES)).astype(BF16)

    def second_taps(tap):
        a, b = tap // 3, tap % 3
        found = [pairs[b, 2 * t + a, 0 : blocks + 1] for t in range(quarter)]
        return jnp.stack(found, axis=1).reshape((blocks + 1) * quarter * 16, LANES)

    for tap in range(0, 9, 2):
        right = [second_taps(x) for x in range(tap, min(tap + 2, 9))]
        found = matmul(left, jnp.concatenate(right, axis=1))
        for n in range(len(right)):
            row = (tap + n) * 192
            lanes = slice(n * LANES, (n + 1) * LANES)
            out_ref[row : row + 64, :] = found[LANES:, lanes].T[64:]
            out_ref[row + 64 : row + 192, :] = found[:LANES, lanes].T

    def pack(values):
        both = jnp.concatenate([values[:, :-1], values[:, 1:]], axis=3)
        return both.reshape(quarter * blocks * 16, 2 * LANES)

    plain = deltas[...].astype(BF16)
    moved = shifted[...]
    here, after = pack(plain[:-1]), pack(plain[1:])
    here_up, after_up = pack(moved[:-1]), pack(moved[1:])

    def back(terms):
        joined = jnp.concatenate([values for values, a, b in terms], axis=1)
        weights = jnp.concatenate([w2b_ref[3 * a + b] for values, a, b in terms], axis=0)
        return matmul(joined, weights).reshape(quarter, blocks, 16, LANES)

    rows = [
        [back([(here, 1, 1)]), back([(here_up, 1, 0), (here, 1, 2)])],
        [
            back([(after, 0, 1), (here, 2, 1)]),
            back([(after_up, 0, 0), (after, 0, 2), (here_up, 2, 0), (here, 2, 2)]),
        ],
    ]
    own_list = []
    for i in range(planes // 2):
        t, parity = i // 2, i % 2
        half = slice(0, 8) if t < quarter else slice(8, 16)
        back_one = jnp.concatenate([rows[parity][p][t % quarter, :, half, :] for p in (0, 1)], axis=1)
        delta = back_one * slopes[i + 1, 1 : blocks + 1]
        own_list.append(jnp.where(own_rows[0], delta, 0.0).astype(BF16))
    left_one = with_next(jnp.stack(own_list, axis=1).reshape(blocks * (planes // 2) * 16, LANES))

    def first_taps(tap):
        a, b = tap // 3, tap % 3
        found = []
        for m in range(blocks + 1):
            for i in range(planes // 2):
                index = 2 * (i + 1) + a
                found.append(rim_tiles[b, index, 0] if m == 0 else tiles[b, index, m - 1])
        return jnp.concatenate(found, axis=0)

    for tap in range(0, 9, 2):
        right = [first_taps(x) for x in range(tap, min(tap + 2, 9))]
        found = matmul(left_one, jnp.concatenate(right, axis=1))
        for n in range(len(right)):
            main = found[:LANES, n * LANES : (n + 1) * LANES]
            prev = found[LANES : LANES + 64, n * LANES : (n + 1) * LANES]
            even = jnp.concatenate([prev[:, 96:], main[:64, :64]], axis=1)
            grad = jnp.concatenate([even + main[64:, 32:], jnp.zeros((64, 32), F32)], axis=1)
            row = SECOND_ROWS + (tap + n) * 64
            out_ref[row : row + 64, :] = grad

    core, square = place_ref[0], place_ref[1]
    squares, size = keep_ref.shape[0], keep_ref.shape[1]
    for n in range(squares):
        for ref, half in ((keep_ref, core), (give_ref, 1 - core)):
            start = pl.multiple_of((half * squares + (square ^ n)) * size, 8)
            ref[n] = out_ref[pl.ds(start, size), :].astype(BF16)


def unpack(place_ref, keep_ref, got_ref, g1_ref, g2_ref, sums):
    core, square = place_ref[0], place_ref[1]
    squares, size = keep_ref.shape[0], keep_ref.shape[1]
    for n in range(squares):
        for ref, half in ((keep_ref, core), (got_ref, 1 - core)):
            start = pl.multiple_of((half * squares + (square ^ n)) * size, 8)
            sums[pl.ds(start, size), :] = ref[n].astype(F32)
    first = sums[SECOND_ROWS:, :]
    g1_ref[...] = jnp.concatenate([first[tap * 64 : (tap + 1) * 64, :96] for tap in range(9)], axis=1)
    g2_ref[...] = sums[:SECOND_ROWS, :]


def local_grads(flags, place, squares, volume, faces, corners, cotangent, weights):
    planes = volume.shape[0]
    blocks = volume.shape[2] // LANES
    hidden_planes = planes // 2 + 3
    out_planes = planes // 4
    rows = SECOND_ROWS + 9 * 64
    whole = pl.BlockSpec(memory_space=pltpu.VMEM)
    smem = pl.BlockSpec(memory_space=pltpu.SMEM)
    dep, row_a, row_b, edge_a, edge_b = faces
    tiles, parts = pl.pallas_call(
        own_blocks,
        out_shape=[
            jax.ShapeDtypeStruct((3, planes + 9, blocks, 16, LANES), BF16),
            jax.ShapeDtypeStruct((hidden_planes + 1, blocks, 16, 2 * LANES), F32),
        ],
        in_specs=[smem] + [whole] * 7,
        out_specs=[whole] * 2,
        scratch_shapes=[pltpu.VMEM((2, blocks, 40, LANES), F32)],
        compiler_params=pltpu.CompilerParams(vmem_limit_bytes=16 * 1024 * 1024),
        cost_estimate=pl.CostEstimate(flops=2 * 10**9, bytes_accessed=10**7, transcendentals=0),
    )(flags, volume, *faces, weights[0])
    scratch = [
        pltpu.VMEM((rows, LANES), F32),
        pltpu.VMEM((4, 2, 40, LANES), F32),
        pltpu.VMEM((3, planes + 7, 2, 16, LANES), BF16),
        pltpu.VMEM((hidden_planes, 2, 16, 2 * LANES), F32),
        pltpu.VMEM((hidden_planes, blocks + 2, 16, LANES), F32),
        pltpu.VMEM((3, hidden_planes, blocks + 2, 8, LANES), F32),
        pltpu.VMEM((3, out_planes + 3, blocks + 2, 16, LANES), BF16),
        pltpu.VMEM((out_planes + 1, blocks + 1, 8, LANES), F32),
        pltpu.VMEM((out_planes // 2 + 1, blocks + 1, 16, LANES), F32),
        pltpu.VMEM((out_planes // 2 + 1, blocks + 1, 16, LANES), BF16),
    ]
    operands = (tiles, parts, *faces, *corners, cotangent, *weights)
    return pl.pallas_call(
        body,
        out_shape=[jax.ShapeDtypeStruct((squares, rows // (2 * squares), LANES), BF16)] * 2,
        in_specs=[smem] * 2 + [whole] * len(operands),
        out_specs=[whole] * 2,
        scratch_shapes=scratch,
        compiler_params=pltpu.CompilerParams(vmem_limit_bytes=28 * 1024 * 1024),
        cost_estimate=pl.CostEstimate(flops=4 * 10**9, bytes_accessed=10**7, transcendentals=0),
    )(flags, place, *operands)


def shards(volume, first_weight, second_weight, cotangent):
    half = lax.axis_index("depth")
    row, col = lax.axis_index("row"), lax.axis_index("col")
    rows, cols = lax.axis_size("row"), lax.axis_size("col")
    inner = [jnp.logical_and(i > 0, i < n - 1).astype(jnp.int32) for i, n in ((row, rows), (col, cols))]
    flags = jnp.stack([half, row % 2, col % 2, *inner])
    whole = pl.BlockSpec(memory_space=pltpu.VMEM)
    smem = pl.BlockSpec(memory_space=pltpu.SMEM)
    small = pltpu.CompilerParams(vmem_limit_bytes=12 * 1024 * 1024)
    planes, high, width = volume.shape
    groups = planes + cotangent.shape[0] // 4
    faces = [(5, high, width)] + [(groups, 4, width)] * 2 + [(5, 4, width)] * 2 + [(groups, high, LANES)] * 2
    dep, row_a, row_b, edge_a, edge_b, side_a, side_b = pl.pallas_call(
        pack,
        out_shape=[jax.ShapeDtypeStruct(shape, BF16) for shape in faces],
        in_specs=[smem] + [whole] * 2,
        out_specs=[whole] * 7,
        compiler_params=small,
    )(flags, volume, cotangent)

    def to_edge(block, kind):
        line = pairs_on_line(rows, kind)
        route = [(d * rows + i, (1 - d) * rows + j) for d in (0, 1) for i, j in line]
        return lax.ppermute(block, ("depth", "row"), route)

    def to_col(block, kind):
        return lax.ppermute(block, "col", pairs_on_line(cols, kind))

    edge_a, edge_b = to_edge(edge_a, 0), to_edge(edge_b, 1)
    row_a = lax.ppermute(row_a, "row", pairs_on_line(rows, 0))
    side_a, side_b = to_col(side_a, 0), to_col(side_b, 1)
    dep = lax.ppermute(dep, "depth", [(0, 1), (1, 0)])
    row_b = lax.ppermute(row_b, "row", pairs_on_line(rows, 1))
    col_a, col_b = pl.pallas_call(
        pack_corners,
        out_shape=[jax.ShapeDtypeStruct((planes + 14, 8, LANES), BF16)] * 2,
        in_specs=[smem] + [whole] * 5,
        out_specs=[whole] * 2,
        compiler_params=small,
    )(flags, dep, row_a, row_b, edge_a, edge_b)
    col_a, col_b, first_taps, second_taps = lax.optimization_barrier((col_a, col_b, first_weight, second_weight.T))
    col_a, col_b = to_col(col_a, 0), to_col(col_b, 1)

    weights = pl.pallas_call(
        bands,
        out_shape=[jax.ShapeDtypeStruct(shape, BF16) for shape in ((1152, 256), (1152, 256), (9, 256, 128))],
        in_specs=[whole] * 2,
        out_specs=[whole] * 3,
        compiler_params=small,
    )(first_taps, second_taps)
    spot = lax.axis_index(("depth", "row"))
    squares = lax.axis_size(("depth", "row")) // 2
    where = jnp.stack([spot % 2, spot // 2])
    faces, corners = (dep, row_a, row_b, edge_a, edge_b), (side_a, side_b, col_a, col_b)
    keep, give = local_grads(flags, where, squares, volume, faces, corners, cotangent, weights)

    def to_square(block, n):
        route = [(2 * i + c, 2 * (i ^ n) + c) for i in range(squares) for c in (0, 1)]
        return lax.ppermute(block, ("depth", "row"), route)

    def to_core(block):
        return lax.ppermute(block, ("depth", "row"), [(i, i ^ 1) for i in range(2 * squares)])

    def along_col(block, n):
        return lax.ppermute(block, "col", [(i, i ^ n) for i in range(cols)])

    both = add_up(keep, to_core(give))
    share = add_up(both[0], *[to_square(both[n], n) for n in range(1, squares)])
    share = add_up(share, *[along_col(share, n) for n in range(1, cols)])
    mine = jnp.stack([share] + [to_square(share, n) for n in range(1, squares)])
    other = to_core(mine)
    grads = [jax.ShapeDtypeStruct(shape, F32) for shape in (first_weight.shape, second_weight.shape[::-1])]
    first_grad, second_grad = pl.pallas_call(
        unpack,
        out_shape=grads,
        in_specs=[smem] + [whole] * 2,
        out_specs=[whole] * 2,
        scratch_shapes=[pltpu.VMEM((mine.shape[0] * mine.shape[1] * 2, LANES), F32)],
        compiler_params=small,
    )(where, mine, other)
    return first_grad, second_grad.T


def solution(mesh):
    placed = (P("depth", "row", "col"), P(), P(), P("depth", "row", "col"))
    return jax.shard_map(shards, mesh=mesh, in_specs=placed, out_specs=(P(), P()), check_vma=False)
```

profile of v0, /device:TPU:0, one launch (start us, length us, event | category | flops | bytes accessed | tf_op | source)
XLA Modules:
  0.0 69.2 jit_solution(13239446482112473936)
XLA Ops:
  0.7 1.2 %copy-done = bf16[32,16,1024]{2,1,0:T(8,128)(2,1)S(1)} copy-done((bf16[32,16,1024]{2,1,0:T(8,128)(2,1)S(1)}, bf16[32,16,1024]{2,1,0:T(8,128)(2,1)}, u32[]{:S(2)}) %copy-start) | copy-done | bytes 1048600
  2.8 1.1 %shard_map.59 = (bf16[5,16,1024]{2,1,0:T(8,128)(2,1)S(1)}, bf16[34,4,1024]{2,1,0:T(4,128)(2,1)S(1)}, bf16[34,4,1024]{2,1,0:T(4,128)(2,1)S(1)}, bf16[5,4,1024]{2,...) custom-call(s32[5]{0:T(128)S(1)} %stack.58.flag_ref, ...), custom_call_target="tpu_custom_call" | custom-call | tf_op jit(solution)/shard_map/pallas_call | solution.py:467
  5.2 2.6 %collective-permute-start = (bf16[5,16,1024]{2,1,0:T(8,128)(2,1)S(1)}, bf16[5,16,1024]{2,1,0:T(8,128)(2,1)S(1)}, u32[]{:S(2)}, u32[]{:S(2)}) collective-permute-start(bf16[5,16,1024]{2,1,0:T(8,128)(2,1)S(1)} %get-tuple-element.24), channel_id=1, source_target_pairs={{0,16},{16,0},{1,17},{17,1},{2,18},{18,2},{3,19},{19,3},{4,20},{20... | collective-permute-start | bytes 491528 | tf_op jit(solution)/shard_map/ppermute | solution.py:486
  7.8 2.7 %collective-permute-start.3 = (bf16[5,4,1024]{2,1,0:T(4,128)(2,1)S(1)}, bf16[5,4,1024]{2,1,0:T(4,128)(2,1)S(1)}, u32[]{:S(2)}, u32[]{:S(2)}) collective-permute-start(bf16[5,4,1024]{2,1,0:T(4,128)(2,1)S(1)} %get-tuple-element.27), channel_id=1, source_target_pairs={{0,20},{8,28},{4,16},{12,24},{16,4},{24,12},{20,0},{28,8},{1,21},{... | collective-permute-start | bytes 122888 | tf_op jit(solution)/shard_map/ppermute | solution.py:478
  10.4 1.5 %collective-permute-start.4 = (bf16[5,4,1024]{2,1,0:T(4,128)(2,1)S(1)}, bf16[5,4,1024]{2,1,0:T(4,128)(2,1)S(1)}, u32[]{:S(2)}, u32[]{:S(2)}) collective-permute-start(bf16[5,4,1024]{2,1,0:T(4,128)(2,1)S(1)} %get-tuple-element.28), channel_id=1, source_target_pairs={{4,24},{8,20},{0,16},{12,28},{20,8},{24,4},{16,0},{28,12},{5,25},{... | collective-permute-start | bytes 122888 | tf_op jit(solution)/shard_map/ppermute | solution.py:478
  12.0 2.2 %collective-permute-done.3.edge_a_ref = bf16[5,4,1024]{2,1,0:T(4,128)(2,1)S(1)} collective-permute-done((bf16[5,4,1024]{2,1,0:T(4,128)(2,1)S(1)}, bf16[5,4,1024]{2,1,0:T(4,128)(2,1)S(1)}, u32[]{:S(2)}, u32[]{:S(2)}) %collective-permute-start.3) | collective-permute-done | bytes 40992 | tf_op jit(solution)/shard_map/ppermute | solution.py:478
  14.2 1.6 %collective-permute-start.5 = (bf16[34,16,128]{2,1,0:T(8,128)(2,1)S(1)}, bf16[34,16,128]{2,1,0:T(8,128)(2,1)S(1)}, u32[]{:S(2)}, u32[]{:S(2)}) collective-permute-start(bf16[34,16,128]{2,1,0:T(8,128)(2,1)S(1)} %get-tuple-element.36), channel_id=1, source_target_pairs={{0,1},{2,3},{1,0},{3,2},{4,5},{6,7},{5,4},{7,6},{8,9},{10,11},{9,8... | collective-permute-start | bytes 417800 | tf_op jit(solution)/shard_map/ppermute | solution.py:481
  17.3 4.5 %collective-permute-start.7 = (bf16[46,8,128]{2,1,0:T(8,128)(2,1)S(1)}, bf16[46,8,128]{2,1,0:T(8,128)(2,1)S(1)}, u32[]{:S(2)}, u32[]{:S(2)}) collective-permute-start(bf16[46,8,128]{2,1,0:T(8,128)(2,1)S(1)} %get-tuple-element.38), channel_id=1, source_target_pairs={{0,1},{2,3},{1,0},{3,2},{4,5},{6,7},{5,4},{7,6},{8,9},{10,11},{9,8... | collective-permute-start | bytes 282632 | tf_op jit(solution)/shard_map/ppermute | solution.py:481
  25.0 1.2 %copy-done.1 = bf16[32,16,1024]{2,1,0:T(8,128)(2,1)S(1)} copy-done((bf16[32,16,1024]{2,1,0:T(8,128)(2,1)S(1)}, bf16[32,16,1024]{2,1,0:T(8,128)(2,1)}, u32[]{:S(2)}) %copy-start.1) | copy-done | bytes 1048600
  26.2 4.7 %shard_map.62 = (bf16[3,41,8,16,128]{4,3,2,1,0:T(8,128)(2,1)S(1)}, f32[20,8,16,256]{3,2,1,0:T(8,128)S(1)}) custom-call(s32[5]{0:T(128)S(1)} %stack.58.flag_ref, bf16[32,16,1024]{2,1,0:T(8,128)(2,1)S(1)} %copy-done.1, bf16[5,16,1024]{2,1,0:T(8,128)(2,1)S(1)} %collective-permute-done.dep_ref, bf16[34,4,1024]{2,1,0:T(4,128)(2,1)S(1)} %collective-permute-done.1.row_a_ref, ...), custom_call_target="tpu_custom_call" | custom-call | flops 2000000000 | bytes 10000000 | tf_op jit(solution)/shard_map/pallas_call | solution.py:419
  31.0 8.0 %shard_map.63 = (bf16[4,288,128]{2,1,0:T(8,128)(2,1)S(1)}, bf16[4,288,128]{2,1,0:T(8,128)(2,1)S(1)}) custom-call(s32[5]{0:T(128)S(1)} %stack.58.flag_ref, s32[2]{0:T(128)S(1)} %pad_add_fusion.place_ref, bf16[3,41,8,16,128]{4,3,2,1,0:T(8,128)(2,1)S(1)} %get-tuple-element.34.tiles, f32[20,8,16,256]{3,2,1,0:T(8,128)S(1)} %get-tuple-element.35.parts, ...), custom_call_target="tpu_custom_call" | custom-call | flops 4000000000 | bytes 10000000 | tf_op jit(solution)/shard_map/pallas_call | solution.py:444
  39.1 1.6 %collective-permute-done.9 = bf16[4,288,128]{2,1,0:T(8,128)(2,1)S(1)} collective-permute-done((bf16[4,288,128]{2,1,0:T(8,128)(2,1)S(1)}, bf16[4,288,128]{2,1,0:T(8,128)(2,1)S(1)}, u32[]{:S(2)}, u32[]{:S(2)}) %collective-permute-start.9) | collective-permute-done | bytes 294944 | tf_op jit(solution)/shard_map/ppermute | solution.py:516
  40.8 1.5 %collective-permute-start.10 = (bf16[288,128]{1,0:T(8,128)(2,1)S(1)}, bf16[288,128]{1,0:T(8,128)(2,1)S(1)}, u32[]{:S(2)}, u32[]{:S(2)}) collective-permute-start(bf16[288,128]{1,0:T(8,128)(2,1)S(1)} %get-tuple-element.46), channel_id=1, source_target_pairs={{0,8},{4,12},{8,0},{12,4},{16,24},{20,28},{24,16},{28,20},{1,9},{5... | collective-permute-start | bytes 221192 | tf_op jit(solution)/shard_map/ppermute | solution.py:513
  42.3 2.3 %collective-permute-start.12 = (bf16[288,128]{1,0:T(8,128)(2,1)S(1)}, bf16[288,128]{1,0:T(8,128)(2,1)S(1)}, u32[]{:S(2)}, u32[]{:S(2)}) collective-permute-start(bf16[288,128]{1,0:T(8,128)(2,1)S(1)} %get-tuple-element.47), channel_id=1, source_target_pairs={{0,24},{4,28},{8,16},{12,20},{16,8},{20,12},{24,0},{28,4},{1,25},{... | collective-permute-start | bytes 221192 | tf_op jit(solution)/shard_map/ppermute | solution.py:513
  45.2 3.4 %collective-permute-done.12 = bf16[288,128]{1,0:T(8,128)(2,1)S(1)} collective-permute-done((bf16[288,128]{1,0:T(8,128)(2,1)S(1)}, bf16[288,128]{1,0:T(8,128)(2,1)S(1)}, u32[]{:S(2)}, u32[]{:S(2)}) %collective-permute-start.12) | collective-permute-done | bytes 73760 | tf_op jit(solution)/shard_map/ppermute | solution.py:513
  50.6 1.9 %collective-permute-start.14 = (bf16[288,128]{1,0:T(8,128)(2,1)S(1)}, bf16[288,128]{1,0:T(8,128)(2,1)S(1)}, u32[]{:S(2)}, u32[]{:S(2)}) collective-permute-start(bf16[288,128]{1,0:T(8,128)(2,1)S(1)} %fusion.1), channel_id=1, source_target_pairs={{0,2},{1,3},{2,0},{3,1},{4,6},{5,7},{6,4},{7,5},{8,10},{9,11},{10,... | collective-permute-start | bytes 221192 | tf_op jit(solution)/shard_map/ppermute | solution.py:519
  52.5 1.6 %collective-permute-start.13 = (bf16[288,128]{1,0:T(8,128)(2,1)S(1)}, bf16[288,128]{1,0:T(8,128)(2,1)S(1)}, u32[]{:S(2)}, u32[]{:S(2)}) collective-permute-start(bf16[288,128]{1,0:T(8,128)(2,1)S(1)} %fusion.1), channel_id=1, source_target_pairs={{0,1},{1,0},{2,3},{3,2},{4,5},{5,4},{6,7},{7,6},{8,9},{9,8},{10,11... | collective-permute-start | bytes 221192 | tf_op jit(solution)/shard_map/ppermute | solution.py:519
  54.1 2.6 %collective-permute-done.15 = bf16[288,128]{1,0:T(8,128)(2,1)S(1)} collective-permute-done((bf16[288,128]{1,0:T(8,128)(2,1)S(1)}, bf16[288,128]{1,0:T(8,128)(2,1)S(1)}, u32[]{:S(2)}, u32[]{:S(2)}) %collective-permute-start.15) | collective-permute-done | bytes 73760 | tf_op jit(solution)/shard_map/ppermute | solution.py:519
  56.7 2.5 %collective-permute-done.14 = bf16[288,128]{1,0:T(8,128)(2,1)S(1)} collective-permute-done((bf16[288,128]{1,0:T(8,128)(2,1)S(1)}, bf16[288,128]{1,0:T(8,128)(2,1)S(1)}, u32[]{:S(2)}, u32[]{:S(2)}) %collective-permute-start.14) | collective-permute-done | bytes 73760 | tf_op jit(solution)/shard_map/ppermute | solution.py:519
  60.0 1.4 %collective-permute-start.17 = (bf16[288,128]{1,0:T(8,128)(2,1)S(1)}, bf16[288,128]{1,0:T(8,128)(2,1)S(1)}, u32[]{:S(2)}, u32[]{:S(2)}) collective-permute-start(bf16[288,128]{1,0:T(8,128)(2,1)S(1)} %add_convert_fusion.1), channel_id=1, source_target_pairs={{0,16},{4,20},{8,24},{12,28},{16,0},{20,4},{24,8},{28,12},{1,17},{... | collective-permute-start | bytes 221192 | tf_op jit(solution)/shard_map/ppermute | solution.py:513
  61.5 1.3 %collective-permute-start.16 = (bf16[288,128]{1,0:T(8,128)(2,1)S(1)}, bf16[288,128]{1,0:T(8,128)(2,1)S(1)}, u32[]{:S(2)}, u32[]{:S(2)}) collective-permute-start(bf16[288,128]{1,0:T(8,128)(2,1)S(1)} %add_convert_fusion.1), channel_id=1, source_target_pairs={{0,8},{4,12},{8,0},{12,4},{16,24},{20,28},{24,16},{28,20},{1,9},{5... | collective-permute-start | bytes 221192 | tf_op jit(solution)/shard_map/ppermute | solution.py:513
  62.7 1.9 %collective-permute-done.18 = bf16[288,128]{1,0:T(8,128)(2,1)S(1)} collective-permute-done((bf16[288,128]{1,0:T(8,128)(2,1)S(1)}, bf16[288,128]{1,0:T(8,128)(2,1)S(1)}, u32[]{:S(2)}, u32[]{:S(2)}) %collective-permute-start.18) | collective-permute-done | bytes 73760 | tf_op jit(solution)/shard_map/ppermute | solution.py:513
  65.9 1.6 %collective-permute-done.19.got_ref = bf16[4,288,128]{2,1,0:T(8,128)(2,1)S(1)} collective-permute-done((bf16[4,288,128]{2,1,0:T(8,128)(2,1)S(1)}, bf16[4,288,128]{2,1,0:T(8,128)(2,1)S(1)}, u32[]{:S(2)}, u32[]{:S(2)}) %collective-permute-start.19) | collective-permute-done | bytes 294944 | tf_op jit(solution)/shard_map/ppermute | solution.py:516
  67.5 1.7 %shard_map.64 = (f32[64,864]{1,0:T(8,128)}, f32[1728,128]{1,0:T(8,128)}) custom-call(s32[2]{0:T(128)S(1)} %pad_add_fusion.place_ref, bf16[4,288,128]{2,1,0:T(8,128)(2,1)S(1)} %pad_maximum_fusion.keep_ref, bf16[4,288,128]{2,1,0:T(8,128)(2,1)S(1)} %collective-permute-done.19.got_ref), custom_call_target="tpu_custom_call" | custom-call | tf_op jit(solution)/shard_map/pallas_call | solution.py:527
  (41 shorter events, 11.9 us)
Async XLA Ops:
  0.7 1.2 %copy-start = (bf16[32,16,1024]{2,1,0:T(8,128)(2,1)S(1)}, bf16[32,16,1024]{2,1,0:T(8,128)(2,1)}, u32[]{:S(2)}) copy-start(bf16[32,16,1024]{2,1,0:T(8,128)(2,1)} %vol_ref.3) | copy-start | bytes 3145732
  4.0 12.5 %collective-permute-start.1 = (bf16[34,4,1024]{2,1,0:T(4,128)(2,1)S(1)}, bf16[34,4,1024]{2,1,0:T(4,128)(2,1)S(1)}, u32[]{:S(2)}, u32[]{:S(2)}) collective-permute-start(bf16[34,4,1024]{2,1,0:T(4,128)(2,1)S(1)} %get-tuple-element.25), channel_id=1, source_target_pairs={{0,4},{8,12},{4,0},{12,8},{1,5},{9,13},{5,1},{13,9},{2,6},{10,14},... | collective-permute-start | bytes 835592 | tf_op jit(solution)/shard_map/ppermute | solution.py:484
  4.5 12.0 %collective-permute-start.2 = (bf16[34,4,1024]{2,1,0:T(4,128)(2,1)S(1)}, bf16[34,4,1024]{2,1,0:T(4,128)(2,1)S(1)}, u32[]{:S(2)}, u32[]{:S(2)}) collective-permute-start(bf16[34,4,1024]{2,1,0:T(4,128)(2,1)S(1)} %get-tuple-element.26), channel_id=1, source_target_pairs={{4,8},{8,4},{0,0},{12,12},{5,9},{9,5},{1,1},{13,13},{6,10},{10,6},... | collective-permute-start | bytes 835592 | tf_op jit(solution)/shard_map/ppermute | solution.py:487
  5.2 11.3 %collective-permute-start = (bf16[5,16,1024]{2,1,0:T(8,128)(2,1)S(1)}, bf16[5,16,1024]{2,1,0:T(8,128)(2,1)S(1)}, u32[]{:S(2)}, u32[]{:S(2)}) collective-permute-start(bf16[5,16,1024]{2,1,0:T(8,128)(2,1)S(1)} %get-tuple-element.24), channel_id=1, source_target_pairs={{0,16},{16,0},{1,17},{17,1},{2,18},{18,2},{3,19},{19,3},{4,20},{20... | collective-permute-start | bytes 491528 | tf_op jit(solution)/shard_map/ppermute | solution.py:486
  7.8 6.4 %collective-permute-start.3 = (bf16[5,4,1024]{2,1,0:T(4,128)(2,1)S(1)}, bf16[5,4,1024]{2,1,0:T(4,128)(2,1)S(1)}, u32[]{:S(2)}, u32[]{:S(2)}) collective-permute-start(bf16[5,4,1024]{2,1,0:T(4,128)(2,1)S(1)} %get-tuple-element.27), channel_id=1, source_target_pairs={{0,20},{8,28},{4,16},{12,24},{16,4},{24,12},{20,0},{28,8},{1,21},{... | collective-permute-start | bytes 122888 | tf_op jit(solution)/shard_map/ppermute | solution.py:478
  10.4 5.3 %collective-permute-start.4 = (bf16[5,4,1024]{2,1,0:T(4,128)(2,1)S(1)}, bf16[5,4,1024]{2,1,0:T(4,128)(2,1)S(1)}, u32[]{:S(2)}, u32[]{:S(2)}) collective-permute-start(bf16[5,4,1024]{2,1,0:T(4,128)(2,1)S(1)} %get-tuple-element.28), channel_id=1, source_target_pairs={{4,24},{8,20},{0,16},{12,28},{20,8},{24,4},{16,0},{28,12},{5,25},{... | collective-permute-start | bytes 122888 | tf_op jit(solution)/shard_map/ppermute | solution.py:478
  14.2 16.8 %collective-permute-start.5 = (bf16[34,16,128]{2,1,0:T(8,128)(2,1)S(1)}, bf16[34,16,128]{2,1,0:T(8,128)(2,1)S(1)}, u32[]{:S(2)}, u32[]{:S(2)}) collective-permute-start(bf16[34,16,128]{2,1,0:T(8,128)(2,1)S(1)} %get-tuple-element.36), channel_id=1, source_target_pairs={{0,1},{2,3},{1,0},{3,2},{4,5},{6,7},{5,4},{7,6},{8,9},{10,11},{9,8... | collective-permute-start | bytes 417800 | tf_op jit(solution)/shard_map/ppermute | solution.py:481
  15.8 15.2 %collective-permute-start.6 = (bf16[34,16,128]{2,1,0:T(8,128)(2,1)S(1)}, bf16[34,16,128]{2,1,0:T(8,128)(2,1)S(1)}, u32[]{:S(2)}, u32[]{:S(2)}) collective-permute-start(bf16[34,16,128]{2,1,0:T(8,128)(2,1)S(1)} %get-tuple-element.37), channel_id=1, source_target_pairs={{1,2},{2,1},{0,0},{3,3},{5,6},{6,5},{4,4},{7,7},{9,10},{10,9},{8,8... | collective-permute-start | bytes 417800 | tf_op jit(solution)/shard_map/ppermute | solution.py:481
  16.5 14.5 %copy-start.5 = (bf16[8,4,1024]{2,1,0:T(4,128)(2,1)S(1)}, bf16[8,4,1024]{2,1,0:T(4,128)(2,1)}, u32[]{:S(2)}) copy-start(bf16[8,4,1024]{2,1,0:T(4,128)(2,1)} %cot_ref.3) | copy-start | bytes 196612
  17.3 13.7 %collective-permute-start.7 = (bf16[46,8,128]{2,1,0:T(8,128)(2,1)S(1)}, bf16[46,8,128]{2,1,0:T(8,128)(2,1)S(1)}, u32[]{:S(2)}, u32[]{:S(2)}) collective-permute-start(bf16[46,8,128]{2,1,0:T(8,128)(2,1)S(1)} %get-tuple-element.38), channel_id=1, source_target_pairs={{0,1},{2,3},{1,0},{3,2},{4,5},{6,7},{5,4},{7,6},{8,9},{10,11},{9,8... | collective-permute-start | bytes 282632 | tf_op jit(solution)/shard_map/ppermute | solution.py:481
  21.8 9.2 %collective-permute-start.8 = (bf16[46,8,128]{2,1,0:T(8,128)(2,1)S(1)}, bf16[46,8,128]{2,1,0:T(8,128)(2,1)S(1)}, u32[]{:S(2)}, u32[]{:S(2)}) collective-permute-start(bf16[46,8,128]{2,1,0:T(8,128)(2,1)S(1)} %get-tuple-element.39), channel_id=1, source_target_pairs={{1,2},{2,1},{0,0},{3,3},{5,6},{6,5},{4,4},{7,7},{9,10},{10,9},{8,8... | collective-permute-start | bytes 282632 | tf_op jit(solution)/shard_map/ppermute | solution.py:481
  22.4 1.0 %copy-start.2 = (bf16[128,1728]{0,1:T(8,128)(2,1)S(1)}, bf16[128,1728]{0,1:T(8,128)(2,1)}, u32[]{:S(2)}) copy-start(bf16[128,1728]{0,1:T(8,128)(2,1)} %param.6) | copy-start | bytes 1327108
  25.0 1.2 %copy-start.1 = (bf16[32,16,1024]{2,1,0:T(8,128)(2,1)S(1)}, bf16[32,16,1024]{2,1,0:T(8,128)(2,1)}, u32[]{:S(2)}) copy-start(bf16[32,16,1024]{2,1,0:T(8,128)(2,1)} %vol_ref.3) | copy-start | bytes 3145732
  39.0 1.6 %collective-permute-start.9 = (bf16[4,288,128]{2,1,0:T(8,128)(2,1)S(1)}, bf16[4,288,128]{2,1,0:T(8,128)(2,1)S(1)}, u32[]{:S(2)}, u32[]{:S(2)}) collective-permute-start(bf16[4,288,128]{2,1,0:T(8,128)(2,1)S(1)} %get-tuple-element.43), channel_id=1, source_target_pairs={{0,4},{4,0},{8,12},{12,8},{16,20},{20,16},{24,28},{28,24},{1,5},{5... | collective-permute-start | bytes 884744 | tf_op jit(solution)/shard_map/ppermute | solution.py:516
  40.8 4.4 %collective-permute-start.10 = (bf16[288,128]{1,0:T(8,128)(2,1)S(1)}, bf16[288,128]{1,0:T(8,128)(2,1)S(1)}, u32[]{:S(2)}, u32[]{:S(2)}) collective-permute-start(bf16[288,128]{1,0:T(8,128)(2,1)S(1)} %get-tuple-element.46), channel_id=1, source_target_pairs={{0,8},{4,12},{8,0},{12,4},{16,24},{20,28},{24,16},{28,20},{1,9},{5... | collective-permute-start | bytes 221192 | tf_op jit(solution)/shard_map/ppermute | solution.py:513
  42.3 6.3 %collective-permute-start.12 = (bf16[288,128]{1,0:T(8,128)(2,1)S(1)}, bf16[288,128]{1,0:T(8,128)(2,1)S(1)}, u32[]{:S(2)}, u32[]{:S(2)}) collective-permute-start(bf16[288,128]{1,0:T(8,128)(2,1)S(1)} %get-tuple-element.47), channel_id=1, source_target_pairs={{0,24},{4,28},{8,16},{12,20},{16,8},{20,12},{24,0},{28,4},{1,25},{... | collective-permute-start | bytes 221192 | tf_op jit(solution)/shard_map/ppermute | solution.py:513
  44.6 5.0 %collective-permute-start.11 = (bf16[288,128]{1,0:T(8,128)(2,1)S(1)}, bf16[288,128]{1,0:T(8,128)(2,1)S(1)}, u32[]{:S(2)}, u32[]{:S(2)}) collective-permute-start(bf16[288,128]{1,0:T(8,128)(2,1)S(1)} %get-tuple-element.48), channel_id=1, source_target_pairs={{0,16},{4,20},{8,24},{12,28},{16,0},{20,4},{24,8},{28,12},{1,17},{... | collective-permute-start | bytes 221192 | tf_op jit(solution)/shard_map/ppermute | solution.py:513
  49.7 7.0 %collective-permute-start.15 = (bf16[288,128]{1,0:T(8,128)(2,1)S(1)}, bf16[288,128]{1,0:T(8,128)(2,1)S(1)}, u32[]{:S(2)}, u32[]{:S(2)}) collective-permute-start(bf16[288,128]{1,0:T(8,128)(2,1)S(1)} %fusion.1), channel_id=1, source_target_pairs={{0,3},{1,2},{2,1},{3,0},{4,7},{5,6},{6,5},{7,4},{8,11},{9,10},{10,... | collective-permute-start | bytes 221192 | tf_op jit(solution)/shard_map/ppermute | solution.py:519
  50.6 8.5 %collective-permute-start.14 = (bf16[288,128]{1,0:T(8,128)(2,1)S(1)}, bf16[288,128]{1,0:T(8,128)(2,1)S(1)}, u32[]{:S(2)}, u32[]{:S(2)}) collective-permute-start(bf16[288,128]{1,0:T(8,128)(2,1)S(1)} %fusion.1), channel_id=1, source_target_pairs={{0,2},{1,3},{2,0},{3,1},{4,6},{5,7},{6,4},{7,5},{8,10},{9,11},{10,... | collective-permute-start | bytes 221192 | tf_op jit(solution)/shard_map/ppermute | solution.py:519
  52.5 6.6 %collective-permute-start.13 = (bf16[288,128]{1,0:T(8,128)(2,1)S(1)}, bf16[288,128]{1,0:T(8,128)(2,1)S(1)}, u32[]{:S(2)}, u32[]{:S(2)}) collective-permute-start(bf16[288,128]{1,0:T(8,128)(2,1)S(1)} %fusion.1), channel_id=1, source_target_pairs={{0,1},{1,0},{2,3},{3,2},{4,5},{5,4},{6,7},{7,6},{8,9},{9,8},{10,11... | collective-permute-start | bytes 221192 | tf_op jit(solution)/shard_map/ppermute | solution.py:519
  59.2 5.4 %collective-permute-start.18 = (bf16[288,128]{1,0:T(8,128)(2,1)S(1)}, bf16[288,128]{1,0:T(8,128)(2,1)S(1)}, u32[]{:S(2)}, u32[]{:S(2)}) collective-permute-start(bf16[288,128]{1,0:T(8,128)(2,1)S(1)} %add_convert_fusion.1), channel_id=1, source_target_pairs={{0,24},{4,28},{8,16},{12,20},{16,8},{20,12},{24,0},{28,4},{1,25},{... | collective-permute-start | bytes 221192 | tf_op jit(solution)/shard_map/ppermute | solution.py:513
  60.0 5.1 %collective-permute-start.17 = (bf16[288,128]{1,0:T(8,128)(2,1)S(1)}, bf16[288,128]{1,0:T(8,128)(2,1)S(1)}, u32[]{:S(2)}, u32[]{:S(2)}) collective-permute-start(bf16[288,128]{1,0:T(8,128)(2,1)S(1)} %add_convert_fusion.1), channel_id=1, source_target_pairs={{0,16},{4,20},{8,24},{12,28},{16,0},{20,4},{24,8},{28,12},{1,17},{... | collective-permute-start | bytes 221192 | tf_op jit(solution)/shard_map/ppermute | solution.py:513
  61.5 4.4 %collective-permute-start.16 = (bf16[288,128]{1,0:T(8,128)(2,1)S(1)}, bf16[288,128]{1,0:T(8,128)(2,1)S(1)}, u32[]{:S(2)}, u32[]{:S(2)}) collective-permute-start(bf16[288,128]{1,0:T(8,128)(2,1)S(1)} %add_convert_fusion.1), channel_id=1, source_target_pairs={{0,8},{4,12},{8,0},{12,4},{16,24},{20,28},{24,16},{28,20},{1,9},{5... | collective-permute-start | bytes 221192 | tf_op jit(solution)/shard_map/ppermute | solution.py:513
  65.9 1.6 %collective-permute-start.19 = (bf16[4,288,128]{2,1,0:T(8,128)(2,1)S(1)}, bf16[4,288,128]{2,1,0:T(8,128)(2,1)S(1)}, u32[]{:S(2)}, u32[]{:S(2)}) collective-permute-start(bf16[4,288,128]{2,1,0:T(8,128)(2,1)S(1)} %pad_maximum_fusion.keep_ref), channel_id=1, source_target_pairs={{0,4},{4,0},{8,12},{12,8},{16,20},{20,16},{24,28},{28,24},{1,5},{5... | collective-permute-start | bytes 884744 | tf_op jit(solution)/shard_map/ppermute | solution.py:516
  (2 other events, 1.7 us)
where the time goes:
time: 69.5 us; the launch traced here: 69.2 us
  starting transfers between devices  27.3 us (39%)
  waiting for transfers between devices  18.4 us (26%)
  Pallas kernels  17 us (24%)
  local copies, waits for them, and re-layouts  5.3 us (8%)
  between operations  0.86 us (1%)
    ppermute x6, waiting for transfers between devices, to_square(): return lax.ppermute(block, ('depth', 'row'), route)  8.06 us
    pallas_call x1, Pallas kernels, local_grads(): pl.pallas_call(body, out_shape=[jax.ShapeDtypeStruct((squares, rows // (2...  7.99 us
    ppermute x6, starting transfers between devices, to_square(): return lax.ppermute(block, ('depth', 'row'), route)  7.41 us
    ppermute x4, starting transfers between devices, to_col(): return lax.ppermute(block, 'col', pairs_on_line(cols, kind))  7.35 us
    unnamed x12, local copies, waits for them, and re-layouts  5.2 us
    ppermute x3, waiting for transfers between devices, along_col(): return lax.ppermute(block, 'col', [(i, i ^ n) for i in range(cols)])  5.02 us
    pallas_call x1, Pallas kernels, local_grads(): pl.pallas_call(own_blocks, out_shape=[jax.ShapeDtypeStruct((3, planes + 9...  4.72 us
    ppermute x3, starting transfers between devices, along_col(): return lax.ppermute(block, 'col', [(i, i ^ n) for i in range(cols)])  4.45 us
  transfers between devices with their start and end apart: 20, of which 11 were waited for; matrix products, arithmetic and copies ran while one was open for 0% of the time, Pallas kernels for 9%

commit v1 on v0

--- a/solution.py
+++ b/solution.py
@@ -7,6 +7,7 @@
 
 LANES = 128
 SECOND_ROWS = 27 * 64
+FIRST_BLOCKS = 7
 F32 = jnp.float32
 BF16 = jnp.bfloat16
 
@@ -18,6 +19,14 @@
     return swapped + [(i, i) for i in range(count) if i not in met]
 
 
+def pairs_of_lines(lines, count, kind):
+    route = []
+    for line in range(lines):
+        for i, j in pairs_on_line(count, kind):
+            route.append((line * count + i, (line ^ 1 if i == j else line) * count + j))
+    return route
+
+
 def add_up(*terms):
     terms = [term.astype(F32) for term in terms]
     while len(terms) > 1:
@@ -29,34 +38,41 @@
     return lax.dot_general(left, right, (((1,), (0,)), ((), ())), preferred_element_type=F32)
 
 
-def pack(flag_ref, vol_ref, cot_ref, dep_ref, row_a_ref, row_b_ref, edge_a_ref, edge_b_ref, col_a_ref, col_b_ref):
-    first_plane, row_even, col_even = flag_ref[0] == 0, flag_ref[1] == 0, flag_ref[2] == 0
+def bring(flag_ref, vol_hbm, cot_hbm, vol_ref, cot_ref, dep_ref, arrived):
+    first_plane = flag_ref[0] == 0
+    planes = vol_ref.shape[0]
+    inner = pl.ds(4, planes - 8)
+    copies = [pltpu.make_async_copy(cot_hbm, cot_ref, arrived.at[0])]
+    for n, part in enumerate((pl.ds(0, 4), pl.ds(planes - 4, 4), inner)):
+        copies.append(pltpu.make_async_copy(vol_hbm.at[part], vol_ref.at[part], arrived.at[1 + n]))
+    for copy in copies:
+        copy.start()
+    for copy in copies[:3]:
+        copy.wait()
+    dep_ref[16] = cot_ref[0]
+    for q in range(4):
+        block = jnp.where(first_plane, vol_ref[planes - 4 + q].astype(F32), vol_ref[q].astype(F32))
+        for g in range(4):
+            dep_ref[4 * q + g] = block[4 * g : 4 * g + 4].astype(BF16)
+    copies[3].wait()
+
+
+def pack(
+    flag_ref, vol_ref, cot_ref, first_hbm, second_hbm, row_a_ref, row_b_ref, col_a_ref, col_b_ref,
+    first_ref, second_ref, arrived,
+):
+    row_even, col_even = flag_ref[1] == 0, flag_ref[2] == 0
     row_inner, col_inner = flag_ref[3] != 0, flag_ref[4] != 0
     planes, high, width = vol_ref.shape
     cots = cot_ref.shape[0]
-
-    def rows(block, a_ref, b_ref, n):
-        low, top = block[:4], block[high - 4 :]
-        a_ref[n] = jnp.where(row_even, top, low).astype(BF16)
-        b_ref[n] = jnp.where(row_inner, jnp.where(row_even, low, top), 0.0).astype(BF16)
-
-    def plane(d, carry):
-        block = vol_ref[d].astype(F32)
-        rows(block, row_a_ref, row_b_ref, d)
-        left, right = block[:, :LANES], block[:, width - LANES :]
-        col_a_ref[d] = jnp.where(col_even, right, left).astype(BF16)
-        col_b_ref[d] = jnp.where(col_inner, jnp.where(col_even, left, right), 0.0).astype(BF16)
-        return carry
-
-    lax.fori_loop(0, planes, plane, 0)
-    for q in range(4):
-        block = jnp.where(first_plane, vol_ref[planes - 4 + q].astype(F32), vol_ref[q].astype(F32))
-        dep_ref[q] = block.astype(BF16)
-        rows(block, edge_a_ref, edge_b_ref, q)
+    copies = [
+        pltpu.make_async_copy(first_hbm, first_ref, arrived.at[0]),
+        pltpu.make_async_copy(second_hbm, second_ref, arrived.at[1]),
+    ]
+    for copy in copies:
+        copy.start()
+
     cot = cot_ref[...].astype(F32)
-    dep_ref[4] = jnp.concatenate([cot[0]] * 4, axis=0).astype(BF16)
-    edge_a_ref[4] = cot[0].astype(BF16)
-    edge_b_ref[4] = jnp.where(row_inner, cot[0], 0.0).astype(BF16)
     for g in range(cots // 4):
         tops = jnp.concatenate([cot[4 * g + n, :1] for n in range(4)], axis=0)
         row_a_ref[planes + g] = tops.astype(BF16)
@@ -65,6 +81,20 @@
         col_a_ref[planes + g] = side.astype(BF16)
         col_b_ref[planes + g] = jnp.where(col_inner, side, 0.0).astype(BF16)
 
+    def plane(d, carry):
+        block = vol_ref[d].astype(F32)
+        low, top = block[:4], block[high - 4 :]
+        row_a_ref[d] = jnp.where(row_even, top, low).astype(BF16)
+        row_b_ref[d] = jnp.where(row_inner, jnp.where(row_even, low, top), 0.0).astype(BF16)
+        left, right = block[:, :LANES], block[:, width - LANES :]
+        col_a_ref[d] = jnp.where(col_even, right, left).astype(BF16)
+        col_b_ref[d] = jnp.where(col_inner, jnp.where(col_even, left, right), 0.0).astype(BF16)
+        return carry
+
+    lax.fori_loop(0, planes, plane, 0, unroll=2)
+    for copy in copies:
+        copy.wait()
+
 
 def pack_corners(flag_ref, dep_ref, row_a_ref, row_b_ref, edge_a_ref, edge_b_ref, col_a_ref, col_b_ref):
     row_even, col_even, col_inner = flag_ref[1] == 0, flag_ref[2] == 0, flag_ref[4] != 0
@@ -91,16 +121,19 @@
     lax.fori_loop(0, planes, plane, 0)
     for q in range(4):
         lower_upper(edge_a_ref, edge_b_ref, q, planes + q)
-        left, right = [dep_ref[q, :, lanes].astype(F32) for lanes in faces]
         for n in range(2):
-            store(planes + 4 + 2 * q + n, left[8 * n : 8 * n + 8], right[8 * n : 8 * n + 8])
+            units = range(4 * q + 2 * n, 4 * q + 2 * n + 2)
+            store(
+                planes + 4 + 2 * q + n,
+                *[jnp.concatenate([dep_ref[u, :, lanes].astype(F32) for u in units], axis=0) for lanes in faces],
+            )
     lanes = faces[0]
     tops = [
         jnp.where(row_even, row_a_ref[g, :, lanes].astype(F32), row_b_ref[g, :, lanes].astype(F32))
         for g in range(planes, groups)
     ]
     corner = jnp.where(row_even, edge_a_ref[4, :, lanes].astype(F32), edge_b_ref[4, :, lanes].astype(F32))
-    own = dep_ref[4, :, lanes].astype(F32)[:4]
+    own = dep_ref[16, :, lanes].astype(F32)
     for n, values in enumerate((jnp.concatenate(tops, axis=0), jnp.concatenate([own, corner], axis=0))):
         col_a_ref[planes + 12 + n] = values.astype(BF16)
         col_b_ref[planes + 12 + n] = jnp.where(col_inner, values, 0.0).astype(BF16)
@@ -174,7 +207,8 @@
 
     def place_halo(target, q, keep):
         place(
-            target % 2, target, lambda lanes: dep_ref[q, :, lanes],
+            target % 2, target,
+            lambda lanes: jnp.concatenate([dep_ref[4 * q + g, :, lanes].astype(F32) for g in range(4)], axis=0),
             lambda lanes: edge_a_ref[q, :, lanes], lambda lanes: edge_b_ref[q, :, lanes], keep,
         )
 
@@ -277,7 +311,7 @@
     for k in range(blocks):
         lanes = slice(k * LANES, (k + 1) * LANES)
         ups[0:half_planes, k, 1:5, :] = cot_ref[:, :, lanes].astype(F32)
-        ups[half_planes, k, 1:5, :] = jnp.where(first_plane, dep_ref[4, 0:4, lanes].astype(F32), 0.0)
+        ups[half_planes, k, 1:5, :] = jnp.where(first_plane, dep_ref[16, :, lanes].astype(F32), 0.0)
         for g in range(half_planes // 4):
             tops = ahead(row_even, row_a_ref[planes + g, :, lanes], row_b_ref[planes + g, :, lanes])
             for n in range(4):
@@ -376,6 +410,7 @@
                 found.append(rim_tiles[b, index, 0] if m == 0 else tiles[b, index, m - 1])
         return jnp.concatenate(found, axis=0)
 
+    grads = []
     for tap in range(0, 9, 2):
         right = [first_taps(x) for x in range(tap, min(tap + 2, 9))]
         found = matmul(left_one, jnp.concatenate(right, axis=1))
@@ -383,9 +418,15 @@
             main = found[:LANES, n * LANES : (n + 1) * LANES]
             prev = found[LANES : LANES + 64, n * LANES : (n + 1) * LANES]
             even = jnp.concatenate([prev[:, 96:], main[:64, :64]], axis=1)
-            grad = jnp.concatenate([even + main[64:, 32:], jnp.zeros((64, 32), F32)], axis=1)
-            row = SECOND_ROWS + (tap + n) * 64
-            out_ref[row : row + 64, :] = grad
+            grads.append(even + main[64:, 32:])
+    grads.append(jnp.zeros((64, FIRST_BLOCKS * LANES - 9 * 96), F32))
+    first = jnp.concatenate(grads, axis=1)
+    for n in range(FIRST_BLOCKS):
+        row = SECOND_ROWS + 64 * n
+        out_ref[row : row + 64, :] = first[:, n * LANES : (n + 1) * LANES]
+    used = SECOND_ROWS + 64 * FIRST_BLOCKS
+    if out_ref.shape[0] > used:
+        out_ref[used:, :] = jnp.zeros((out_ref.shape[0] - used, LANES), F32)
 
     core, square = place_ref[0], place_ref[1]
     squares, size = keep_ref.shape[0], keep_ref.shape[1]
@@ -402,8 +443,8 @@
         for ref, half in ((keep_ref, core), (got_ref, 1 - core)):
             start = pl.multiple_of((half * squares + (square ^ n)) * size, 8)
             sums[pl.ds(start, size), :] = ref[n].astype(F32)
-    first = sums[SECOND_ROWS:, :]
-    g1_ref[...] = jnp.concatenate([first[tap * 64 : (tap + 1) * 64, :96] for tap in range(9)], axis=1)
+    first = [sums[SECOND_ROWS + 64 * n : SECOND_ROWS + 64 * (n + 1), :] for n in range(FIRST_BLOCKS)]
+    g1_ref[...] = jnp.concatenate(first, axis=1)[:, : g1_ref.shape[1]]
     g2_ref[...] = sums[:SECOND_ROWS, :]
 
 
@@ -412,7 +453,8 @@
     blocks = volume.shape[2] // LANES
     hidden_planes = planes // 2 + 3
     out_planes = planes // 4
-    rows = SECOND_ROWS + 9 * 64
+    unit = 2 * squares * 16
+    rows = -(-(SECOND_ROWS + 64 * FIRST_BLOCKS) // unit) * unit
     whole = pl.BlockSpec(memory_space=pltpu.VMEM)
     smem = pl.BlockSpec(memory_space=pltpu.SMEM)
     dep, row_a, row_b, edge_a, edge_b = faces
@@ -463,28 +505,53 @@
     small = pltpu.CompilerParams(vmem_limit_bytes=12 * 1024 * 1024)
     planes, high, width = volume.shape
     groups = planes + cotangent.shape[0] // 4
-    faces = [(5, high, width)] + [(groups, 4, width)] * 2 + [(5, 4, width)] * 2 + [(groups, high, LANES)] * 2
-    dep, row_a, row_b, edge_a, edge_b, side_a, side_b = pl.pallas_call(
+    in_hbm = pl.BlockSpec(memory_space=pltpu.HBM)
+
+    def stay(argument):
+        return pltpu.with_memory_space_constraint(argument, pltpu.HBM)
+
+    volume, cotangent, dep = pl.pallas_call(
+        bring,
+        out_shape=[jax.ShapeDtypeStruct(shape, BF16) for shape in (volume.shape, cotangent.shape, (17, 4, width))],
+        in_specs=[smem] + [in_hbm] * 2,
+        out_specs=[whole] * 3,
+        scratch_shapes=[pltpu.SemaphoreType.DMA((4,))],
+        compiler_params=small,
+    )(flags, stay(volume), stay(cotangent))
+    weights = (first_weight, second_weight.T)
+    shapes = [(groups, 4, width)] * 2 + [(groups, high, LANES)] * 2
+    shapes += [weight.shape for weight in weights]
+    row_a, row_b, side_a, side_b, first_taps, second_taps = pl.pallas_call(
         pack,
-        out_shape=[jax.ShapeDtypeStruct(shape, BF16) for shape in faces],
-        in_specs=[smem] + [whole] * 2,
-        out_specs=[whole] * 7,
+        out_shape=[jax.ShapeDtypeStruct(shape, BF16) for shape in shapes],
+        in_specs=[smem] + [whole] * 2 + [in_hbm] * 2,
+        out_specs=[whole] * len(shapes),
+        scratch_shapes=[pltpu.SemaphoreType.DMA((2,))],
         compiler_params=small,
-    )(flags, volume, cotangent)
-
-    def to_edge(block, kind):
-        line = pairs_on_line(rows, kind)
-        route = [(d * rows + i, (1 - d) * rows + j) for d in (0, 1) for i, j in line]
-        return lax.ppermute(block, ("depth", "row"), route)
+    )(flags, volume, cotangent, *[stay(weight) for weight in weights])
 
     def to_col(block, kind):
-        return lax.ppermute(block, "col", pairs_on_line(cols, kind))
-
-    edge_a, edge_b = to_edge(edge_a, 0), to_edge(edge_b, 1)
+        return lax.ppermute(block, ("row", "col"), pairs_of_lines(rows, cols, kind))
+
+    dep = lax.ppermute(dep, "depth", [(0, 1), (1, 0)])
     row_a = lax.ppermute(row_a, "row", pairs_on_line(rows, 0))
+    row_b = lax.ppermute(row_b, "row", pairs_on_line(rows, 1))
+    row_a, side_a, side_b = lax.optimization_barrier((row_a, side_a, side_b))
     side_a, side_b = to_col(side_a, 0), to_col(side_b, 1)
-    dep = lax.ppermute(dep, "depth", [(0, 1), (1, 0)])
-    row_b = lax.ppermute(row_b, "row", pairs_on_line(rows, 1))
+
+    low, top = [jnp.concatenate([dep[n : n + 1] for n in (*range(k, 16, 4), 16)], axis=0) for k in (0, 3)]
+    even, ends = row % 2 == 0, jnp.logical_or(row == 0, row == rows - 1)
+    edge_a = jnp.where(even, top, low)
+    edge_b = jnp.where(ends, 0, jnp.where(even, low, top))
+    edge_a = lax.ppermute(edge_a, "row", pairs_on_line(rows, 0))
+    edge_b = lax.ppermute(edge_b, ("depth", "row"), pairs_of_lines(2, rows, 1))
+    weights = pl.pallas_call(
+        bands,
+        out_shape=[jax.ShapeDtypeStruct(shape, BF16) for shape in ((1152, 256), (1152, 256), (9, 256, 128))],
+        in_specs=[whole] * 2,
+        out_specs=[whole] * 3,
+        compiler_params=small,
+    )(first_taps, second_taps)
     col_a, col_b = pl.pallas_call(
         pack_corners,
         out_shape=[jax.ShapeDtypeStruct((planes + 14, 8, LANES), BF16)] * 2,
@@ -492,16 +559,9 @@
         out_specs=[whole] * 2,
         compiler_params=small,
     )(flags, dep, row_a, row_b, edge_a, edge_b)
-    col_a, col_b, first_taps, second_taps = lax.optimization_barrier((col_a, col_b, first_weight, second_weight.T))
+    col_a, col_b, volume = lax.optimization_barrier((col_a, col_b, volume))
     col_a, col_b = to_col(col_a, 0), to_col(col_b, 1)
 
-    weights = pl.pallas_call(
-        bands,
-        out_shape=[jax.ShapeDtypeStruct(shape, BF16) for shape in ((1152, 256), (1152, 256), (9, 256, 128))],
-        in_specs=[whole] * 2,
-        out_specs=[whole] * 3,
-        compiler_params=small,
-    )(first_taps, second_taps)
     spot = lax.axis_index(("depth", "row"))
     squares = lax.axis_size(("depth", "row")) // 2
     where = jnp.stack([spot % 2, spot // 2])

time: 69.5 us -> 61.3 us (0.88)
  local copies, waits for them, and re-layouts: 5.3 us -> 0.18 us
  starting transfers between devices: 27.3 us -> 23.2 us
  Pallas kernels: 17 us -> 19.4 us
  waiting for transfers between devices: 18.4 us -> 17.2 us
    unnamed x12 -> x4, local copies, waits for them, and re-layouts: 5.2 us -> 0.04 us
    ppermute x6, starting transfers between devices: 11.5 us -> 7.57 us  [the longest x4 5.26 us: to_col(): return lax.ppermute(block, ('row', 'col'), pairs_of_lines(rows, cols, kind))]
    ppermute x6, waiting for transfers between devices: 2.17 us -> 0.02 us  [the longest x4 0.01 us: to_col(): return lax.ppermute(block, ('row', 'col'), pairs_of_lines(rows, cols, kind))]
    pallas_call x0 -> x1, Pallas kernels: none -> 1.88 us  [shards(): pl.pallas_call(bring, out_shape=[jax.ShapeDtypeStruct(shape, BF16) for sh...]
    ppermute x1, waiting for transfers between devices: 0.01 us -> 1.23 us  [shards(): dep = lax.ppermute(dep, 'depth', [(0, 1), (1, 0)])]
  transfers between devices with their start and end apart: 20 -> 20, of which waited for: 11 -> 11; matrix products, arithmetic and copies ran while one was open for 0% -> 0% of each run, Pallas kernels for 9% -> 13%
where the time goes in v1:
time: 61.3 us; the launch traced here: 61.1 us
  starting transfers between devices  23.2 us (38%)
  Pallas kernels  19.4 us (32%)
  waiting for transfers between devices  17.2 us (28%)
  between operations  0.89 us (1%)
    ppermute x6, waiting for transfers between devices, to_square(): return lax.ppermute(block, ('depth', 'row'), route)  8.5 us
    pallas_call x1, Pallas kernels, local_grads(): pl.pallas_call(body, out_shape=[jax.ShapeDtypeStruct((squares, rows // (2...  7.98 us
    ppermute x6, starting transfers between devices, to_square(): return lax.ppermute(block, ('depth', 'row'), route)  7.13 us
    ppermute x4, starting transfers between devices, to_col(): return lax.ppermute(block, ('row', 'col'), pairs_of_lines(rows, cols, kind))  5.26 us
    pallas_call x1, Pallas kernels, local_grads(): pl.pallas_call(own_blocks, out_shape=[jax.ShapeDtypeStruct((3, planes + 9...  4.75 us
    ppermute x3, starting transfers between devices, along_col(): return lax.ppermute(block, 'col', [(i, i ^ n) for i in range(cols)])  4.45 us
    ppermute x3, waiting for transfers between devices, along_col(): return lax.ppermute(block, 'col', [(i, i ^ n) for i in range(cols)])  4.42 us
    ppermute x1, starting transfers between devices, shards(): dep = lax.ppermute(dep, 'depth', [(0, 1), (1, 0)])  3.03 us
  transfers between devices with their start and end apart: 20, of which 11 were waited for; matrix products, arithmetic and copies ran while one was open for 0% of the time, Pallas kernels for 13%

profile of v1, /device:TPU:0, one launch (start us, length us, event | category | flops | bytes accessed | tf_op | source)
XLA Modules:
  0.0 61.1 jit_solution(8064485313351938397)
XLA Ops:
  0.7 1.9 %shard_map.59 = (bf16[32,16,1024]{2,1,0:T(8,128)(2,1)S(1)}, bf16[8,4,1024]{2,1,0:T(4,128)(2,1)S(1)}, bf16[17,4,1024]{2,1,0:T(4,128)(2,1)S(1)}) custom-call(s32[5]{0:T(128)S(1)} %stack.58.flag_ref, bf16[32,16,1024]{2,1,0:T(8,128)(2,1)} %vol_hbm.1, bf16[8,4,1024]{2,1,0:T(4,128)(2,1)} %cot_hbm.1), custom_call_target="tpu_custom_call" | custom-call | tf_op jit(solution)/shard_map/pallas_call | solution.py:513
  2.6 3.0 %collective-permute-start = (bf16[17,4,1024]{2,1,0:T(4,128)(2,1)S(1)}, bf16[17,4,1024]{2,1,0:T(4,128)(2,1)S(1)}, u32[]{:S(2)}, u32[]{:S(2)}) collective-permute-start(bf16[17,4,1024]{2,1,0:T(4,128)(2,1)S(1)} %get-tuple-element.28), channel_id=1, source_target_pairs={{0,16},{16,0},{1,17},{17,1},{2,18},{18,2},{3,19},{19,3},{4,20},{20... | collective-permute-start | bytes 417800 | tf_op jit(solution)/shard_map/ppermute | solution.py:536
  5.7 1.6 %shard_map.60 = (bf16[34,4,1024]{2,1,0:T(4,128)(2,1)S(1)}, bf16[34,4,1024]{2,1,0:T(4,128)(2,1)S(1)}, bf16[34,16,128]{2,1,0:T(8,128)(2,1)S(1)}, bf16[34,16,128]{2...) custom-call(s32[5]{0:T(128)S(1)} %stack.58.flag_ref, ...), custom_call_target="tpu_custom_call" | custom-call | tf_op jit(solution)/shard_map/pallas_call | solution.py:524
  8.1 1.2 %collective-permute-done.dep_ref = bf16[17,4,1024]{2,1,0:T(4,128)(2,1)S(1)} collective-permute-done((bf16[17,4,1024]{2,1,0:T(4,128)(2,1)S(1)}, bf16[17,4,1024]{2,1,0:T(4,128)(2,1)S(1)}, u32[]{:S(2)}, u32[]{:S(2)}) %collective-permute-start) | collective-permute-done | bytes 139296 | tf_op jit(solution)/shard_map/ppermute | solution.py:536
  9.5 1.8 %collective-permute-start.4 = (bf16[5,4,1024]{2,1,0:T(4,128)(2,1)S(1)}, bf16[5,4,1024]{2,1,0:T(4,128)(2,1)S(1)}, u32[]{:S(2)}, u32[]{:S(2)}) collective-permute-start(bf16[5,4,1024]{2,1,0:T(4,128)(2,1)S(1)} %get-tuple-element.61), channel_id=1, source_target_pairs={{4,8},{8,4},{0,16},{12,28},{20,24},{24,20},{16,0},{28,12},{5,9},{9... | collective-permute-start | bytes 122888 | tf_op jit(solution)/shard_map/ppermute | solution.py:547
  12.6 1.6 %collective-permute-start.5 = (bf16[34,16,128]{2,1,0:T(8,128)(2,1)S(1)}, bf16[34,16,128]{2,1,0:T(8,128)(2,1)S(1)}, u32[]{:S(2)}, u32[]{:S(2)}) collective-permute-start(bf16[34,16,128]{2,1,0:T(8,128)(2,1)S(1)} %get-tuple-element.44), channel_id=1, source_target_pairs={{0,1},{2,3},{1,0},{3,2},{4,5},{6,7},{5,4},{7,6},{8,9},{10,11},{9,8... | collective-permute-start | bytes 417800 | tf_op jit(solution)/shard_map/ppermute | solution.py:534
  15.1 3.2 %collective-permute-start.7 = (bf16[46,8,128]{2,1,0:T(8,128)(2,1)S(1)}, bf16[46,8,128]{2,1,0:T(8,128)(2,1)S(1)}, u32[]{:S(2)}, u32[]{:S(2)}) collective-permute-start(bf16[46,8,128]{2,1,0:T(8,128)(2,1)S(1)} %get-tuple-element.46), channel_id=1, source_target_pairs={{0,1},{2,3},{1,0},{3,2},{4,5},{6,7},{5,4},{7,6},{8,9},{10,11},{9,8... | collective-permute-start | bytes 282632 | tf_op jit(solution)/shard_map/ppermute | solution.py:534
  18.7 4.8 %shard_map.63 = (bf16[3,41,8,16,128]{4,3,2,1,0:T(8,128)(2,1)S(1)}, f32[20,8,16,256]{3,2,1,0:T(8,128)S(1)}) custom-call(s32[5]{0:T(128)S(1)} %stack.58.flag_ref, bf16[32,16,1024]{2,1,0:T(8,128)(2,1)S(1)} %get-tuple-element.38.vol_ref, bf16[17,4,1024]{2,1,0:T(4,128)(2,1)S(1)} %collective-permute-done.dep_ref, ...), custom_call_target="tpu_custom_call" | custom-call | flops 2000000000 | bytes 10000000 | tf_op jit(solution)/shard_map/pallas_call | solution.py:461
  23.5 8.0 %shard_map.64 = (bf16[4,272,128]{2,1,0:T(8,128)(2,1)S(1)}, bf16[4,272,128]{2,1,0:T(8,128)(2,1)S(1)}) custom-call(s32[5]{0:T(128)S(1)} %stack.58.flag_ref, s32[2]{0:T(128)S(1)} %pad_add_fusion.place_ref, bf16[3,41,8,16,128]{4,3,2,1,0:T(8,128)(2,1)S(1)} %get-tuple-element.42.tiles, f32[20,8,16,256]{3,2,1,0:T(8,128)S(1)} %get-tuple-element.43.parts, ...), custom_call_target="tpu_custom_call" | custom-call | flops 4000000000 | bytes 10000000 | tf_op jit(solution)/shard_map/pallas_call | solution.py:486
  31.6 1.5 %collective-permute-done.9 = bf16[4,272,128]{2,1,0:T(8,128)(2,1)S(1)} collective-permute-done((bf16[4,272,128]{2,1,0:T(8,128)(2,1)S(1)}, bf16[4,272,128]{2,1,0:T(8,128)(2,1)S(1)}, u32[]{:S(2)}, u32[]{:S(2)}) %collective-permute-start.9) | collective-permute-done | bytes 278560 | tf_op jit(solution)/shard_map/ppermute | solution.py:576
  33.2 1.2 %collective-permute-start.10 = (bf16[272,128]{1,0:T(8,128)(2,1)S(1)}, bf16[272,128]{1,0:T(8,128)(2,1)S(1)}, u32[]{:S(2)}, u32[]{:S(2)}) collective-permute-start(bf16[272,128]{1,0:T(8,128)(2,1)S(1)} %get-tuple-element.54), channel_id=1, source_target_pairs={{0,8},{4,12},{8,0},{12,4},{16,24},{20,28},{24,16},{28,20},{1,9},{5... | collective-permute-start | bytes 208904 | tf_op jit(solution)/shard_map/ppermute | solution.py:573
  35.6 1.2 %collective-permute-start.11 = (bf16[272,128]{1,0:T(8,128)(2,1)S(1)}, bf16[272,128]{1,0:T(8,128)(2,1)S(1)}, u32[]{:S(2)}, u32[]{:S(2)}) collective-permute-start(bf16[272,128]{1,0:T(8,128)(2,1)S(1)} %get-tuple-element.56), channel_id=1, source_target_pairs={{0,16},{4,20},{8,24},{12,28},{16,0},{20,4},{24,8},{28,12},{1,17},{... | collective-permute-start | bytes 208904 | tf_op jit(solution)/shard_map/ppermute | solution.py:573
  36.8 1.4 %collective-permute-done.10 = bf16[272,128]{1,0:T(8,128)(2,1)S(1)} collective-permute-done((bf16[272,128]{1,0:T(8,128)(2,1)S(1)}, bf16[272,128]{1,0:T(8,128)(2,1)S(1)}, u32[]{:S(2)}, u32[]{:S(2)}) %collective-permute-start.10) | collective-permute-done | bytes 69664 | tf_op jit(solution)/shard_map/ppermute | solution.py:573
  38.1 1.5 %collective-permute-done.12 = bf16[272,128]{1,0:T(8,128)(2,1)S(1)} collective-permute-done((bf16[272,128]{1,0:T(8,128)(2,1)S(1)}, bf16[272,128]{1,0:T(8,128)(2,1)S(1)}, u32[]{:S(2)}, u32[]{:S(2)}) %collective-permute-start.12) | collective-permute-done | bytes 69664 | tf_op jit(solution)/shard_map/ppermute | solution.py:573
  39.7 1.3 %collective-permute-done.11 = bf16[272,128]{1,0:T(8,128)(2,1)S(1)} collective-permute-done((bf16[272,128]{1,0:T(8,128)(2,1)S(1)}, bf16[272,128]{1,0:T(8,128)(2,1)S(1)}, u32[]{:S(2)}, u32[]{:S(2)}) %collective-permute-start.11) | collective-permute-done | bytes 69664 | tf_op jit(solution)/shard_map/ppermute | solution.py:573
  41.0 1.8 %collective-permute-start.15 = (bf16[272,128]{1,0:T(8,128)(2,1)S(1)}, bf16[272,128]{1,0:T(8,128)(2,1)S(1)}, u32[]{:S(2)}, u32[]{:S(2)}) collective-permute-start(bf16[272,128]{1,0:T(8,128)(2,1)S(1)} %fusion.1), channel_id=1, source_target_pairs={{0,3},{1,2},{2,1},{3,0},{4,7},{5,6},{6,5},{7,4},{8,11},{9,10},{10,... | collective-permute-start | bytes 208904 | tf_op jit(solution)/shard_map/ppermute | solution.py:579
  42.8 1.8 %collective-permute-start.14 = (bf16[272,128]{1,0:T(8,128)(2,1)S(1)}, bf16[272,128]{1,0:T(8,128)(2,1)S(1)}, u32[]{:S(2)}, u32[]{:S(2)}) collective-permute-start(bf16[272,128]{1,0:T(8,128)(2,1)S(1)} %fusion.1), channel_id=1, source_target_pairs={{0,2},{1,3},{2,0},{3,1},{4,6},{5,7},{6,4},{7,5},{8,10},{9,11},{10,... | collective-permute-start | bytes 208904 | tf_op jit(solution)/shard_map/ppermute | solution.py:579
  45.5 2.5 %collective-permute-done.15 = bf16[272,128]{1,0:T(8,128)(2,1)S(1)} collective-permute-done((bf16[272,128]{1,0:T(8,128)(2,1)S(1)}, bf16[272,128]{1,0:T(8,128)(2,1)S(1)}, u32[]{:S(2)}, u32[]{:S(2)}) %collective-permute-start.15) | collective-permute-done | bytes 69664 | tf_op jit(solution)/shard_map/ppermute | solution.py:579
  47.9 1.9 %collective-permute-done.14 = bf16[272,128]{1,0:T(8,128)(2,1)S(1)} collective-permute-done((bf16[272,128]{1,0:T(8,128)(2,1)S(1)}, bf16[272,128]{1,0:T(8,128)(2,1)S(1)}, u32[]{:S(2)}, u32[]{:S(2)}) %collective-permute-start.14) | collective-permute-done | bytes 69664 | tf_op jit(solution)/shard_map/ppermute | solution.py:579
  49.9 2.8 %collective-permute-start.18 = (bf16[272,128]{1,0:T(8,128)(2,1)S(1)}, bf16[272,128]{1,0:T(8,128)(2,1)S(1)}, u32[]{:S(2)}, u32[]{:S(2)}) collective-permute-start(bf16[272,128]{1,0:T(8,128)(2,1)S(1)} %add_convert_fusion.1), channel_id=1, source_target_pairs={{0,24},{4,28},{8,16},{12,20},{16,8},{20,12},{24,0},{28,4},{1,25},{... | collective-permute-start | bytes 208904 | tf_op jit(solution)/shard_map/ppermute | solution.py:573
  53.5 1.7 %collective-permute-done.18 = bf16[272,128]{1,0:T(8,128)(2,1)S(1)} collective-permute-done((bf16[272,128]{1,0:T(8,128)(2,1)S(1)}, bf16[272,128]{1,0:T(8,128)(2,1)S(1)}, u32[]{:S(2)}, u32[]{:S(2)}) %collective-permute-start.18) | collective-permute-done | bytes 69664 | tf_op jit(solution)/shard_map/ppermute | solution.py:573
  55.2 1.8 %collective-permute-done.17 = bf16[272,128]{1,0:T(8,128)(2,1)S(1)} collective-permute-done((bf16[272,128]{1,0:T(8,128)(2,1)S(1)}, bf16[272,128]{1,0:T(8,128)(2,1)S(1)}, u32[]{:S(2)}, u32[]{:S(2)}) %collective-permute-start.17) | collective-permute-done | bytes 69664 | tf_op jit(solution)/shard_map/ppermute | solution.py:573
  57.9 1.5 %collective-permute-done.19.got_ref = bf16[4,272,128]{2,1,0:T(8,128)(2,1)S(1)} collective-permute-done((bf16[4,272,128]{2,1,0:T(8,128)(2,1)S(1)}, bf16[4,272,128]{2,1,0:T(8,128)(2,1)S(1)}, u32[]{:S(2)}, u32[]{:S(2)}) %collective-permute-start.19) | collective-permute-done | bytes 278560 | tf_op jit(solution)/shard_map/ppermute | solution.py:576
  59.5 1.6 %shard_map.65 = (f32[64,864]{1,0:T(8,128)}, f32[1728,128]{1,0:T(8,128)}) custom-call(s32[2]{0:T(128)S(1)} %pad_add_fusion.place_ref, bf16[4,272,128]{2,1,0:T(8,128)(2,1)S(1)} %pad_maximum_fusion.keep_ref, bf16[4,272,128]{2,1,0:T(8,128)(2,1)S(1)} %collective-permute-done.19.got_ref), custom_call_target="tpu_custom_call" | custom-call | tf_op jit(solution)/shard_map/pallas_call | solution.py:587
  (37 shorter events, 7.5 us)
Async XLA Ops:
  2.6 6.7 %collective-permute-start = (bf16[17,4,1024]{2,1,0:T(4,128)(2,1)S(1)}, bf16[17,4,1024]{2,1,0:T(4,128)(2,1)S(1)}, u32[]{:S(2)}, u32[]{:S(2)}) collective-permute-start(bf16[17,4,1024]{2,1,0:T(4,128)(2,1)S(1)} %get-tuple-element.28), channel_id=1, source_target_pairs={{0,16},{16,0},{1,17},{17,1},{2,18},{18,2},{3,19},{19,3},{4,20},{20... | collective-permute-start | bytes 417800 | tf_op jit(solution)/shard_map/ppermute | solution.py:536
  7.3 5.2 %collective-permute-start.1 = (bf16[34,4,1024]{2,1,0:T(4,128)(2,1)S(1)}, bf16[34,4,1024]{2,1,0:T(4,128)(2,1)S(1)}, u32[]{:S(2)}, u32[]{:S(2)}) collective-permute-start(bf16[34,4,1024]{2,1,0:T(4,128)(2,1)S(1)} %get-tuple-element.31), channel_id=1, source_target_pairs={{0,4},{8,12},{4,0},{12,8},{1,5},{9,13},{5,1},{13,9},{2,6},{10,14},... | collective-permute-start | bytes 835592 | tf_op jit(solution)/shard_map/ppermute | solution.py:537
  7.4 6.8 %collective-permute-start.2 = (bf16[34,4,1024]{2,1,0:T(4,128)(2,1)S(1)}, bf16[34,4,1024]{2,1,0:T(4,128)(2,1)S(1)}, u32[]{:S(2)}, u32[]{:S(2)}) collective-permute-start(bf16[34,4,1024]{2,1,0:T(4,128)(2,1)S(1)} %get-tuple-element.35), channel_id=1, source_target_pairs={{4,8},{8,4},{0,0},{12,12},{5,9},{9,5},{1,1},{13,13},{6,10},{10,6},... | collective-permute-start | bytes 835592 | tf_op jit(solution)/shard_map/ppermute | solution.py:538
  9.5 4.7 %collective-permute-start.4 = (bf16[5,4,1024]{2,1,0:T(4,128)(2,1)S(1)}, bf16[5,4,1024]{2,1,0:T(4,128)(2,1)S(1)}, u32[]{:S(2)}, u32[]{:S(2)}) collective-permute-start(bf16[5,4,1024]{2,1,0:T(4,128)(2,1)S(1)} %get-tuple-element.61), channel_id=1, source_target_pairs={{4,8},{8,4},{0,16},{12,28},{20,24},{24,20},{16,0},{28,12},{5,9},{9... | collective-permute-start | bytes 122888 | tf_op jit(solution)/shard_map/ppermute | solution.py:547
  11.3 2.9 %collective-permute-start.3 = (bf16[5,4,1024]{2,1,0:T(4,128)(2,1)S(1)}, bf16[5,4,1024]{2,1,0:T(4,128)(2,1)S(1)}, u32[]{:S(2)}, u32[]{:S(2)}) collective-permute-start(bf16[5,4,1024]{2,1,0:T(4,128)(2,1)S(1)} %get-tuple-element.62), channel_id=1, source_target_pairs={{0,4},{8,12},{4,0},{12,8},{1,5},{9,13},{5,1},{13,9},{2,6},{10,14},... | collective-permute-start | bytes 122888 | tf_op jit(solution)/shard_map/ppermute | solution.py:546
  12.6 10.9 %collective-permute-start.5 = (bf16[34,16,128]{2,1,0:T(8,128)(2,1)S(1)}, bf16[34,16,128]{2,1,0:T(8,128)(2,1)S(1)}, u32[]{:S(2)}, u32[]{:S(2)}) collective-permute-start(bf16[34,16,128]{2,1,0:T(8,128)(2,1)S(1)} %get-tuple-element.44), channel_id=1, source_target_pairs={{0,1},{2,3},{1,0},{3,2},{4,5},{6,7},{5,4},{7,6},{8,9},{10,11},{9,8... | collective-permute-start | bytes 417800 | tf_op jit(solution)/shard_map/ppermute | solution.py:534
  14.2 9.3 %collective-permute-start.6 = (bf16[34,16,128]{2,1,0:T(8,128)(2,1)S(1)}, bf16[34,16,128]{2,1,0:T(8,128)(2,1)S(1)}, u32[]{:S(2)}, u32[]{:S(2)}) collective-permute-start(bf16[34,16,128]{2,1,0:T(8,128)(2,1)S(1)} %get-tuple-element.45), channel_id=1, source_target_pairs={{1,2},{2,1},{0,4},{3,7},{5,6},{6,5},{4,0},{7,3},{9,10},{10,9},{8,1... | collective-permute-start | bytes 417800 | tf_op jit(solution)/shard_map/ppermute | solution.py:534
  15.1 8.4 %collective-permute-start.7 = (bf16[46,8,128]{2,1,0:T(8,128)(2,1)S(1)}, bf16[46,8,128]{2,1,0:T(8,128)(2,1)S(1)}, u32[]{:S(2)}, u32[]{:S(2)}) collective-permute-start(bf16[46,8,128]{2,1,0:T(8,128)(2,1)S(1)} %get-tuple-element.46), channel_id=1, source_target_pairs={{0,1},{2,3},{1,0},{3,2},{4,5},{6,7},{5,4},{7,6},{8,9},{10,11},{9,8... | collective-permute-start | bytes 282632 | tf_op jit(solution)/shard_map/ppermute | solution.py:534
  18.3 5.2 %collective-permute-start.8 = (bf16[46,8,128]{2,1,0:T(8,128)(2,1)S(1)}, bf16[46,8,128]{2,1,0:T(8,128)(2,1)S(1)}, u32[]{:S(2)}, u32[]{:S(2)}) collective-permute-start(bf16[46,8,128]{2,1,0:T(8,128)(2,1)S(1)} %get-tuple-element.47), channel_id=1, source_target_pairs={{1,2},{2,1},{0,4},{3,7},{5,6},{6,5},{4,0},{7,3},{9,10},{10,9},{8,1... | collective-permute-start | bytes 282632 | tf_op jit(solution)/shard_map/ppermute | solution.py:534
  31.5 1.6 %collective-permute-start.9 = (bf16[4,272,128]{2,1,0:T(8,128)(2,1)S(1)}, bf16[4,272,128]{2,1,0:T(8,128)(2,1)S(1)}, u32[]{:S(2)}, u32[]{:S(2)}) collective-permute-start(bf16[4,272,128]{2,1,0:T(8,128)(2,1)S(1)} %get-tuple-element.51), channel_id=1, source_target_pairs={{0,4},{4,0},{8,12},{12,8},{16,20},{20,16},{24,28},{28,24},{1,5},{5... | collective-permute-start | bytes 835592 | tf_op jit(solution)/shard_map/ppermute | solution.py:576
  33.2 4.9 %collective-permute-start.10 = (bf16[272,128]{1,0:T(8,128)(2,1)S(1)}, bf16[272,128]{1,0:T(8,128)(2,1)S(1)}, u32[]{:S(2)}, u32[]{:S(2)}) collective-permute-start(bf16[272,128]{1,0:T(8,128)(2,1)S(1)} %get-tuple-element.54), channel_id=1, source_target_pairs={{0,8},{4,12},{8,0},{12,4},{16,24},{20,28},{24,16},{28,20},{1,9},{5... | collective-permute-start | bytes 208904 | tf_op jit(solution)/shard_map/ppermute | solution.py:573
  34.4 5.3 %collective-permute-start.12 = (bf16[272,128]{1,0:T(8,128)(2,1)S(1)}, bf16[272,128]{1,0:T(8,128)(2,1)S(1)}, u32[]{:S(2)}, u32[]{:S(2)}) collective-permute-start(bf16[272,128]{1,0:T(8,128)(2,1)S(1)} %get-tuple-element.55), channel_id=1, source_target_pairs={{0,24},{4,28},{8,16},{12,20},{16,8},{20,12},{24,0},{28,4},{1,25},{... | collective-permute-start | bytes 208904 | tf_op jit(solution)/shard_map/ppermute | solution.py:573
  35.6 5.4 %collective-permute-start.11 = (bf16[272,128]{1,0:T(8,128)(2,1)S(1)}, bf16[272,128]{1,0:T(8,128)(2,1)S(1)}, u32[]{:S(2)}, u32[]{:S(2)}) collective-permute-start(bf16[272,128]{1,0:T(8,128)(2,1)S(1)} %get-tuple-element.56), channel_id=1, source_target_pairs={{0,16},{4,20},{8,24},{12,28},{16,0},{20,4},{24,8},{28,12},{1,17},{... | collective-permute-start | bytes 208904 | tf_op jit(solution)/shard_map/ppermute | solution.py:573
  41.0 6.9 %collective-permute-start.15 = (bf16[272,128]{1,0:T(8,128)(2,1)S(1)}, bf16[272,128]{1,0:T(8,128)(2,1)S(1)}, u32[]{:S(2)}, u32[]{:S(2)}) collective-permute-start(bf16[272,128]{1,0:T(8,128)(2,1)S(1)} %fusion.1), channel_id=1, source_target_pairs={{0,3},{1,2},{2,1},{3,0},{4,7},{5,6},{6,5},{7,4},{8,11},{9,10},{10,... | collective-permute-start | bytes 208904 | tf_op jit(solution)/shard_map/ppermute | solution.py:579
  42.8 7.1 %collective-permute-start.14 = (bf16[272,128]{1,0:T(8,128)(2,1)S(1)}, bf16[272,128]{1,0:T(8,128)(2,1)S(1)}, u32[]{:S(2)}, u32[]{:S(2)}) collective-permute-start(bf16[272,128]{1,0:T(8,128)(2,1)S(1)} %fusion.1), channel_id=1, source_target_pairs={{0,2},{1,3},{2,0},{3,1},{4,6},{5,7},{6,4},{7,5},{8,10},{9,11},{10,... | collective-permute-start | bytes 208904 | tf_op jit(solution)/shard_map/ppermute | solution.py:579
  44.6 5.3 %collective-permute-start.13 = (bf16[272,128]{1,0:T(8,128)(2,1)S(1)}, bf16[272,128]{1,0:T(8,128)(2,1)S(1)}, u32[]{:S(2)}, u32[]{:S(2)}) collective-permute-start(bf16[272,128]{1,0:T(8,128)(2,1)S(1)} %fusion.1), channel_id=1, source_target_pairs={{0,1},{1,0},{2,3},{3,2},{4,5},{5,4},{6,7},{7,6},{8,9},{9,8},{10,11... | collective-permute-start | bytes 208904 | tf_op jit(solution)/shard_map/ppermute | solution.py:579
  49.9 5.3 %collective-permute-start.18 = (bf16[272,128]{1,0:T(8,128)(2,1)S(1)}, bf16[272,128]{1,0:T(8,128)(2,1)S(1)}, u32[]{:S(2)}, u32[]{:S(2)}) collective-permute-start(bf16[272,128]{1,0:T(8,128)(2,1)S(1)} %add_convert_fusion.1), channel_id=1, source_target_pairs={{0,24},{4,28},{8,16},{12,20},{16,8},{20,12},{24,0},{28,4},{1,25},{... | collective-permute-start | bytes 208904 | tf_op jit(solution)/shard_map/ppermute | solution.py:573
  52.7 4.3 %collective-permute-start.17 = (bf16[272,128]{1,0:T(8,128)(2,1)S(1)}, bf16[272,128]{1,0:T(8,128)(2,1)S(1)}, u32[]{:S(2)}, u32[]{:S(2)}) collective-permute-start(bf16[272,128]{1,0:T(8,128)(2,1)S(1)} %add_convert_fusion.1), channel_id=1, source_target_pairs={{0,16},{4,20},{8,24},{12,28},{16,0},{20,4},{24,8},{28,12},{1,17},{... | collective-permute-start | bytes 208904 | tf_op jit(solution)/shard_map/ppermute | solution.py:573
  53.5 4.3 %collective-permute-start.16 = (bf16[272,128]{1,0:T(8,128)(2,1)S(1)}, bf16[272,128]{1,0:T(8,128)(2,1)S(1)}, u32[]{:S(2)}, u32[]{:S(2)}) collective-permute-start(bf16[272,128]{1,0:T(8,128)(2,1)S(1)} %add_convert_fusion.1), channel_id=1, source_target_pairs={{0,8},{4,12},{8,0},{12,4},{16,24},{20,28},{24,16},{28,20},{1,9},{5... | collective-permute-start | bytes 208904 | tf_op jit(solution)/shard_map/ppermute | solution.py:573
  57.8 1.6 %collective-permute-start.19 = (bf16[4,272,128]{2,1,0:T(8,128)(2,1)S(1)}, bf16[4,272,128]{2,1,0:T(8,128)(2,1)S(1)}, u32[]{:S(2)}, u32[]{:S(2)}) collective-permute-start(bf16[4,272,128]{2,1,0:T(8,128)(2,1)S(1)} %pad_maximum_fusion.keep_ref), channel_id=1, source_target_pairs={{0,4},{4,0},{8,12},{12,8},{16,20},{20,16},{24,28},{28,24},{1,5},{5... | collective-permute-start | bytes 835592 | tf_op jit(solution)/shard_map/ppermute | solution.py:576

commit v2 on v1

--- a/solution.py
+++ b/solution.py
@@ -58,7 +58,7 @@
 
 
 def pack(
-    flag_ref, vol_ref, cot_ref, first_hbm, second_hbm, row_a_ref, row_b_ref, col_a_ref, col_b_ref,
+    flag_ref, vol_ref, cot_ref, first_hbm, second_hbm, row_b_ref, row_a_ref, col_a_ref, col_b_ref,
     first_ref, second_ref, arrived,
 ):
     row_even, col_even = flag_ref[1] == 0, flag_ref[2] == 0
@@ -219,17 +219,20 @@
         place_halo(planes + 3 + q, q, first_plane)
     tiles[:, planes + 7 :] = jnp.zeros((3, 2, blocks, 16, LANES), BF16)
 
-    def product(pair, carry):
+    group = 5
+
+    def product(step, carry):
         taps = []
         for a in range(3):
             for b in range(3):
-                both = [tiles[b, 4 * pair + 2 * n + a].reshape(blocks * 16, LANES) for n in range(2)]
-                taps.append(jnp.concatenate(both, axis=0))
+                start = 2 * group * step + a
+                found = [tiles[b, start + 2 * n].reshape(blocks * 16, LANES) for n in range(group)]
+                taps.append(jnp.concatenate(found, axis=0))
         found = matmul(jnp.concatenate(taps, axis=1), w1_ref[...])
-        parts[pl.ds(2 * pair, 2)] = found.reshape(2, blocks, 16, 2 * LANES)
+        parts[pl.ds(group * step, group)] = found.reshape(group, blocks, 16, 2 * LANES)
         return carry
 
-    lax.fori_loop(0, planes // 4 + 2, product, 0)
+    lax.fori_loop(0, parts.shape[0] // group, product, 0)
 
 
 def body(
@@ -287,9 +290,10 @@
         rim, rim_prev = rim_parts[i, :, :, :LANES], rim_parts[i, 0:1, :, LANES:]
         blank = jnp.zeros((1, 16, LANES), F32)
         pre = jnp.concatenate([rim[:1], main, rim[1:]], axis=0) + jnp.concatenate([blank, rim_prev, prev], axis=0)
-        root = jnp.sqrt(pre * pre + 1.0)
-        slopes[i] = 0.6 + 0.4 * pre / root
-        hidden = (0.6 * pre + 0.4 * (root - 1.0)).astype(BF16).astype(F32)
+        square = pre * pre + 1.0
+        inverse = lax.rsqrt(square)
+        slopes[i] = 0.6 + 0.4 * (pre * inverse)
+        hidden = (0.6 * pre + 0.4 * (square * inverse - 1.0)).astype(BF16).astype(F32)
         odd = hidden[:, 8:, :]
         hid[0, i] = pltpu.roll(odd, 1, 1)
         hid[1, i] = hidden[:, :8, :]
@@ -330,32 +334,33 @@
 
     quarter = half_planes // 2
 
-    def conv_two(t, carry):
-        taps = [pairs[b, 2 * t + a].reshape(wide, LANES) for a in range(3) for b in range(3)]
-        parts = matmul(jnp.concatenate(taps, axis=1), w2_ref[...]).reshape(blocks + 2, 16, 2 * LANES)
-        pre = parts[1:, :, :LANES] + parts[:-1, :, LANES:]
-        slope = 0.6 + 0.4 * pre / jnp.sqrt(pre * pre + 1.0)
+    taps = []
+    for a in range(3):
+        for b in range(3):
+            rows = [pairs[b, 2 * t + a].reshape(wide, LANES) for t in range(quarter + 1)]
+            taps.append(jnp.concatenate(rows, axis=0))
+    found = matmul(jnp.concatenate(taps, axis=1), w2_ref[...]).reshape(quarter + 1, blocks + 2, 16, 2 * LANES)
+    for t in range(quarter + 1):
+        pre = found[t, 1:, :, :LANES] + found[t, :-1, :, LANES:]
+        slope = 0.6 + 0.4 * (pre * lax.rsqrt(pre * pre + 1.0))
         upstream = jnp.concatenate([ups[t], ups[t + quarter]], axis=1)
         delta = (upstream * slope).astype(BF16).astype(F32)
         moved = jnp.concatenate([pltpu.roll(delta[:, :8], 7, 1), pltpu.roll(delta[:, 8:], 7, 1)], axis=1)
         deltas[t] = delta
         shifted[t] = moved.astype(BF16)
-        return carry
-
-    lax.fori_loop(0, quarter + 1, conv_two, 0)
 
     sublane = lax.broadcasted_iota(jnp.int32, (1, 1, 16, 1), 2) % 8
     own_rows = jnp.logical_and(sublane >= 1, sublane <= 4)
 
-    def with_next(values):
+    def with_next(values, needed):
         values = values.T
         edge = jnp.zeros((LANES, values.shape[1] // blocks), values.dtype)
         here = jnp.concatenate([edge, values], axis=1)
-        after = jnp.concatenate([values, edge], axis=1)
+        after = jnp.concatenate([values, edge], axis=1)[:needed]
         return jnp.concatenate([here, after], axis=0)
 
     own_delta = [jnp.where(own_rows[0], deltas[t, 0:blocks], 0.0) for t in range(quarter)]
-    left = with_next(jnp.stack(own_delta, axis=1).reshape(blocks * quarter * 16, LANES)).astype(BF16)
+    left = with_next(jnp.stack(own_delta, axis=1).reshape(blocks * quarter * 16, LANES), LANES).astype(BF16)
 
     def second_taps(tap):
         a, b = tap // 3, tap % 3
@@ -399,7 +404,7 @@
         back_one = jnp.concatenate([rows[parity][p][t % quarter, :, half, :] for p in (0, 1)], axis=1)
         delta = back_one * slopes[i + 1, 1 : blocks + 1]
         own_list.append(jnp.where(own_rows[0], delta, 0.0).astype(BF16))
-    left_one = with_next(jnp.stack(own_list, axis=1).reshape(blocks * (planes // 2) * 16, LANES))
+    left_one = with_next(jnp.stack(own_list, axis=1).reshape(blocks * (planes // 2) * 16, LANES), 64)
 
     def first_taps(tap):
         a, b = tap // 3, tap % 3
@@ -416,7 +421,7 @@
         found = matmul(left_one, jnp.concatenate(right, axis=1))
         for n in range(len(right)):
             main = found[:LANES, n * LANES : (n + 1) * LANES]
-            prev = found[LANES : LANES + 64, n * LANES : (n + 1) * LANES]
+            prev = found[LANES:, n * LANES : (n + 1) * LANES]
             even = jnp.concatenate([prev[:, 96:], main[:64, :64]], axis=1)
             grads.append(even + main[64:, 32:])
     grads.append(jnp.zeros((64, FIRST_BLOCKS * LANES - 9 * 96), F32))
@@ -521,7 +526,7 @@
     weights = (first_weight, second_weight.T)
     shapes = [(groups, 4, width)] * 2 + [(groups, high, LANES)] * 2
     shapes += [weight.shape for weight in weights]
-    row_a, row_b, side_a, side_b, first_taps, second_taps = pl.pallas_call(
+    row_b, row_a, side_a, side_b, first_taps, second_taps = pl.pallas_call(
         pack,
         out_shape=[jax.ShapeDtypeStruct(shape, BF16) for shape in shapes],
         in_specs=[smem] + [whole] * 2 + [in_hbm] * 2,
@@ -535,7 +540,7 @@
 
     dep = lax.ppermute(dep, "depth", [(0, 1), (1, 0)])
     row_a = lax.ppermute(row_a, "row", pairs_on_line(rows, 0))
-    row_b = lax.ppermute(row_b, "row", pairs_on_line(rows, 1))
+    row_b = lax.ppermute(row_b, ("depth", "row"), pairs_of_lines(2, rows, 1))
     row_a, side_a, side_b = lax.optimization_barrier((row_a, side_a, side_b))
     side_a, side_b = to_col(side_a, 0), to_col(side_b, 1)
 

time: 61.3 us -> 58.4 us (0.953)
  Pallas kernels: 19.4 us -> 17.5 us
  starting transfers between devices: 23.2 us -> 21.7 us
    pallas_call x1, Pallas kernels: 4.75 us -> 3.75 us  [local_grads(): pl.pallas_call(own_blocks, out_shape=[jax.ShapeDtypeStruct((3, planes + 9...]
    pallas_call x1, Pallas kernels: 7.98 us -> 7.09 us  [local_grads(): pl.pallas_call(body, out_shape=[jax.ShapeDtypeStruct((squares, rows // (2...]
    ppermute x4, starting transfers between devices: 5.26 us -> 4.37 us  [to_col(): return lax.ppermute(block, ('row', 'col'), pairs_of_lines(rows, cols, kind))]
    ppermute x6, waiting for transfers between devices: 8.5 us -> 7.69 us  [to_square(): return lax.ppermute(block, ('depth', 'row'), route)]
  transfers between devices with their start and end apart: 20 -> 20, of which waited for: 11 -> 12; matrix products, arithmetic and copies ran while one was open for 0% -> 0% of each run, Pallas kernels for 13% -> 12%
where the time goes in v2:
time: 58.4 us; the launch traced here: 58.2 us
  starting transfers between devices  21.7 us (37%)
  waiting for transfers between devices  17.7 us (30%)
  Pallas kernels  17.5 us (30%)
  between operations  0.87 us (1%)
    ppermute x6, waiting for transfers between devices, to_square(): return lax.ppermute(block, ('depth', 'row'), route)  7.69 us
    ppermute x6, starting transfers between devices, to_square(): return lax.ppermute(block, ('depth', 'row'), route)  7.12 us
    pallas_call x1, Pallas kernels, local_grads(): pl.pallas_call(body, out_shape=[jax.ShapeDtypeStruct((squares, rows // (2...  7.09 us
    ppermute x3, waiting for transfers between devices, along_col(): return lax.ppermute(block, 'col', [(i, i ^ n) for i in range(cols)])  4.92 us
    ppermute x3, starting transfers between devices, along_col(): return lax.ppermute(block, 'col', [(i, i ^ n) for i in range(cols)])  4.45 us
    ppermute x4, starting transfers between devices, to_col(): return lax.ppermute(block, ('row', 'col'), pairs_of_lines(rows, cols, kind))  4.37 us
    pallas_call x1, Pallas kernels, local_grads(): pl.pallas_call(own_blocks, out_shape=[jax.ShapeDtypeStruct((3, planes + 9...  3.75 us
    ppermute x1, starting transfers between devices, shards(): dep = lax.ppermute(dep, 'depth', [(0, 1), (1, 0)])  3.03 us
  transfers between devices with their start and end apart: 20, of which 12 were waited for; matrix products, arithmetic and copies ran while one was open for 0% of the time, Pallas kernels for 12%

profile of v2, /device:TPU:0, one launch (start us, length us, event | category | flops | bytes accessed | tf_op | source)
XLA Modules:
  0.0 58.2 jit_solution(13978299169021641147)
XLA Ops:
  0.7 1.9 %shard_map.59 = (bf16[32,16,1024]{2,1,0:T(8,128)(2,1)S(1)}, bf16[8,4,1024]{2,1,0:T(4,128)(2,1)S(1)}, bf16[17,4,1024]{2,1,0:T(4,128)(2,1)S(1)}) custom-call(s32[5]{0:T(128)S(1)} %stack.58.flag_ref, bf16[32,16,1024]{2,1,0:T(8,128)(2,1)} %vol_hbm.1, bf16[8,4,1024]{2,1,0:T(4,128)(2,1)} %cot_hbm.1), custom_call_target="tpu_custom_call" | custom-call | tf_op jit(solution)/shard_map/pallas_call | solution.py:518
  2.6 3.0 %collective-permute-start = (bf16[17,4,1024]{2,1,0:T(4,128)(2,1)S(1)}, bf16[17,4,1024]{2,1,0:T(4,128)(2,1)S(1)}, u32[]{:S(2)}, u32[]{:S(2)}) collective-permute-start(bf16[17,4,1024]{2,1,0:T(4,128)(2,1)S(1)} %get-tuple-element.28), channel_id=1, source_target_pairs={{0,16},{16,0},{1,17},{17,1},{2,18},{18,2},{3,19},{19,3},{4,20},{20... | collective-permute-start | bytes 417800 | tf_op jit(solution)/shard_map/ppermute | solution.py:541
  5.7 1.6 %shard_map.60 = (bf16[34,4,1024]{2,1,0:T(4,128)(2,1)S(1)}, bf16[34,4,1024]{2,1,0:T(4,128)(2,1)S(1)}, bf16[34,16,128]{2,1,0:T(8,128)(2,1)S(1)}, bf16[34,16,128]{2...) custom-call(s32[5]{0:T(128)S(1)} %stack.58.flag_ref, ...), custom_call_target="tpu_custom_call" | custom-call | tf_op jit(solution)/shard_map/pallas_call | solution.py:529
  7.5 1.8 %collective-permute-done.dep_ref = bf16[17,4,1024]{2,1,0:T(4,128)(2,1)S(1)} collective-permute-done((bf16[17,4,1024]{2,1,0:T(4,128)(2,1)S(1)}, bf16[17,4,1024]{2,1,0:T(4,128)(2,1)S(1)}, u32[]{:S(2)}, u32[]{:S(2)}) %collective-permute-start) | collective-permute-done | bytes 139296 | tf_op jit(solution)/shard_map/ppermute | solution.py:541
  9.5 1.8 %collective-permute-start.4 = (bf16[5,4,1024]{2,1,0:T(4,128)(2,1)S(1)}, bf16[5,4,1024]{2,1,0:T(4,128)(2,1)S(1)}, u32[]{:S(2)}, u32[]{:S(2)}) collective-permute-start(bf16[5,4,1024]{2,1,0:T(4,128)(2,1)S(1)} %get-tuple-element.61), channel_id=1, source_target_pairs={{4,8},{8,4},{0,16},{12,28},{20,24},{24,20},{16,0},{28,12},{5,9},{9... | collective-permute-start | bytes 122888 | tf_op jit(solution)/shard_map/ppermute | solution.py:552
  12.1 1.6 %collective-permute-start.5 = (bf16[34,16,128]{2,1,0:T(8,128)(2,1)S(1)}, bf16[34,16,128]{2,1,0:T(8,128)(2,1)S(1)}, u32[]{:S(2)}, u32[]{:S(2)}) collective-permute-start(bf16[34,16,128]{2,1,0:T(8,128)(2,1)S(1)} %get-tuple-element.44), channel_id=1, source_target_pairs={{0,1},{2,3},{1,0},{3,2},{4,5},{6,7},{5,4},{7,6},{8,9},{10,11},{9,8... | collective-permute-start | bytes 417800 | tf_op jit(solution)/shard_map/ppermute | solution.py:539
  15.3 2.6 %collective-permute-start.7 = (bf16[46,8,128]{2,1,0:T(8,128)(2,1)S(1)}, bf16[46,8,128]{2,1,0:T(8,128)(2,1)S(1)}, u32[]{:S(2)}, u32[]{:S(2)}) collective-permute-start(bf16[46,8,128]{2,1,0:T(8,128)(2,1)S(1)} %get-tuple-element.46), channel_id=1, source_target_pairs={{0,1},{2,3},{1,0},{3,2},{4,5},{6,7},{5,4},{7,6},{8,9},{10,11},{9,8... | collective-permute-start | bytes 282632 | tf_op jit(solution)/shard_map/ppermute | solution.py:539
  17.9 3.8 %shard_map.63 = (bf16[3,41,8,16,128]{4,3,2,1,0:T(8,128)(2,1)S(1)}, f32[20,8,16,256]{3,2,1,0:T(8,128)S(1)}) custom-call(s32[5]{0:T(128)S(1)} %stack.58.flag_ref, bf16[32,16,1024]{2,1,0:T(8,128)(2,1)S(1)} %get-tuple-element.38.vol_ref, bf16[17,4,1024]{2,1,0:T(4,128)(2,1)S(1)} %collective-permute-done.dep_ref, ...), custom_call_target="tpu_custom_call" | custom-call | flops 2000000000 | bytes 10000000 | tf_op jit(solution)/shard_map/pallas_call | solution.py:466
  21.7 7.1 %shard_map.64 = (bf16[4,272,128]{2,1,0:T(8,128)(2,1)S(1)}, bf16[4,272,128]{2,1,0:T(8,128)(2,1)S(1)}) custom-call(s32[5]{0:T(128)S(1)} %stack.58.flag_ref, s32[2]{0:T(128)S(1)} %pad_add_fusion.place_ref, bf16[3,41,8,16,128]{4,3,2,1,0:T(8,128)(2,1)S(1)} %get-tuple-element.42.tiles, f32[20,8,16,256]{3,2,1,0:T(8,128)S(1)} %get-tuple-element.43.parts, ...), custom_call_target="tpu_custom_call" | custom-call | flops 4000000000 | bytes 10000000 | tf_op jit(solution)/shard_map/pallas_call | solution.py:491
  29.3 1.2 %collective-permute-done.9 = bf16[4,272,128]{2,1,0:T(8,128)(2,1)S(1)} collective-permute-done((bf16[4,272,128]{2,1,0:T(8,128)(2,1)S(1)}, bf16[4,272,128]{2,1,0:T(8,128)(2,1)S(1)}, u32[]{:S(2)}, u32[]{:S(2)}) %collective-permute-start.9) | collective-permute-done | bytes 278560 | tf_op jit(solution)/shard_map/ppermute | solution.py:581
  30.8 2.9 %collective-permute-start.12 = (bf16[272,128]{1,0:T(8,128)(2,1)S(1)}, bf16[272,128]{1,0:T(8,128)(2,1)S(1)}, u32[]{:S(2)}, u32[]{:S(2)}) collective-permute-start(bf16[272,128]{1,0:T(8,128)(2,1)S(1)} %get-tuple-element.55), channel_id=1, source_target_pairs={{0,24},{4,28},{8,16},{12,20},{16,8},{20,12},{24,0},{28,4},{1,25},{... | collective-permute-start | bytes 208904 | tf_op jit(solution)/shard_map/ppermute | solution.py:578
  34.2 1.4 %collective-permute-done.10 = bf16[272,128]{1,0:T(8,128)(2,1)S(1)} collective-permute-done((bf16[272,128]{1,0:T(8,128)(2,1)S(1)}, bf16[272,128]{1,0:T(8,128)(2,1)S(1)}, u32[]{:S(2)}, u32[]{:S(2)}) %collective-permute-start.10) | collective-permute-done | bytes 69664 | tf_op jit(solution)/shard_map/ppermute | solution.py:578
  35.6 2.1 %collective-permute-done.12 = bf16[272,128]{1,0:T(8,128)(2,1)S(1)} collective-permute-done((bf16[272,128]{1,0:T(8,128)(2,1)S(1)}, bf16[272,128]{1,0:T(8,128)(2,1)S(1)}, u32[]{:S(2)}, u32[]{:S(2)}) %collective-permute-start.12) | collective-permute-done | bytes 69664 | tf_op jit(solution)/shard_map/ppermute | solution.py:578
  37.7 1.1 %collective-permute-done.11 = bf16[272,128]{1,0:T(8,128)(2,1)S(1)} collective-permute-done((bf16[272,128]{1,0:T(8,128)(2,1)S(1)}, bf16[272,128]{1,0:T(8,128)(2,1)S(1)}, u32[]{:S(2)}, u32[]{:S(2)}) %collective-permute-start.11) | collective-permute-done | bytes 69664 | tf_op jit(solution)/shard_map/ppermute | solution.py:578
  38.9 1.4 %collective-permute-start.15 = (bf16[272,128]{1,0:T(8,128)(2,1)S(1)}, bf16[272,128]{1,0:T(8,128)(2,1)S(1)}, u32[]{:S(2)}, u32[]{:S(2)}) collective-permute-start(bf16[272,128]{1,0:T(8,128)(2,1)S(1)} %fusion.1), channel_id=1, source_target_pairs={{0,3},{1,2},{2,1},{3,0},{4,7},{5,6},{6,5},{7,4},{8,11},{9,10},{10,... | collective-permute-start | bytes 208904 | tf_op jit(solution)/shard_map/ppermute | solution.py:584
  40.3 1.4 %collective-permute-start.14 = (bf16[272,128]{1,0:T(8,128)(2,1)S(1)}, bf16[272,128]{1,0:T(8,128)(2,1)S(1)}, u32[]{:S(2)}, u32[]{:S(2)}) collective-permute-start(bf16[272,128]{1,0:T(8,128)(2,1)S(1)} %fusion.1), channel_id=1, source_target_pairs={{0,2},{1,3},{2,0},{3,1},{4,6},{5,7},{6,4},{7,5},{8,10},{9,11},{10,... | collective-permute-start | bytes 208904 | tf_op jit(solution)/shard_map/ppermute | solution.py:584
  41.7 1.6 %collective-permute-start.13 = (bf16[272,128]{1,0:T(8,128)(2,1)S(1)}, bf16[272,128]{1,0:T(8,128)(2,1)S(1)}, u32[]{:S(2)}, u32[]{:S(2)}) collective-permute-start(bf16[272,128]{1,0:T(8,128)(2,1)S(1)} %fusion.1), channel_id=1, source_target_pairs={{0,1},{1,0},{2,3},{3,2},{4,5},{5,4},{6,7},{7,6},{8,9},{9,8},{10,11... | collective-permute-start | bytes 208904 | tf_op jit(solution)/shard_map/ppermute | solution.py:584
  43.3 2.5 %collective-permute-done.15 = bf16[272,128]{1,0:T(8,128)(2,1)S(1)} collective-permute-done((bf16[272,128]{1,0:T(8,128)(2,1)S(1)}, bf16[272,128]{1,0:T(8,128)(2,1)S(1)}, u32[]{:S(2)}, u32[]{:S(2)}) %collective-permute-start.15) | collective-permute-done | bytes 69664 | tf_op jit(solution)/shard_map/ppermute | solution.py:584
  45.8 2.4 %collective-permute-done.14 = bf16[272,128]{1,0:T(8,128)(2,1)S(1)} collective-permute-done((bf16[272,128]{1,0:T(8,128)(2,1)S(1)}, bf16[272,128]{1,0:T(8,128)(2,1)S(1)}, u32[]{:S(2)}, u32[]{:S(2)}) %collective-permute-start.14) | collective-permute-done | bytes 69664 | tf_op jit(solution)/shard_map/ppermute | solution.py:584
  49.1 1.5 %collective-permute-start.17 = (bf16[272,128]{1,0:T(8,128)(2,1)S(1)}, bf16[272,128]{1,0:T(8,128)(2,1)S(1)}, u32[]{:S(2)}, u32[]{:S(2)}) collective-permute-start(bf16[272,128]{1,0:T(8,128)(2,1)S(1)} %add_convert_fusion.1), channel_id=1, source_target_pairs={{0,16},{4,20},{8,24},{12,28},{16,0},{20,4},{24,8},{28,12},{1,17},{... | collective-permute-start | bytes 208904 | tf_op jit(solution)/shard_map/ppermute | solution.py:578
  50.6 1.2 %collective-permute-start.16 = (bf16[272,128]{1,0:T(8,128)(2,1)S(1)}, bf16[272,128]{1,0:T(8,128)(2,1)S(1)}, u32[]{:S(2)}, u32[]{:S(2)}) collective-permute-start(bf16[272,128]{1,0:T(8,128)(2,1)S(1)} %add_convert_fusion.1), channel_id=1, source_target_pairs={{0,8},{4,12},{8,0},{12,4},{16,24},{20,28},{24,16},{28,20},{1,9},{5... | collective-permute-start | bytes 208904 | tf_op jit(solution)/shard_map/ppermute | solution.py:578
  51.9 1.8 %collective-permute-done.18 = bf16[272,128]{1,0:T(8,128)(2,1)S(1)} collective-permute-done((bf16[272,128]{1,0:T(8,128)(2,1)S(1)}, bf16[272,128]{1,0:T(8,128)(2,1)S(1)}, u32[]{:S(2)}, u32[]{:S(2)}) %collective-permute-start.18) | collective-permute-done | bytes 69664 | tf_op jit(solution)/shard_map/ppermute | solution.py:578
  55.0 1.5 %collective-permute-done.19.got_ref = bf16[4,272,128]{2,1,0:T(8,128)(2,1)S(1)} collective-permute-done((bf16[4,272,128]{2,1,0:T(8,128)(2,1)S(1)}, bf16[4,272,128]{2,1,0:T(8,128)(2,1)S(1)}, u32[]{:S(2)}, u32[]{:S(2)}) %collective-permute-start.19) | collective-permute-done | bytes 278560 | tf_op jit(solution)/shard_map/ppermute | solution.py:581
  56.6 1.6 %shard_map.65 = (f32[64,864]{1,0:T(8,128)}, f32[1728,128]{1,0:T(8,128)}) custom-call(s32[2]{0:T(128)S(1)} %pad_add_fusion.place_ref, bf16[4,272,128]{2,1,0:T(8,128)(2,1)S(1)} %pad_maximum_fusion.keep_ref, bf16[4,272,128]{2,1,0:T(8,128)(2,1)S(1)} %collective-permute-done.19.got_ref), custom_call_target="tpu_custom_call" | custom-call | tf_op jit(solution)/shard_map/pallas_call | solution.py:592
  (37 shorter events, 6.3 us)
Async XLA Ops:
  2.6 6.7 %collective-permute-start = (bf16[17,4,1024]{2,1,0:T(4,128)(2,1)S(1)}, bf16[17,4,1024]{2,1,0:T(4,128)(2,1)S(1)}, u32[]{:S(2)}, u32[]{:S(2)}) collective-permute-start(bf16[17,4,1024]{2,1,0:T(4,128)(2,1)S(1)} %get-tuple-element.28), channel_id=1, source_target_pairs={{0,16},{16,0},{1,17},{17,1},{2,18},{18,2},{3,19},{19,3},{4,20},{20... | collective-permute-start | bytes 417800 | tf_op jit(solution)/shard_map/ppermute | solution.py:541
  7.3 4.8 %collective-permute-start.1 = (bf16[34,4,1024]{2,1,0:T(4,128)(2,1)S(1)}, bf16[34,4,1024]{2,1,0:T(4,128)(2,1)S(1)}, u32[]{:S(2)}, u32[]{:S(2)}) collective-permute-start(bf16[34,4,1024]{2,1,0:T(4,128)(2,1)S(1)} %get-tuple-element.31), channel_id=1, source_target_pairs={{0,4},{8,12},{4,0},{12,8},{1,5},{9,13},{5,1},{13,9},{2,6},{10,14},... | collective-permute-start | bytes 835592 | tf_op jit(solution)/shard_map/ppermute | solution.py:542
  7.4 7.1 %collective-permute-start.2 = (bf16[34,4,1024]{2,1,0:T(4,128)(2,1)S(1)}, bf16[34,4,1024]{2,1,0:T(4,128)(2,1)S(1)}, u32[]{:S(2)}, u32[]{:S(2)}) collective-permute-start(bf16[34,4,1024]{2,1,0:T(4,128)(2,1)S(1)} %get-tuple-element.35), channel_id=1, source_target_pairs={{4,8},{8,4},{0,16},{12,28},{20,24},{24,20},{16,0},{28,12},{5,9},{9... | collective-permute-start | bytes 835592 | tf_op jit(solution)/shard_map/ppermute | solution.py:543
  9.5 4.9 %collective-permute-start.4 = (bf16[5,4,1024]{2,1,0:T(4,128)(2,1)S(1)}, bf16[5,4,1024]{2,1,0:T(4,128)(2,1)S(1)}, u32[]{:S(2)}, u32[]{:S(2)}) collective-permute-start(bf16[5,4,1024]{2,1,0:T(4,128)(2,1)S(1)} %get-tuple-element.61), channel_id=1, source_target_pairs={{4,8},{8,4},{0,16},{12,28},{20,24},{24,20},{16,0},{28,12},{5,9},{9... | collective-permute-start | bytes 122888 | tf_op jit(solution)/shard_map/ppermute | solution.py:552
  11.3 3.1 %collective-permute-start.3 = (bf16[5,4,1024]{2,1,0:T(4,128)(2,1)S(1)}, bf16[5,4,1024]{2,1,0:T(4,128)(2,1)S(1)}, u32[]{:S(2)}, u32[]{:S(2)}) collective-permute-start(bf16[5,4,1024]{2,1,0:T(4,128)(2,1)S(1)} %get-tuple-element.62), channel_id=1, source_target_pairs={{0,4},{8,12},{4,0},{12,8},{1,5},{9,13},{5,1},{13,9},{2,6},{10,14},... | collective-permute-start | bytes 122888 | tf_op jit(solution)/shard_map/ppermute | solution.py:551
  12.1 9.5 %collective-permute-start.5 = (bf16[34,16,128]{2,1,0:T(8,128)(2,1)S(1)}, bf16[34,16,128]{2,1,0:T(8,128)(2,1)S(1)}, u32[]{:S(2)}, u32[]{:S(2)}) collective-permute-start(bf16[34,16,128]{2,1,0:T(8,128)(2,1)S(1)} %get-tuple-element.44), channel_id=1, source_target_pairs={{0,1},{2,3},{1,0},{3,2},{4,5},{6,7},{5,4},{7,6},{8,9},{10,11},{9,8... | collective-permute-start | bytes 417800 | tf_op jit(solution)/shard_map/ppermute | solution.py:539
  13.8 7.9 %collective-permute-start.6 = (bf16[34,16,128]{2,1,0:T(8,128)(2,1)S(1)}, bf16[34,16,128]{2,1,0:T(8,128)(2,1)S(1)}, u32[]{:S(2)}, u32[]{:S(2)}) collective-permute-start(bf16[34,16,128]{2,1,0:T(8,128)(2,1)S(1)} %get-tuple-element.45), channel_id=1, source_target_pairs={{1,2},{2,1},{0,4},{3,7},{5,6},{6,5},{4,0},{7,3},{9,10},{10,9},{8,1... | collective-permute-start | bytes 417800 | tf_op jit(solution)/shard_map/ppermute | solution.py:539
  15.3 6.3 %collective-permute-start.7 = (bf16[46,8,128]{2,1,0:T(8,128)(2,1)S(1)}, bf16[46,8,128]{2,1,0:T(8,128)(2,1)S(1)}, u32[]{:S(2)}, u32[]{:S(2)}) collective-permute-start(bf16[46,8,128]{2,1,0:T(8,128)(2,1)S(1)} %get-tuple-element.46), channel_id=1, source_target_pairs={{0,1},{2,3},{1,0},{3,2},{4,5},{6,7},{5,4},{7,6},{8,9},{10,11},{9,8... | collective-permute-start | bytes 282632 | tf_op jit(solution)/shard_map/ppermute | solution.py:539
  17.9 3.8 %collective-permute-start.8 = (bf16[46,8,128]{2,1,0:T(8,128)(2,1)S(1)}, bf16[46,8,128]{2,1,0:T(8,128)(2,1)S(1)}, u32[]{:S(2)}, u32[]{:S(2)}) collective-permute-start(bf16[46,8,128]{2,1,0:T(8,128)(2,1)S(1)} %get-tuple-element.47), channel_id=1, source_target_pairs={{1,2},{2,1},{0,4},{3,7},{5,6},{6,5},{4,0},{7,3},{9,10},{10,9},{8,1... | collective-permute-start | bytes 282632 | tf_op jit(solution)/shard_map/ppermute | solution.py:539
  28.8 1.8 %collective-permute-start.9 = (bf16[4,272,128]{2,1,0:T(8,128)(2,1)S(1)}, bf16[4,272,128]{2,1,0:T(8,128)(2,1)S(1)}, u32[]{:S(2)}, u32[]{:S(2)}) collective-permute-start(bf16[4,272,128]{2,1,0:T(8,128)(2,1)S(1)} %get-tuple-element.51), channel_id=1, source_target_pairs={{0,4},{4,0},{8,12},{12,8},{16,20},{20,16},{24,28},{28,24},{1,5},{5... | collective-permute-start | bytes 835592 | tf_op jit(solution)/shard_map/ppermute | solution.py:581
  30.6 5.0 %collective-permute-start.10 = (bf16[272,128]{1,0:T(8,128)(2,1)S(1)}, bf16[272,128]{1,0:T(8,128)(2,1)S(1)}, u32[]{:S(2)}, u32[]{:S(2)}) collective-permute-start(bf16[272,128]{1,0:T(8,128)(2,1)S(1)} %get-tuple-element.54), channel_id=1, source_target_pairs={{0,8},{4,12},{8,0},{12,4},{16,24},{20,28},{24,16},{28,20},{1,9},{5... | collective-permute-start | bytes 208904 | tf_op jit(solution)/shard_map/ppermute | solution.py:578
  30.8 6.9 %collective-permute-start.12 = (bf16[272,128]{1,0:T(8,128)(2,1)S(1)}, bf16[272,128]{1,0:T(8,128)(2,1)S(1)}, u32[]{:S(2)}, u32[]{:S(2)}) collective-permute-start(bf16[272,128]{1,0:T(8,128)(2,1)S(1)} %get-tuple-element.55), channel_id=1, source_target_pairs={{0,24},{4,28},{8,16},{12,20},{16,8},{20,12},{24,0},{28,4},{1,25},{... | collective-permute-start | bytes 208904 | tf_op jit(solution)/shard_map/ppermute | solution.py:578
  33.7 5.1 %collective-permute-start.11 = (bf16[272,128]{1,0:T(8,128)(2,1)S(1)}, bf16[272,128]{1,0:T(8,128)(2,1)S(1)}, u32[]{:S(2)}, u32[]{:S(2)}) collective-permute-start(bf16[272,128]{1,0:T(8,128)(2,1)S(1)} %get-tuple-element.56), channel_id=1, source_target_pairs={{0,16},{4,20},{8,24},{12,28},{16,0},{20,4},{24,8},{28,12},{1,17},{... | collective-permute-start | bytes 208904 | tf_op jit(solution)/shard_map/ppermute | solution.py:578
  38.9 6.9 %collective-permute-start.15 = (bf16[272,128]{1,0:T(8,128)(2,1)S(1)}, bf16[272,128]{1,0:T(8,128)(2,1)S(1)}, u32[]{:S(2)}, u32[]{:S(2)}) collective-permute-start(bf16[272,128]{1,0:T(8,128)(2,1)S(1)} %fusion.1), channel_id=1, source_target_pairs={{0,3},{1,2},{2,1},{3,0},{4,7},{5,6},{6,5},{7,4},{8,11},{9,10},{10,... | collective-permute-start | bytes 208904 | tf_op jit(solution)/shard_map/ppermute | solution.py:584
  40.3 8.0 %collective-permute-start.14 = (bf16[272,128]{1,0:T(8,128)(2,1)S(1)}, bf16[272,128]{1,0:T(8,128)(2,1)S(1)}, u32[]{:S(2)}, u32[]{:S(2)}) collective-permute-start(bf16[272,128]{1,0:T(8,128)(2,1)S(1)} %fusion.1), channel_id=1, source_target_pairs={{0,2},{1,3},{2,0},{3,1},{4,6},{5,7},{6,4},{7,5},{8,10},{9,11},{10,... | collective-permute-start | bytes 208904 | tf_op jit(solution)/shard_map/ppermute | solution.py:584
  41.7 6.6 %collective-permute-start.13 = (bf16[272,128]{1,0:T(8,128)(2,1)S(1)}, bf16[272,128]{1,0:T(8,128)(2,1)S(1)}, u32[]{:S(2)}, u32[]{:S(2)}) collective-permute-start(bf16[272,128]{1,0:T(8,128)(2,1)S(1)} %fusion.1), channel_id=1, source_target_pairs={{0,1},{1,0},{2,3},{3,2},{4,5},{5,4},{6,7},{7,6},{8,9},{9,8},{10,11... | collective-permute-start | bytes 208904 | tf_op jit(solution)/shard_map/ppermute | solution.py:584
  48.3 5.4 %collective-permute-start.18 = (bf16[272,128]{1,0:T(8,128)(2,1)S(1)}, bf16[272,128]{1,0:T(8,128)(2,1)S(1)}, u32[]{:S(2)}, u32[]{:S(2)}) collective-permute-start(bf16[272,128]{1,0:T(8,128)(2,1)S(1)} %add_convert_fusion.1), channel_id=1, source_target_pairs={{0,24},{4,28},{8,16},{12,20},{16,8},{20,12},{24,0},{28,4},{1,25},{... | collective-permute-start | bytes 208904 | tf_op jit(solution)/shard_map/ppermute | solution.py:578
  49.1 5.1 %collective-permute-start.17 = (bf16[272,128]{1,0:T(8,128)(2,1)S(1)}, bf16[272,128]{1,0:T(8,128)(2,1)S(1)}, u32[]{:S(2)}, u32[]{:S(2)}) collective-permute-start(bf16[272,128]{1,0:T(8,128)(2,1)S(1)} %add_convert_fusion.1), channel_id=1, source_target_pairs={{0,16},{4,20},{8,24},{12,28},{16,0},{20,4},{24,8},{28,12},{1,17},{... | collective-permute-start | bytes 208904 | tf_op jit(solution)/shard_map/ppermute | solution.py:578
  50.6 4.3 %collective-permute-start.16 = (bf16[272,128]{1,0:T(8,128)(2,1)S(1)}, bf16[272,128]{1,0:T(8,128)(2,1)S(1)}, u32[]{:S(2)}, u32[]{:S(2)}) collective-permute-start(bf16[272,128]{1,0:T(8,128)(2,1)S(1)} %add_convert_fusion.1), channel_id=1, source_target_pairs={{0,8},{4,12},{8,0},{12,4},{16,24},{20,28},{24,16},{28,20},{1,9},{5... | collective-permute-start | bytes 208904 | tf_op jit(solution)/shard_map/ppermute | solution.py:578
  55.0 1.6 %collective-permute-start.19 = (bf16[4,272,128]{2,1,0:T(8,128)(2,1)S(1)}, bf16[4,272,128]{2,1,0:T(8,128)(2,1)S(1)}, u32[]{:S(2)}, u32[]{:S(2)}) collective-permute-start(bf16[4,272,128]{2,1,0:T(8,128)(2,1)S(1)} %pad_maximum_fusion.keep_ref), channel_id=1, source_target_pairs={{0,4},{4,0},{8,12},{12,8},{16,20},{20,16},{24,28},{28,24},{1,5},{5... | collective-permute-start | bytes 835592 | tf_op jit(solution)/shard_map/ppermute | solution.py:581

commit v3 on v2

--- a/solution.py
+++ b/solution.py
@@ -1,3 +1,5 @@
+import functools
+
 import jax
 import jax.numpy as jnp
 from jax import lax
@@ -235,10 +237,33 @@
     lax.fori_loop(0, parts.shape[0] // group, product, 0)
 
 
+def own_rows():
+    sublane = lax.broadcasted_iota(jnp.int32, (1, 16, 1), 1) % 8
+    return jnp.logical_and(sublane >= 1, sublane <= 4)
+
+
+def with_next(blocks, values, needed):
+    values = values.T
+    edge = jnp.zeros((LANES, values.shape[1] // blocks), values.dtype)
+    here = jnp.concatenate([edge, values], axis=1)
+    after = jnp.concatenate([values, edge], axis=1)[:needed]
+    return jnp.concatenate([here, after], axis=0)
+
+
+def hand_out(place_ref, out_ref, keep_ref, give_ref):
+    core, square = place_ref[0], place_ref[1]
+    squares, size = keep_ref.shape[0], keep_ref.shape[1]
+    for n in range(squares):
+        for ref, half in ((keep_ref, core), (give_ref, 1 - core)):
+            start = pl.multiple_of((half * squares + (square ^ n)) * size, 8)
+            ref[n] = out_ref[pl.ds(start, size), :].astype(BF16)
+
+
 def body(
     flag_ref, place_ref, tiles, parts, dep_ref, row_a_ref, row_b_ref, edge_a_ref, edge_b_ref,
-    side_a_ref, side_b_ref, col_a_ref, col_b_ref, cot_ref, w1_ref, w2_ref, w2b_ref, keep_ref, give_ref,
-    out_ref, stage, rim_tiles, rim_parts, slopes, hid, pairs, ups, deltas, shifted,
+    side_a_ref, side_b_ref, col_a_ref, col_b_ref, cot_ref, w1_ref, w2_ref,
+    keep_ref, give_ref, tail_ref, rim_tiles, slopes, deltas, shifted,
+    out_ref, stage, rim_parts, hid, pairs, ups,
 ):
     first_plane, row_even, col_even = flag_ref[0] == 0, flag_ref[1] == 0, flag_ref[2] == 0
     planes = tiles.shape[1] - 9
@@ -349,18 +374,8 @@
         deltas[t] = delta
         shifted[t] = moved.astype(BF16)
 
-    sublane = lax.broadcasted_iota(jnp.int32, (1, 1, 16, 1), 2) % 8
-    own_rows = jnp.logical_and(sublane >= 1, sublane <= 4)
-
-    def with_next(values, needed):
-        values = values.T
-        edge = jnp.zeros((LANES, values.shape[1] // blocks), values.dtype)
-        here = jnp.concatenate([edge, values], axis=1)
-        after = jnp.concatenate([values, edge], axis=1)[:needed]
-        return jnp.concatenate([here, after], axis=0)
-
-    own_delta = [jnp.where(own_rows[0], deltas[t, 0:blocks], 0.0) for t in range(quarter)]
-    left = with_next(jnp.stack(own_delta, axis=1).reshape(blocks * quarter * 16, LANES), LANES).astype(BF16)
+    own_delta = [jnp.where(own_rows(), deltas[t, 0:blocks], 0.0) for t in range(quarter)]
+    left = with_next(blocks, jnp.stack(own_delta, axis=1).reshape(blocks * quarter * 16, LANES), LANES).astype(BF16)
 
     def second_taps(tap):
         a, b = tap // 3, tap % 3
@@ -375,6 +390,17 @@
             lanes = slice(n * LANES, (n + 1) * LANES)
             out_ref[row : row + 64, :] = found[LANES:, lanes].T[64:]
             out_ref[row + 64 : row + 192, :] = found[:LANES, lanes].T
+
+    cut = tail_ref.shape[0]
+    tail_ref[...] = out_ref[out_ref.shape[0] - cut :, :]
+    hand_out(place_ref, out_ref, keep_ref, give_ref)
+
+
+def transposed(
+    place_ref, tiles, rim_tiles, slopes, deltas, shifted, w2b_ref, tail_ref, keep_ref, give_ref, out_ref
+):
+    planes, blocks = tiles.shape[1] - 9, tiles.shape[2]
+    quarter = planes // 8
 
     def pack(values):
         both = jnp.concatenate([values[:, :-1], values[:, 1:]], axis=3)
@@ -403,8 +429,8 @@
         half = slice(0, 8) if t < quarter else slice(8, 16)
         back_one = jnp.concatenate([rows[parity][p][t % quarter, :, half, :] for p in (0, 1)], axis=1)
         delta = back_one * slopes[i + 1, 1 : blocks + 1]
-        own_list.append(jnp.where(own_rows[0], delta, 0.0).astype(BF16))
-    left_one = with_next(jnp.stack(own_list, axis=1).reshape(blocks * (planes // 2) * 16, LANES), 64)
+        own_list.append(jnp.where(own_rows(), delta, 0.0).astype(BF16))
+    left_one = with_next(blocks, jnp.stack(own_list, axis=1).reshape(blocks * (planes // 2) * 16, LANES), 64)
 
     def first_taps(tap):
         a, b = tap // 3, tap % 3
@@ -426,28 +452,26 @@
             grads.append(even + main[64:, 32:])
     grads.append(jnp.zeros((64, FIRST_BLOCKS * LANES - 9 * 96), F32))
     first = jnp.concatenate(grads, axis=1)
+    start = tail_ref.shape[0]
+    out_ref[:start, :] = tail_ref[...]
     for n in range(FIRST_BLOCKS):
-        row = SECOND_ROWS + 64 * n
-        out_ref[row : row + 64, :] = first[:, n * LANES : (n + 1) * LANES]
-    used = SECOND_ROWS + 64 * FIRST_BLOCKS
+        out_ref[start + 64 * n : start + 64 * (n + 1), :] = first[:, n * LANES : (n + 1) * LANES]
+    used = start + 64 * FIRST_BLOCKS
     if out_ref.shape[0] > used:
         out_ref[used:, :] = jnp.zeros((out_ref.shape[0] - used, LANES), F32)
-
-    core, square = place_ref[0], place_ref[1]
-    squares, size = keep_ref.shape[0], keep_ref.shape[1]
-    for n in range(squares):
-        for ref, half in ((keep_ref, core), (give_ref, 1 - core)):
-            start = pl.multiple_of((half * squares + (square ^ n)) * size, 8)
-            ref[n] = out_ref[pl.ds(start, size), :].astype(BF16)
-
-
-def unpack(place_ref, keep_ref, got_ref, g1_ref, g2_ref, sums):
+    hand_out(place_ref, out_ref, keep_ref, give_ref)
+
+
+def unpack(place_ref, keep_ref, got_ref, g1_ref, g2_ref, sums, share):
     core, square = place_ref[0], place_ref[1]
     squares, size = keep_ref.shape[0], keep_ref.shape[1]
     for n in range(squares):
         for ref, half in ((keep_ref, core), (got_ref, 1 - core)):
-            start = pl.multiple_of((half * squares + (square ^ n)) * size, 8)
-            sums[pl.ds(start, size), :] = ref[n].astype(F32)
+            number = half * squares + (square ^ n)
+            values = ref[n].astype(F32)
+            sums[pl.ds(pl.multiple_of(number * share, 8), share), :] = values[:share]
+            start = pl.multiple_of(2 * squares * share + number * (size - share), 8)
+            sums[pl.ds(start, size - share), :] = values[share:]
     first = [sums[SECOND_ROWS + 64 * n : SECOND_ROWS + 64 * (n + 1), :] for n in range(FIRST_BLOCKS)]
     g1_ref[...] = jnp.concatenate(first, axis=1)[:, : g1_ref.shape[1]]
     g2_ref[...] = sums[:SECOND_ROWS, :]
@@ -458,8 +482,6 @@
     blocks = volume.shape[2] // LANES
     hidden_planes = planes // 2 + 3
     out_planes = planes // 4
-    unit = 2 * squares * 16
-    rows = -(-(SECOND_ROWS + 64 * FIRST_BLOCKS) // unit) * unit
     whole = pl.BlockSpec(memory_space=pltpu.VMEM)
     smem = pl.BlockSpec(memory_space=pltpu.SMEM)
     dep, row_a, row_b, edge_a, edge_b = faces
@@ -475,28 +497,53 @@
         compiler_params=pltpu.CompilerParams(vmem_limit_bytes=16 * 1024 * 1024),
         cost_estimate=pl.CostEstimate(flops=2 * 10**9, bytes_accessed=10**7, transcendentals=0),
     )(flags, volume, *faces, weights[0])
-    scratch = [
-        pltpu.VMEM((rows, LANES), F32),
-        pltpu.VMEM((4, 2, 40, LANES), F32),
-        pltpu.VMEM((3, planes + 7, 2, 16, LANES), BF16),
-        pltpu.VMEM((hidden_planes, 2, 16, 2 * LANES), F32),
-        pltpu.VMEM((hidden_planes, blocks + 2, 16, LANES), F32),
-        pltpu.VMEM((3, hidden_planes, blocks + 2, 8, LANES), F32),
-        pltpu.VMEM((3, out_planes + 3, blocks + 2, 16, LANES), BF16),
-        pltpu.VMEM((out_planes + 1, blocks + 1, 8, LANES), F32),
-        pltpu.VMEM((out_planes // 2 + 1, blocks + 1, 16, LANES), F32),
-        pltpu.VMEM((out_planes // 2 + 1, blocks + 1, 16, LANES), BF16),
-    ]
-    operands = (tiles, parts, *faces, *corners, cotangent, *weights)
-    return pl.pallas_call(
+    unit = 2 * squares * 16
+    early = SECOND_ROWS // unit * unit
+    late = -(-(SECOND_ROWS - early + 64 * FIRST_BLOCKS) // unit) * unit
+
+    def shares(rows):
+        return [jax.ShapeDtypeStruct((squares, rows // (2 * squares), LANES), BF16)] * 2
+
+    operands = (tiles, parts, *faces, *corners, cotangent, *weights[:2])
+    keep, give, tail, rim_tiles, slopes, deltas, shifted = pl.pallas_call(
         body,
-        out_shape=[jax.ShapeDtypeStruct((squares, rows // (2 * squares), LANES), BF16)] * 2,
+        out_shape=shares(early)
+        + [
+            jax.ShapeDtypeStruct((SECOND_ROWS - early, LANES), F32),
+            jax.ShapeDtypeStruct((3, planes + 7, 2, 16, LANES), BF16),
+            jax.ShapeDtypeStruct((hidden_planes, blocks + 2, 16, LANES), F32),
+            jax.ShapeDtypeStruct((out_planes // 2 + 1, blocks + 1, 16, LANES), F32),
+            jax.ShapeDtypeStruct((out_planes // 2 + 1, blocks + 1, 16, LANES), BF16),
+        ],
         in_specs=[smem] * 2 + [whole] * len(operands),
-        out_specs=[whole] * 2,
-        scratch_shapes=scratch,
-        compiler_params=pltpu.CompilerParams(vmem_limit_bytes=28 * 1024 * 1024),
+        out_specs=[whole] * 7,
+        scratch_shapes=[
+            pltpu.VMEM((SECOND_ROWS, LANES), F32),
+            pltpu.VMEM((4, 2, 40, LANES), F32),
+            pltpu.VMEM((hidden_planes, 2, 16, 2 * LANES), F32),
+            pltpu.VMEM((3, hidden_planes, blocks + 2, 8, LANES), F32),
+            pltpu.VMEM((3, out_planes + 3, blocks + 2, 16, LANES), BF16),
+            pltpu.VMEM((out_planes + 1, blocks + 1, 8, LANES), F32),
+        ],
+        compiler_params=pltpu.CompilerParams(vmem_limit_bytes=24 * 1024 * 1024),
         cost_estimate=pl.CostEstimate(flops=4 * 10**9, bytes_accessed=10**7, transcendentals=0),
     )(flags, place, *operands)
+    rest = (tiles, rim_tiles, slopes, deltas, shifted, weights[2], tail)
+    return keep, give, rest, shares(late)
+
+
+def late_grads(place, rest, out_shape):
+    whole = pl.BlockSpec(memory_space=pltpu.VMEM)
+    squares, size = out_shape[0].shape[0], out_shape[0].shape[1]
+    return pl.pallas_call(
+        transposed,
+        out_shape=out_shape,
+        in_specs=[pl.BlockSpec(memory_space=pltpu.SMEM)] + [whole] * len(rest),
+        out_specs=[whole] * 2,
+        scratch_shapes=[pltpu.VMEM((2 * squares * size, LANES), F32)],
+        compiler_params=pltpu.CompilerParams(vmem_limit_bytes=24 * 1024 * 1024),
+        cost_estimate=pl.CostEstimate(flops=2 * 10**9, bytes_accessed=10**7, transcendentals=0),
+    )(place, *rest)
 
 
 def shards(volume, first_weight, second_weight, cotangent):
@@ -570,9 +617,6 @@
     spot = lax.axis_index(("depth", "row"))
     squares = lax.axis_size(("depth", "row")) // 2
     where = jnp.stack([spot % 2, spot // 2])
-    faces, corners = (dep, row_a, row_b, edge_a, edge_b), (side_a, side_b, col_a, col_b)
-    keep, give = local_grads(flags, where, squares, volume, faces, corners, cotangent, weights)
-
     def to_square(block, n):
         route = [(2 * i + c, 2 * (i ^ n) + c) for i in range(squares) for c in (0, 1)]
         return lax.ppermute(block, ("depth", "row"), route)
@@ -583,14 +627,25 @@
     def along_col(block, n):
         return lax.ppermute(block, "col", [(i, i ^ n) for i in range(cols)])
 
+    faces, corners = (dep, row_a, row_b, edge_a, edge_b), (side_a, side_b, col_a, col_b)
+    keep, give, rest, late_shape = local_grads(flags, where, squares, volume, faces, corners, cotangent, weights)
+    got, rest = lax.optimization_barrier((to_core(give), rest))
+    both = add_up(keep, got)
+    near = [to_square(both[n], n) for n in range(1, squares)]
+    keep, give = late_grads(where, rest, late_shape)
+    near, give = lax.optimization_barrier((near, give))
+    share = add_up(both[0], *near)
+    far = [along_col(share, n) for n in range(1, cols)]
     both = add_up(keep, to_core(give))
-    share = add_up(both[0], *[to_square(both[n], n) for n in range(1, squares)])
-    share = add_up(share, *[along_col(share, n) for n in range(1, cols)])
+    late = add_up(both[0], *[to_square(both[n], n) for n in range(1, squares)])
+    far, late = lax.optimization_barrier((far, late))
+    found = [add_up(share, *far), add_up(late, *[along_col(late, n) for n in range(1, cols)])]
+    share = jnp.concatenate(found, axis=0)
     mine = jnp.stack([share] + [to_square(share, n) for n in range(1, squares)])
     other = to_core(mine)
     grads = [jax.ShapeDtypeStruct(shape, F32) for shape in (first_weight.shape, second_weight.shape[::-1])]
     first_grad, second_grad = pl.pallas_call(
-        unpack,
+        functools.partial(unpack, share=found[0].shape[0]),
         out_shape=grads,
         in_specs=[smem] + [whole] * 2,
         out_specs=[whole] * 2,

time: 58.4 us -> 65.8 us (1.13)
  starting transfers between devices: 21.7 us -> 29.7 us
  waiting for transfers between devices: 17.7 us -> 16 us
  Pallas kernels: 17.5 us -> 18.5 us
    ppermute x3 -> x6, starting transfers between devices: 4.45 us -> 8.84 us  [along_col(): return lax.ppermute(block, 'col', [(i, i ^ n) for i in range(cols)])]
    ppermute x6 -> x9, waiting for transfers between devices: 7.69 us -> 4.07 us  [to_square(): return lax.ppermute(block, ('depth', 'row'), route)]
    ppermute x6 -> x9, starting transfers between devices: 7.12 us -> 10.7 us  [to_square(): return lax.ppermute(block, ('depth', 'row'), route)]
    ppermute x2 -> x3, waiting for transfers between devices: 2.73 us -> 3.88 us  [to_core(): lax.ppermute(block, ('depth', 'row'), [(i, i ^ 1) for i in range(2 * squa...]
    pallas_call x2 -> x3, Pallas kernels: 8.71 us -> 9.74 us  [the longest x1 5 us: local_grads(): pl.pallas_call(body, out_shape=shares(early) + [jax.ShapeDtypeStruct((SEC...]
    ppermute x3 -> x6, waiting for transfers between devices: 4.92 us -> 5.67 us  [along_col(): return lax.ppermute(block, 'col', [(i, i ^ n) for i in range(cols)])]
  transfers between devices with their start and end apart: 20 -> 27, of which waited for: 12 -> 13; matrix products, arithmetic and copies ran while one was open for 0% -> 0% of each run, Pallas kernels for 12% -> 15%
where the time goes in v3:
time: 65.8 us; the launch traced here: 65.6 us
  starting transfers between devices  29.7 us (45%)
  Pallas kernels  18.5 us (28%)
  waiting for transfers between devices  16 us (24%)
  between operations  0.93 us (1%)
    ppermute x9, starting transfers between devices, to_square(): return lax.ppermute(block, ('depth', 'row'), route)  10.7 us
    ppermute x6, starting transfers between devices, along_col(): return lax.ppermute(block, 'col', [(i, i ^ n) for i in range(cols)])  8.84 us
    ppermute x6, waiting for transfers between devices, along_col(): return lax.ppermute(block, 'col', [(i, i ^ n) for i in range(cols)])  5.67 us
    pallas_call x1, Pallas kernels, local_grads(): pl.pallas_call(body, out_shape=shares(early) + [jax.ShapeDtypeStruct((SEC...  5 us
    ppermute x4, starting transfers between devices, to_col(): return lax.ppermute(block, ('row', 'col'), pairs_of_lines(rows, cols, kind))  4.37 us
    ppermute x9, waiting for transfers between devices, to_square(): return lax.ppermute(block, ('depth', 'row'), route)  4.07 us
    ppermute x3, waiting for transfers between devices, to_core(): lax.ppermute(block, ('depth', 'row'), [(i, i ^ 1) for i in range(2 * squa...  3.88 us
    pallas_call x1, Pallas kernels, local_grads(): pl.pallas_call(own_blocks, out_shape=[jax.ShapeDtypeStruct((3, planes + 9...  3.75 us
  transfers between devices with their start and end apart: 27, of which 13 were waited for; matrix products, arithmetic and copies ran while one was open for 0% of the time, Pallas kernels for 15%

profile of v3, /device:TPU:0, one launch (start us, length us, event | category | flops | bytes accessed | tf_op | source)
XLA Modules:
  0.0 65.6 jit_solution(9758992125429829675)
XLA Ops:
  0.7 1.9 %shard_map.59 = (bf16[32,16,1024]{2,1,0:T(8,128)(2,1)S(1)}, bf16[8,4,1024]{2,1,0:T(4,128)(2,1)S(1)}, bf16[17,4,1024]{2,1,0:T(4,128)(2,1)S(1)}) custom-call(s32[5]{0:T(128)S(1)} %stack.58.flag_ref, bf16[32,16,1024]{2,1,0:T(8,128)(2,1)} %vol_hbm.1, bf16[8,4,1024]{2,1,0:T(4,128)(2,1)} %cot_hbm.1), custom_call_target="tpu_custom_call" | custom-call | tf_op jit(solution)/shard_map/pallas_call | solution.py:565
  2.6 3.0 %collective-permute-start = (bf16[17,4,1024]{2,1,0:T(4,128)(2,1)S(1)}, bf16[17,4,1024]{2,1,0:T(4,128)(2,1)S(1)}, u32[]{:S(2)}, u32[]{:S(2)}) collective-permute-start(bf16[17,4,1024]{2,1,0:T(4,128)(2,1)S(1)} %get-tuple-element.51), channel_id=1, source_target_pairs={{0,16},{16,0},{1,17},{17,1},{2,18},{18,2},{3,19},{19,3},{4,20},{20... | collective-permute-start | bytes 417800 | tf_op jit(solution)/shard_map/ppermute | solution.py:588
  5.7 1.6 %shard_map.60 = (bf16[34,4,1024]{2,1,0:T(4,128)(2,1)S(1)}, bf16[34,4,1024]{2,1,0:T(4,128)(2,1)S(1)}, bf16[34,16,128]{2,1,0:T(8,128)(2,1)S(1)}, bf16[34,16,128]{2...) custom-call(s32[5]{0:T(128)S(1)} %stack.58.flag_ref, ...), custom_call_target="tpu_custom_call" | custom-call | tf_op jit(solution)/shard_map/pallas_call | solution.py:576
  7.5 1.8 %collective-permute-done.dep_ref = bf16[17,4,1024]{2,1,0:T(4,128)(2,1)S(1)} collective-permute-done((bf16[17,4,1024]{2,1,0:T(4,128)(2,1)S(1)}, bf16[17,4,1024]{2,1,0:T(4,128)(2,1)S(1)}, u32[]{:S(2)}, u32[]{:S(2)}) %collective-permute-start) | collective-permute-done | bytes 139296 | tf_op jit(solution)/shard_map/ppermute | solution.py:588
  9.5 1.8 %collective-permute-start.4 = (bf16[5,4,1024]{2,1,0:T(4,128)(2,1)S(1)}, bf16[5,4,1024]{2,1,0:T(4,128)(2,1)S(1)}, u32[]{:S(2)}, u32[]{:S(2)}) collective-permute-start(bf16[5,4,1024]{2,1,0:T(4,128)(2,1)S(1)} %get-tuple-element.107), channel_id=1, source_target_pairs={{4,8},{8,4},{0,16},{12,28},{20,24},{24,20},{16,0},{28,12},{5,9},{9... | collective-permute-start | bytes 122888 | tf_op jit(solution)/shard_map/ppermute | solution.py:599
  12.1 1.6 %collective-permute-start.5 = (bf16[34,16,128]{2,1,0:T(8,128)(2,1)S(1)}, bf16[34,16,128]{2,1,0:T(8,128)(2,1)S(1)}, u32[]{:S(2)}, u32[]{:S(2)}) collective-permute-start(bf16[34,16,128]{2,1,0:T(8,128)(2,1)S(1)} %get-tuple-element.67), channel_id=1, source_target_pairs={{0,1},{2,3},{1,0},{3,2},{4,5},{6,7},{5,4},{7,6},{8,9},{10,11},{9,8... | collective-permute-start | bytes 417800 | tf_op jit(solution)/shard_map/ppermute | solution.py:586
  15.3 2.6 %collective-permute-start.7 = (bf16[46,8,128]{2,1,0:T(8,128)(2,1)S(1)}, bf16[46,8,128]{2,1,0:T(8,128)(2,1)S(1)}, u32[]{:S(2)}, u32[]{:S(2)}) collective-permute-start(bf16[46,8,128]{2,1,0:T(8,128)(2,1)S(1)} %get-tuple-element.69), channel_id=1, source_target_pairs={{0,1},{2,3},{1,0},{3,2},{4,5},{6,7},{5,4},{7,6},{8,9},{10,11},{9,8... | collective-permute-start | bytes 282632 | tf_op jit(solution)/shard_map/ppermute | solution.py:586
  17.9 3.8 %shard_map.63 = (bf16[3,41,8,16,128]{4,3,2,1,0:T(8,128)(2,1)S(1)}, f32[20,8,16,256]{3,2,1,0:T(8,128)S(1)}) custom-call(s32[5]{0:T(128)S(1)} %stack.58.flag_ref, bf16[32,16,1024]{2,1,0:T(8,128)(2,1)S(1)} %get-tuple-element.61.vol_ref, bf16[17,4,1024]{2,1,0:T(4,128)(2,1)S(1)} %collective-permute-done.dep_ref, ...), custom_call_target="tpu_custom_call" | custom-call | flops 2000000000 | bytes 10000000 | tf_op jit(solution)/shard_map/pallas_call | solution.py:488
  21.7 5.0 %shard_map.64 = (bf16[4,208,128]{2,1,0:T(8,128)(2,1)S(1)}, bf16[4,208,128]{2,1,0:T(8,128)(2,1)S(1)}, f32[64,128]{1,0:T(8,128)S(1)}, bf16[3,39,2,16,128]{4,3,2,1,...) custom-call(s32[5]{0:T(128)S(1)} %stack.58.flag_ref, ...), custom_call_target="tpu_custom_call" | custom-call | flops 4000000000 | bytes 10000000 | tf_op jit(solution)/shard_map/pallas_call | solution.py:508
  30.1 1.9 %collective-permute-start.10 = (bf16[208,128]{1,0:T(8,128)(2,1)S(1)}, bf16[208,128]{1,0:T(8,128)(2,1)S(1)}, u32[]{:S(2)}, u32[]{:S(2)}) collective-permute-start(bf16[208,128]{1,0:T(8,128)(2,1)S(1)} %get-tuple-element.102), channel_id=1, source_target_pairs={{0,8},{4,12},{8,0},{12,4},{16,24},{20,28},{24,16},{28,20},{1,9},{5... | collective-permute-start | bytes 159752 | tf_op jit(solution)/shard_map/ppermute | solution.py:622
  32.0 3.1 %shard_map.65 = (bf16[4,64,128]{2,1,0:T(8,128)(2,1)S(1)}, bf16[4,64,128]{2,1,0:T(8,128)(2,1)S(1)}) custom-call(s32[2]{0:T(128)S(1)} %pad_add_fusion.place_ref, bf16[3,41,8,16,128]{4,3,2,1,0:T(8,128)(2,1)S(1)} %get-tuple-element.81.tiles, bf16[3,39,2,16,128]{4,3,2,1,0:T(8,128)(2,1)S(1)} %get-tuple-element.82.rim_tiles, ...), custom_call_target="tpu_custom_call" | custom-call | flops 2000000000 | bytes 10000000 | tf_op jit(solution)/shard_map/pallas_call | solution.py:538
  35.2 1.2 %collective-permute-done.16 = bf16[4,64,128]{2,1,0:T(8,128)(2,1)S(1)} collective-permute-done((bf16[4,64,128]{2,1,0:T(8,128)(2,1)S(1)}, bf16[4,64,128]{2,1,0:T(8,128)(2,1)S(1)}, u32[]{:S(2)}, u32[]{:S(2)}) %collective-permute-start.16) | collective-permute-done | bytes 65568 | tf_op jit(solution)/shard_map/ppermute | solution.py:625
  37.5 2.1 %collective-permute-start.19 = (bf16[64,128]{1,0:T(8,128)(2,1)S(1)}, bf16[64,128]{1,0:T(8,128)(2,1)S(1)}, u32[]{:S(2)}, u32[]{:S(2)}) collective-permute-start(bf16[64,128]{1,0:T(8,128)(2,1)S(1)} %get-tuple-element.112), channel_id=1, source_target_pairs={{0,24},{4,28},{8,16},{12,20},{16,8},{20,12},{24,0},{28,4},{1,25},{... | collective-permute-start | bytes 49160 | tf_op jit(solution)/shard_map/ppermute | solution.py:622
  40.1 2.1 %collective-permute-start.15 = (bf16[208,128]{1,0:T(8,128)(2,1)S(1)}, bf16[208,128]{1,0:T(8,128)(2,1)S(1)}, u32[]{:S(2)}, u32[]{:S(2)}) collective-permute-start(bf16[208,128]{1,0:T(8,128)(2,1)S(1)} %fusion.1), channel_id=1, source_target_pairs={{0,3},{1,2},{2,1},{3,0},{4,7},{5,6},{6,5},{7,4},{8,11},{9,10},{10,... | collective-permute-start | bytes 159752 | tf_op jit(solution)/shard_map/ppermute | solution.py:628
  42.2 1.5 %collective-permute-start.14 = (bf16[208,128]{1,0:T(8,128)(2,1)S(1)}, bf16[208,128]{1,0:T(8,128)(2,1)S(1)}, u32[]{:S(2)}, u32[]{:S(2)}) collective-permute-start(bf16[208,128]{1,0:T(8,128)(2,1)S(1)} %fusion.1), channel_id=1, source_target_pairs={{0,2},{1,3},{2,0},{3,1},{4,6},{5,7},{6,4},{7,5},{8,10},{9,11},{10,... | collective-permute-start | bytes 159752 | tf_op jit(solution)/shard_map/ppermute | solution.py:628
  44.6 1.9 %collective-permute-done.15 = bf16[208,128]{1,0:T(8,128)(2,1)S(1)} collective-permute-done((bf16[208,128]{1,0:T(8,128)(2,1)S(1)}, bf16[208,128]{1,0:T(8,128)(2,1)S(1)}, u32[]{:S(2)}, u32[]{:S(2)}) %collective-permute-start.15) | collective-permute-done | bytes 53280 | tf_op jit(solution)/shard_map/ppermute | solution.py:628
  46.5 1.8 %collective-permute-done.14 = bf16[208,128]{1,0:T(8,128)(2,1)S(1)} collective-permute-done((bf16[208,128]{1,0:T(8,128)(2,1)S(1)}, bf16[208,128]{1,0:T(8,128)(2,1)S(1)}, u32[]{:S(2)}, u32[]{:S(2)}) %collective-permute-start.14) | collective-permute-done | bytes 53280 | tf_op jit(solution)/shard_map/ppermute | solution.py:628
  48.4 1.5 %collective-permute-start.22 = (bf16[64,128]{1,0:T(8,128)(2,1)S(1)}, bf16[64,128]{1,0:T(8,128)(2,1)S(1)}, u32[]{:S(2)}, u32[]{:S(2)}) collective-permute-start(bf16[64,128]{1,0:T(8,128)(2,1)S(1)} %fusion.3), channel_id=1, source_target_pairs={{0,3},{1,2},{2,1},{3,0},{4,7},{5,6},{6,5},{7,4},{8,11},{9,10},{10,... | collective-permute-start | bytes 49160 | tf_op jit(solution)/shard_map/ppermute | solution.py:628
  50.2 2.6 %collective-permute-start.20 = (bf16[64,128]{1,0:T(8,128)(2,1)S(1)}, bf16[64,128]{1,0:T(8,128)(2,1)S(1)}, u32[]{:S(2)}, u32[]{:S(2)}) collective-permute-start(bf16[64,128]{1,0:T(8,128)(2,1)S(1)} %fusion.3), channel_id=1, source_target_pairs={{0,1},{1,0},{2,3},{3,2},{4,5},{5,4},{6,7},{7,6},{8,9},{9,8},{10,11... | collective-permute-start | bytes 49160 | tf_op jit(solution)/shard_map/ppermute | solution.py:628
  54.7 1.5 %collective-permute-start.24 = (bf16[272,128]{1,0:T(8,128)(2,1)S(1)}, bf16[272,128]{1,0:T(8,128)(2,1)S(1)}, u32[]{:S(2)}, u32[]{:S(2)}) collective-permute-start(bf16[272,128]{1,0:T(8,128)(2,1)S(1)} %get-tuple-element.110), channel_id=1, source_target_pairs={{0,16},{4,20},{8,24},{12,28},{16,0},{20,4},{24,8},{28,12},{1,17},{... | collective-permute-start | bytes 208904 | tf_op jit(solution)/shard_map/ppermute | solution.py:622
  58.3 1.4 %collective-permute-done.24 = bf16[272,128]{1,0:T(8,128)(2,1)S(1)} collective-permute-done((bf16[272,128]{1,0:T(8,128)(2,1)S(1)}, bf16[272,128]{1,0:T(8,128)(2,1)S(1)}, u32[]{:S(2)}, u32[]{:S(2)}) %collective-permute-start.24) | collective-permute-done | bytes 69664 | tf_op jit(solution)/shard_map/ppermute | solution.py:622
  60.5 1.8 %collective-permute-done.25 = bf16[272,128]{1,0:T(8,128)(2,1)S(1)} collective-permute-done((bf16[272,128]{1,0:T(8,128)(2,1)S(1)}, bf16[272,128]{1,0:T(8,128)(2,1)S(1)}, u32[]{:S(2)}, u32[]{:S(2)}) %collective-permute-start.25) | collective-permute-done | bytes 69664 | tf_op jit(solution)/shard_map/ppermute | solution.py:622
  62.5 1.5 %collective-permute-done.26.got_ref = bf16[4,272,128]{2,1,0:T(8,128)(2,1)S(1)} collective-permute-done((bf16[4,272,128]{2,1,0:T(8,128)(2,1)S(1)}, bf16[4,272,128]{2,1,0:T(8,128)(2,1)S(1)}, u32[]{:S(2)}, u32[]{:S(2)}) %collective-permute-start.26) | collective-permute-done | bytes 278560 | tf_op jit(solution)/shard_map/ppermute | solution.py:625
  64.0 1.6 %shard_map.66 = (f32[64,864]{1,0:T(8,128)}, f32[1728,128]{1,0:T(8,128)}) custom-call(s32[2]{0:T(128)S(1)} %pad_add_fusion.place_ref, bf16[4,272,128]{2,1,0:T(8,128)(2,1)S(1)} %pad_maximum_fusion.keep_ref, bf16[4,272,128]{2,1,0:T(8,128)(2,1)S(1)} %collective-permute-done.26.got_ref), custom_call_target="tpu_custom_call" | custom-call | tf_op jit(solution)/shard_map/pallas_call | solution.py:647
  (57 shorter events, 13.9 us)
Async XLA Ops:
  2.6 6.7 %collective-permute-start = (bf16[17,4,1024]{2,1,0:T(4,128)(2,1)S(1)}, bf16[17,4,1024]{2,1,0:T(4,128)(2,1)S(1)}, u32[]{:S(2)}, u32[]{:S(2)}) collective-permute-start(bf16[17,4,1024]{2,1,0:T(4,128)(2,1)S(1)} %get-tuple-element.51), channel_id=1, source_target_pairs={{0,16},{16,0},{1,17},{17,1},{2,18},{18,2},{3,19},{19,3},{4,20},{20... | collective-permute-start | bytes 417800 | tf_op jit(solution)/shard_map/ppermute | solution.py:588
  7.3 4.8 %collective-permute-start.1 = (bf16[34,4,1024]{2,1,0:T(4,128)(2,1)S(1)}, bf16[34,4,1024]{2,1,0:T(4,128)(2,1)S(1)}, u32[]{:S(2)}, u32[]{:S(2)}) collective-permute-start(bf16[34,4,1024]{2,1,0:T(4,128)(2,1)S(1)} %get-tuple-element.54), channel_id=1, source_target_pairs={{0,4},{8,12},{4,0},{12,8},{1,5},{9,13},{5,1},{13,9},{2,6},{10,14},... | collective-permute-start | bytes 835592 | tf_op jit(solution)/shard_map/ppermute | solution.py:589
  7.4 7.1 %collective-permute-start.2 = (bf16[34,4,1024]{2,1,0:T(4,128)(2,1)S(1)}, bf16[34,4,1024]{2,1,0:T(4,128)(2,1)S(1)}, u32[]{:S(2)}, u32[]{:S(2)}) collective-permute-start(bf16[34,4,1024]{2,1,0:T(4,128)(2,1)S(1)} %get-tuple-element.58), channel_id=1, source_target_pairs={{4,8},{8,4},{0,16},{12,28},{20,24},{24,20},{16,0},{28,12},{5,9},{9... | collective-permute-start | bytes 835592 | tf_op jit(solution)/shard_map/ppermute | solution.py:590
  9.5 4.9 %collective-permute-start.4 = (bf16[5,4,1024]{2,1,0:T(4,128)(2,1)S(1)}, bf16[5,4,1024]{2,1,0:T(4,128)(2,1)S(1)}, u32[]{:S(2)}, u32[]{:S(2)}) collective-permute-start(bf16[5,4,1024]{2,1,0:T(4,128)(2,1)S(1)} %get-tuple-element.107), channel_id=1, source_target_pairs={{4,8},{8,4},{0,16},{12,28},{20,24},{24,20},{16,0},{28,12},{5,9},{9... | collective-permute-start | bytes 122888 | tf_op jit(solution)/shard_map/ppermute | solution.py:599
  11.3 3.1 %collective-permute-start.3 = (bf16[5,4,1024]{2,1,0:T(4,128)(2,1)S(1)}, bf16[5,4,1024]{2,1,0:T(4,128)(2,1)S(1)}, u32[]{:S(2)}, u32[]{:S(2)}) collective-permute-start(bf16[5,4,1024]{2,1,0:T(4,128)(2,1)S(1)} %get-tuple-element.108), channel_id=1, source_target_pairs={{0,4},{8,12},{4,0},{12,8},{1,5},{9,13},{5,1},{13,9},{2,6},{10,14},... | collective-permute-start | bytes 122888 | tf_op jit(solution)/shard_map/ppermute | solution.py:598
  12.1 9.5 %collective-permute-start.5 = (bf16[34,16,128]{2,1,0:T(8,128)(2,1)S(1)}, bf16[34,16,128]{2,1,0:T(8,128)(2,1)S(1)}, u32[]{:S(2)}, u32[]{:S(2)}) collective-permute-start(bf16[34,16,128]{2,1,0:T(8,128)(2,1)S(1)} %get-tuple-element.67), channel_id=1, source_target_pairs={{0,1},{2,3},{1,0},{3,2},{4,5},{6,7},{5,4},{7,6},{8,9},{10,11},{9,8... | collective-permute-start | bytes 417800 | tf_op jit(solution)/shard_map/ppermute | solution.py:586
  13.8 7.9 %collective-permute-start.6 = (bf16[34,16,128]{2,1,0:T(8,128)(2,1)S(1)}, bf16[34,16,128]{2,1,0:T(8,128)(2,1)S(1)}, u32[]{:S(2)}, u32[]{:S(2)}) collective-permute-start(bf16[34,16,128]{2,1,0:T(8,128)(2,1)S(1)} %get-tuple-element.68), channel_id=1, source_target_pairs={{1,2},{2,1},{0,4},{3,7},{5,6},{6,5},{4,0},{7,3},{9,10},{10,9},{8,1... | collective-permute-start | bytes 417800 | tf_op jit(solution)/shard_map/ppermute | solution.py:586
  15.3 6.3 %collective-permute-start.7 = (bf16[46,8,128]{2,1,0:T(8,128)(2,1)S(1)}, bf16[46,8,128]{2,1,0:T(8,128)(2,1)S(1)}, u32[]{:S(2)}, u32[]{:S(2)}) collective-permute-start(bf16[46,8,128]{2,1,0:T(8,128)(2,1)S(1)} %get-tuple-element.69), channel_id=1, source_target_pairs={{0,1},{2,3},{1,0},{3,2},{4,5},{6,7},{5,4},{7,6},{8,9},{10,11},{9,8... | collective-permute-start | bytes 282632 | tf_op jit(solution)/shard_map/ppermute | solution.py:586
  17.9 3.8 %collective-permute-start.8 = (bf16[46,8,128]{2,1,0:T(8,128)(2,1)S(1)}, bf16[46,8,128]{2,1,0:T(8,128)(2,1)S(1)}, u32[]{:S(2)}, u32[]{:S(2)}) collective-permute-start(bf16[46,8,128]{2,1,0:T(8,128)(2,1)S(1)} %get-tuple-element.70), channel_id=1, source_target_pairs={{1,2},{2,1},{0,4},{3,7},{5,6},{6,5},{4,0},{7,3},{9,10},{10,9},{8,1... | collective-permute-start | bytes 282632 | tf_op jit(solution)/shard_map/ppermute | solution.py:586
  28.4 6.7 %collective-permute-start.12 = (bf16[208,128]{1,0:T(8,128)(2,1)S(1)}, bf16[208,128]{1,0:T(8,128)(2,1)S(1)}, u32[]{:S(2)}, u32[]{:S(2)}) collective-permute-start(bf16[208,128]{1,0:T(8,128)(2,1)S(1)} %get-tuple-element.100), channel_id=1, source_target_pairs={{0,24},{4,28},{8,16},{12,20},{16,8},{20,12},{24,0},{28,4},{1,25},{... | collective-permute-start | bytes 159752 | tf_op jit(solution)/shard_map/ppermute | solution.py:622
  29.5 5.7 %collective-permute-start.11 = (bf16[208,128]{1,0:T(8,128)(2,1)S(1)}, bf16[208,128]{1,0:T(8,128)(2,1)S(1)}, u32[]{:S(2)}, u32[]{:S(2)}) collective-permute-start(bf16[208,128]{1,0:T(8,128)(2,1)S(1)} %get-tuple-element.101), channel_id=1, source_target_pairs={{0,16},{4,20},{8,24},{12,28},{16,0},{20,4},{24,8},{28,12},{1,17},{... | collective-permute-start | bytes 159752 | tf_op jit(solution)/shard_map/ppermute | solution.py:622
  30.1 5.0 %collective-permute-start.10 = (bf16[208,128]{1,0:T(8,128)(2,1)S(1)}, bf16[208,128]{1,0:T(8,128)(2,1)S(1)}, u32[]{:S(2)}, u32[]{:S(2)}) collective-permute-start(bf16[208,128]{1,0:T(8,128)(2,1)S(1)} %get-tuple-element.102), channel_id=1, source_target_pairs={{0,8},{4,12},{8,0},{12,4},{16,24},{20,28},{24,16},{28,20},{1,9},{5... | collective-permute-start | bytes 159752 | tf_op jit(solution)/shard_map/ppermute | solution.py:622
  36.5 7.2 %collective-permute-start.17 = (bf16[64,128]{1,0:T(8,128)(2,1)S(1)}, bf16[64,128]{1,0:T(8,128)(2,1)S(1)}, u32[]{:S(2)}, u32[]{:S(2)}) collective-permute-start(bf16[64,128]{1,0:T(8,128)(2,1)S(1)} %get-tuple-element.111), channel_id=1, source_target_pairs={{0,8},{4,12},{8,0},{12,4},{16,24},{20,28},{24,16},{28,20},{1,9},{5... | collective-permute-start | bytes 49160 | tf_op jit(solution)/shard_map/ppermute | solution.py:622
  37.5 7.1 %collective-permute-start.19 = (bf16[64,128]{1,0:T(8,128)(2,1)S(1)}, bf16[64,128]{1,0:T(8,128)(2,1)S(1)}, u32[]{:S(2)}, u32[]{:S(2)}) collective-permute-start(bf16[64,128]{1,0:T(8,128)(2,1)S(1)} %get-tuple-element.112), channel_id=1, source_target_pairs={{0,24},{4,28},{8,16},{12,20},{16,8},{20,12},{24,0},{28,4},{1,25},{... | collective-permute-start | bytes 49160 | tf_op jit(solution)/shard_map/ppermute | solution.py:622
  39.6 5.0 %collective-permute-start.18 = (bf16[64,128]{1,0:T(8,128)(2,1)S(1)}, bf16[64,128]{1,0:T(8,128)(2,1)S(1)}, u32[]{:S(2)}, u32[]{:S(2)}) collective-permute-start(bf16[64,128]{1,0:T(8,128)(2,1)S(1)} %get-tuple-element.113), channel_id=1, source_target_pairs={{0,16},{4,20},{8,24},{12,28},{16,0},{20,4},{24,8},{28,12},{1,17},{... | collective-permute-start | bytes 49160 | tf_op jit(solution)/shard_map/ppermute | solution.py:622
  40.1 6.4 %collective-permute-start.15 = (bf16[208,128]{1,0:T(8,128)(2,1)S(1)}, bf16[208,128]{1,0:T(8,128)(2,1)S(1)}, u32[]{:S(2)}, u32[]{:S(2)}) collective-permute-start(bf16[208,128]{1,0:T(8,128)(2,1)S(1)} %fusion.1), channel_id=1, source_target_pairs={{0,3},{1,2},{2,1},{3,0},{4,7},{5,6},{6,5},{7,4},{8,11},{9,10},{10,... | collective-permute-start | bytes 159752 | tf_op jit(solution)/shard_map/ppermute | solution.py:628
  42.2 6.1 %collective-permute-start.14 = (bf16[208,128]{1,0:T(8,128)(2,1)S(1)}, bf16[208,128]{1,0:T(8,128)(2,1)S(1)}, u32[]{:S(2)}, u32[]{:S(2)}) collective-permute-start(bf16[208,128]{1,0:T(8,128)(2,1)S(1)} %fusion.1), channel_id=1, source_target_pairs={{0,2},{1,3},{2,0},{3,1},{4,6},{5,7},{6,4},{7,5},{8,10},{9,11},{10,... | collective-permute-start | bytes 159752 | tf_op jit(solution)/shard_map/ppermute | solution.py:628
  43.7 4.7 %collective-permute-start.13 = (bf16[208,128]{1,0:T(8,128)(2,1)S(1)}, bf16[208,128]{1,0:T(8,128)(2,1)S(1)}, u32[]{:S(2)}, u32[]{:S(2)}) collective-permute-start(bf16[208,128]{1,0:T(8,128)(2,1)S(1)} %fusion.1), channel_id=1, source_target_pairs={{0,1},{1,0},{2,3},{3,2},{4,5},{5,4},{6,7},{7,6},{8,9},{9,8},{10,11... | collective-permute-start | bytes 159752 | tf_op jit(solution)/shard_map/ppermute | solution.py:628
  48.4 5.5 %collective-permute-start.22 = (bf16[64,128]{1,0:T(8,128)(2,1)S(1)}, bf16[64,128]{1,0:T(8,128)(2,1)S(1)}, u32[]{:S(2)}, u32[]{:S(2)}) collective-permute-start(bf16[64,128]{1,0:T(8,128)(2,1)S(1)} %fusion.3), channel_id=1, source_target_pairs={{0,3},{1,2},{2,1},{3,0},{4,7},{5,6},{6,5},{7,4},{8,11},{9,10},{10,... | collective-permute-start | bytes 49160 | tf_op jit(solution)/shard_map/ppermute | solution.py:628
  50.0 4.7 %collective-permute-start.21 = (bf16[64,128]{1,0:T(8,128)(2,1)S(1)}, bf16[64,128]{1,0:T(8,128)(2,1)S(1)}, u32[]{:S(2)}, u32[]{:S(2)}) collective-permute-start(bf16[64,128]{1,0:T(8,128)(2,1)S(1)} %fusion.3), channel_id=1, source_target_pairs={{0,2},{1,3},{2,0},{3,1},{4,6},{5,7},{6,4},{7,5},{8,10},{9,11},{10,... | collective-permute-start | bytes 49160 | tf_op jit(solution)/shard_map/ppermute | solution.py:628
  50.2 4.5 %collective-permute-start.20 = (bf16[64,128]{1,0:T(8,128)(2,1)S(1)}, bf16[64,128]{1,0:T(8,128)(2,1)S(1)}, u32[]{:S(2)}, u32[]{:S(2)}) collective-permute-start(bf16[64,128]{1,0:T(8,128)(2,1)S(1)} %fusion.3), channel_id=1, source_target_pairs={{0,1},{1,0},{2,3},{3,2},{4,5},{5,4},{6,7},{7,6},{8,9},{9,8},{10,11... | collective-permute-start | bytes 49160 | tf_op jit(solution)/shard_map/ppermute | solution.py:628
  54.7 5.0 %collective-permute-start.24 = (bf16[272,128]{1,0:T(8,128)(2,1)S(1)}, bf16[272,128]{1,0:T(8,128)(2,1)S(1)}, u32[]{:S(2)}, u32[]{:S(2)}) collective-permute-start(bf16[272,128]{1,0:T(8,128)(2,1)S(1)} %get-tuple-element.110), channel_id=1, source_target_pairs={{0,16},{4,20},{8,24},{12,28},{16,0},{20,4},{24,8},{28,12},{1,17},{... | collective-permute-start | bytes 208904 | tf_op jit(solution)/shard_map/ppermute | solution.py:622
  56.2 4.3 %collective-permute-start.23 = (bf16[272,128]{1,0:T(8,128)(2,1)S(1)}, bf16[272,128]{1,0:T(8,128)(2,1)S(1)}, u32[]{:S(2)}, u32[]{:S(2)}) collective-permute-start(bf16[272,128]{1,0:T(8,128)(2,1)S(1)} %get-tuple-element.110), channel_id=1, source_target_pairs={{0,8},{4,12},{8,0},{12,4},{16,24},{20,28},{24,16},{28,20},{1,9},{5... | collective-permute-start | bytes 208904 | tf_op jit(solution)/shard_map/ppermute | solution.py:622
  57.1 5.2 %collective-permute-start.25 = (bf16[272,128]{1,0:T(8,128)(2,1)S(1)}, bf16[272,128]{1,0:T(8,128)(2,1)S(1)}, u32[]{:S(2)}, u32[]{:S(2)}) collective-permute-start(bf16[272,128]{1,0:T(8,128)(2,1)S(1)} %get-tuple-element.110), channel_id=1, source_target_pairs={{0,24},{4,28},{8,16},{12,20},{16,8},{20,12},{24,0},{28,4},{1,25},{... | collective-permute-start | bytes 208904 | tf_op jit(solution)/shard_map/ppermute | solution.py:622
  (3 other events, 4.6 us)

commit v4 on v2

--- a/solution.py
+++ b/solution.py
@@ -233,6 +233,15 @@
         return carry
 
     lax.fori_loop(0, parts.shape[0] // group, product, 0)
+
+
+def mirrored(number, squares):
+    bits = squares.bit_length() - 1
+    return sum((number >> n & 1) << (bits - 1 - n) for n in range(bits))
+
+
+def share_number(place_ref, half, squares, n):
+    return half * squares + (place_ref[1] ^ jnp.where(half == 0, mirrored(n, squares), n))
 
 
 def body(
@@ -433,20 +442,18 @@
     if out_ref.shape[0] > used:
         out_ref[used:, :] = jnp.zeros((out_ref.shape[0] - used, LANES), F32)
 
-    core, square = place_ref[0], place_ref[1]
-    squares, size = keep_ref.shape[0], keep_ref.shape[1]
+    core, squares, size = place_ref[0], keep_ref.shape[0], keep_ref.shape[1]
     for n in range(squares):
         for ref, half in ((keep_ref, core), (give_ref, 1 - core)):
-            start = pl.multiple_of((half * squares + (square ^ n)) * size, 8)
-            ref[n] = out_ref[pl.ds(start, size), :].astype(BF16)
+            start = pl.multiple_of(share_number(place_ref, half, squares, n) * size, 8)
+            ref[n] = out_ref[pl.ds(start, size), :].astype(ref.dtype)
 
 
 def unpack(place_ref, keep_ref, got_ref, g1_ref, g2_ref, sums):
-    core, square = place_ref[0], place_ref[1]
-    squares, size = keep_ref.shape[0], keep_ref.shape[1]
+    core, squares, size = place_ref[0], keep_ref.shape[0], keep_ref.shape[1]
     for n in range(squares):
         for ref, half in ((keep_ref, core), (got_ref, 1 - core)):
-            start = pl.multiple_of((half * squares + (square ^ n)) * size, 8)
+            start = pl.multiple_of(share_number(place_ref, half, squares, n) * size, 8)
             sums[pl.ds(start, size), :] = ref[n].astype(F32)
     first = [sums[SECOND_ROWS + 64 * n : SECOND_ROWS + 64 * (n + 1), :] for n in range(FIRST_BLOCKS)]
     g1_ref[...] = jnp.concatenate(first, axis=1)[:, : g1_ref.shape[1]]
@@ -490,7 +497,7 @@
     operands = (tiles, parts, *faces, *corners, cotangent, *weights)
     return pl.pallas_call(
         body,
-        out_shape=[jax.ShapeDtypeStruct((squares, rows // (2 * squares), LANES), BF16)] * 2,
+        out_shape=[jax.ShapeDtypeStruct((squares, rows // (2 * squares), LANES), dtype) for dtype in (F32, BF16)],
         in_specs=[smem] * 2 + [whole] * len(operands),
         out_specs=[whole] * 2,
         scratch_shapes=scratch,
@@ -573,8 +580,11 @@
     faces, corners = (dep, row_a, row_b, edge_a, edge_b), (side_a, side_b, col_a, col_b)
     keep, give = local_grads(flags, where, squares, volume, faces, corners, cotangent, weights)
 
-    def to_square(block, n):
-        route = [(2 * i + c, 2 * (i ^ n) + c) for i in range(squares) for c in (0, 1)]
+    steps = squares.bit_length() - 1
+
+    def to_square(block, step):
+        bits = (1 << step, 1 << (steps - 1 - step))
+        route = [(2 * i + c, 2 * (i ^ bits[c]) + c) for i in range(squares) for c in (0, 1)]
         return lax.ppermute(block, ("depth", "row"), route)
 
     def to_core(block):
@@ -583,10 +593,14 @@
     def along_col(block, n):
         return lax.ppermute(block, "col", [(i, i ^ n) for i in range(cols)])
 
-    both = add_up(keep, to_core(give))
-    share = add_up(both[0], *[to_square(both[n], n) for n in range(1, squares)])
-    share = add_up(share, *[along_col(share, n) for n in range(1, cols)])
-    mine = jnp.stack([share] + [to_square(share, n) for n in range(1, squares)])
+    both = keep + to_core(give).astype(F32)
+    for step in range(steps):
+        half = both.shape[0] // 2
+        both = both[:half] + to_square(both[half:].astype(BF16), step).astype(F32)
+    mine = both.astype(BF16)
+    mine = add_up(mine, *[along_col(mine, n) for n in range(1, cols)])
+    for step in reversed(range(steps)):
+        mine = jnp.concatenate([mine, to_square(mine, step)], axis=0)
     other = to_core(mine)
     grads = [jax.ShapeDtypeStruct(shape, F32) for shape in (first_weight.shape, second_weight.shape[::-1])]
     first_grad, second_grad = pl.pallas_call(

time: 58.4 us -> 62.5 us (1.070)
  waiting for transfers between devices: 17.7 us -> 25.1 us
  starting transfers between devices: 21.7 us -> 18.4 us
    ppermute x6 -> x4, waiting for transfers between devices: 7.69 us -> 15.9 us  [to_square(): return lax.ppermute(block, ('depth', 'row'), route)]
    ppermute x6 -> x4, starting transfers between devices: 7.12 us -> 3.81 us  [to_square(): return lax.ppermute(block, ('depth', 'row'), route)]
    ppermute x3, waiting for transfers between devices: 4.92 us -> 4.06 us  [along_col(): return lax.ppermute(block, 'col', [(i, i ^ n) for i in range(cols)])]
  transfers between devices with their start and end apart: 20 -> 18, of which waited for: 12 -> 11; matrix products, arithmetic and copies ran while one was open for 0% -> 0% of each run, Pallas kernels for 12% -> 11%
where the time goes in v4:
time: 62.5 us; the launch traced here: 62.3 us
  waiting for transfers between devices  25.1 us (40%)
  starting transfers between devices  18.4 us (29%)
  Pallas kernels  17.5 us (28%)
  between operations  0.88 us (1%)
    ppermute x4, waiting for transfers between devices, to_square(): return lax.ppermute(block, ('depth', 'row'), route)  15.9 us
    pallas_call x1, Pallas kernels, local_grads(): pl.pallas_call(body, out_shape=[jax.ShapeDtypeStruct((squares, rows // (2...  7.1 us
    ppermute x3, starting transfers between devices, along_col(): return lax.ppermute(block, 'col', [(i, i ^ n) for i in range(cols)])  4.45 us
    ppermute x4, starting transfers between devices, to_col(): return lax.ppermute(block, ('row', 'col'), pairs_of_lines(rows, cols, kind))  4.37 us
    ppermute x3, waiting for transfers between devices, along_col(): return lax.ppermute(block, 'col', [(i, i ^ n) for i in range(cols)])  4.06 us
    ppermute x4, starting transfers between devices, to_square(): return lax.ppermute(block, ('depth', 'row'), route)  3.81 us
    pallas_call x1, Pallas kernels, local_grads(): pl.pallas_call(own_blocks, out_shape=[jax.ShapeDtypeStruct((3, planes + 9...  3.75 us
    ppermute x1, starting transfers between devices, shards(): dep = lax.ppermute(dep, 'depth', [(0, 1), (1, 0)])  3.03 us
  transfers between devices with their start and end apart: 18, of which 11 were waited for; matrix products, arithmetic and copies ran while one was open for 0% of the time, Pallas kernels for 11%

profile of v4, /device:TPU:0, one launch (start us, length us, event | category | flops | bytes accessed | tf_op | source)
XLA Modules:
  0.0 62.3 jit_solution(7036063294620978455)
XLA Ops:
  0.7 1.9 %shard_map.59 = (bf16[32,16,1024]{2,1,0:T(8,128)(2,1)S(1)}, bf16[8,4,1024]{2,1,0:T(4,128)(2,1)S(1)}, bf16[17,4,1024]{2,1,0:T(4,128)(2,1)S(1)}) custom-call(s32[5]{0:T(128)S(1)} %stack.43.flag_ref, bf16[32,16,1024]{2,1,0:T(8,128)(2,1)} %vol_hbm.1, bf16[8,4,1024]{2,1,0:T(4,128)(2,1)} %cot_hbm.1), custom_call_target="tpu_custom_call" | custom-call | tf_op jit(solution)/shard_map/pallas_call | solution.py:525
  2.6 3.0 %collective-permute-start = (bf16[17,4,1024]{2,1,0:T(4,128)(2,1)S(1)}, bf16[17,4,1024]{2,1,0:T(4,128)(2,1)S(1)}, u32[]{:S(2)}, u32[]{:S(2)}) collective-permute-start(bf16[17,4,1024]{2,1,0:T(4,128)(2,1)S(1)} %get-tuple-element.28), channel_id=1, source_target_pairs={{0,16},{16,0},{1,17},{17,1},{2,18},{18,2},{3,19},{19,3},{4,20},{20... | collective-permute-start | bytes 417800 | tf_op jit(solution)/shard_map/ppermute | solution.py:548
  5.7 1.6 %shard_map.60 = (bf16[34,4,1024]{2,1,0:T(4,128)(2,1)S(1)}, bf16[34,4,1024]{2,1,0:T(4,128)(2,1)S(1)}, bf16[34,16,128]{2,1,0:T(8,128)(2,1)S(1)}, bf16[34,16,128]{2...) custom-call(s32[5]{0:T(128)S(1)} %stack.43.flag_ref, ...), custom_call_target="tpu_custom_call" | custom-call | tf_op jit(solution)/shard_map/pallas_call | solution.py:536
  7.5 1.8 %collective-permute-done.dep_ref = bf16[17,4,1024]{2,1,0:T(4,128)(2,1)S(1)} collective-permute-done((bf16[17,4,1024]{2,1,0:T(4,128)(2,1)S(1)}, bf16[17,4,1024]{2,1,0:T(4,128)(2,1)S(1)}, u32[]{:S(2)}, u32[]{:S(2)}) %collective-permute-start) | collective-permute-done | bytes 139296 | tf_op jit(solution)/shard_map/ppermute | solution.py:548
  9.5 1.8 %collective-permute-start.4 = (bf16[5,4,1024]{2,1,0:T(4,128)(2,1)S(1)}, bf16[5,4,1024]{2,1,0:T(4,128)(2,1)S(1)}, u32[]{:S(2)}, u32[]{:S(2)}) collective-permute-start(bf16[5,4,1024]{2,1,0:T(4,128)(2,1)S(1)} %get-tuple-element.58), channel_id=1, source_target_pairs={{4,8},{8,4},{0,16},{12,28},{20,24},{24,20},{16,0},{28,12},{5,9},{9... | collective-permute-start | bytes 122888 | tf_op jit(solution)/shard_map/ppermute | solution.py:559
  12.1 1.6 %collective-permute-start.5 = (bf16[34,16,128]{2,1,0:T(8,128)(2,1)S(1)}, bf16[34,16,128]{2,1,0:T(8,128)(2,1)S(1)}, u32[]{:S(2)}, u32[]{:S(2)}) collective-permute-start(bf16[34,16,128]{2,1,0:T(8,128)(2,1)S(1)} %get-tuple-element.44), channel_id=1, source_target_pairs={{0,1},{2,3},{1,0},{3,2},{4,5},{6,7},{5,4},{7,6},{8,9},{10,11},{9,8... | collective-permute-start | bytes 417800 | tf_op jit(solution)/shard_map/ppermute | solution.py:546
  14.4 0.8 %shard_map.61 = (bf16[46,8,128]{2,1,0:T(8,128)(2,1)S(1)}, bf16[46,8,128]{2,1,0:T(8,128)(2,1)S(1)}) custom-call(s32[5]{0:T(128)S(1)} %stack.43.flag_ref, bf16[17,4,1024]{2,1,0:T(4,128)(2,1)S(1)} %collective-permute-done.dep_ref, bf16[34,4,1024]{2,1,0:T(4,128)(2,1)S(1)} %collective-permute-done.1.row_a_ref, ...), custom_call_target="tpu_custom_call" | custom-call | tf_op jit(solution)/shard_map/pallas_call | solution.py:567
  15.3 2.6 %collective-permute-start.7 = (bf16[46,8,128]{2,1,0:T(8,128)(2,1)S(1)}, bf16[46,8,128]{2,1,0:T(8,128)(2,1)S(1)}, u32[]{:S(2)}, u32[]{:S(2)}) collective-permute-start(bf16[46,8,128]{2,1,0:T(8,128)(2,1)S(1)} %get-tuple-element.46), channel_id=1, source_target_pairs={{0,1},{2,3},{1,0},{3,2},{4,5},{6,7},{5,4},{7,6},{8,9},{10,11},{9,8... | collective-permute-start | bytes 282632 | tf_op jit(solution)/shard_map/ppermute | solution.py:546
  17.9 3.8 %shard_map.63 = (bf16[3,41,8,16,128]{4,3,2,1,0:T(8,128)(2,1)S(1)}, f32[20,8,16,256]{3,2,1,0:T(8,128)S(1)}) custom-call(s32[5]{0:T(128)S(1)} %stack.43.flag_ref, bf16[32,16,1024]{2,1,0:T(8,128)(2,1)S(1)} %get-tuple-element.38.vol_ref, bf16[17,4,1024]{2,1,0:T(4,128)(2,1)S(1)} %collective-permute-done.dep_ref, ...), custom_call_target="tpu_custom_call" | custom-call | flops 2000000000 | bytes 10000000 | tf_op jit(solution)/shard_map/pallas_call | solution.py:473
  21.7 7.1 %shard_map.64 = (f32[4,272,128]{2,1,0:T(8,128)S(1)}, bf16[4,272,128]{2,1,0:T(8,128)(2,1)S(1)}) custom-call(s32[5]{0:T(128)S(1)} %stack.43.flag_ref, s32[2]{0:T(128)S(1)} %pad_add_fusion.place_ref, bf16[3,41,8,16,128]{4,3,2,1,0:T(8,128)(2,1)S(1)} %get-tuple-element.42.tiles, f32[20,8,16,256]{3,2,1,0:T(8,128)S(1)} %get-tuple-element.43.parts, ...), custom_call_target="tpu_custom_call" | custom-call | flops 4000000000 | bytes 10000000 | tf_op jit(solution)/shard_map/pallas_call | solution.py:498
  29.4 1.2 %collective-permute-done.9 = bf16[4,272,128]{2,1,0:T(8,128)(2,1)S(1)} collective-permute-done((bf16[4,272,128]{2,1,0:T(8,128)(2,1)S(1)}, bf16[4,272,128]{2,1,0:T(8,128)(2,1)S(1)}, u32[]{:S(2)}, u32[]{:S(2)}) %collective-permute-start.9) | collective-permute-done | bytes 278560 | tf_op jit(solution)/shard_map/ppermute | solution.py:591
  30.8 4.9 %collective-permute-done.10 = bf16[2,272,128]{2,1,0:T(8,128)(2,1)S(1)} collective-permute-done((bf16[2,272,128]{2,1,0:T(8,128)(2,1)S(1)}, bf16[2,272,128]{2,1,0:T(8,128)(2,1)S(1)}, u32[]{:S(2)}, u32[]{:S(2)}) %collective-permute-start.10) | collective-permute-done | bytes 139296 | tf_op jit(solution)/shard_map/ppermute | solution.py:588
  35.8 1.6 %collective-permute-start.11 = (bf16[1,272,128]{2,1,0:T(8,128)(2,1)S(1)}, bf16[1,272,128]{2,1,0:T(8,128)(2,1)S(1)}, u32[]{:S(2)}, u32[]{:S(2)}) collective-permute-start(bf16[1,272,128]{2,1,0:T(8,128)(2,1)S(1)} %slice.81), channel_id=1, source_target_pairs={{0,16},{4,12},{8,24},{12,4},{16,0},{20,28},{24,8},{28,20},{1,17},{... | collective-permute-start | bytes 208904 | tf_op jit(solution)/shard_map/ppermute | solution.py:588
  37.4 2.8 %collective-permute-done.11 = bf16[1,272,128]{2,1,0:T(8,128)(2,1)S(1)} collective-permute-done((bf16[1,272,128]{2,1,0:T(8,128)(2,1)S(1)}, bf16[1,272,128]{2,1,0:T(8,128)(2,1)S(1)}, u32[]{:S(2)}, u32[]{:S(2)}) %collective-permute-start.11) | collective-permute-done | bytes 69664 | tf_op jit(solution)/shard_map/ppermute | solution.py:588
  40.2 2.1 %collective-permute-start.14 = (bf16[1,272,128]{2,1,0:T(8,128)(2,1)S(1)}, bf16[1,272,128]{2,1,0:T(8,128)(2,1)S(1)}, u32[]{:S(2)}, u32[]{:S(2)}) collective-permute-start(bf16[1,272,128]{2,1,0:T(8,128)(2,1)S(1)} %fusion), channel_id=1, source_target_pairs={{0,3},{1,2},{2,1},{3,0},{4,7},{5,6},{6,5},{7,4},{8,11},{9,10},{10,... | collective-permute-start | bytes 208904 | tf_op jit(solution)/shard_map/ppermute | solution.py:594
  42.3 1.5 %collective-permute-start.13 = (bf16[1,272,128]{2,1,0:T(8,128)(2,1)S(1)}, bf16[1,272,128]{2,1,0:T(8,128)(2,1)S(1)}, u32[]{:S(2)}, u32[]{:S(2)}) collective-permute-start(bf16[1,272,128]{2,1,0:T(8,128)(2,1)S(1)} %fusion), channel_id=1, source_target_pairs={{0,2},{1,3},{2,0},{3,1},{4,6},{5,7},{6,4},{7,5},{8,10},{9,11},{10,... | collective-permute-start | bytes 208904 | tf_op jit(solution)/shard_map/ppermute | solution.py:594
  44.6 1.8 %collective-permute-done.14 = bf16[1,272,128]{2,1,0:T(8,128)(2,1)S(1)} collective-permute-done((bf16[1,272,128]{2,1,0:T(8,128)(2,1)S(1)}, bf16[1,272,128]{2,1,0:T(8,128)(2,1)S(1)}, u32[]{:S(2)}, u32[]{:S(2)}) %collective-permute-start.14) | collective-permute-done | bytes 69664 | tf_op jit(solution)/shard_map/ppermute | solution.py:594
  46.5 2.1 %collective-permute-done.13 = bf16[1,272,128]{2,1,0:T(8,128)(2,1)S(1)} collective-permute-done((bf16[1,272,128]{2,1,0:T(8,128)(2,1)S(1)}, bf16[1,272,128]{2,1,0:T(8,128)(2,1)S(1)}, u32[]{:S(2)}, u32[]{:S(2)}) %collective-permute-start.13) | collective-permute-done | bytes 69664 | tf_op jit(solution)/shard_map/ppermute | solution.py:594
  48.8 1.1 %collective-permute-start.15 = (bf16[1,272,128]{2,1,0:T(8,128)(2,1)S(1)}, bf16[1,272,128]{2,1,0:T(8,128)(2,1)S(1)}, u32[]{:S(2)}, u32[]{:S(2)}) collective-permute-start(bf16[1,272,128]{2,1,0:T(8,128)(2,1)S(1)} %add_convert_fusion), channel_id=1, source_target_pairs={{0,16},{4,12},{8,24},{12,4},{16,0},{20,28},{24,8},{28,20},{1,17},{... | collective-permute-start | bytes 208904 | tf_op jit(solution)/shard_map/ppermute | solution.py:588
  49.9 4.0 %collective-permute-done.15 = bf16[1,272,128]{2,1,0:T(8,128)(2,1)S(1)} collective-permute-done((bf16[1,272,128]{2,1,0:T(8,128)(2,1)S(1)}, bf16[1,272,128]{2,1,0:T(8,128)(2,1)S(1)}, u32[]{:S(2)}, u32[]{:S(2)}) %collective-permute-start.15) | collective-permute-done | bytes 69664 | tf_op jit(solution)/shard_map/ppermute | solution.py:588
  53.9 0.9 %collective-permute-start.16 = (bf16[2,272,128]{2,1,0:T(8,128)(2,1)S(1)}, bf16[2,272,128]{2,1,0:T(8,128)(2,1)S(1)}, u32[]{:S(2)}, u32[]{:S(2)}) collective-permute-start(bf16[2,272,128]{2,1,0:T(8,128)(2,1)S(1)} %pad_maximum_fusion.1), channel_id=1, source_target_pairs={{0,8},{4,20},{8,0},{12,28},{16,24},{20,4},{24,16},{28,12},{1,9},{5... | collective-permute-start | bytes 417800 | tf_op jit(solution)/shard_map/ppermute | solution.py:588
  54.8 4.2 %collective-permute-done.16 = bf16[2,272,128]{2,1,0:T(8,128)(2,1)S(1)} collective-permute-done((bf16[2,272,128]{2,1,0:T(8,128)(2,1)S(1)}, bf16[2,272,128]{2,1,0:T(8,128)(2,1)S(1)}, u32[]{:S(2)}, u32[]{:S(2)}) %collective-permute-start.16) | collective-permute-done | bytes 139296 | tf_op jit(solution)/shard_map/ppermute | solution.py:588
  59.1 1.5 %collective-permute-done.17.got_ref = bf16[4,272,128]{2,1,0:T(8,128)(2,1)S(1)} collective-permute-done((bf16[4,272,128]{2,1,0:T(8,128)(2,1)S(1)}, bf16[4,272,128]{2,1,0:T(8,128)(2,1)S(1)}, u32[]{:S(2)}, u32[]{:S(2)}) %collective-permute-start.17) | collective-permute-done | bytes 278560 | tf_op jit(solution)/shard_map/ppermute | solution.py:591
  60.7 1.6 %shard_map.65 = (f32[64,864]{1,0:T(8,128)}, f32[1728,128]{1,0:T(8,128)}) custom-call(s32[2]{0:T(128)S(1)} %pad_add_fusion.place_ref, bf16[4,272,128]{2,1,0:T(8,128)(2,1)S(1)} %pad_maximum_fusion.keep_ref, bf16[4,272,128]{2,1,0:T(8,128)(2,1)S(1)} %collective-permute-done.17.got_ref), custom_call_target="tpu_custom_call" | custom-call | tf_op jit(solution)/shard_map/pallas_call | solution.py:606
  (36 shorter events, 3.9 us)
Async XLA Ops:
  2.6 6.7 %collective-permute-start = (bf16[17,4,1024]{2,1,0:T(4,128)(2,1)S(1)}, bf16[17,4,1024]{2,1,0:T(4,128)(2,1)S(1)}, u32[]{:S(2)}, u32[]{:S(2)}) collective-permute-start(bf16[17,4,1024]{2,1,0:T(4,128)(2,1)S(1)} %get-tuple-element.28), channel_id=1, source_target_pairs={{0,16},{16,0},{1,17},{17,1},{2,18},{18,2},{3,19},{19,3},{4,20},{20... | collective-permute-start | bytes 417800 | tf_op jit(solution)/shard_map/ppermute | solution.py:548
  7.3 4.8 %collective-permute-start.1 = (bf16[34,4,1024]{2,1,0:T(4,128)(2,1)S(1)}, bf16[34,4,1024]{2,1,0:T(4,128)(2,1)S(1)}, u32[]{:S(2)}, u32[]{:S(2)}) collective-permute-start(bf16[34,4,1024]{2,1,0:T(4,128)(2,1)S(1)} %get-tuple-element.31), channel_id=1, source_target_pairs={{0,4},{8,12},{4,0},{12,8},{1,5},{9,13},{5,1},{13,9},{2,6},{10,14},... | collective-permute-start | bytes 835592 | tf_op jit(solution)/shard_map/ppermute | solution.py:549
  7.4 7.1 %collective-permute-start.2 = (bf16[34,4,1024]{2,1,0:T(4,128)(2,1)S(1)}, bf16[34,4,1024]{2,1,0:T(4,128)(2,1)S(1)}, u32[]{:S(2)}, u32[]{:S(2)}) collective-permute-start(bf16[34,4,1024]{2,1,0:T(4,128)(2,1)S(1)} %get-tuple-element.35), channel_id=1, source_target_pairs={{4,8},{8,4},{0,16},{12,28},{20,24},{24,20},{16,0},{28,12},{5,9},{9... | collective-permute-start | bytes 835592 | tf_op jit(solution)/shard_map/ppermute | solution.py:550
  9.5 4.9 %collective-permute-start.4 = (bf16[5,4,1024]{2,1,0:T(4,128)(2,1)S(1)}, bf16[5,4,1024]{2,1,0:T(4,128)(2,1)S(1)}, u32[]{:S(2)}, u32[]{:S(2)}) collective-permute-start(bf16[5,4,1024]{2,1,0:T(4,128)(2,1)S(1)} %get-tuple-element.58), channel_id=1, source_target_pairs={{4,8},{8,4},{0,16},{12,28},{20,24},{24,20},{16,0},{28,12},{5,9},{9... | collective-permute-start | bytes 122888 | tf_op jit(solution)/shard_map/ppermute | solution.py:559
  11.3 3.1 %collective-permute-start.3 = (bf16[5,4,1024]{2,1,0:T(4,128)(2,1)S(1)}, bf16[5,4,1024]{2,1,0:T(4,128)(2,1)S(1)}, u32[]{:S(2)}, u32[]{:S(2)}) collective-permute-start(bf16[5,4,1024]{2,1,0:T(4,128)(2,1)S(1)} %get-tuple-element.59), channel_id=1, source_target_pairs={{0,4},{8,12},{4,0},{12,8},{1,5},{9,13},{5,1},{13,9},{2,6},{10,14},... | collective-permute-start | bytes 122888 | tf_op jit(solution)/shard_map/ppermute | solution.py:558
  12.1 9.5 %collective-permute-start.5 = (bf16[34,16,128]{2,1,0:T(8,128)(2,1)S(1)}, bf16[34,16,128]{2,1,0:T(8,128)(2,1)S(1)}, u32[]{:S(2)}, u32[]{:S(2)}) collective-permute-start(bf16[34,16,128]{2,1,0:T(8,128)(2,1)S(1)} %get-tuple-element.44), channel_id=1, source_target_pairs={{0,1},{2,3},{1,0},{3,2},{4,5},{6,7},{5,4},{7,6},{8,9},{10,11},{9,8... | collective-permute-start | bytes 417800 | tf_op jit(solution)/shard_map/ppermute | solution.py:546
  13.8 7.9 %collective-permute-start.6 = (bf16[34,16,128]{2,1,0:T(8,128)(2,1)S(1)}, bf16[34,16,128]{2,1,0:T(8,128)(2,1)S(1)}, u32[]{:S(2)}, u32[]{:S(2)}) collective-permute-start(bf16[34,16,128]{2,1,0:T(8,128)(2,1)S(1)} %get-tuple-element.45), channel_id=1, source_target_pairs={{1,2},{2,1},{0,4},{3,7},{5,6},{6,5},{4,0},{7,3},{9,10},{10,9},{8,1... | collective-permute-start | bytes 417800 | tf_op jit(solution)/shard_map/ppermute | solution.py:546
  15.3 6.3 %collective-permute-start.7 = (bf16[46,8,128]{2,1,0:T(8,128)(2,1)S(1)}, bf16[46,8,128]{2,1,0:T(8,128)(2,1)S(1)}, u32[]{:S(2)}, u32[]{:S(2)}) collective-permute-start(bf16[46,8,128]{2,1,0:T(8,128)(2,1)S(1)} %get-tuple-element.46), channel_id=1, source_target_pairs={{0,1},{2,3},{1,0},{3,2},{4,5},{6,7},{5,4},{7,6},{8,9},{10,11},{9,8... | collective-permute-start | bytes 282632 | tf_op jit(solution)/shard_map/ppermute | solution.py:546
  17.9 3.8 %collective-permute-start.8 = (bf16[46,8,128]{2,1,0:T(8,128)(2,1)S(1)}, bf16[46,8,128]{2,1,0:T(8,128)(2,1)S(1)}, u32[]{:S(2)}, u32[]{:S(2)}) collective-permute-start(bf16[46,8,128]{2,1,0:T(8,128)(2,1)S(1)} %get-tuple-element.47), channel_id=1, source_target_pairs={{1,2},{2,1},{0,4},{3,7},{5,6},{6,5},{4,0},{7,3},{9,10},{10,9},{8,1... | collective-permute-start | bytes 282632 | tf_op jit(solution)/shard_map/ppermute | solution.py:546
  28.8 1.8 %collective-permute-start.9 = (bf16[4,272,128]{2,1,0:T(8,128)(2,1)S(1)}, bf16[4,272,128]{2,1,0:T(8,128)(2,1)S(1)}, u32[]{:S(2)}, u32[]{:S(2)}) collective-permute-start(bf16[4,272,128]{2,1,0:T(8,128)(2,1)S(1)} %get-tuple-element.51), channel_id=1, source_target_pairs={{0,4},{4,0},{8,12},{12,8},{16,20},{20,16},{24,28},{28,24},{1,5},{5... | collective-permute-start | bytes 835592 | tf_op jit(solution)/shard_map/ppermute | solution.py:591
  30.6 5.1 %collective-permute-start.10 = (bf16[2,272,128]{2,1,0:T(8,128)(2,1)S(1)}, bf16[2,272,128]{2,1,0:T(8,128)(2,1)S(1)}, u32[]{:S(2)}, u32[]{:S(2)}) collective-permute-start(bf16[2,272,128]{2,1,0:T(8,128)(2,1)S(1)} %slice.80), channel_id=1, source_target_pairs={{0,8},{4,20},{8,0},{12,28},{16,24},{20,4},{24,16},{28,12},{1,9},{5... | collective-permute-start | bytes 417800 | tf_op jit(solution)/shard_map/ppermute | solution.py:588
  35.8 4.4 %collective-permute-start.11 = (bf16[1,272,128]{2,1,0:T(8,128)(2,1)S(1)}, bf16[1,272,128]{2,1,0:T(8,128)(2,1)S(1)}, u32[]{:S(2)}, u32[]{:S(2)}) collective-permute-start(bf16[1,272,128]{2,1,0:T(8,128)(2,1)S(1)} %slice.81), channel_id=1, source_target_pairs={{0,16},{4,12},{8,24},{12,4},{16,0},{20,28},{24,8},{28,20},{1,17},{... | collective-permute-start | bytes 208904 | tf_op jit(solution)/shard_map/ppermute | solution.py:588
  40.2 6.3 %collective-permute-start.14 = (bf16[1,272,128]{2,1,0:T(8,128)(2,1)S(1)}, bf16[1,272,128]{2,1,0:T(8,128)(2,1)S(1)}, u32[]{:S(2)}, u32[]{:S(2)}) collective-permute-start(bf16[1,272,128]{2,1,0:T(8,128)(2,1)S(1)} %fusion), channel_id=1, source_target_pairs={{0,3},{1,2},{2,1},{3,0},{4,7},{5,6},{6,5},{7,4},{8,11},{9,10},{10,... | collective-permute-start | bytes 208904 | tf_op jit(solution)/shard_map/ppermute | solution.py:594
  42.3 6.3 %collective-permute-start.13 = (bf16[1,272,128]{2,1,0:T(8,128)(2,1)S(1)}, bf16[1,272,128]{2,1,0:T(8,128)(2,1)S(1)}, u32[]{:S(2)}, u32[]{:S(2)}) collective-permute-start(bf16[1,272,128]{2,1,0:T(8,128)(2,1)S(1)} %fusion), channel_id=1, source_target_pairs={{0,2},{1,3},{2,0},{3,1},{4,6},{5,7},{6,4},{7,5},{8,10},{9,11},{10,... | collective-permute-start | bytes 208904 | tf_op jit(solution)/shard_map/ppermute | solution.py:594
  43.8 4.9 %collective-permute-start.12 = (bf16[1,272,128]{2,1,0:T(8,128)(2,1)S(1)}, bf16[1,272,128]{2,1,0:T(8,128)(2,1)S(1)}, u32[]{:S(2)}, u32[]{:S(2)}) collective-permute-start(bf16[1,272,128]{2,1,0:T(8,128)(2,1)S(1)} %fusion), channel_id=1, source_target_pairs={{0,1},{1,0},{2,3},{3,2},{4,5},{5,4},{6,7},{7,6},{8,9},{9,8},{10,11... | collective-permute-start | bytes 208904 | tf_op jit(solution)/shard_map/ppermute | solution.py:594
  48.8 5.1 %collective-permute-start.15 = (bf16[1,272,128]{2,1,0:T(8,128)(2,1)S(1)}, bf16[1,272,128]{2,1,0:T(8,128)(2,1)S(1)}, u32[]{:S(2)}, u32[]{:S(2)}) collective-permute-start(bf16[1,272,128]{2,1,0:T(8,128)(2,1)S(1)} %add_convert_fusion), channel_id=1, source_target_pairs={{0,16},{4,12},{8,24},{12,4},{16,0},{20,28},{24,8},{28,20},{1,17},{... | collective-permute-start | bytes 208904 | tf_op jit(solution)/shard_map/ppermute | solution.py:588
  53.9 5.1 %collective-permute-start.16 = (bf16[2,272,128]{2,1,0:T(8,128)(2,1)S(1)}, bf16[2,272,128]{2,1,0:T(8,128)(2,1)S(1)}, u32[]{:S(2)}, u32[]{:S(2)}) collective-permute-start(bf16[2,272,128]{2,1,0:T(8,128)(2,1)S(1)} %pad_maximum_fusion.1), channel_id=1, source_target_pairs={{0,8},{4,20},{8,0},{12,28},{16,24},{20,4},{24,16},{28,12},{1,9},{5... | collective-permute-start | bytes 417800 | tf_op jit(solution)/shard_map/ppermute | solution.py:588
  59.1 1.6 %collective-permute-start.17 = (bf16[4,272,128]{2,1,0:T(8,128)(2,1)S(1)}, bf16[4,272,128]{2,1,0:T(8,128)(2,1)S(1)}, u32[]{:S(2)}, u32[]{:S(2)}) collective-permute-start(bf16[4,272,128]{2,1,0:T(8,128)(2,1)S(1)} %pad_maximum_fusion.keep_ref), channel_id=1, source_target_pairs={{0,4},{4,0},{8,12},{12,8},{16,20},{20,16},{24,28},{28,24},{1,5},{5... | collective-permute-start | bytes 835592 | tf_op jit(solution)/shard_map/ppermute | solution.py:591

commit v5 on v2

--- a/solution.py
+++ b/solution.py
@@ -57,12 +57,31 @@
     copies[3].wait()
 
 
-def pack(
-    flag_ref, vol_ref, cot_ref, first_hbm, second_hbm, row_b_ref, row_a_ref, col_a_ref, col_b_ref,
-    first_ref, second_ref, arrived,
+def pack_rows(flag_ref, vol_ref, cot_ref, row_b_ref, row_a_ref):
+    row_even, row_inner = flag_ref[1] == 0, flag_ref[3] != 0
+    planes, high, width = vol_ref.shape
+    cots = cot_ref.shape[0]
+
+    def plane(d, carry):
+        for m in range(width // LANES):
+            lanes = slice(m * LANES, (m + 1) * LANES)
+            block = vol_ref[d, :, lanes].astype(F32)
+            low, top = block[:4], block[high - 4 :]
+            row_a_ref[d, :, lanes] = jnp.where(row_even, top, low).astype(BF16)
+            row_b_ref[d, :, lanes] = jnp.where(row_inner, jnp.where(row_even, low, top), 0.0).astype(BF16)
+        return carry
+
+    lax.fori_loop(0, planes, plane, 0, unroll=4)
+    for g in range(cots // 4):
+        tops = jnp.concatenate([cot_ref[4 * g + n].astype(F32)[:1] for n in range(4)], axis=0)
+        row_a_ref[planes + g] = tops.astype(BF16)
+        row_b_ref[planes + g] = jnp.where(row_inner, tops, 0.0).astype(BF16)
+
+
+def pack_sides(
+    flag_ref, vol_ref, cot_ref, first_hbm, second_hbm, col_a_ref, col_b_ref, first_ref, second_ref, arrived
 ):
-    row_even, col_even = flag_ref[1] == 0, flag_ref[2] == 0
-    row_inner, col_inner = flag_ref[3] != 0, flag_ref[4] != 0
+    col_even, col_inner = flag_ref[2] == 0, flag_ref[4] != 0
     planes, high, width = vol_ref.shape
     cots = cot_ref.shape[0]
     copies = [
@@ -71,32 +90,24 @@
     ]
     for copy in copies:
         copy.start()
-
-    cot = cot_ref[...].astype(F32)
     for g in range(cots // 4):
-        tops = jnp.concatenate([cot[4 * g + n, :1] for n in range(4)], axis=0)
-        row_a_ref[planes + g] = tops.astype(BF16)
-        row_b_ref[planes + g] = jnp.where(row_inner, tops, 0.0).astype(BF16)
-        side = jnp.concatenate([cot[4 * g + n, :, :LANES] for n in range(4)], axis=0)
+        side = jnp.concatenate([cot_ref[4 * g + n, :, :LANES].astype(F32) for n in range(4)], axis=0)
         col_a_ref[planes + g] = side.astype(BF16)
         col_b_ref[planes + g] = jnp.where(col_inner, side, 0.0).astype(BF16)
 
     def plane(d, carry):
-        block = vol_ref[d].astype(F32)
-        low, top = block[:4], block[high - 4 :]
-        row_a_ref[d] = jnp.where(row_even, top, low).astype(BF16)
-        row_b_ref[d] = jnp.where(row_inner, jnp.where(row_even, low, top), 0.0).astype(BF16)
-        left, right = block[:, :LANES], block[:, width - LANES :]
+        left = vol_ref[d, :, :LANES].astype(F32)
+        right = vol_ref[d, :, width - LANES :].astype(F32)
         col_a_ref[d] = jnp.where(col_even, right, left).astype(BF16)
         col_b_ref[d] = jnp.where(col_inner, jnp.where(col_even, left, right), 0.0).astype(BF16)
         return carry
 
-    lax.fori_loop(0, planes, plane, 0, unroll=2)
+    lax.fori_loop(0, planes, plane, 0, unroll=4)
     for copy in copies:
         copy.wait()
 
 
-def pack_corners(flag_ref, dep_ref, row_a_ref, row_b_ref, edge_a_ref, edge_b_ref, col_a_ref, col_b_ref):
+def pack_corners(flag_ref, row_b_ref, row_a_ref, dep_ref, edge_a_ref, edge_b_ref, col_a_ref, col_b_ref):
     row_even, col_even, col_inner = flag_ref[1] == 0, flag_ref[2] == 0, flag_ref[4] != 0
     width = dep_ref.shape[2]
     groups = row_a_ref.shape[0]
@@ -118,7 +129,7 @@
         lower_upper(row_a_ref, row_b_ref, d, d)
         return carry
 
-    lax.fori_loop(0, planes, plane, 0)
+    lax.fori_loop(0, planes, plane, 0, unroll=4)
     for q in range(4):
         lower_upper(edge_a_ref, edge_b_ref, q, planes + q)
         for n in range(2):
@@ -438,19 +449,24 @@
     for n in range(squares):
         for ref, half in ((keep_ref, core), (give_ref, 1 - core)):
             start = pl.multiple_of((half * squares + (square ^ n)) * size, 8)
-            ref[n] = out_ref[pl.ds(start, size), :].astype(BF16)
-
-
-def unpack(place_ref, keep_ref, got_ref, g1_ref, g2_ref, sums):
+            ref[n] = out_ref[pl.ds(start, size), :].astype(ref.dtype)
+
+
+def unpack(place_ref, keep_ref, got_ref, g1_hbm, g2_hbm, sums, first, sent):
     core, square = place_ref[0], place_ref[1]
     squares, size = keep_ref.shape[0], keep_ref.shape[1]
     for n in range(squares):
         for ref, half in ((keep_ref, core), (got_ref, 1 - core)):
             start = pl.multiple_of((half * squares + (square ^ n)) * size, 8)
             sums[pl.ds(start, size), :] = ref[n].astype(F32)
-    first = [sums[SECOND_ROWS + 64 * n : SECOND_ROWS + 64 * (n + 1), :] for n in range(FIRST_BLOCKS)]
-    g1_ref[...] = jnp.concatenate(first, axis=1)[:, : g1_ref.shape[1]]
-    g2_ref[...] = sums[:SECOND_ROWS, :]
+    second = pltpu.make_async_copy(sums.at[pl.ds(0, SECOND_ROWS)], g2_hbm, sent.at[0])
+    second.start()
+    found = [sums[SECOND_ROWS + 64 * n : SECOND_ROWS + 64 * (n + 1), :] for n in range(FIRST_BLOCKS)]
+    first[...] = jnp.concatenate(found, axis=1)[:, : first.shape[1]]
+    copy = pltpu.make_async_copy(first, g1_hbm, sent.at[1])
+    copy.start()
+    copy.wait()
+    second.wait()
 
 
 def local_grads(flags, place, squares, volume, faces, corners, cotangent, weights):
@@ -490,7 +506,7 @@
     operands = (tiles, parts, *faces, *corners, cotangent, *weights)
     return pl.pallas_call(
         body,
-        out_shape=[jax.ShapeDtypeStruct((squares, rows // (2 * squares), LANES), BF16)] * 2,
+        out_shape=[jax.ShapeDtypeStruct((squares, rows // (2 * squares), LANES), dtype) for dtype in (F32, BF16)],
         in_specs=[smem] * 2 + [whole] * len(operands),
         out_specs=[whole] * 2,
         scratch_shapes=scratch,
@@ -523,11 +539,28 @@
         scratch_shapes=[pltpu.SemaphoreType.DMA((4,))],
         compiler_params=small,
     )(flags, stay(volume), stay(cotangent))
+    row_b, row_a = pl.pallas_call(
+        pack_rows,
+        out_shape=[jax.ShapeDtypeStruct((groups, 4, width), BF16)] * 2,
+        in_specs=[smem] + [whole] * 2,
+        out_specs=[whole] * 2,
+        compiler_params=small,
+    )(flags, volume, cotangent)
+
+    def to_col(block, kind):
+        return lax.ppermute(block, ("row", "col"), pairs_of_lines(rows, cols, kind))
+
+    dep = lax.ppermute(dep, "depth", [(0, 1), (1, 0)])
+    route = []
+    for i, j in pairs_on_line(rows, 1):
+        route += [((d * rows + i) * cols + c, (d * rows + j) * cols + (c ^ 1 if i == j else c)) for d in (0, 1) for c in range(cols)]
+    row_b = lax.ppermute(row_b, ("depth", "row", "col"), route)
+    row_a = lax.ppermute(row_a, "row", pairs_on_line(rows, 0))
+    row_a, volume, cotangent = lax.optimization_barrier((row_a, volume, cotangent))
     weights = (first_weight, second_weight.T)
-    shapes = [(groups, 4, width)] * 2 + [(groups, high, LANES)] * 2
-    shapes += [weight.shape for weight in weights]
-    row_b, row_a, side_a, side_b, first_taps, second_taps = pl.pallas_call(
-        pack,
+    shapes = [(groups, high, LANES)] * 2 + [weight.shape for weight in weights]
+    side_a, side_b, first_taps, second_taps = pl.pallas_call(
+        pack_sides,
         out_shape=[jax.ShapeDtypeStruct(shape, BF16) for shape in shapes],
         in_specs=[smem] + [whole] * 2 + [in_hbm] * 2,
         out_specs=[whole] * len(shapes),
@@ -535,15 +568,7 @@
         compiler_params=small,
     )(flags, volume, cotangent, *[stay(weight) for weight in weights])
 
-    def to_col(block, kind):
-        return lax.ppermute(block, ("row", "col"), pairs_of_lines(rows, cols, kind))
-
-    dep = lax.ppermute(dep, "depth", [(0, 1), (1, 0)])
-    row_a = lax.ppermute(row_a, "row", pairs_on_line(rows, 0))
-    row_b = lax.ppermute(row_b, ("depth", "row"), pairs_of_lines(2, rows, 1))
-    row_a, side_a, side_b = lax.optimization_barrier((row_a, side_a, side_b))
     side_a, side_b = to_col(side_a, 0), to_col(side_b, 1)
-
     low, top = [jnp.concatenate([dep[n : n + 1] for n in (*range(k, 16, 4), 16)], axis=0) for k in (0, 3)]
     even, ends = row % 2 == 0, jnp.logical_or(row == 0, row == rows - 1)
     edge_a = jnp.where(even, top, low)
@@ -557,13 +582,14 @@
         out_specs=[whole] * 3,
         compiler_params=small,
     )(first_taps, second_taps)
+    row_b, weights = lax.optimization_barrier((row_b, weights))
     col_a, col_b = pl.pallas_call(
         pack_corners,
         out_shape=[jax.ShapeDtypeStruct((planes + 14, 8, LANES), BF16)] * 2,
         in_specs=[smem] + [whole] * 5,
         out_specs=[whole] * 2,
         compiler_params=small,
-    )(flags, dep, row_a, row_b, edge_a, edge_b)
+    )(flags, row_b, row_a, dep, edge_a, edge_b)
     col_a, col_b, volume = lax.optimization_barrier((col_a, col_b, volume))
     col_a, col_b = to_col(col_a, 0), to_col(col_b, 1)
 
@@ -583,8 +609,9 @@
     def along_col(block, n):
         return lax.ppermute(block, "col", [(i, i ^ n) for i in range(cols)])
 
-    both = add_up(keep, to_core(give))
-    share = add_up(both[0], *[to_square(both[n], n) for n in range(1, squares)])
+    both = keep + to_core(give).astype(F32)
+    near = both.astype(BF16)
+    share = add_up(both[0], *[to_square(near[n], n) for n in range(1, squares)])
     share = add_up(share, *[along_col(share, n) for n in range(1, cols)])
     mine = jnp.stack([share] + [to_square(share, n) for n in range(1, squares)])
     other = to_core(mine)
@@ -593,8 +620,12 @@
         unpack,
         out_shape=grads,
         in_specs=[smem] + [whole] * 2,
-        out_specs=[whole] * 2,
-        scratch_shapes=[pltpu.VMEM((mine.shape[0] * mine.shape[1] * 2, LANES), F32)],
+        out_specs=[in_hbm] * 2,
+        scratch_shapes=[
+            pltpu.VMEM((mine.shape[0] * mine.shape[1] * 2, LANES), F32),
+            pltpu.VMEM(first_weight.shape, F32),
+            pltpu.SemaphoreType.DMA((2,)),
+        ],
         compiler_params=small,
     )(where, mine, other)
     return first_grad, second_grad.T

time: 58.4 us -> 59 us (1.010)
  waiting for transfers between devices: 17.7 us -> 15.5 us
  starting transfers between devices: 21.7 us -> 23.7 us
  Pallas kernels: 17.5 us -> 18.3 us
    ppermute x1, starting transfers between devices: 0.08 us -> 1.64 us  [shards(): row_b = lax.ppermute(row_b, ('depth', 'row', 'col'), route)]
    pallas_call x1 -> x2, Pallas kernels: 1.63 us -> 2.62 us  [the longest x1 1.64 us: shards(): pl.pallas_call(pack_sides, out_shape=[jax.ShapeDtypeStruct(shape, BF16) f...]
    ppermute x1, waiting for transfers between devices: 1.84 us -> 1.01 us  [shards(): dep = lax.ppermute(dep, 'depth', [(0, 1), (1, 0)])]
    ppermute x3, waiting for transfers between devices: 4.92 us -> 4.18 us  [along_col(): return lax.ppermute(block, 'col', [(i, i ^ n) for i in range(cols)])]
  transfers between devices with their start and end apart: 20 -> 20, of which waited for: 12 -> 11; matrix products, arithmetic and copies ran while one was open for 0% -> 0% of each run, Pallas kernels for 12% -> 13%
where the time goes in v5:
time: 59 us; the launch traced here: 58.8 us
  starting transfers between devices  23.7 us (40%)
  Pallas kernels  18.3 us (31%)
  waiting for transfers between devices  15.5 us (26%)
  between operations  0.85 us (1%)
    ppermute x6, waiting for transfers between devices, to_square(): return lax.ppermute(block, ('depth', 'row'), route)  7.55 us
    ppermute x6, starting transfers between devices, to_square(): return lax.ppermute(block, ('depth', 'row'), route)  7.12 us
    pallas_call x1, Pallas kernels, local_grads(): pl.pallas_call(body, out_shape=[jax.ShapeDtypeStruct((squares, rows // (2...  7.1 us
    ppermute x4, starting transfers between devices, to_col(): return lax.ppermute(block, ('row', 'col'), pairs_of_lines(rows, cols, kind))  4.86 us
    ppermute x3, starting transfers between devices, along_col(): return lax.ppermute(block, 'col', [(i, i ^ n) for i in range(cols)])  4.45 us
    ppermute x3, waiting for transfers between devices, along_col(): return lax.ppermute(block, 'col', [(i, i ^ n) for i in range(cols)])  4.18 us
    pallas_call x1, Pallas kernels, local_grads(): pl.pallas_call(own_blocks, out_shape=[jax.ShapeDtypeStruct((3, planes + 9...  3.76 us
    ppermute x1, starting transfers between devices, shards(): dep = lax.ppermute(dep, 'depth', [(0, 1), (1, 0)])  3.03 us
  transfers between devices with their start and end apart: 20, of which 11 were waited for; matrix products, arithmetic and copies ran while one was open for 0% of the time, Pallas kernels for 13%

profile of v5, /device:TPU:0, one launch (start us, length us, event | category | flops | bytes accessed | tf_op | source)
XLA Modules:
  0.0 58.8 jit_solution(12570772309733349285)
XLA Ops:
  0.7 1.9 %shard_map.59 = (bf16[32,16,1024]{2,1,0:T(8,128)(2,1)S(1)}, bf16[8,4,1024]{2,1,0:T(4,128)(2,1)S(1)}, bf16[17,4,1024]{2,1,0:T(4,128)(2,1)S(1)}) custom-call(s32[5]{0:T(128)S(1)} %stack.58.flag_ref, bf16[32,16,1024]{2,1,0:T(8,128)(2,1)} %vol_hbm.1, bf16[8,4,1024]{2,1,0:T(4,128)(2,1)} %cot_hbm.1), custom_call_target="tpu_custom_call" | custom-call | tf_op jit(solution)/shard_map/pallas_call | solution.py:534
  2.6 3.0 %collective-permute-start.2 = (bf16[17,4,1024]{2,1,0:T(4,128)(2,1)S(1)}, bf16[17,4,1024]{2,1,0:T(4,128)(2,1)S(1)}, u32[]{:S(2)}, u32[]{:S(2)}) collective-permute-start(bf16[17,4,1024]{2,1,0:T(4,128)(2,1)S(1)} %get-tuple-element.45), channel_id=1, source_target_pairs={{0,16},{16,0},{1,17},{17,1},{2,18},{18,2},{3,19},{19,3},{4,20},{20... | collective-permute-start | bytes 417800 | tf_op jit(solution)/shard_map/ppermute | solution.py:553
  6.7 1.6 %collective-permute-start = (bf16[34,4,1024]{2,1,0:T(4,128)(2,1)S(1)}, bf16[34,4,1024]{2,1,0:T(4,128)(2,1)S(1)}, u32[]{:S(2)}, u32[]{:S(2)}) collective-permute-start(bf16[34,4,1024]{2,1,0:T(4,128)(2,1)S(1)} %get-tuple-element.34), channel_id=1, source_target_pairs={{4,8},{5,9},{6,10},{7,11},{20,24},{21,25},{22,26},{23,27},{8,4},{9... | collective-permute-start | bytes 835592 | tf_op jit(solution)/shard_map/ppermute | solution.py:557
  8.3 1.0 %collective-permute-done.2.dep_ref = bf16[17,4,1024]{2,1,0:T(4,128)(2,1)S(1)} collective-permute-done((bf16[17,4,1024]{2,1,0:T(4,128)(2,1)S(1)}, bf16[17,4,1024]{2,1,0:T(4,128)(2,1)S(1)}, u32[]{:S(2)}, u32[]{:S(2)}) %collective-permute-start.2) | collective-permute-done | bytes 139296 | tf_op jit(solution)/shard_map/ppermute | solution.py:553
  9.5 1.8 %collective-permute-start.4 = (bf16[5,4,1024]{2,1,0:T(4,128)(2,1)S(1)}, bf16[5,4,1024]{2,1,0:T(4,128)(2,1)S(1)}, u32[]{:S(2)}, u32[]{:S(2)}) collective-permute-start(bf16[5,4,1024]{2,1,0:T(4,128)(2,1)S(1)} %get-tuple-element.71), channel_id=1, source_target_pairs={{4,8},{8,4},{0,16},{12,28},{20,24},{24,20},{16,0},{28,12},{5,9},{9... | collective-permute-start | bytes 122888 | tf_op jit(solution)/shard_map/ppermute | solution.py:577
  11.5 1.6 %shard_map.61 = (bf16[34,16,128]{2,1,0:T(8,128)(2,1)S(1)}, bf16[34,16,128]{2,1,0:T(8,128)(2,1)S(1)}, bf16[64,864]{1,0:T(8,128)(2,1)S(1)}, bf16[1728,128]{1,0:T(8,128)(2,1)S(1)}) custom-call(s32[5]{0:T(128)S(1)} %stack.58.flag_ref, bf16[32,16,1024]{2,1,0:T(8,128)(2,1)S(1)} %get-tuple-element.48.vol_ref, bf16[8,4,1024]{2,1,0:T(4,128)(2,1)S(1)} %get-tuple-element.37.cot_ref, ...), custom_call_target="tpu_custom_call" | custom-call | tf_op jit(solution)/shard_map/pallas_call | solution.py:562
  13.1 1.6 %collective-permute-start.5 = (bf16[34,16,128]{2,1,0:T(8,128)(2,1)S(1)}, bf16[34,16,128]{2,1,0:T(8,128)(2,1)S(1)}, u32[]{:S(2)}, u32[]{:S(2)}) collective-permute-start(bf16[34,16,128]{2,1,0:T(8,128)(2,1)S(1)} %get-tuple-element.52), channel_id=1, source_target_pairs={{0,1},{2,3},{1,0},{3,2},{4,5},{6,7},{5,4},{7,6},{8,9},{10,11},{9,8... | collective-permute-start | bytes 417800 | tf_op jit(solution)/shard_map/ppermute | solution.py:551
  16.3 3.1 %collective-permute-start.7 = (bf16[46,8,128]{2,1,0:T(8,128)(2,1)S(1)}, bf16[46,8,128]{2,1,0:T(8,128)(2,1)S(1)}, u32[]{:S(2)}, u32[]{:S(2)}) collective-permute-start(bf16[46,8,128]{2,1,0:T(8,128)(2,1)S(1)} %get-tuple-element.54), channel_id=1, source_target_pairs={{0,1},{2,3},{1,0},{3,2},{4,5},{6,7},{5,4},{7,6},{8,9},{10,11},{9,8... | collective-permute-start | bytes 282632 | tf_op jit(solution)/shard_map/ppermute | solution.py:551
  19.4 3.8 %shard_map.64 = (bf16[3,41,8,16,128]{4,3,2,1,0:T(8,128)(2,1)S(1)}, f32[20,8,16,256]{3,2,1,0:T(8,128)S(1)}) custom-call(s32[5]{0:T(128)S(1)} %stack.58.flag_ref, bf16[32,16,1024]{2,1,0:T(8,128)(2,1)S(1)} %get-tuple-element.48.vol_ref, bf16[17,4,1024]{2,1,0:T(4,128)(2,1)S(1)} %collective-permute-done.2.dep_ref, ...), custom_call_target="tpu_custom_call" | custom-call | flops 2000000000 | bytes 10000000 | tf_op jit(solution)/shard_map/pallas_call | solution.py:482
  23.2 7.1 %shard_map.65 = (f32[4,272,128]{2,1,0:T(8,128)S(1)}, bf16[4,272,128]{2,1,0:T(8,128)(2,1)S(1)}) custom-call(s32[5]{0:T(128)S(1)} %stack.58.flag_ref, s32[2]{0:T(128)S(1)} %pad_add_fusion.place_ref, bf16[3,41,8,16,128]{4,3,2,1,0:T(8,128)(2,1)S(1)} %get-tuple-element.50.tiles, f32[20,8,16,256]{3,2,1,0:T(8,128)S(1)} %get-tuple-element.51.parts, ...), custom_call_target="tpu_custom_call" | custom-call | flops 4000000000 | bytes 10000000 | tf_op jit(solution)/shard_map/pallas_call | solution.py:507
  30.9 1.2 %collective-permute-done.9 = bf16[4,272,128]{2,1,0:T(8,128)(2,1)S(1)} collective-permute-done((bf16[4,272,128]{2,1,0:T(8,128)(2,1)S(1)}, bf16[4,272,128]{2,1,0:T(8,128)(2,1)S(1)}, u32[]{:S(2)}, u32[]{:S(2)}) %collective-permute-start.9) | collective-permute-done | bytes 278560 | tf_op jit(solution)/shard_map/ppermute | solution.py:607
  32.3 2.9 %collective-permute-start.12 = (bf16[272,128]{1,0:T(8,128)(2,1)S(1)}, bf16[272,128]{1,0:T(8,128)(2,1)S(1)}, u32[]{:S(2)}, u32[]{:S(2)}) collective-permute-start(bf16[272,128]{1,0:T(8,128)(2,1)S(1)} %get-tuple-element.65), channel_id=1, source_target_pairs={{0,24},{4,28},{8,16},{12,20},{16,8},{20,12},{24,0},{28,4},{1,25},{... | collective-permute-start | bytes 208904 | tf_op jit(solution)/shard_map/ppermute | solution.py:604
  35.7 1.4 %collective-permute-done.10 = bf16[272,128]{1,0:T(8,128)(2,1)S(1)} collective-permute-done((bf16[272,128]{1,0:T(8,128)(2,1)S(1)}, bf16[272,128]{1,0:T(8,128)(2,1)S(1)}, u32[]{:S(2)}, u32[]{:S(2)}) %collective-permute-start.10) | collective-permute-done | bytes 69664 | tf_op jit(solution)/shard_map/ppermute | solution.py:604
  37.1 2.1 %collective-permute-done.12 = bf16[272,128]{1,0:T(8,128)(2,1)S(1)} collective-permute-done((bf16[272,128]{1,0:T(8,128)(2,1)S(1)}, bf16[272,128]{1,0:T(8,128)(2,1)S(1)}, u32[]{:S(2)}, u32[]{:S(2)}) %collective-permute-start.12) | collective-permute-done | bytes 69664 | tf_op jit(solution)/shard_map/ppermute | solution.py:604
  39.2 1.1 %collective-permute-done.11 = bf16[272,128]{1,0:T(8,128)(2,1)S(1)} collective-permute-done((bf16[272,128]{1,0:T(8,128)(2,1)S(1)}, bf16[272,128]{1,0:T(8,128)(2,1)S(1)}, u32[]{:S(2)}, u32[]{:S(2)}) %collective-permute-start.11) | collective-permute-done | bytes 69664 | tf_op jit(solution)/shard_map/ppermute | solution.py:604
  41.2 1.0 %collective-permute-start.14 = (bf16[272,128]{1,0:T(8,128)(2,1)S(1)}, bf16[272,128]{1,0:T(8,128)(2,1)S(1)}, u32[]{:S(2)}, u32[]{:S(2)}) collective-permute-start(bf16[272,128]{1,0:T(8,128)(2,1)S(1)} %fusion.2), channel_id=1, source_target_pairs={{0,2},{1,3},{2,0},{3,1},{4,6},{5,7},{6,4},{7,5},{8,10},{9,11},{10,... | collective-permute-start | bytes 208904 | tf_op jit(solution)/shard_map/ppermute | solution.py:610
  42.2 2.6 %collective-permute-start.13 = (bf16[272,128]{1,0:T(8,128)(2,1)S(1)}, bf16[272,128]{1,0:T(8,128)(2,1)S(1)}, u32[]{:S(2)}, u32[]{:S(2)}) collective-permute-start(bf16[272,128]{1,0:T(8,128)(2,1)S(1)} %fusion.2), channel_id=1, source_target_pairs={{0,1},{1,0},{2,3},{3,2},{4,5},{5,4},{6,7},{7,6},{8,9},{9,8},{10,11... | collective-permute-start | bytes 208904 | tf_op jit(solution)/shard_map/ppermute | solution.py:610
  44.8 2.5 %collective-permute-done.15 = bf16[272,128]{1,0:T(8,128)(2,1)S(1)} collective-permute-done((bf16[272,128]{1,0:T(8,128)(2,1)S(1)}, bf16[272,128]{1,0:T(8,128)(2,1)S(1)}, u32[]{:S(2)}, u32[]{:S(2)}) %collective-permute-start.15) | collective-permute-done | bytes 69664 | tf_op jit(solution)/shard_map/ppermute | solution.py:610
  47.3 1.7 %collective-permute-done.14 = bf16[272,128]{1,0:T(8,128)(2,1)S(1)} collective-permute-done((bf16[272,128]{1,0:T(8,128)(2,1)S(1)}, bf16[272,128]{1,0:T(8,128)(2,1)S(1)}, u32[]{:S(2)}, u32[]{:S(2)}) %collective-permute-start.14) | collective-permute-done | bytes 69664 | tf_op jit(solution)/shard_map/ppermute | solution.py:610
  49.7 1.5 %collective-permute-start.17 = (bf16[272,128]{1,0:T(8,128)(2,1)S(1)}, bf16[272,128]{1,0:T(8,128)(2,1)S(1)}, u32[]{:S(2)}, u32[]{:S(2)}) collective-permute-start(bf16[272,128]{1,0:T(8,128)(2,1)S(1)} %add_convert_fusion), channel_id=1, source_target_pairs={{0,16},{4,20},{8,24},{12,28},{16,0},{20,4},{24,8},{28,12},{1,17},{... | collective-permute-start | bytes 208904 | tf_op jit(solution)/shard_map/ppermute | solution.py:604
  51.2 1.4 %collective-permute-start.16 = (bf16[272,128]{1,0:T(8,128)(2,1)S(1)}, bf16[272,128]{1,0:T(8,128)(2,1)S(1)}, u32[]{:S(2)}, u32[]{:S(2)}) collective-permute-start(bf16[272,128]{1,0:T(8,128)(2,1)S(1)} %add_convert_fusion), channel_id=1, source_target_pairs={{0,8},{4,12},{8,0},{12,4},{16,24},{20,28},{24,16},{28,20},{1,9},{5... | collective-permute-start | bytes 208904 | tf_op jit(solution)/shard_map/ppermute | solution.py:604
  52.6 2.0 %collective-permute-done.18 = bf16[272,128]{1,0:T(8,128)(2,1)S(1)} collective-permute-done((bf16[272,128]{1,0:T(8,128)(2,1)S(1)}, bf16[272,128]{1,0:T(8,128)(2,1)S(1)}, u32[]{:S(2)}, u32[]{:S(2)}) %collective-permute-start.18) | collective-permute-done | bytes 69664 | tf_op jit(solution)/shard_map/ppermute | solution.py:604
  55.7 1.5 %collective-permute-done.19.got_ref = bf16[4,272,128]{2,1,0:T(8,128)(2,1)S(1)} collective-permute-done((bf16[4,272,128]{2,1,0:T(8,128)(2,1)S(1)}, bf16[4,272,128]{2,1,0:T(8,128)(2,1)S(1)}, u32[]{:S(2)}, u32[]{:S(2)}) %collective-permute-start.19) | collective-permute-done | bytes 278560 | tf_op jit(solution)/shard_map/ppermute | solution.py:607
  57.2 1.6 %shard_map.66 = (f32[64,864]{1,0:T(8,128)}, f32[1728,128]{1,0:T(8,128)}) custom-call(s32[2]{0:T(128)S(1)} %pad_add_fusion.place_ref, bf16[4,272,128]{2,1,0:T(8,128)(2,1)S(1)} %pad_maximum_fusion.keep_ref, bf16[4,272,128]{2,1,0:T(8,128)(2,1)S(1)} %collective-permute-done.19.got_ref), custom_call_target="tpu_custom_call" | custom-call | tf_op jit(solution)/shard_map/pallas_call | solution.py:619
  (38 shorter events, 7.0 us)
Async XLA Ops:
  2.6 6.7 %collective-permute-start.2 = (bf16[17,4,1024]{2,1,0:T(4,128)(2,1)S(1)}, bf16[17,4,1024]{2,1,0:T(4,128)(2,1)S(1)}, u32[]{:S(2)}, u32[]{:S(2)}) collective-permute-start(bf16[17,4,1024]{2,1,0:T(4,128)(2,1)S(1)} %get-tuple-element.45), channel_id=1, source_target_pairs={{0,16},{16,0},{1,17},{17,1},{2,18},{18,2},{3,19},{19,3},{4,20},{20... | collective-permute-start | bytes 417800 | tf_op jit(solution)/shard_map/ppermute | solution.py:553
  6.7 8.9 %collective-permute-start = (bf16[34,4,1024]{2,1,0:T(4,128)(2,1)S(1)}, bf16[34,4,1024]{2,1,0:T(4,128)(2,1)S(1)}, u32[]{:S(2)}, u32[]{:S(2)}) collective-permute-start(bf16[34,4,1024]{2,1,0:T(4,128)(2,1)S(1)} %get-tuple-element.34), channel_id=1, source_target_pairs={{4,8},{5,9},{6,10},{7,11},{20,24},{21,25},{22,26},{23,27},{8,4},{9... | collective-permute-start | bytes 835592 | tf_op jit(solution)/shard_map/ppermute | solution.py:557
  8.3 3.2 %collective-permute-start.1 = (bf16[34,4,1024]{2,1,0:T(4,128)(2,1)S(1)}, bf16[34,4,1024]{2,1,0:T(4,128)(2,1)S(1)}, u32[]{:S(2)}, u32[]{:S(2)}) collective-permute-start(bf16[34,4,1024]{2,1,0:T(4,128)(2,1)S(1)} %get-tuple-element.35), channel_id=1, source_target_pairs={{0,4},{8,12},{4,0},{12,8},{1,5},{9,13},{5,1},{13,9},{2,6},{10,14},... | collective-permute-start | bytes 835592 | tf_op jit(solution)/shard_map/ppermute | solution.py:558
  9.5 6.1 %collective-permute-start.4 = (bf16[5,4,1024]{2,1,0:T(4,128)(2,1)S(1)}, bf16[5,4,1024]{2,1,0:T(4,128)(2,1)S(1)}, u32[]{:S(2)}, u32[]{:S(2)}) collective-permute-start(bf16[5,4,1024]{2,1,0:T(4,128)(2,1)S(1)} %get-tuple-element.71), channel_id=1, source_target_pairs={{4,8},{8,4},{0,16},{12,28},{20,24},{24,20},{16,0},{28,12},{5,9},{9... | collective-permute-start | bytes 122888 | tf_op jit(solution)/shard_map/ppermute | solution.py:577
  11.3 4.3 %collective-permute-start.3 = (bf16[5,4,1024]{2,1,0:T(4,128)(2,1)S(1)}, bf16[5,4,1024]{2,1,0:T(4,128)(2,1)S(1)}, u32[]{:S(2)}, u32[]{:S(2)}) collective-permute-start(bf16[5,4,1024]{2,1,0:T(4,128)(2,1)S(1)} %get-tuple-element.72), channel_id=1, source_target_pairs={{0,4},{8,12},{4,0},{12,8},{1,5},{9,13},{5,1},{13,9},{2,6},{10,14},... | collective-permute-start | bytes 122888 | tf_op jit(solution)/shard_map/ppermute | solution.py:576
  13.1 10.0 %collective-permute-start.5 = (bf16[34,16,128]{2,1,0:T(8,128)(2,1)S(1)}, bf16[34,16,128]{2,1,0:T(8,128)(2,1)S(1)}, u32[]{:S(2)}, u32[]{:S(2)}) collective-permute-start(bf16[34,16,128]{2,1,0:T(8,128)(2,1)S(1)} %get-tuple-element.52), channel_id=1, source_target_pairs={{0,1},{2,3},{1,0},{3,2},{4,5},{6,7},{5,4},{7,6},{8,9},{10,11},{9,8... | collective-permute-start | bytes 417800 | tf_op jit(solution)/shard_map/ppermute | solution.py:551
  14.8 8.4 %collective-permute-start.6 = (bf16[34,16,128]{2,1,0:T(8,128)(2,1)S(1)}, bf16[34,16,128]{2,1,0:T(8,128)(2,1)S(1)}, u32[]{:S(2)}, u32[]{:S(2)}) collective-permute-start(bf16[34,16,128]{2,1,0:T(8,128)(2,1)S(1)} %get-tuple-element.53), channel_id=1, source_target_pairs={{1,2},{2,1},{0,4},{3,7},{5,6},{6,5},{4,0},{7,3},{9,10},{10,9},{8,1... | collective-permute-start | bytes 417800 | tf_op jit(solution)/shard_map/ppermute | solution.py:551
  16.3 6.8 %collective-permute-start.7 = (bf16[46,8,128]{2,1,0:T(8,128)(2,1)S(1)}, bf16[46,8,128]{2,1,0:T(8,128)(2,1)S(1)}, u32[]{:S(2)}, u32[]{:S(2)}) collective-permute-start(bf16[46,8,128]{2,1,0:T(8,128)(2,1)S(1)} %get-tuple-element.54), channel_id=1, source_target_pairs={{0,1},{2,3},{1,0},{3,2},{4,5},{6,7},{5,4},{7,6},{8,9},{10,11},{9,8... | collective-permute-start | bytes 282632 | tf_op jit(solution)/shard_map/ppermute | solution.py:551
  19.4 3.8 %collective-permute-start.8 = (bf16[46,8,128]{2,1,0:T(8,128)(2,1)S(1)}, bf16[46,8,128]{2,1,0:T(8,128)(2,1)S(1)}, u32[]{:S(2)}, u32[]{:S(2)}) collective-permute-start(bf16[46,8,128]{2,1,0:T(8,128)(2,1)S(1)} %get-tuple-element.55), channel_id=1, source_target_pairs={{1,2},{2,1},{0,4},{3,7},{5,6},{6,5},{4,0},{7,3},{9,10},{10,9},{8,1... | collective-permute-start | bytes 282632 | tf_op jit(solution)/shard_map/ppermute | solution.py:551
  30.3 1.8 %collective-permute-start.9 = (bf16[4,272,128]{2,1,0:T(8,128)(2,1)S(1)}, bf16[4,272,128]{2,1,0:T(8,128)(2,1)S(1)}, u32[]{:S(2)}, u32[]{:S(2)}) collective-permute-start(bf16[4,272,128]{2,1,0:T(8,128)(2,1)S(1)} %get-tuple-element.59), channel_id=1, source_target_pairs={{0,4},{4,0},{8,12},{12,8},{16,20},{20,16},{24,28},{28,24},{1,5},{5... | collective-permute-start | bytes 835592 | tf_op jit(solution)/shard_map/ppermute | solution.py:607
  32.2 5.0 %collective-permute-start.10 = (bf16[272,128]{1,0:T(8,128)(2,1)S(1)}, bf16[272,128]{1,0:T(8,128)(2,1)S(1)}, u32[]{:S(2)}, u32[]{:S(2)}) collective-permute-start(bf16[272,128]{1,0:T(8,128)(2,1)S(1)} %get-tuple-element.64), channel_id=1, source_target_pairs={{0,8},{4,12},{8,0},{12,4},{16,24},{20,28},{24,16},{28,20},{1,9},{5... | collective-permute-start | bytes 208904 | tf_op jit(solution)/shard_map/ppermute | solution.py:604
  32.3 6.9 %collective-permute-start.12 = (bf16[272,128]{1,0:T(8,128)(2,1)S(1)}, bf16[272,128]{1,0:T(8,128)(2,1)S(1)}, u32[]{:S(2)}, u32[]{:S(2)}) collective-permute-start(bf16[272,128]{1,0:T(8,128)(2,1)S(1)} %get-tuple-element.65), channel_id=1, source_target_pairs={{0,24},{4,28},{8,16},{12,20},{16,8},{20,12},{24,0},{28,4},{1,25},{... | collective-permute-start | bytes 208904 | tf_op jit(solution)/shard_map/ppermute | solution.py:604
  35.2 5.1 %collective-permute-start.11 = (bf16[272,128]{1,0:T(8,128)(2,1)S(1)}, bf16[272,128]{1,0:T(8,128)(2,1)S(1)}, u32[]{:S(2)}, u32[]{:S(2)}) collective-permute-start(bf16[272,128]{1,0:T(8,128)(2,1)S(1)} %get-tuple-element.66), channel_id=1, source_target_pairs={{0,16},{4,20},{8,24},{12,28},{16,0},{20,4},{24,8},{28,12},{1,17},{... | collective-permute-start | bytes 208904 | tf_op jit(solution)/shard_map/ppermute | solution.py:604
  40.4 7.0 %collective-permute-start.15 = (bf16[272,128]{1,0:T(8,128)(2,1)S(1)}, bf16[272,128]{1,0:T(8,128)(2,1)S(1)}, u32[]{:S(2)}, u32[]{:S(2)}) collective-permute-start(bf16[272,128]{1,0:T(8,128)(2,1)S(1)} %fusion.2), channel_id=1, source_target_pairs={{0,3},{1,2},{2,1},{3,0},{4,7},{5,6},{6,5},{7,4},{8,11},{9,10},{10,... | collective-permute-start | bytes 208904 | tf_op jit(solution)/shard_map/ppermute | solution.py:610
  41.2 7.8 %collective-permute-start.14 = (bf16[272,128]{1,0:T(8,128)(2,1)S(1)}, bf16[272,128]{1,0:T(8,128)(2,1)S(1)}, u32[]{:S(2)}, u32[]{:S(2)}) collective-permute-start(bf16[272,128]{1,0:T(8,128)(2,1)S(1)} %fusion.2), channel_id=1, source_target_pairs={{0,2},{1,3},{2,0},{3,1},{4,6},{5,7},{6,4},{7,5},{8,10},{9,11},{10,... | collective-permute-start | bytes 208904 | tf_op jit(solution)/shard_map/ppermute | solution.py:610
  42.2 6.8 %collective-permute-start.13 = (bf16[272,128]{1,0:T(8,128)(2,1)S(1)}, bf16[272,128]{1,0:T(8,128)(2,1)S(1)}, u32[]{:S(2)}, u32[]{:S(2)}) collective-permute-start(bf16[272,128]{1,0:T(8,128)(2,1)S(1)} %fusion.2), channel_id=1, source_target_pairs={{0,1},{1,0},{2,3},{3,2},{4,5},{5,4},{6,7},{7,6},{8,9},{9,8},{10,11... | collective-permute-start | bytes 208904 | tf_op jit(solution)/shard_map/ppermute | solution.py:610
  49.0 5.5 %collective-permute-start.18 = (bf16[272,128]{1,0:T(8,128)(2,1)S(1)}, bf16[272,128]{1,0:T(8,128)(2,1)S(1)}, u32[]{:S(2)}, u32[]{:S(2)}) collective-permute-start(bf16[272,128]{1,0:T(8,128)(2,1)S(1)} %add_convert_fusion), channel_id=1, source_target_pairs={{0,24},{4,28},{8,16},{12,20},{16,8},{20,12},{24,0},{28,4},{1,25},{... | collective-permute-start | bytes 208904 | tf_op jit(solution)/shard_map/ppermute | solution.py:604
  49.7 5.1 %collective-permute-start.17 = (bf16[272,128]{1,0:T(8,128)(2,1)S(1)}, bf16[272,128]{1,0:T(8,128)(2,1)S(1)}, u32[]{:S(2)}, u32[]{:S(2)}) collective-permute-start(bf16[272,128]{1,0:T(8,128)(2,1)S(1)} %add_convert_fusion), channel_id=1, source_target_pairs={{0,16},{4,20},{8,24},{12,28},{16,0},{20,4},{24,8},{28,12},{1,17},{... | collective-permute-start | bytes 208904 | tf_op jit(solution)/shard_map/ppermute | solution.py:604
  51.2 4.3 %collective-permute-start.16 = (bf16[272,128]{1,0:T(8,128)(2,1)S(1)}, bf16[272,128]{1,0:T(8,128)(2,1)S(1)}, u32[]{:S(2)}, u32[]{:S(2)}) collective-permute-start(bf16[272,128]{1,0:T(8,128)(2,1)S(1)} %add_convert_fusion), channel_id=1, source_target_pairs={{0,8},{4,12},{8,0},{12,4},{16,24},{20,28},{24,16},{28,20},{1,9},{5... | collective-permute-start | bytes 208904 | tf_op jit(solution)/shard_map/ppermute | solution.py:604
  55.6 1.6 %collective-permute-start.19 = (bf16[4,272,128]{2,1,0:T(8,128)(2,1)S(1)}, bf16[4,272,128]{2,1,0:T(8,128)(2,1)S(1)}, u32[]{:S(2)}, u32[]{:S(2)}) collective-permute-start(bf16[4,272,128]{2,1,0:T(8,128)(2,1)S(1)} %pad_maximum_fusion.keep_ref), channel_id=1, source_target_pairs={{0,4},{4,0},{8,12},{12,8},{16,20},{20,16},{24,28},{28,24},{1,5},{5... | collective-permute-start | bytes 835592 | tf_op jit(solution)/shard_map/ppermute | solution.py:607

commit v6 on v5

--- a/solution.py
+++ b/solution.py
@@ -38,23 +38,31 @@
     return lax.dot_general(left, right, (((1,), (0,)), ((), ())), preferred_element_type=F32)
 
 
-def bring(flag_ref, vol_hbm, cot_hbm, vol_ref, cot_ref, dep_ref, arrived):
+def bring(
+    flag_ref, vol_hbm, cot_hbm, first_hbm, second_hbm, vol_ref, cot_ref, first_ref, second_ref, dep_ref, arrived
+):
     first_plane = flag_ref[0] == 0
-    planes = vol_ref.shape[0]
+    planes, width = vol_ref.shape[0], vol_ref.shape[2]
     inner = pl.ds(4, planes - 8)
     copies = [pltpu.make_async_copy(cot_hbm, cot_ref, arrived.at[0])]
     for n, part in enumerate((pl.ds(0, 4), pl.ds(planes - 4, 4), inner)):
         copies.append(pltpu.make_async_copy(vol_hbm.at[part], vol_ref.at[part], arrived.at[1 + n]))
+    copies.append(pltpu.make_async_copy(first_hbm, first_ref, arrived.at[4]))
+    copies.append(pltpu.make_async_copy(second_hbm, second_ref, arrived.at[5]))
     for copy in copies:
         copy.start()
     for copy in copies[:3]:
         copy.wait()
     dep_ref[16] = cot_ref[0]
     for q in range(4):
-        block = jnp.where(first_plane, vol_ref[planes - 4 + q].astype(F32), vol_ref[q].astype(F32))
-        for g in range(4):
-            dep_ref[4 * q + g] = block[4 * g : 4 * g + 4].astype(BF16)
-    copies[3].wait()
+        for m in range(width // LANES):
+            lanes = slice(m * LANES, (m + 1) * LANES)
+            last, start = vol_ref[planes - 4 + q, :, lanes].astype(F32), vol_ref[q, :, lanes].astype(F32)
+            block = jnp.where(first_plane, last, start)
+            for g in range(4):
+                dep_ref[4 * q + g, :, lanes] = block[4 * g : 4 * g + 4].astype(BF16)
+    for copy in copies[3:]:
+        copy.wait()
 
 
 def pack_rows(flag_ref, vol_ref, cot_ref, row_b_ref, row_a_ref):
@@ -78,18 +86,10 @@
         row_b_ref[planes + g] = jnp.where(row_inner, tops, 0.0).astype(BF16)
 
 
-def pack_sides(
-    flag_ref, vol_ref, cot_ref, first_hbm, second_hbm, col_a_ref, col_b_ref, first_ref, second_ref, arrived
-):
+def pack_sides(flag_ref, vol_ref, cot_ref, col_a_ref, col_b_ref):
     col_even, col_inner = flag_ref[2] == 0, flag_ref[4] != 0
     planes, high, width = vol_ref.shape
     cots = cot_ref.shape[0]
-    copies = [
-        pltpu.make_async_copy(first_hbm, first_ref, arrived.at[0]),
-        pltpu.make_async_copy(second_hbm, second_ref, arrived.at[1]),
-    ]
-    for copy in copies:
-        copy.start()
     for g in range(cots // 4):
         side = jnp.concatenate([cot_ref[4 * g + n, :, :LANES].astype(F32) for n in range(4)], axis=0)
         col_a_ref[planes + g] = side.astype(BF16)
@@ -103,8 +103,6 @@
         return carry
 
     lax.fori_loop(0, planes, plane, 0, unroll=4)
-    for copy in copies:
-        copy.wait()
 
 
 def pack_corners(flag_ref, row_b_ref, row_a_ref, dep_ref, edge_a_ref, edge_b_ref, col_a_ref, col_b_ref):
@@ -531,14 +529,16 @@
     def stay(argument):
         return pltpu.with_memory_space_constraint(argument, pltpu.HBM)
 
-    volume, cotangent, dep = pl.pallas_call(
+    arguments = (volume, cotangent, first_weight, second_weight.T)
+    shapes = [argument.shape for argument in arguments] + [(17, 4, width)]
+    volume, cotangent, first_taps, second_taps, dep = pl.pallas_call(
         bring,
-        out_shape=[jax.ShapeDtypeStruct(shape, BF16) for shape in (volume.shape, cotangent.shape, (17, 4, width))],
-        in_specs=[smem] + [in_hbm] * 2,
-        out_specs=[whole] * 3,
-        scratch_shapes=[pltpu.SemaphoreType.DMA((4,))],
+        out_shape=[jax.ShapeDtypeStruct(shape, BF16) for shape in shapes],
+        in_specs=[smem] + [in_hbm] * 4,
+        out_specs=[whole] * len(shapes),
+        scratch_shapes=[pltpu.SemaphoreType.DMA((6,))],
         compiler_params=small,
-    )(flags, stay(volume), stay(cotangent))
+    )(flags, *[stay(argument) for argument in arguments])
     row_b, row_a = pl.pallas_call(
         pack_rows,
         out_shape=[jax.ShapeDtypeStruct((groups, 4, width), BF16)] * 2,
@@ -557,17 +557,13 @@
     row_b = lax.ppermute(row_b, ("depth", "row", "col"), route)
     row_a = lax.ppermute(row_a, "row", pairs_on_line(rows, 0))
     row_a, volume, cotangent = lax.optimization_barrier((row_a, volume, cotangent))
-    weights = (first_weight, second_weight.T)
-    shapes = [(groups, high, LANES)] * 2 + [weight.shape for weight in weights]
-    side_a, side_b, first_taps, second_taps = pl.pallas_call(
+    side_a, side_b = pl.pallas_call(
         pack_sides,
-        out_shape=[jax.ShapeDtypeStruct(shape, BF16) for shape in shapes],
-        in_specs=[smem] + [whole] * 2 + [in_hbm] * 2,
-        out_specs=[whole] * len(shapes),
-        scratch_shapes=[pltpu.SemaphoreType.DMA((2,))],
+        out_shape=[jax.ShapeDtypeStruct((groups, high, LANES), BF16)] * 2,
+        in_specs=[smem] + [whole] * 2,
+        out_specs=[whole] * 2,
         compiler_params=small,
-    )(flags, volume, cotangent, *[stay(weight) for weight in weights])
-
+    )(flags, volume, cotangent)
     side_a, side_b = to_col(side_a, 0), to_col(side_b, 1)
     low, top = [jnp.concatenate([dep[n : n + 1] for n in (*range(k, 16, 4), 16)], axis=0) for k in (0, 3)]
     even, ends = row % 2 == 0, jnp.logical_or(row == 0, row == rows - 1)

time: 59 us -> 58.7 us (level)
  Pallas kernels: 18.3 us -> 17.5 us
  waiting for transfers between devices: 15.5 us -> 16.1 us
    pallas_call x1, Pallas kernels: 1.64 us -> 0.63 us  [shards(): pl.pallas_call(pack_sides, out_shape=[jax.ShapeDtypeStruct((groups, high,...]
  transfers between devices with their start and end apart: 20 -> 20, of which waited for: 11 -> 10; matrix products, arithmetic and copies ran while one was open for 0% -> 0% of each run, Pallas kernels for 13% -> 11%
where the time goes in v6:
time: 58.7 us; the launch traced here: 58.6 us
  starting transfers between devices  23.7 us (40%)
  Pallas kernels  17.5 us (30%)
  waiting for transfers between devices  16.1 us (27%)
  between operations  0.84 us (1%)
    ppermute x6, waiting for transfers between devices, to_square(): return lax.ppermute(block, ('depth', 'row'), route)  8 us
    ppermute x6, starting transfers between devices, to_square(): return lax.ppermute(block, ('depth', 'row'), route)  7.12 us
    pallas_call x1, Pallas kernels, local_grads(): pl.pallas_call(body, out_shape=[jax.ShapeDtypeStruct((squares, rows // (2...  7.1 us
    ppermute x4, starting transfers between devices, to_col(): return lax.ppermute(block, ('row', 'col'), pairs_of_lines(rows, cols, kind))  4.86 us
    ppermute x3, starting transfers between devices, along_col(): return lax.ppermute(block, 'col', [(i, i ^ n) for i in range(cols)])  4.45 us
    ppermute x3, waiting for transfers between devices, along_col(): return lax.ppermute(block, 'col', [(i, i ^ n) for i in range(cols)])  4.33 us
    pallas_call x1, Pallas kernels, local_grads(): pl.pallas_call(own_blocks, out_shape=[jax.ShapeDtypeStruct((3, planes + 9...  3.75 us
    ppermute x1, starting transfers between devices, shards(): dep = lax.ppermute(dep, 'depth', [(0, 1), (1, 0)])  3.03 us
  transfers between devices with their start and end apart: 20, of which 10 were waited for; matrix products, arithmetic and copies ran while one was open for 0% of the time, Pallas kernels for 11%

profile of v6, /device:TPU:0, one launch (start us, length us, event | category | flops | bytes accessed | tf_op | source)
XLA Modules:
  0.0 58.6 jit_solution(7927650136570478579)
XLA Ops:
  0.7 2.0 %shard_map.59 = (bf16[32,16,1024]{2,1,0:T(8,128)(2,1)S(1)}, bf16[8,4,1024]{2,1,0:T(4,128)(2,1)S(1)}, bf16[64,864]{1,0:T(8,128)(2,1)S(1)}, bf16[1728,128]{1,0:T(8,128)(2,1)S(1)}, bf16[17,4,1024]{2,1,0:T(4,128)(2,1)S(1)}) custom-call(s32[5]{0:T(128)S(1)} %stack.58.flag_ref, bf16[32,16,1024]{2,1,0:T(8,128)(2,1)} %vol_hbm.1, bf16[8,4,1024]{2,1,0:T(4,128)(2,1)} %cot_hbm.1, ...), custom_call_target="tpu_custom_call" | custom-call | tf_op jit(solution)/shard_map/pallas_call | solution.py:534
  2.8 3.0 %collective-permute-start.2 = (bf16[17,4,1024]{2,1,0:T(4,128)(2,1)S(1)}, bf16[17,4,1024]{2,1,0:T(4,128)(2,1)S(1)}, u32[]{:S(2)}, u32[]{:S(2)}) collective-permute-start(bf16[17,4,1024]{2,1,0:T(4,128)(2,1)S(1)} %get-tuple-element.43), channel_id=1, source_target_pairs={{0,16},{16,0},{1,17},{17,1},{2,18},{18,2},{3,19},{19,3},{4,20},{20... | collective-permute-start | bytes 417800 | tf_op jit(solution)/shard_map/ppermute | solution.py:553
  5.8 1.0 %shard_map.60 = (bf16[34,4,1024]{2,1,0:T(4,128)(2,1)S(1)}, bf16[34,4,1024]{2,1,0:T(4,128)(2,1)S(1)}) custom-call(s32[5]{0:T(128)S(1)} %stack.58.flag_ref, bf16[32,16,1024]{2,1,0:T(8,128)(2,1)S(1)} %get-tuple-element.47.vol_ref, bf16[8,4,1024]{2,1,0:T(4,128)(2,1)S(1)} %get-tuple-element.51.cot_ref), custom_call_target="tpu_custom_call" | custom-call | tf_op jit(solution)/shard_map/pallas_call | solution.py:542
  6.8 1.6 %collective-permute-start = (bf16[34,4,1024]{2,1,0:T(4,128)(2,1)S(1)}, bf16[34,4,1024]{2,1,0:T(4,128)(2,1)S(1)}, u32[]{:S(2)}, u32[]{:S(2)}) collective-permute-start(bf16[34,4,1024]{2,1,0:T(4,128)(2,1)S(1)} %get-tuple-element.34), channel_id=1, source_target_pairs={{4,8},{5,9},{6,10},{7,11},{20,24},{21,25},{22,26},{23,27},{8,4},{9... | collective-permute-start | bytes 835592 | tf_op jit(solution)/shard_map/ppermute | solution.py:557
  8.5 1.0 %collective-permute-done.2.dep_ref = bf16[17,4,1024]{2,1,0:T(4,128)(2,1)S(1)} collective-permute-done((bf16[17,4,1024]{2,1,0:T(4,128)(2,1)S(1)}, bf16[17,4,1024]{2,1,0:T(4,128)(2,1)S(1)}, u32[]{:S(2)}, u32[]{:S(2)}) %collective-permute-start.2) | collective-permute-done | bytes 139296 | tf_op jit(solution)/shard_map/ppermute | solution.py:553
  9.7 1.8 %collective-permute-start.4 = (bf16[5,4,1024]{2,1,0:T(4,128)(2,1)S(1)}, bf16[5,4,1024]{2,1,0:T(4,128)(2,1)S(1)}, u32[]{:S(2)}, u32[]{:S(2)}) collective-permute-start(bf16[5,4,1024]{2,1,0:T(4,128)(2,1)S(1)} %get-tuple-element.71), channel_id=1, source_target_pairs={{4,8},{8,4},{0,16},{12,28},{20,24},{24,20},{16,0},{28,12},{5,9},{9... | collective-permute-start | bytes 122888 | tf_op jit(solution)/shard_map/ppermute | solution.py:573
  12.9 1.6 %collective-permute-start.5 = (bf16[34,16,128]{2,1,0:T(8,128)(2,1)S(1)}, bf16[34,16,128]{2,1,0:T(8,128)(2,1)S(1)}, u32[]{:S(2)}, u32[]{:S(2)}) collective-permute-start(bf16[34,16,128]{2,1,0:T(8,128)(2,1)S(1)} %get-tuple-element.52), channel_id=1, source_target_pairs={{0,1},{2,3},{1,0},{3,2},{4,5},{6,7},{5,4},{7,6},{8,9},{10,11},{9,8... | collective-permute-start | bytes 417800 | tf_op jit(solution)/shard_map/ppermute | solution.py:551
  15.5 3.1 %collective-permute-start.7 = (bf16[46,8,128]{2,1,0:T(8,128)(2,1)S(1)}, bf16[46,8,128]{2,1,0:T(8,128)(2,1)S(1)}, u32[]{:S(2)}, u32[]{:S(2)}) collective-permute-start(bf16[46,8,128]{2,1,0:T(8,128)(2,1)S(1)} %get-tuple-element.54), channel_id=1, source_target_pairs={{0,1},{2,3},{1,0},{3,2},{4,5},{6,7},{5,4},{7,6},{8,9},{10,11},{9,8... | collective-permute-start | bytes 282632 | tf_op jit(solution)/shard_map/ppermute | solution.py:551
  18.5 3.8 %shard_map.63 = (bf16[3,41,8,16,128]{4,3,2,1,0:T(8,128)(2,1)S(1)}, f32[20,8,16,256]{3,2,1,0:T(8,128)S(1)}) custom-call(s32[5]{0:T(128)S(1)} %stack.58.flag_ref, bf16[32,16,1024]{2,1,0:T(8,128)(2,1)S(1)} %get-tuple-element.47.vol_ref, bf16[17,4,1024]{2,1,0:T(4,128)(2,1)S(1)} %collective-permute-done.2.dep_ref, ...), custom_call_target="tpu_custom_call" | custom-call | flops 2000000000 | bytes 10000000 | tf_op jit(solution)/shard_map/pallas_call | solution.py:480
  22.3 7.1 %shard_map.65 = (f32[4,272,128]{2,1,0:T(8,128)S(1)}, bf16[4,272,128]{2,1,0:T(8,128)(2,1)S(1)}) custom-call(s32[5]{0:T(128)S(1)} %stack.58.flag_ref, s32[2]{0:T(128)S(1)} %pad_add_fusion.place_ref, bf16[3,41,8,16,128]{4,3,2,1,0:T(8,128)(2,1)S(1)} %get-tuple-element.49.tiles, f32[20,8,16,256]{3,2,1,0:T(8,128)S(1)} %get-tuple-element.50.parts, ...), custom_call_target="tpu_custom_call" | custom-call | flops 4000000000 | bytes 10000000 | tf_op jit(solution)/shard_map/pallas_call | solution.py:505
  30.0 1.2 %collective-permute-done.9 = bf16[4,272,128]{2,1,0:T(8,128)(2,1)S(1)} collective-permute-done((bf16[4,272,128]{2,1,0:T(8,128)(2,1)S(1)}, bf16[4,272,128]{2,1,0:T(8,128)(2,1)S(1)}, u32[]{:S(2)}, u32[]{:S(2)}) %collective-permute-start.9) | collective-permute-done | bytes 278560 | tf_op jit(solution)/shard_map/ppermute | solution.py:603
  31.5 2.9 %collective-permute-start.12 = (bf16[272,128]{1,0:T(8,128)(2,1)S(1)}, bf16[272,128]{1,0:T(8,128)(2,1)S(1)}, u32[]{:S(2)}, u32[]{:S(2)}) collective-permute-start(bf16[272,128]{1,0:T(8,128)(2,1)S(1)} %get-tuple-element.65), channel_id=1, source_target_pairs={{0,24},{4,28},{8,16},{12,20},{16,8},{20,12},{24,0},{28,4},{1,25},{... | collective-permute-start | bytes 208904 | tf_op jit(solution)/shard_map/ppermute | solution.py:600
  34.9 1.4 %collective-permute-done.10 = bf16[272,128]{1,0:T(8,128)(2,1)S(1)} collective-permute-done((bf16[272,128]{1,0:T(8,128)(2,1)S(1)}, bf16[272,128]{1,0:T(8,128)(2,1)S(1)}, u32[]{:S(2)}, u32[]{:S(2)}) %collective-permute-start.10) | collective-permute-done | bytes 69664 | tf_op jit(solution)/shard_map/ppermute | solution.py:600
  36.3 2.1 %collective-permute-done.12 = bf16[272,128]{1,0:T(8,128)(2,1)S(1)} collective-permute-done((bf16[272,128]{1,0:T(8,128)(2,1)S(1)}, bf16[272,128]{1,0:T(8,128)(2,1)S(1)}, u32[]{:S(2)}, u32[]{:S(2)}) %collective-permute-start.12) | collective-permute-done | bytes 69664 | tf_op jit(solution)/shard_map/ppermute | solution.py:600
  38.4 1.1 %collective-permute-done.11 = bf16[272,128]{1,0:T(8,128)(2,1)S(1)} collective-permute-done((bf16[272,128]{1,0:T(8,128)(2,1)S(1)}, bf16[272,128]{1,0:T(8,128)(2,1)S(1)}, u32[]{:S(2)}, u32[]{:S(2)}) %collective-permute-start.11) | collective-permute-done | bytes 69664 | tf_op jit(solution)/shard_map/ppermute | solution.py:600
  39.5 1.5 %collective-permute-start.15 = (bf16[272,128]{1,0:T(8,128)(2,1)S(1)}, bf16[272,128]{1,0:T(8,128)(2,1)S(1)}, u32[]{:S(2)}, u32[]{:S(2)}) collective-permute-start(bf16[272,128]{1,0:T(8,128)(2,1)S(1)} %fusion.2), channel_id=1, source_target_pairs={{0,3},{1,2},{2,1},{3,0},{4,7},{5,6},{6,5},{7,4},{8,11},{9,10},{10,... | collective-permute-start | bytes 208904 | tf_op jit(solution)/shard_map/ppermute | solution.py:606
  41.5 2.4 %collective-permute-start.13 = (bf16[272,128]{1,0:T(8,128)(2,1)S(1)}, bf16[272,128]{1,0:T(8,128)(2,1)S(1)}, u32[]{:S(2)}, u32[]{:S(2)}) collective-permute-start(bf16[272,128]{1,0:T(8,128)(2,1)S(1)} %fusion.2), channel_id=1, source_target_pairs={{0,1},{1,0},{2,3},{3,2},{4,5},{5,4},{6,7},{7,6},{8,9},{9,8},{10,11... | collective-permute-start | bytes 208904 | tf_op jit(solution)/shard_map/ppermute | solution.py:606
  44.0 2.6 %collective-permute-done.15 = bf16[272,128]{1,0:T(8,128)(2,1)S(1)} collective-permute-done((bf16[272,128]{1,0:T(8,128)(2,1)S(1)}, bf16[272,128]{1,0:T(8,128)(2,1)S(1)}, u32[]{:S(2)}, u32[]{:S(2)}) %collective-permute-start.15) | collective-permute-done | bytes 69664 | tf_op jit(solution)/shard_map/ppermute | solution.py:606
  46.5 1.8 %collective-permute-done.14 = bf16[272,128]{1,0:T(8,128)(2,1)S(1)} collective-permute-done((bf16[272,128]{1,0:T(8,128)(2,1)S(1)}, bf16[272,128]{1,0:T(8,128)(2,1)S(1)}, u32[]{:S(2)}, u32[]{:S(2)}) %collective-permute-start.14) | collective-permute-done | bytes 69664 | tf_op jit(solution)/shard_map/ppermute | solution.py:606
  48.9 2.1 %collective-permute-start.17 = (bf16[272,128]{1,0:T(8,128)(2,1)S(1)}, bf16[272,128]{1,0:T(8,128)(2,1)S(1)}, u32[]{:S(2)}, u32[]{:S(2)}) collective-permute-start(bf16[272,128]{1,0:T(8,128)(2,1)S(1)} %add_convert_fusion), channel_id=1, source_target_pairs={{0,16},{4,20},{8,24},{12,28},{16,0},{20,4},{24,8},{28,12},{1,17},{... | collective-permute-start | bytes 208904 | tf_op jit(solution)/shard_map/ppermute | solution.py:600
  51.9 2.2 %collective-permute-done.18 = bf16[272,128]{1,0:T(8,128)(2,1)S(1)} collective-permute-done((bf16[272,128]{1,0:T(8,128)(2,1)S(1)}, bf16[272,128]{1,0:T(8,128)(2,1)S(1)}, u32[]{:S(2)}, u32[]{:S(2)}) %collective-permute-start.18) | collective-permute-done | bytes 69664 | tf_op jit(solution)/shard_map/ppermute | solution.py:600
  54.2 1.1 %collective-permute-done.16 = bf16[272,128]{1,0:T(8,128)(2,1)S(1)} collective-permute-done((bf16[272,128]{1,0:T(8,128)(2,1)S(1)}, bf16[272,128]{1,0:T(8,128)(2,1)S(1)}, u32[]{:S(2)}, u32[]{:S(2)}) %collective-permute-start.16) | collective-permute-done | bytes 69664 | tf_op jit(solution)/shard_map/ppermute | solution.py:600
  55.4 1.5 %collective-permute-done.19.got_ref = bf16[4,272,128]{2,1,0:T(8,128)(2,1)S(1)} collective-permute-done((bf16[4,272,128]{2,1,0:T(8,128)(2,1)S(1)}, bf16[4,272,128]{2,1,0:T(8,128)(2,1)S(1)}, u32[]{:S(2)}, u32[]{:S(2)}) %collective-permute-start.19) | collective-permute-done | bytes 278560 | tf_op jit(solution)/shard_map/ppermute | solution.py:603
  57.0 1.6 %shard_map.66 = (f32[64,864]{1,0:T(8,128)}, f32[1728,128]{1,0:T(8,128)}) custom-call(s32[2]{0:T(128)S(1)} %pad_add_fusion.place_ref, bf16[4,272,128]{2,1,0:T(8,128)(2,1)S(1)} %pad_maximum_fusion.keep_ref, bf16[4,272,128]{2,1,0:T(8,128)(2,1)S(1)} %collective-permute-done.19.got_ref), custom_call_target="tpu_custom_call" | custom-call | tf_op jit(solution)/shard_map/pallas_call | solution.py:615
  (38 shorter events, 6.2 us)
Async XLA Ops:
  2.8 6.7 %collective-permute-start.2 = (bf16[17,4,1024]{2,1,0:T(4,128)(2,1)S(1)}, bf16[17,4,1024]{2,1,0:T(4,128)(2,1)S(1)}, u32[]{:S(2)}, u32[]{:S(2)}) collective-permute-start(bf16[17,4,1024]{2,1,0:T(4,128)(2,1)S(1)} %get-tuple-element.43), channel_id=1, source_target_pairs={{0,16},{16,0},{1,17},{17,1},{2,18},{18,2},{3,19},{19,3},{4,20},{20... | collective-permute-start | bytes 417800 | tf_op jit(solution)/shard_map/ppermute | solution.py:553
  6.8 7.9 %collective-permute-start = (bf16[34,4,1024]{2,1,0:T(4,128)(2,1)S(1)}, bf16[34,4,1024]{2,1,0:T(4,128)(2,1)S(1)}, u32[]{:S(2)}, u32[]{:S(2)}) collective-permute-start(bf16[34,4,1024]{2,1,0:T(4,128)(2,1)S(1)} %get-tuple-element.34), channel_id=1, source_target_pairs={{4,8},{5,9},{6,10},{7,11},{20,24},{21,25},{22,26},{23,27},{8,4},{9... | collective-permute-start | bytes 835592 | tf_op jit(solution)/shard_map/ppermute | solution.py:557
  8.5 3.8 %collective-permute-start.1 = (bf16[34,4,1024]{2,1,0:T(4,128)(2,1)S(1)}, bf16[34,4,1024]{2,1,0:T(4,128)(2,1)S(1)}, u32[]{:S(2)}, u32[]{:S(2)}) collective-permute-start(bf16[34,4,1024]{2,1,0:T(4,128)(2,1)S(1)} %get-tuple-element.41), channel_id=1, source_target_pairs={{0,4},{8,12},{4,0},{12,8},{1,5},{9,13},{5,1},{13,9},{2,6},{10,14},... | collective-permute-start | bytes 835592 | tf_op jit(solution)/shard_map/ppermute | solution.py:558
  9.7 5.1 %collective-permute-start.4 = (bf16[5,4,1024]{2,1,0:T(4,128)(2,1)S(1)}, bf16[5,4,1024]{2,1,0:T(4,128)(2,1)S(1)}, u32[]{:S(2)}, u32[]{:S(2)}) collective-permute-start(bf16[5,4,1024]{2,1,0:T(4,128)(2,1)S(1)} %get-tuple-element.71), channel_id=1, source_target_pairs={{4,8},{8,4},{0,16},{12,28},{20,24},{24,20},{16,0},{28,12},{5,9},{9... | collective-permute-start | bytes 122888 | tf_op jit(solution)/shard_map/ppermute | solution.py:573
  11.5 3.3 %collective-permute-start.3 = (bf16[5,4,1024]{2,1,0:T(4,128)(2,1)S(1)}, bf16[5,4,1024]{2,1,0:T(4,128)(2,1)S(1)}, u32[]{:S(2)}, u32[]{:S(2)}) collective-permute-start(bf16[5,4,1024]{2,1,0:T(4,128)(2,1)S(1)} %get-tuple-element.72), channel_id=1, source_target_pairs={{0,4},{8,12},{4,0},{12,8},{1,5},{9,13},{5,1},{13,9},{2,6},{10,14},... | collective-permute-start | bytes 122888 | tf_op jit(solution)/shard_map/ppermute | solution.py:572
  12.9 9.4 %collective-permute-start.5 = (bf16[34,16,128]{2,1,0:T(8,128)(2,1)S(1)}, bf16[34,16,128]{2,1,0:T(8,128)(2,1)S(1)}, u32[]{:S(2)}, u32[]{:S(2)}) collective-permute-start(bf16[34,16,128]{2,1,0:T(8,128)(2,1)S(1)} %get-tuple-element.52), channel_id=1, source_target_pairs={{0,1},{2,3},{1,0},{3,2},{4,5},{6,7},{5,4},{7,6},{8,9},{10,11},{9,8... | collective-permute-start | bytes 417800 | tf_op jit(solution)/shard_map/ppermute | solution.py:551
  14.6 7.7 %collective-permute-start.6 = (bf16[34,16,128]{2,1,0:T(8,128)(2,1)S(1)}, bf16[34,16,128]{2,1,0:T(8,128)(2,1)S(1)}, u32[]{:S(2)}, u32[]{:S(2)}) collective-permute-start(bf16[34,16,128]{2,1,0:T(8,128)(2,1)S(1)} %get-tuple-element.53), channel_id=1, source_target_pairs={{1,2},{2,1},{0,4},{3,7},{5,6},{6,5},{4,0},{7,3},{9,10},{10,9},{8,1... | collective-permute-start | bytes 417800 | tf_op jit(solution)/shard_map/ppermute | solution.py:551
  15.5 6.8 %collective-permute-start.7 = (bf16[46,8,128]{2,1,0:T(8,128)(2,1)S(1)}, bf16[46,8,128]{2,1,0:T(8,128)(2,1)S(1)}, u32[]{:S(2)}, u32[]{:S(2)}) collective-permute-start(bf16[46,8,128]{2,1,0:T(8,128)(2,1)S(1)} %get-tuple-element.54), channel_id=1, source_target_pairs={{0,1},{2,3},{1,0},{3,2},{4,5},{6,7},{5,4},{7,6},{8,9},{10,11},{9,8... | collective-permute-start | bytes 282632 | tf_op jit(solution)/shard_map/ppermute | solution.py:551
  18.5 3.8 %collective-permute-start.8 = (bf16[46,8,128]{2,1,0:T(8,128)(2,1)S(1)}, bf16[46,8,128]{2,1,0:T(8,128)(2,1)S(1)}, u32[]{:S(2)}, u32[]{:S(2)}) collective-permute-start(bf16[46,8,128]{2,1,0:T(8,128)(2,1)S(1)} %get-tuple-element.55), channel_id=1, source_target_pairs={{1,2},{2,1},{0,4},{3,7},{5,6},{6,5},{4,0},{7,3},{9,10},{10,9},{8,1... | collective-permute-start | bytes 282632 | tf_op jit(solution)/shard_map/ppermute | solution.py:551
  29.4 1.8 %collective-permute-start.9 = (bf16[4,272,128]{2,1,0:T(8,128)(2,1)S(1)}, bf16[4,272,128]{2,1,0:T(8,128)(2,1)S(1)}, u32[]{:S(2)}, u32[]{:S(2)}) collective-permute-start(bf16[4,272,128]{2,1,0:T(8,128)(2,1)S(1)} %get-tuple-element.59), channel_id=1, source_target_pairs={{0,4},{4,0},{8,12},{12,8},{16,20},{20,16},{24,28},{28,24},{1,5},{5... | collective-permute-start | bytes 835592 | tf_op jit(solution)/shard_map/ppermute | solution.py:603
  31.3 5.0 %collective-permute-start.10 = (bf16[272,128]{1,0:T(8,128)(2,1)S(1)}, bf16[272,128]{1,0:T(8,128)(2,1)S(1)}, u32[]{:S(2)}, u32[]{:S(2)}) collective-permute-start(bf16[272,128]{1,0:T(8,128)(2,1)S(1)} %get-tuple-element.64), channel_id=1, source_target_pairs={{0,8},{4,12},{8,0},{12,4},{16,24},{20,28},{24,16},{28,20},{1,9},{5... | collective-permute-start | bytes 208904 | tf_op jit(solution)/shard_map/ppermute | solution.py:600
  31.5 6.9 %collective-permute-start.12 = (bf16[272,128]{1,0:T(8,128)(2,1)S(1)}, bf16[272,128]{1,0:T(8,128)(2,1)S(1)}, u32[]{:S(2)}, u32[]{:S(2)}) collective-permute-start(bf16[272,128]{1,0:T(8,128)(2,1)S(1)} %get-tuple-element.65), channel_id=1, source_target_pairs={{0,24},{4,28},{8,16},{12,20},{16,8},{20,12},{24,0},{28,4},{1,25},{... | collective-permute-start | bytes 208904 | tf_op jit(solution)/shard_map/ppermute | solution.py:600
  34.4 5.1 %collective-permute-start.11 = (bf16[272,128]{1,0:T(8,128)(2,1)S(1)}, bf16[272,128]{1,0:T(8,128)(2,1)S(1)}, u32[]{:S(2)}, u32[]{:S(2)}) collective-permute-start(bf16[272,128]{1,0:T(8,128)(2,1)S(1)} %get-tuple-element.66), channel_id=1, source_target_pairs={{0,16},{4,20},{8,24},{12,28},{16,0},{20,4},{24,8},{28,12},{1,17},{... | collective-permute-start | bytes 208904 | tf_op jit(solution)/shard_map/ppermute | solution.py:600
  39.5 7.0 %collective-permute-start.15 = (bf16[272,128]{1,0:T(8,128)(2,1)S(1)}, bf16[272,128]{1,0:T(8,128)(2,1)S(1)}, u32[]{:S(2)}, u32[]{:S(2)}) collective-permute-start(bf16[272,128]{1,0:T(8,128)(2,1)S(1)} %fusion.2), channel_id=1, source_target_pairs={{0,3},{1,2},{2,1},{3,0},{4,7},{5,6},{6,5},{7,4},{8,11},{9,10},{10,... | collective-permute-start | bytes 208904 | tf_op jit(solution)/shard_map/ppermute | solution.py:606
  41.0 7.3 %collective-permute-start.14 = (bf16[272,128]{1,0:T(8,128)(2,1)S(1)}, bf16[272,128]{1,0:T(8,128)(2,1)S(1)}, u32[]{:S(2)}, u32[]{:S(2)}) collective-permute-start(bf16[272,128]{1,0:T(8,128)(2,1)S(1)} %fusion.2), channel_id=1, source_target_pairs={{0,2},{1,3},{2,0},{3,1},{4,6},{5,7},{6,4},{7,5},{8,10},{9,11},{10,... | collective-permute-start | bytes 208904 | tf_op jit(solution)/shard_map/ppermute | solution.py:606
  41.5 6.8 %collective-permute-start.13 = (bf16[272,128]{1,0:T(8,128)(2,1)S(1)}, bf16[272,128]{1,0:T(8,128)(2,1)S(1)}, u32[]{:S(2)}, u32[]{:S(2)}) collective-permute-start(bf16[272,128]{1,0:T(8,128)(2,1)S(1)} %fusion.2), channel_id=1, source_target_pairs={{0,1},{1,0},{2,3},{3,2},{4,5},{5,4},{6,7},{7,6},{8,9},{9,8},{10,11... | collective-permute-start | bytes 208904 | tf_op jit(solution)/shard_map/ppermute | solution.py:606
  48.4 5.8 %collective-permute-start.18 = (bf16[272,128]{1,0:T(8,128)(2,1)S(1)}, bf16[272,128]{1,0:T(8,128)(2,1)S(1)}, u32[]{:S(2)}, u32[]{:S(2)}) collective-permute-start(bf16[272,128]{1,0:T(8,128)(2,1)S(1)} %add_convert_fusion), channel_id=1, source_target_pairs={{0,24},{4,28},{8,16},{12,20},{16,8},{20,12},{24,0},{28,4},{1,25},{... | collective-permute-start | bytes 208904 | tf_op jit(solution)/shard_map/ppermute | solution.py:600
  48.9 5.3 %collective-permute-start.17 = (bf16[272,128]{1,0:T(8,128)(2,1)S(1)}, bf16[272,128]{1,0:T(8,128)(2,1)S(1)}, u32[]{:S(2)}, u32[]{:S(2)}) collective-permute-start(bf16[272,128]{1,0:T(8,128)(2,1)S(1)} %add_convert_fusion), channel_id=1, source_target_pairs={{0,16},{4,20},{8,24},{12,28},{16,0},{20,4},{24,8},{28,12},{1,17},{... | collective-permute-start | bytes 208904 | tf_op jit(solution)/shard_map/ppermute | solution.py:600
  51.0 4.3 %collective-permute-start.16 = (bf16[272,128]{1,0:T(8,128)(2,1)S(1)}, bf16[272,128]{1,0:T(8,128)(2,1)S(1)}, u32[]{:S(2)}, u32[]{:S(2)}) collective-permute-start(bf16[272,128]{1,0:T(8,128)(2,1)S(1)} %add_convert_fusion), channel_id=1, source_target_pairs={{0,8},{4,12},{8,0},{12,4},{16,24},{20,28},{24,16},{28,20},{1,9},{5... | collective-permute-start | bytes 208904 | tf_op jit(solution)/shard_map/ppermute | solution.py:600
  55.3 1.6 %collective-permute-start.19 = (bf16[4,272,128]{2,1,0:T(8,128)(2,1)S(1)}, bf16[4,272,128]{2,1,0:T(8,128)(2,1)S(1)}, u32[]{:S(2)}, u32[]{:S(2)}) collective-permute-start(bf16[4,272,128]{2,1,0:T(8,128)(2,1)S(1)} %pad_maximum_fusion.keep_ref), channel_id=1, source_target_pairs={{0,4},{4,0},{8,12},{12,8},{16,20},{20,16},{24,28},{28,24},{1,5},{5... | collective-permute-start | bytes 835592 | tf_op jit(solution)/shard_map/ppermute | solution.py:603

commit v7 on v6

--- a/solution.py
+++ b/solution.py
@@ -205,9 +205,9 @@
             stage[n, m, 24:28, :] = kept(ahead(row_even, a(lanes), b(lanes)))
         split_rows(stage.at[n], tiles, target, range(blocks))
 
-    def place_own(pair, carry):
-        for n in range(2):
-            d = 2 * pair + n
+    def place_own(group, carry):
+        for n in range(4):
+            d = 4 * group + n
             place(
                 n, d + 3, lambda lanes: vol_ref[d, :, lanes],
                 lambda lanes: row_a_ref[d, :, lanes], lambda lanes: row_b_ref[d, :, lanes], None,
@@ -216,12 +216,12 @@
 
     def place_halo(target, q, keep):
         place(
-            target % 2, target,
+            target % 4, target,
             lambda lanes: jnp.concatenate([dep_ref[4 * q + g, :, lanes].astype(F32) for g in range(4)], axis=0),
             lambda lanes: edge_a_ref[q, :, lanes], lambda lanes: edge_b_ref[q, :, lanes], keep,
         )
 
-    lax.fori_loop(0, planes // 2, place_own, 0)
+    lax.fori_loop(0, planes // 4, place_own, 0)
     for q in range(3):
         place_halo(q, q + 1, jnp.logical_not(first_plane))
     for q in range(4):
@@ -280,7 +280,7 @@
         side_b = jnp.concatenate([col_b_ref[start].astype(F32), col_b_ref[start + 1].astype(F32)], axis=0)
         place(target % 4, target, planes + q, side_a, side_b, keep)
 
-    lax.fori_loop(0, planes // 4, place_own, 0)
+    lax.fori_loop(0, planes // 4, place_own, 0, unroll=2)
     for q in range(3):
         place_halo(q, q + 1, jnp.logical_not(first_plane))
     for q in range(4):
@@ -309,7 +309,7 @@
         hid[2, i] = odd
         return carry
 
-    lax.fori_loop(0, hidden_planes, conv_one, 0)
+    lax.fori_loop(0, hidden_planes, conv_one, 0, unroll=True)
 
     wide = (blocks + 2) * 16
 
@@ -318,7 +318,7 @@
             pairs[b, i] = jnp.concatenate([hid[b, i], hid[b, i + half_planes]], axis=1).astype(BF16)
         return carry
 
-    lax.fori_loop(0, half_planes + 3, pair, 0)
+    lax.fori_loop(0, half_planes + 3, pair, 0, unroll=True)
 
     ups[...] = jnp.zeros_like(ups)
     for k in range(blocks):
@@ -485,7 +485,7 @@
         ],
         in_specs=[smem] + [whole] * 7,
         out_specs=[whole] * 2,
-        scratch_shapes=[pltpu.VMEM((2, blocks, 40, LANES), F32)],
+        scratch_shapes=[pltpu.VMEM((4, blocks, 40, LANES), F32)],
         compiler_params=pltpu.CompilerParams(vmem_limit_bytes=16 * 1024 * 1024),
         cost_estimate=pl.CostEstimate(flops=2 * 10**9, bytes_accessed=10**7, transcendentals=0),
     )(flags, volume, *faces, weights[0])

time: 58.7 us -> 57.8 us (0.985)
  Pallas kernels: 17.5 us -> 16.5 us
    pallas_call x1, Pallas kernels: 7.1 us -> 6.11 us  [local_grads(): pl.pallas_call(body, out_shape=[jax.ShapeDtypeStruct((squares, rows // (2...]
  transfers between devices with their start and end apart: 20 -> 20, of which waited for: 10 -> 11; matrix products, arithmetic and copies ran while one was open for 0% -> 0% of each run, Pallas kernels for 11% -> 12%
where the time goes in v7:
time: 57.8 us; the launch traced here: 57.6 us
  starting transfers between devices  23.7 us (41%)
  Pallas kernels  16.5 us (29%)
  waiting for transfers between devices  16.1 us (28%)
  between operations  0.84 us (1%)
    ppermute x6, waiting for transfers between devices, to_square(): return lax.ppermute(block, ('depth', 'row'), route)  8 us
    ppermute x6, starting transfers between devices, to_square(): return lax.ppermute(block, ('depth', 'row'), route)  7.12 us
    pallas_call x1, Pallas kernels, local_grads(): pl.pallas_call(body, out_shape=[jax.ShapeDtypeStruct((squares, rows // (2...  6.11 us
    ppermute x4, starting transfers between devices, to_col(): return lax.ppermute(block, ('row', 'col'), pairs_of_lines(rows, cols, kind))  4.86 us
    ppermute x3, starting transfers between devices, along_col(): return lax.ppermute(block, 'col', [(i, i ^ n) for i in range(cols)])  4.45 us
    ppermute x3, waiting for transfers between devices, along_col(): return lax.ppermute(block, 'col', [(i, i ^ n) for i in range(cols)])  4.33 us
    pallas_call x1, Pallas kernels, local_grads(): pl.pallas_call(own_blocks, out_shape=[jax.ShapeDtypeStruct((3, planes + 9...  3.77 us
    ppermute x1, starting transfers between devices, shards(): dep = lax.ppermute(dep, 'depth', [(0, 1), (1, 0)])  3.03 us
  transfers between devices with their start and end apart: 20, of which 11 were waited for; matrix products, arithmetic and copies ran while one was open for 0% of the time, Pallas kernels for 12%

profile of v7, /device:TPU:0, one launch (start us, length us, event | category | flops | bytes accessed | tf_op | source)
XLA Modules:
  0.0 57.6 jit_solution(14654848809789331926)
XLA Ops:
  0.7 2.0 %shard_map.59 = (bf16[32,16,1024]{2,1,0:T(8,128)(2,1)S(1)}, bf16[8,4,1024]{2,1,0:T(4,128)(2,1)S(1)}, bf16[64,864]{1,0:T(8,128)(2,1)S(1)}, bf16[1728,128]{1,0:T(8,128)(2,1)S(1)}, bf16[17,4,1024]{2,1,0:T(4,128)(2,1)S(1)}) custom-call(s32[5]{0:T(128)S(1)} %stack.58.flag_ref, bf16[32,16,1024]{2,1,0:T(8,128)(2,1)} %vol_hbm.1, bf16[8,4,1024]{2,1,0:T(4,128)(2,1)} %cot_hbm.1, ...), custom_call_target="tpu_custom_call" | custom-call | tf_op jit(solution)/shard_map/pallas_call | solution.py:534
  2.8 3.0 %collective-permute-start.2 = (bf16[17,4,1024]{2,1,0:T(4,128)(2,1)S(1)}, bf16[17,4,1024]{2,1,0:T(4,128)(2,1)S(1)}, u32[]{:S(2)}, u32[]{:S(2)}) collective-permute-start(bf16[17,4,1024]{2,1,0:T(4,128)(2,1)S(1)} %get-tuple-element.43), channel_id=1, source_target_pairs={{0,16},{16,0},{1,17},{17,1},{2,18},{18,2},{3,19},{19,3},{4,20},{20... | collective-permute-start | bytes 417800 | tf_op jit(solution)/shard_map/ppermute | solution.py:553
  5.8 1.0 %shard_map.60 = (bf16[34,4,1024]{2,1,0:T(4,128)(2,1)S(1)}, bf16[34,4,1024]{2,1,0:T(4,128)(2,1)S(1)}) custom-call(s32[5]{0:T(128)S(1)} %stack.58.flag_ref, bf16[32,16,1024]{2,1,0:T(8,128)(2,1)S(1)} %get-tuple-element.47.vol_ref, bf16[8,4,1024]{2,1,0:T(4,128)(2,1)S(1)} %get-tuple-element.51.cot_ref), custom_call_target="tpu_custom_call" | custom-call | tf_op jit(solution)/shard_map/pallas_call | solution.py:542
  6.8 1.6 %collective-permute-start = (bf16[34,4,1024]{2,1,0:T(4,128)(2,1)S(1)}, bf16[34,4,1024]{2,1,0:T(4,128)(2,1)S(1)}, u32[]{:S(2)}, u32[]{:S(2)}) collective-permute-start(bf16[34,4,1024]{2,1,0:T(4,128)(2,1)S(1)} %get-tuple-element.34), channel_id=1, source_target_pairs={{4,8},{5,9},{6,10},{7,11},{20,24},{21,25},{22,26},{23,27},{8,4},{9... | collective-permute-start | bytes 835592 | tf_op jit(solution)/shard_map/ppermute | solution.py:557
  8.5 1.0 %collective-permute-done.2.dep_ref = bf16[17,4,1024]{2,1,0:T(4,128)(2,1)S(1)} collective-permute-done((bf16[17,4,1024]{2,1,0:T(4,128)(2,1)S(1)}, bf16[17,4,1024]{2,1,0:T(4,128)(2,1)S(1)}, u32[]{:S(2)}, u32[]{:S(2)}) %collective-permute-start.2) | collective-permute-done | bytes 139296 | tf_op jit(solution)/shard_map/ppermute | solution.py:553
  9.7 1.8 %collective-permute-start.4 = (bf16[5,4,1024]{2,1,0:T(4,128)(2,1)S(1)}, bf16[5,4,1024]{2,1,0:T(4,128)(2,1)S(1)}, u32[]{:S(2)}, u32[]{:S(2)}) collective-permute-start(bf16[5,4,1024]{2,1,0:T(4,128)(2,1)S(1)} %get-tuple-element.71), channel_id=1, source_target_pairs={{4,8},{8,4},{0,16},{12,28},{20,24},{24,20},{16,0},{28,12},{5,9},{9... | collective-permute-start | bytes 122888 | tf_op jit(solution)/shard_map/ppermute | solution.py:573
  12.9 1.6 %collective-permute-start.5 = (bf16[34,16,128]{2,1,0:T(8,128)(2,1)S(1)}, bf16[34,16,128]{2,1,0:T(8,128)(2,1)S(1)}, u32[]{:S(2)}, u32[]{:S(2)}) collective-permute-start(bf16[34,16,128]{2,1,0:T(8,128)(2,1)S(1)} %get-tuple-element.52), channel_id=1, source_target_pairs={{0,1},{2,3},{1,0},{3,2},{4,5},{6,7},{5,4},{7,6},{8,9},{10,11},{9,8... | collective-permute-start | bytes 417800 | tf_op jit(solution)/shard_map/ppermute | solution.py:551
  15.5 3.1 %collective-permute-start.7 = (bf16[46,8,128]{2,1,0:T(8,128)(2,1)S(1)}, bf16[46,8,128]{2,1,0:T(8,128)(2,1)S(1)}, u32[]{:S(2)}, u32[]{:S(2)}) collective-permute-start(bf16[46,8,128]{2,1,0:T(8,128)(2,1)S(1)} %get-tuple-element.54), channel_id=1, source_target_pairs={{0,1},{2,3},{1,0},{3,2},{4,5},{6,7},{5,4},{7,6},{8,9},{10,11},{9,8... | collective-permute-start | bytes 282632 | tf_op jit(solution)/shard_map/ppermute | solution.py:551
  18.5 3.8 %shard_map.63 = (bf16[3,41,8,16,128]{4,3,2,1,0:T(8,128)(2,1)S(1)}, f32[20,8,16,256]{3,2,1,0:T(8,128)S(1)}) custom-call(s32[5]{0:T(128)S(1)} %stack.58.flag_ref, bf16[32,16,1024]{2,1,0:T(8,128)(2,1)S(1)} %get-tuple-element.47.vol_ref, bf16[17,4,1024]{2,1,0:T(4,128)(2,1)S(1)} %collective-permute-done.2.dep_ref, ...), custom_call_target="tpu_custom_call" | custom-call | flops 2000000000 | bytes 10000000 | tf_op jit(solution)/shard_map/pallas_call | solution.py:480
  22.3 6.1 %shard_map.65 = (f32[4,272,128]{2,1,0:T(8,128)S(1)}, bf16[4,272,128]{2,1,0:T(8,128)(2,1)S(1)}) custom-call(s32[5]{0:T(128)S(1)} %stack.58.flag_ref, s32[2]{0:T(128)S(1)} %pad_add_fusion.place_ref, bf16[3,41,8,16,128]{4,3,2,1,0:T(8,128)(2,1)S(1)} %get-tuple-element.49.tiles, f32[20,8,16,256]{3,2,1,0:T(8,128)S(1)} %get-tuple-element.50.parts, ...), custom_call_target="tpu_custom_call" | custom-call | flops 4000000000 | bytes 10000000 | tf_op jit(solution)/shard_map/pallas_call | solution.py:505
  29.0 1.2 %collective-permute-done.9 = bf16[4,272,128]{2,1,0:T(8,128)(2,1)S(1)} collective-permute-done((bf16[4,272,128]{2,1,0:T(8,128)(2,1)S(1)}, bf16[4,272,128]{2,1,0:T(8,128)(2,1)S(1)}, u32[]{:S(2)}, u32[]{:S(2)}) %collective-permute-start.9) | collective-permute-done | bytes 278560 | tf_op jit(solution)/shard_map/ppermute | solution.py:603
  30.5 2.9 %collective-permute-start.12 = (bf16[272,128]{1,0:T(8,128)(2,1)S(1)}, bf16[272,128]{1,0:T(8,128)(2,1)S(1)}, u32[]{:S(2)}, u32[]{:S(2)}) collective-permute-start(bf16[272,128]{1,0:T(8,128)(2,1)S(1)} %get-tuple-element.65), channel_id=1, source_target_pairs={{0,24},{4,28},{8,16},{12,20},{16,8},{20,12},{24,0},{28,4},{1,25},{... | collective-permute-start | bytes 208904 | tf_op jit(solution)/shard_map/ppermute | solution.py:600
  33.9 1.4 %collective-permute-done.10 = bf16[272,128]{1,0:T(8,128)(2,1)S(1)} collective-permute-done((bf16[272,128]{1,0:T(8,128)(2,1)S(1)}, bf16[272,128]{1,0:T(8,128)(2,1)S(1)}, u32[]{:S(2)}, u32[]{:S(2)}) %collective-permute-start.10) | collective-permute-done | bytes 69664 | tf_op jit(solution)/shard_map/ppermute | solution.py:600
  35.3 2.1 %collective-permute-done.12 = bf16[272,128]{1,0:T(8,128)(2,1)S(1)} collective-permute-done((bf16[272,128]{1,0:T(8,128)(2,1)S(1)}, bf16[272,128]{1,0:T(8,128)(2,1)S(1)}, u32[]{:S(2)}, u32[]{:S(2)}) %collective-permute-start.12) | collective-permute-done | bytes 69664 | tf_op jit(solution)/shard_map/ppermute | solution.py:600
  37.4 1.1 %collective-permute-done.11 = bf16[272,128]{1,0:T(8,128)(2,1)S(1)} collective-permute-done((bf16[272,128]{1,0:T(8,128)(2,1)S(1)}, bf16[272,128]{1,0:T(8,128)(2,1)S(1)}, u32[]{:S(2)}, u32[]{:S(2)}) %collective-permute-start.11) | collective-permute-done | bytes 69664 | tf_op jit(solution)/shard_map/ppermute | solution.py:600
  38.5 1.5 %collective-permute-start.15 = (bf16[272,128]{1,0:T(8,128)(2,1)S(1)}, bf16[272,128]{1,0:T(8,128)(2,1)S(1)}, u32[]{:S(2)}, u32[]{:S(2)}) collective-permute-start(bf16[272,128]{1,0:T(8,128)(2,1)S(1)} %fusion.2), channel_id=1, source_target_pairs={{0,3},{1,2},{2,1},{3,0},{4,7},{5,6},{6,5},{7,4},{8,11},{9,10},{10,... | collective-permute-start | bytes 208904 | tf_op jit(solution)/shard_map/ppermute | solution.py:606
  40.6 2.4 %collective-permute-start.13 = (bf16[272,128]{1,0:T(8,128)(2,1)S(1)}, bf16[272,128]{1,0:T(8,128)(2,1)S(1)}, u32[]{:S(2)}, u32[]{:S(2)}) collective-permute-start(bf16[272,128]{1,0:T(8,128)(2,1)S(1)} %fusion.2), channel_id=1, source_target_pairs={{0,1},{1,0},{2,3},{3,2},{4,5},{5,4},{6,7},{7,6},{8,9},{9,8},{10,11... | collective-permute-start | bytes 208904 | tf_op jit(solution)/shard_map/ppermute | solution.py:606
  43.0 2.5 %collective-permute-done.15 = bf16[272,128]{1,0:T(8,128)(2,1)S(1)} collective-permute-done((bf16[272,128]{1,0:T(8,128)(2,1)S(1)}, bf16[272,128]{1,0:T(8,128)(2,1)S(1)}, u32[]{:S(2)}, u32[]{:S(2)}) %collective-permute-start.15) | collective-permute-done | bytes 69664 | tf_op jit(solution)/shard_map/ppermute | solution.py:606
  45.5 1.8 %collective-permute-done.14 = bf16[272,128]{1,0:T(8,128)(2,1)S(1)} collective-permute-done((bf16[272,128]{1,0:T(8,128)(2,1)S(1)}, bf16[272,128]{1,0:T(8,128)(2,1)S(1)}, u32[]{:S(2)}, u32[]{:S(2)}) %collective-permute-start.14) | collective-permute-done | bytes 69664 | tf_op jit(solution)/shard_map/ppermute | solution.py:606
  47.9 2.1 %collective-permute-start.17 = (bf16[272,128]{1,0:T(8,128)(2,1)S(1)}, bf16[272,128]{1,0:T(8,128)(2,1)S(1)}, u32[]{:S(2)}, u32[]{:S(2)}) collective-permute-start(bf16[272,128]{1,0:T(8,128)(2,1)S(1)} %add_convert_fusion), channel_id=1, source_target_pairs={{0,16},{4,20},{8,24},{12,28},{16,0},{20,4},{24,8},{28,12},{1,17},{... | collective-permute-start | bytes 208904 | tf_op jit(solution)/shard_map/ppermute | solution.py:600
  50.9 2.2 %collective-permute-done.18 = bf16[272,128]{1,0:T(8,128)(2,1)S(1)} collective-permute-done((bf16[272,128]{1,0:T(8,128)(2,1)S(1)}, bf16[272,128]{1,0:T(8,128)(2,1)S(1)}, u32[]{:S(2)}, u32[]{:S(2)}) %collective-permute-start.18) | collective-permute-done | bytes 69664 | tf_op jit(solution)/shard_map/ppermute | solution.py:600
  53.3 1.1 %collective-permute-done.16 = bf16[272,128]{1,0:T(8,128)(2,1)S(1)} collective-permute-done((bf16[272,128]{1,0:T(8,128)(2,1)S(1)}, bf16[272,128]{1,0:T(8,128)(2,1)S(1)}, u32[]{:S(2)}, u32[]{:S(2)}) %collective-permute-start.16) | collective-permute-done | bytes 69664 | tf_op jit(solution)/shard_map/ppermute | solution.py:600
  54.4 1.5 %collective-permute-done.19.got_ref = bf16[4,272,128]{2,1,0:T(8,128)(2,1)S(1)} collective-permute-done((bf16[4,272,128]{2,1,0:T(8,128)(2,1)S(1)}, bf16[4,272,128]{2,1,0:T(8,128)(2,1)S(1)}, u32[]{:S(2)}, u32[]{:S(2)}) %collective-permute-start.19) | collective-permute-done | bytes 278560 | tf_op jit(solution)/shard_map/ppermute | solution.py:603
  56.0 1.6 %shard_map.66 = (f32[64,864]{1,0:T(8,128)}, f32[1728,128]{1,0:T(8,128)}) custom-call(s32[2]{0:T(128)S(1)} %pad_add_fusion.place_ref, bf16[4,272,128]{2,1,0:T(8,128)(2,1)S(1)} %pad_maximum_fusion.keep_ref, bf16[4,272,128]{2,1,0:T(8,128)(2,1)S(1)} %collective-permute-done.19.got_ref), custom_call_target="tpu_custom_call" | custom-call | tf_op jit(solution)/shard_map/pallas_call | solution.py:615
  (38 shorter events, 6.2 us)
Async XLA Ops:
  2.8 6.7 %collective-permute-start.2 = (bf16[17,4,1024]{2,1,0:T(4,128)(2,1)S(1)}, bf16[17,4,1024]{2,1,0:T(4,128)(2,1)S(1)}, u32[]{:S(2)}, u32[]{:S(2)}) collective-permute-start(bf16[17,4,1024]{2,1,0:T(4,128)(2,1)S(1)} %get-tuple-element.43), channel_id=1, source_target_pairs={{0,16},{16,0},{1,17},{17,1},{2,18},{18,2},{3,19},{19,3},{4,20},{20... | collective-permute-start | bytes 417800 | tf_op jit(solution)/shard_map/ppermute | solution.py:553
  6.8 7.9 %collective-permute-start = (bf16[34,4,1024]{2,1,0:T(4,128)(2,1)S(1)}, bf16[34,4,1024]{2,1,0:T(4,128)(2,1)S(1)}, u32[]{:S(2)}, u32[]{:S(2)}) collective-permute-start(bf16[34,4,1024]{2,1,0:T(4,128)(2,1)S(1)} %get-tuple-element.34), channel_id=1, source_target_pairs={{4,8},{5,9},{6,10},{7,11},{20,24},{21,25},{22,26},{23,27},{8,4},{9... | collective-permute-start | bytes 835592 | tf_op jit(solution)/shard_map/ppermute | solution.py:557
  8.5 3.8 %collective-permute-start.1 = (bf16[34,4,1024]{2,1,0:T(4,128)(2,1)S(1)}, bf16[34,4,1024]{2,1,0:T(4,128)(2,1)S(1)}, u32[]{:S(2)}, u32[]{:S(2)}) collective-permute-start(bf16[34,4,1024]{2,1,0:T(4,128)(2,1)S(1)} %get-tuple-element.41), channel_id=1, source_target_pairs={{0,4},{8,12},{4,0},{12,8},{1,5},{9,13},{5,1},{13,9},{2,6},{10,14},... | collective-permute-start | bytes 835592 | tf_op jit(solution)/shard_map/ppermute | solution.py:558
  9.7 5.1 %collective-permute-start.4 = (bf16[5,4,1024]{2,1,0:T(4,128)(2,1)S(1)}, bf16[5,4,1024]{2,1,0:T(4,128)(2,1)S(1)}, u32[]{:S(2)}, u32[]{:S(2)}) collective-permute-start(bf16[5,4,1024]{2,1,0:T(4,128)(2,1)S(1)} %get-tuple-element.71), channel_id=1, source_target_pairs={{4,8},{8,4},{0,16},{12,28},{20,24},{24,20},{16,0},{28,12},{5,9},{9... | collective-permute-start | bytes 122888 | tf_op jit(solution)/shard_map/ppermute | solution.py:573
  11.5 3.3 %collective-permute-start.3 = (bf16[5,4,1024]{2,1,0:T(4,128)(2,1)S(1)}, bf16[5,4,1024]{2,1,0:T(4,128)(2,1)S(1)}, u32[]{:S(2)}, u32[]{:S(2)}) collective-permute-start(bf16[5,4,1024]{2,1,0:T(4,128)(2,1)S(1)} %get-tuple-element.72), channel_id=1, source_target_pairs={{0,4},{8,12},{4,0},{12,8},{1,5},{9,13},{5,1},{13,9},{2,6},{10,14},... | collective-permute-start | bytes 122888 | tf_op jit(solution)/shard_map/ppermute | solution.py:572
  12.9 9.4 %collective-permute-start.5 = (bf16[34,16,128]{2,1,0:T(8,128)(2,1)S(1)}, bf16[34,16,128]{2,1,0:T(8,128)(2,1)S(1)}, u32[]{:S(2)}, u32[]{:S(2)}) collective-permute-start(bf16[34,16,128]{2,1,0:T(8,128)(2,1)S(1)} %get-tuple-element.52), channel_id=1, source_target_pairs={{0,1},{2,3},{1,0},{3,2},{4,5},{6,7},{5,4},{7,6},{8,9},{10,11},{9,8... | collective-permute-start | bytes 417800 | tf_op jit(solution)/shard_map/ppermute | solution.py:551
  14.6 7.7 %collective-permute-start.6 = (bf16[34,16,128]{2,1,0:T(8,128)(2,1)S(1)}, bf16[34,16,128]{2,1,0:T(8,128)(2,1)S(1)}, u32[]{:S(2)}, u32[]{:S(2)}) collective-permute-start(bf16[34,16,128]{2,1,0:T(8,128)(2,1)S(1)} %get-tuple-element.53), channel_id=1, source_target_pairs={{1,2},{2,1},{0,4},{3,7},{5,6},{6,5},{4,0},{7,3},{9,10},{10,9},{8,1... | collective-permute-start | bytes 417800 | tf_op jit(solution)/shard_map/ppermute | solution.py:551
  15.5 6.8 %collective-permute-start.7 = (bf16[46,8,128]{2,1,0:T(8,128)(2,1)S(1)}, bf16[46,8,128]{2,1,0:T(8,128)(2,1)S(1)}, u32[]{:S(2)}, u32[]{:S(2)}) collective-permute-start(bf16[46,8,128]{2,1,0:T(8,128)(2,1)S(1)} %get-tuple-element.54), channel_id=1, source_target_pairs={{0,1},{2,3},{1,0},{3,2},{4,5},{6,7},{5,4},{7,6},{8,9},{10,11},{9,8... | collective-permute-start | bytes 282632 | tf_op jit(solution)/shard_map/ppermute | solution.py:551
  18.5 3.8 %collective-permute-start.8 = (bf16[46,8,128]{2,1,0:T(8,128)(2,1)S(1)}, bf16[46,8,128]{2,1,0:T(8,128)(2,1)S(1)}, u32[]{:S(2)}, u32[]{:S(2)}) collective-permute-start(bf16[46,8,128]{2,1,0:T(8,128)(2,1)S(1)} %get-tuple-element.55), channel_id=1, source_target_pairs={{1,2},{2,1},{0,4},{3,7},{5,6},{6,5},{4,0},{7,3},{9,10},{10,9},{8,1... | collective-permute-start | bytes 282632 | tf_op jit(solution)/shard_map/ppermute | solution.py:551
  28.5 1.7 %collective-permute-start.9 = (bf16[4,272,128]{2,1,0:T(8,128)(2,1)S(1)}, bf16[4,272,128]{2,1,0:T(8,128)(2,1)S(1)}, u32[]{:S(2)}, u32[]{:S(2)}) collective-permute-start(bf16[4,272,128]{2,1,0:T(8,128)(2,1)S(1)} %get-tuple-element.59), channel_id=1, source_target_pairs={{0,4},{4,0},{8,12},{12,8},{16,20},{20,16},{24,28},{28,24},{1,5},{5... | collective-permute-start | bytes 835592 | tf_op jit(solution)/shard_map/ppermute | solution.py:603
  30.3 5.0 %collective-permute-start.10 = (bf16[272,128]{1,0:T(8,128)(2,1)S(1)}, bf16[272,128]{1,0:T(8,128)(2,1)S(1)}, u32[]{:S(2)}, u32[]{:S(2)}) collective-permute-start(bf16[272,128]{1,0:T(8,128)(2,1)S(1)} %get-tuple-element.64), channel_id=1, source_target_pairs={{0,8},{4,12},{8,0},{12,4},{16,24},{20,28},{24,16},{28,20},{1,9},{5... | collective-permute-start | bytes 208904 | tf_op jit(solution)/shard_map/ppermute | solution.py:600
  30.5 6.9 %collective-permute-start.12 = (bf16[272,128]{1,0:T(8,128)(2,1)S(1)}, bf16[272,128]{1,0:T(8,128)(2,1)S(1)}, u32[]{:S(2)}, u32[]{:S(2)}) collective-permute-start(bf16[272,128]{1,0:T(8,128)(2,1)S(1)} %get-tuple-element.65), channel_id=1, source_target_pairs={{0,24},{4,28},{8,16},{12,20},{16,8},{20,12},{24,0},{28,4},{1,25},{... | collective-permute-start | bytes 208904 | tf_op jit(solution)/shard_map/ppermute | solution.py:600
  33.4 5.1 %collective-permute-start.11 = (bf16[272,128]{1,0:T(8,128)(2,1)S(1)}, bf16[272,128]{1,0:T(8,128)(2,1)S(1)}, u32[]{:S(2)}, u32[]{:S(2)}) collective-permute-start(bf16[272,128]{1,0:T(8,128)(2,1)S(1)} %get-tuple-element.66), channel_id=1, source_target_pairs={{0,16},{4,20},{8,24},{12,28},{16,0},{20,4},{24,8},{28,12},{1,17},{... | collective-permute-start | bytes 208904 | tf_op jit(solution)/shard_map/ppermute | solution.py:600
  38.5 7.0 %collective-permute-start.15 = (bf16[272,128]{1,0:T(8,128)(2,1)S(1)}, bf16[272,128]{1,0:T(8,128)(2,1)S(1)}, u32[]{:S(2)}, u32[]{:S(2)}) collective-permute-start(bf16[272,128]{1,0:T(8,128)(2,1)S(1)} %fusion.2), channel_id=1, source_target_pairs={{0,3},{1,2},{2,1},{3,0},{4,7},{5,6},{6,5},{7,4},{8,11},{9,10},{10,... | collective-permute-start | bytes 208904 | tf_op jit(solution)/shard_map/ppermute | solution.py:606
  40.0 7.3 %collective-permute-start.14 = (bf16[272,128]{1,0:T(8,128)(2,1)S(1)}, bf16[272,128]{1,0:T(8,128)(2,1)S(1)}, u32[]{:S(2)}, u32[]{:S(2)}) collective-permute-start(bf16[272,128]{1,0:T(8,128)(2,1)S(1)} %fusion.2), channel_id=1, source_target_pairs={{0,2},{1,3},{2,0},{3,1},{4,6},{5,7},{6,4},{7,5},{8,10},{9,11},{10,... | collective-permute-start | bytes 208904 | tf_op jit(solution)/shard_map/ppermute | solution.py:606
  40.6 6.8 %collective-permute-start.13 = (bf16[272,128]{1,0:T(8,128)(2,1)S(1)}, bf16[272,128]{1,0:T(8,128)(2,1)S(1)}, u32[]{:S(2)}, u32[]{:S(2)}) collective-permute-start(bf16[272,128]{1,0:T(8,128)(2,1)S(1)} %fusion.2), channel_id=1, source_target_pairs={{0,1},{1,0},{2,3},{3,2},{4,5},{5,4},{6,7},{7,6},{8,9},{9,8},{10,11... | collective-permute-start | bytes 208904 | tf_op jit(solution)/shard_map/ppermute | solution.py:606
  47.4 5.8 %collective-permute-start.18 = (bf16[272,128]{1,0:T(8,128)(2,1)S(1)}, bf16[272,128]{1,0:T(8,128)(2,1)S(1)}, u32[]{:S(2)}, u32[]{:S(2)}) collective-permute-start(bf16[272,128]{1,0:T(8,128)(2,1)S(1)} %add_convert_fusion), channel_id=1, source_target_pairs={{0,24},{4,28},{8,16},{12,20},{16,8},{20,12},{24,0},{28,4},{1,25},{... | collective-permute-start | bytes 208904 | tf_op jit(solution)/shard_map/ppermute | solution.py:600
  47.9 5.4 %collective-permute-start.17 = (bf16[272,128]{1,0:T(8,128)(2,1)S(1)}, bf16[272,128]{1,0:T(8,128)(2,1)S(1)}, u32[]{:S(2)}, u32[]{:S(2)}) collective-permute-start(bf16[272,128]{1,0:T(8,128)(2,1)S(1)} %add_convert_fusion), channel_id=1, source_target_pairs={{0,16},{4,20},{8,24},{12,28},{16,0},{20,4},{24,8},{28,12},{1,17},{... | collective-permute-start | bytes 208904 | tf_op jit(solution)/shard_map/ppermute | solution.py:600
  50.0 4.3 %collective-permute-start.16 = (bf16[272,128]{1,0:T(8,128)(2,1)S(1)}, bf16[272,128]{1,0:T(8,128)(2,1)S(1)}, u32[]{:S(2)}, u32[]{:S(2)}) collective-permute-start(bf16[272,128]{1,0:T(8,128)(2,1)S(1)} %add_convert_fusion), channel_id=1, source_target_pairs={{0,8},{4,12},{8,0},{12,4},{16,24},{20,28},{24,16},{28,20},{1,9},{5... | collective-permute-start | bytes 208904 | tf_op jit(solution)/shard_map/ppermute | solution.py:600
  54.4 1.6 %collective-permute-start.19 = (bf16[4,272,128]{2,1,0:T(8,128)(2,1)S(1)}, bf16[4,272,128]{2,1,0:T(8,128)(2,1)S(1)}, u32[]{:S(2)}, u32[]{:S(2)}) collective-permute-start(bf16[4,272,128]{2,1,0:T(8,128)(2,1)S(1)} %pad_maximum_fusion.keep_ref), channel_id=1, source_target_pairs={{0,4},{4,0},{8,12},{12,8},{16,20},{20,16},{24,28},{28,24},{1,5},{5... | collective-permute-start | bytes 835592 | tf_op jit(solution)/shard_map/ppermute | solution.py:603

commit v8 on v7

--- a/solution.py
+++ b/solution.py
@@ -456,7 +456,7 @@
     for n in range(squares):
         for ref, half in ((keep_ref, core), (got_ref, 1 - core)):
             start = pl.multiple_of((half * squares + (square ^ n)) * size, 8)
-            sums[pl.ds(start, size), :] = ref[n].astype(F32)
+            sums[pl.ds(start, size), :] = ref[-n % squares].astype(F32)
     second = pltpu.make_async_copy(sums.at[pl.ds(0, SECOND_ROWS)], g2_hbm, sent.at[0])
     second.start()
     found = [sums[SECOND_ROWS + 64 * n : SECOND_ROWS + 64 * (n + 1), :] for n in range(FIRST_BLOCKS)]
@@ -607,9 +607,10 @@
 
     both = keep + to_core(give).astype(F32)
     near = both.astype(BF16)
-    share = add_up(both[0], *[to_square(near[n], n) for n in range(1, squares)])
+    order = [1, *reversed(range(2, squares))]
+    share = add_up(both[0], *[to_square(near[n], n) for n in order])
     share = add_up(share, *[along_col(share, n) for n in range(1, cols)])
-    mine = jnp.stack([share] + [to_square(share, n) for n in range(1, squares)])
+    mine = jnp.stack([share] + [to_square(share, n) for n in reversed(range(1, squares))])
     other = to_core(mine)
     grads = [jax.ShapeDtypeStruct(shape, F32) for shape in (first_weight.shape, second_weight.shape[::-1])]
     first_grad, second_grad = pl.pallas_call(

time: 57.8 us -> 56.9 us (0.984)
  waiting for transfers between devices: 16.1 us -> 15.3 us
    ppermute x6, waiting for transfers between devices: 8 us -> 6.81 us  [to_square(): return lax.ppermute(block, ('depth', 'row'), route)]
  transfers between devices with their start and end apart: 20 -> 20, of which waited for: 11 -> 10; matrix products, arithmetic and copies ran while one was open for 0% -> 0% of each run, Pallas kernels for 12% -> 12%
where the time goes in v8:
time: 56.9 us; the launch traced here: 56.8 us
  starting transfers between devices  23.7 us (42%)
  Pallas kernels  16.5 us (29%)
  waiting for transfers between devices  15.3 us (27%)
  between operations  0.84 us (1%)
    ppermute x6, starting transfers between devices, to_square(): return lax.ppermute(block, ('depth', 'row'), route)  7.12 us
    ppermute x6, waiting for transfers between devices, to_square(): return lax.ppermute(block, ('depth', 'row'), route)  6.81 us
    pallas_call x1, Pallas kernels, local_grads(): pl.pallas_call(body, out_shape=[jax.ShapeDtypeStruct((squares, rows // (2...  6.11 us
    ppermute x4, starting transfers between devices, to_col(): return lax.ppermute(block, ('row', 'col'), pairs_of_lines(rows, cols, kind))  4.86 us
    ppermute x3, waiting for transfers between devices, along_col(): return lax.ppermute(block, 'col', [(i, i ^ n) for i in range(cols)])  4.7 us
    ppermute x3, starting transfers between devices, along_col(): return lax.ppermute(block, 'col', [(i, i ^ n) for i in range(cols)])  4.45 us
    pallas_call x1, Pallas kernels, local_grads(): pl.pallas_call(own_blocks, out_shape=[jax.ShapeDtypeStruct((3, planes + 9...  3.77 us
    ppermute x1, starting transfers between devices, shards(): dep = lax.ppermute(dep, 'depth', [(0, 1), (1, 0)])  3.03 us
  transfers between devices with their start and end apart: 20, of which 10 were waited for; matrix products, arithmetic and copies ran while one was open for 0% of the time, Pallas kernels for 12%

profile of v8, /device:TPU:0, one launch (start us, length us, event | category | flops | bytes accessed | tf_op | source)
XLA Modules:
  0.0 56.8 jit_solution(2916749301901680558)
XLA Ops:
  0.7 2.0 %shard_map.59 = (bf16[32,16,1024]{2,1,0:T(8,128)(2,1)S(1)}, bf16[8,4,1024]{2,1,0:T(4,128)(2,1)S(1)}, bf16[64,864]{1,0:T(8,128)(2,1)S(1)}, bf16[1728,128]{1,0:T(8,128)(2,1)S(1)}, bf16[17,4,1024]{2,1,0:T(4,128)(2,1)S(1)}) custom-call(s32[5]{0:T(128)S(1)} %stack.58.flag_ref, bf16[32,16,1024]{2,1,0:T(8,128)(2,1)} %vol_hbm.1, bf16[8,4,1024]{2,1,0:T(4,128)(2,1)} %cot_hbm.1, ...), custom_call_target="tpu_custom_call" | custom-call | tf_op jit(solution)/shard_map/pallas_call | solution.py:534
  2.8 3.0 %collective-permute-start.2 = (bf16[17,4,1024]{2,1,0:T(4,128)(2,1)S(1)}, bf16[17,4,1024]{2,1,0:T(4,128)(2,1)S(1)}, u32[]{:S(2)}, u32[]{:S(2)}) collective-permute-start(bf16[17,4,1024]{2,1,0:T(4,128)(2,1)S(1)} %get-tuple-element.43), channel_id=1, source_target_pairs={{0,16},{16,0},{1,17},{17,1},{2,18},{18,2},{3,19},{19,3},{4,20},{20... | collective-permute-start | bytes 417800 | tf_op jit(solution)/shard_map/ppermute | solution.py:553
  6.8 1.6 %collective-permute-start = (bf16[34,4,1024]{2,1,0:T(4,128)(2,1)S(1)}, bf16[34,4,1024]{2,1,0:T(4,128)(2,1)S(1)}, u32[]{:S(2)}, u32[]{:S(2)}) collective-permute-start(bf16[34,4,1024]{2,1,0:T(4,128)(2,1)S(1)} %get-tuple-element.34), channel_id=1, source_target_pairs={{4,8},{5,9},{6,10},{7,11},{20,24},{21,25},{22,26},{23,27},{8,4},{9... | collective-permute-start | bytes 835592 | tf_op jit(solution)/shard_map/ppermute | solution.py:557
  8.5 1.0 %collective-permute-done.2.dep_ref = bf16[17,4,1024]{2,1,0:T(4,128)(2,1)S(1)} collective-permute-done((bf16[17,4,1024]{2,1,0:T(4,128)(2,1)S(1)}, bf16[17,4,1024]{2,1,0:T(4,128)(2,1)S(1)}, u32[]{:S(2)}, u32[]{:S(2)}) %collective-permute-start.2) | collective-permute-done | bytes 139296 | tf_op jit(solution)/shard_map/ppermute | solution.py:553
  9.7 1.8 %collective-permute-start.4 = (bf16[5,4,1024]{2,1,0:T(4,128)(2,1)S(1)}, bf16[5,4,1024]{2,1,0:T(4,128)(2,1)S(1)}, u32[]{:S(2)}, u32[]{:S(2)}) collective-permute-start(bf16[5,4,1024]{2,1,0:T(4,128)(2,1)S(1)} %get-tuple-element.71), channel_id=1, source_target_pairs={{4,8},{8,4},{0,16},{12,28},{20,24},{24,20},{16,0},{28,12},{5,9},{9... | collective-permute-start | bytes 122888 | tf_op jit(solution)/shard_map/ppermute | solution.py:573
  12.9 1.6 %collective-permute-start.5 = (bf16[34,16,128]{2,1,0:T(8,128)(2,1)S(1)}, bf16[34,16,128]{2,1,0:T(8,128)(2,1)S(1)}, u32[]{:S(2)}, u32[]{:S(2)}) collective-permute-start(bf16[34,16,128]{2,1,0:T(8,128)(2,1)S(1)} %get-tuple-element.52), channel_id=1, source_target_pairs={{0,1},{2,3},{1,0},{3,2},{4,5},{6,7},{5,4},{7,6},{8,9},{10,11},{9,8... | collective-permute-start | bytes 417800 | tf_op jit(solution)/shard_map/ppermute | solution.py:551
  15.5 3.1 %collective-permute-start.7 = (bf16[46,8,128]{2,1,0:T(8,128)(2,1)S(1)}, bf16[46,8,128]{2,1,0:T(8,128)(2,1)S(1)}, u32[]{:S(2)}, u32[]{:S(2)}) collective-permute-start(bf16[46,8,128]{2,1,0:T(8,128)(2,1)S(1)} %get-tuple-element.54), channel_id=1, source_target_pairs={{0,1},{2,3},{1,0},{3,2},{4,5},{6,7},{5,4},{7,6},{8,9},{10,11},{9,8... | collective-permute-start | bytes 282632 | tf_op jit(solution)/shard_map/ppermute | solution.py:551
  18.5 3.8 %shard_map.63 = (bf16[3,41,8,16,128]{4,3,2,1,0:T(8,128)(2,1)S(1)}, f32[20,8,16,256]{3,2,1,0:T(8,128)S(1)}) custom-call(s32[5]{0:T(128)S(1)} %stack.58.flag_ref, bf16[32,16,1024]{2,1,0:T(8,128)(2,1)S(1)} %get-tuple-element.47.vol_ref, bf16[17,4,1024]{2,1,0:T(4,128)(2,1)S(1)} %collective-permute-done.2.dep_ref, ...), custom_call_target="tpu_custom_call" | custom-call | flops 2000000000 | bytes 10000000 | tf_op jit(solution)/shard_map/pallas_call | solution.py:480
  22.3 6.1 %shard_map.65 = (f32[4,272,128]{2,1,0:T(8,128)S(1)}, bf16[4,272,128]{2,1,0:T(8,128)(2,1)S(1)}) custom-call(s32[5]{0:T(128)S(1)} %stack.58.flag_ref, s32[2]{0:T(128)S(1)} %pad_add_fusion.place_ref, bf16[3,41,8,16,128]{4,3,2,1,0:T(8,128)(2,1)S(1)} %get-tuple-element.49.tiles, f32[20,8,16,256]{3,2,1,0:T(8,128)S(1)} %get-tuple-element.50.parts, ...), custom_call_target="tpu_custom_call" | custom-call | flops 4000000000 | bytes 10000000 | tf_op jit(solution)/shard_map/pallas_call | solution.py:505
  29.0 1.2 %collective-permute-done.9 = bf16[4,272,128]{2,1,0:T(8,128)(2,1)S(1)} collective-permute-done((bf16[4,272,128]{2,1,0:T(8,128)(2,1)S(1)}, bf16[4,272,128]{2,1,0:T(8,128)(2,1)S(1)}, u32[]{:S(2)}, u32[]{:S(2)}) %collective-permute-start.9) | collective-permute-done | bytes 278560 | tf_op jit(solution)/shard_map/ppermute | solution.py:603
  30.5 1.5 %collective-permute-start.12 = (bf16[272,128]{1,0:T(8,128)(2,1)S(1)}, bf16[272,128]{1,0:T(8,128)(2,1)S(1)}, u32[]{:S(2)}, u32[]{:S(2)}) collective-permute-start(bf16[272,128]{1,0:T(8,128)(2,1)S(1)} %get-tuple-element.65), channel_id=1, source_target_pairs={{0,16},{4,20},{8,24},{12,28},{16,0},{20,4},{24,8},{28,12},{1,17},{... | collective-permute-start | bytes 208904 | tf_op jit(solution)/shard_map/ppermute | solution.py:600
  32.0 1.9 %collective-permute-start.11 = (bf16[272,128]{1,0:T(8,128)(2,1)S(1)}, bf16[272,128]{1,0:T(8,128)(2,1)S(1)}, u32[]{:S(2)}, u32[]{:S(2)}) collective-permute-start(bf16[272,128]{1,0:T(8,128)(2,1)S(1)} %get-tuple-element.66), channel_id=1, source_target_pairs={{0,24},{4,28},{8,16},{12,20},{16,8},{20,12},{24,0},{28,4},{1,25},{... | collective-permute-start | bytes 208904 | tf_op jit(solution)/shard_map/ppermute | solution.py:600
  33.9 1.2 %collective-permute-done.10 = bf16[272,128]{1,0:T(8,128)(2,1)S(1)} collective-permute-done((bf16[272,128]{1,0:T(8,128)(2,1)S(1)}, bf16[272,128]{1,0:T(8,128)(2,1)S(1)}, u32[]{:S(2)}, u32[]{:S(2)}) %collective-permute-start.10) | collective-permute-done | bytes 69664 | tf_op jit(solution)/shard_map/ppermute | solution.py:600
  35.1 2.2 %collective-permute-done.11 = bf16[272,128]{1,0:T(8,128)(2,1)S(1)} collective-permute-done((bf16[272,128]{1,0:T(8,128)(2,1)S(1)}, bf16[272,128]{1,0:T(8,128)(2,1)S(1)}, u32[]{:S(2)}, u32[]{:S(2)}) %collective-permute-start.11) | collective-permute-done | bytes 69664 | tf_op jit(solution)/shard_map/ppermute | solution.py:600
  37.3 2.1 %collective-permute-start.15 = (bf16[272,128]{1,0:T(8,128)(2,1)S(1)}, bf16[272,128]{1,0:T(8,128)(2,1)S(1)}, u32[]{:S(2)}, u32[]{:S(2)}) collective-permute-start(bf16[272,128]{1,0:T(8,128)(2,1)S(1)} %fusion.2), channel_id=1, source_target_pairs={{0,3},{1,2},{2,1},{3,0},{4,7},{5,6},{6,5},{7,4},{8,11},{9,10},{10,... | collective-permute-start | bytes 208904 | tf_op jit(solution)/shard_map/ppermute | solution.py:606
  40.4 1.4 %collective-permute-start.13 = (bf16[272,128]{1,0:T(8,128)(2,1)S(1)}, bf16[272,128]{1,0:T(8,128)(2,1)S(1)}, u32[]{:S(2)}, u32[]{:S(2)}) collective-permute-start(bf16[272,128]{1,0:T(8,128)(2,1)S(1)} %fusion.2), channel_id=1, source_target_pairs={{0,1},{1,0},{2,3},{3,2},{4,5},{5,4},{6,7},{7,6},{8,9},{9,8},{10,11... | collective-permute-start | bytes 208904 | tf_op jit(solution)/shard_map/ppermute | solution.py:606
  41.8 2.5 %collective-permute-done.15 = bf16[272,128]{1,0:T(8,128)(2,1)S(1)} collective-permute-done((bf16[272,128]{1,0:T(8,128)(2,1)S(1)}, bf16[272,128]{1,0:T(8,128)(2,1)S(1)}, u32[]{:S(2)}, u32[]{:S(2)}) %collective-permute-start.15) | collective-permute-done | bytes 69664 | tf_op jit(solution)/shard_map/ppermute | solution.py:606
  44.3 2.2 %collective-permute-done.14 = bf16[272,128]{1,0:T(8,128)(2,1)S(1)} collective-permute-done((bf16[272,128]{1,0:T(8,128)(2,1)S(1)}, bf16[272,128]{1,0:T(8,128)(2,1)S(1)}, u32[]{:S(2)}, u32[]{:S(2)}) %collective-permute-start.14) | collective-permute-done | bytes 69664 | tf_op jit(solution)/shard_map/ppermute | solution.py:606
  46.5 1.1 %collective-permute-start.18 = (bf16[272,128]{1,0:T(8,128)(2,1)S(1)}, bf16[272,128]{1,0:T(8,128)(2,1)S(1)}, u32[]{:S(2)}, u32[]{:S(2)}) collective-permute-start(bf16[272,128]{1,0:T(8,128)(2,1)S(1)} %add_convert_fusion), channel_id=1, source_target_pairs={{0,8},{4,12},{8,0},{12,4},{16,24},{20,28},{24,16},{28,20},{1,9},{5... | collective-permute-start | bytes 208904 | tf_op jit(solution)/shard_map/ppermute | solution.py:600
  48.3 1.8 %collective-permute-start.16 = (bf16[272,128]{1,0:T(8,128)(2,1)S(1)}, bf16[272,128]{1,0:T(8,128)(2,1)S(1)}, u32[]{:S(2)}, u32[]{:S(2)}) collective-permute-start(bf16[272,128]{1,0:T(8,128)(2,1)S(1)} %add_convert_fusion), channel_id=1, source_target_pairs={{0,24},{4,28},{8,16},{12,20},{16,8},{20,12},{24,0},{28,4},{1,25},{... | collective-permute-start | bytes 208904 | tf_op jit(solution)/shard_map/ppermute | solution.py:600
  50.1 1.5 %collective-permute-done.18 = bf16[272,128]{1,0:T(8,128)(2,1)S(1)} collective-permute-done((bf16[272,128]{1,0:T(8,128)(2,1)S(1)}, bf16[272,128]{1,0:T(8,128)(2,1)S(1)}, u32[]{:S(2)}, u32[]{:S(2)}) %collective-permute-start.18) | collective-permute-done | bytes 69664 | tf_op jit(solution)/shard_map/ppermute | solution.py:600
  52.0 1.5 %collective-permute-done.16 = bf16[272,128]{1,0:T(8,128)(2,1)S(1)} collective-permute-done((bf16[272,128]{1,0:T(8,128)(2,1)S(1)}, bf16[272,128]{1,0:T(8,128)(2,1)S(1)}, u32[]{:S(2)}, u32[]{:S(2)}) %collective-permute-start.16) | collective-permute-done | bytes 69664 | tf_op jit(solution)/shard_map/ppermute | solution.py:600
  53.6 1.5 %collective-permute-done.19.got_ref = bf16[4,272,128]{2,1,0:T(8,128)(2,1)S(1)} collective-permute-done((bf16[4,272,128]{2,1,0:T(8,128)(2,1)S(1)}, bf16[4,272,128]{2,1,0:T(8,128)(2,1)S(1)}, u32[]{:S(2)}, u32[]{:S(2)}) %collective-permute-start.19) | collective-permute-done | bytes 278560 | tf_op jit(solution)/shard_map/ppermute | solution.py:603
  55.2 1.6 %shard_map.66 = (f32[64,864]{1,0:T(8,128)}, f32[1728,128]{1,0:T(8,128)}) custom-call(s32[2]{0:T(128)S(1)} %pad_add_fusion.place_ref, bf16[4,272,128]{2,1,0:T(8,128)(2,1)S(1)} %pad_maximum_fusion.keep_ref, bf16[4,272,128]{2,1,0:T(8,128)(2,1)S(1)} %collective-permute-done.19.got_ref), custom_call_target="tpu_custom_call" | custom-call | tf_op jit(solution)/shard_map/pallas_call | solution.py:616
  (38 shorter events, 6.6 us)
Async XLA Ops:
  2.8 6.7 %collective-permute-start.2 = (bf16[17,4,1024]{2,1,0:T(4,128)(2,1)S(1)}, bf16[17,4,1024]{2,1,0:T(4,128)(2,1)S(1)}, u32[]{:S(2)}, u32[]{:S(2)}) collective-permute-start(bf16[17,4,1024]{2,1,0:T(4,128)(2,1)S(1)} %get-tuple-element.43), channel_id=1, source_target_pairs={{0,16},{16,0},{1,17},{17,1},{2,18},{18,2},{3,19},{19,3},{4,20},{20... | collective-permute-start | bytes 417800 | tf_op jit(solution)/shard_map/ppermute | solution.py:553
  6.8 7.9 %collective-permute-start = (bf16[34,4,1024]{2,1,0:T(4,128)(2,1)S(1)}, bf16[34,4,1024]{2,1,0:T(4,128)(2,1)S(1)}, u32[]{:S(2)}, u32[]{:S(2)}) collective-permute-start(bf16[34,4,1024]{2,1,0:T(4,128)(2,1)S(1)} %get-tuple-element.34), channel_id=1, source_target_pairs={{4,8},{5,9},{6,10},{7,11},{20,24},{21,25},{22,26},{23,27},{8,4},{9... | collective-permute-start | bytes 835592 | tf_op jit(solution)/shard_map/ppermute | solution.py:557
  8.5 3.8 %collective-permute-start.1 = (bf16[34,4,1024]{2,1,0:T(4,128)(2,1)S(1)}, bf16[34,4,1024]{2,1,0:T(4,128)(2,1)S(1)}, u32[]{:S(2)}, u32[]{:S(2)}) collective-permute-start(bf16[34,4,1024]{2,1,0:T(4,128)(2,1)S(1)} %get-tuple-element.41), channel_id=1, source_target_pairs={{0,4},{8,12},{4,0},{12,8},{1,5},{9,13},{5,1},{13,9},{2,6},{10,14},... | collective-permute-start | bytes 835592 | tf_op jit(solution)/shard_map/ppermute | solution.py:558
  9.7 5.1 %collective-permute-start.4 = (bf16[5,4,1024]{2,1,0:T(4,128)(2,1)S(1)}, bf16[5,4,1024]{2,1,0:T(4,128)(2,1)S(1)}, u32[]{:S(2)}, u32[]{:S(2)}) collective-permute-start(bf16[5,4,1024]{2,1,0:T(4,128)(2,1)S(1)} %get-tuple-element.71), channel_id=1, source_target_pairs={{4,8},{8,4},{0,16},{12,28},{20,24},{24,20},{16,0},{28,12},{5,9},{9... | collective-permute-start | bytes 122888 | tf_op jit(solution)/shard_map/ppermute | solution.py:573
  11.5 3.3 %collective-permute-start.3 = (bf16[5,4,1024]{2,1,0:T(4,128)(2,1)S(1)}, bf16[5,4,1024]{2,1,0:T(4,128)(2,1)S(1)}, u32[]{:S(2)}, u32[]{:S(2)}) collective-permute-start(bf16[5,4,1024]{2,1,0:T(4,128)(2,1)S(1)} %get-tuple-element.72), channel_id=1, source_target_pairs={{0,4},{8,12},{4,0},{12,8},{1,5},{9,13},{5,1},{13,9},{2,6},{10,14},... | collective-permute-start | bytes 122888 | tf_op jit(solution)/shard_map/ppermute | solution.py:572
  12.9 9.4 %collective-permute-start.5 = (bf16[34,16,128]{2,1,0:T(8,128)(2,1)S(1)}, bf16[34,16,128]{2,1,0:T(8,128)(2,1)S(1)}, u32[]{:S(2)}, u32[]{:S(2)}) collective-permute-start(bf16[34,16,128]{2,1,0:T(8,128)(2,1)S(1)} %get-tuple-element.52), channel_id=1, source_target_pairs={{0,1},{2,3},{1,0},{3,2},{4,5},{6,7},{5,4},{7,6},{8,9},{10,11},{9,8... | collective-permute-start | bytes 417800 | tf_op jit(solution)/shard_map/ppermute | solution.py:551
  14.6 7.7 %collective-permute-start.6 = (bf16[34,16,128]{2,1,0:T(8,128)(2,1)S(1)}, bf16[34,16,128]{2,1,0:T(8,128)(2,1)S(1)}, u32[]{:S(2)}, u32[]{:S(2)}) collective-permute-start(bf16[34,16,128]{2,1,0:T(8,128)(2,1)S(1)} %get-tuple-element.53), channel_id=1, source_target_pairs={{1,2},{2,1},{0,4},{3,7},{5,6},{6,5},{4,0},{7,3},{9,10},{10,9},{8,1... | collective-permute-start | bytes 417800 | tf_op jit(solution)/shard_map/ppermute | solution.py:551
  15.5 6.8 %collective-permute-start.7 = (bf16[46,8,128]{2,1,0:T(8,128)(2,1)S(1)}, bf16[46,8,128]{2,1,0:T(8,128)(2,1)S(1)}, u32[]{:S(2)}, u32[]{:S(2)}) collective-permute-start(bf16[46,8,128]{2,1,0:T(8,128)(2,1)S(1)} %get-tuple-element.54), channel_id=1, source_target_pairs={{0,1},{2,3},{1,0},{3,2},{4,5},{6,7},{5,4},{7,6},{8,9},{10,11},{9,8... | collective-permute-start | bytes 282632 | tf_op jit(solution)/shard_map/ppermute | solution.py:551
  18.5 3.8 %collective-permute-start.8 = (bf16[46,8,128]{2,1,0:T(8,128)(2,1)S(1)}, bf16[46,8,128]{2,1,0:T(8,128)(2,1)S(1)}, u32[]{:S(2)}, u32[]{:S(2)}) collective-permute-start(bf16[46,8,128]{2,1,0:T(8,128)(2,1)S(1)} %get-tuple-element.55), channel_id=1, source_target_pairs={{1,2},{2,1},{0,4},{3,7},{5,6},{6,5},{4,0},{7,3},{9,10},{10,9},{8,1... | collective-permute-start | bytes 282632 | tf_op jit(solution)/shard_map/ppermute | solution.py:551
  28.5 1.7 %collective-permute-start.9 = (bf16[4,272,128]{2,1,0:T(8,128)(2,1)S(1)}, bf16[4,272,128]{2,1,0:T(8,128)(2,1)S(1)}, u32[]{:S(2)}, u32[]{:S(2)}) collective-permute-start(bf16[4,272,128]{2,1,0:T(8,128)(2,1)S(1)} %get-tuple-element.59), channel_id=1, source_target_pairs={{0,4},{4,0},{8,12},{12,8},{16,20},{20,16},{24,28},{28,24},{1,5},{5... | collective-permute-start | bytes 835592 | tf_op jit(solution)/shard_map/ppermute | solution.py:603
  30.3 4.8 %collective-permute-start.10 = (bf16[272,128]{1,0:T(8,128)(2,1)S(1)}, bf16[272,128]{1,0:T(8,128)(2,1)S(1)}, u32[]{:S(2)}, u32[]{:S(2)}) collective-permute-start(bf16[272,128]{1,0:T(8,128)(2,1)S(1)} %get-tuple-element.64), channel_id=1, source_target_pairs={{0,8},{4,12},{8,0},{12,4},{16,24},{20,28},{24,16},{28,20},{1,9},{5... | collective-permute-start | bytes 208904 | tf_op jit(solution)/shard_map/ppermute | solution.py:600
  30.5 4.6 %collective-permute-start.12 = (bf16[272,128]{1,0:T(8,128)(2,1)S(1)}, bf16[272,128]{1,0:T(8,128)(2,1)S(1)}, u32[]{:S(2)}, u32[]{:S(2)}) collective-permute-start(bf16[272,128]{1,0:T(8,128)(2,1)S(1)} %get-tuple-element.65), channel_id=1, source_target_pairs={{0,16},{4,20},{8,24},{12,28},{16,0},{20,4},{24,8},{28,12},{1,17},{... | collective-permute-start | bytes 208904 | tf_op jit(solution)/shard_map/ppermute | solution.py:600
  32.0 5.3 %collective-permute-start.11 = (bf16[272,128]{1,0:T(8,128)(2,1)S(1)}, bf16[272,128]{1,0:T(8,128)(2,1)S(1)}, u32[]{:S(2)}, u32[]{:S(2)}) collective-permute-start(bf16[272,128]{1,0:T(8,128)(2,1)S(1)} %get-tuple-element.66), channel_id=1, source_target_pairs={{0,24},{4,28},{8,16},{12,20},{16,8},{20,12},{24,0},{28,4},{1,25},{... | collective-permute-start | bytes 208904 | tf_op jit(solution)/shard_map/ppermute | solution.py:600
  37.3 7.0 %collective-permute-start.15 = (bf16[272,128]{1,0:T(8,128)(2,1)S(1)}, bf16[272,128]{1,0:T(8,128)(2,1)S(1)}, u32[]{:S(2)}, u32[]{:S(2)}) collective-permute-start(bf16[272,128]{1,0:T(8,128)(2,1)S(1)} %fusion.2), channel_id=1, source_target_pairs={{0,3},{1,2},{2,1},{3,0},{4,7},{5,6},{6,5},{7,4},{8,11},{9,10},{10,... | collective-permute-start | bytes 208904 | tf_op jit(solution)/shard_map/ppermute | solution.py:606
  39.4 7.0 %collective-permute-start.14 = (bf16[272,128]{1,0:T(8,128)(2,1)S(1)}, bf16[272,128]{1,0:T(8,128)(2,1)S(1)}, u32[]{:S(2)}, u32[]{:S(2)}) collective-permute-start(bf16[272,128]{1,0:T(8,128)(2,1)S(1)} %fusion.2), channel_id=1, source_target_pairs={{0,2},{1,3},{2,0},{3,1},{4,6},{5,7},{6,4},{7,5},{8,10},{9,11},{10,... | collective-permute-start | bytes 208904 | tf_op jit(solution)/shard_map/ppermute | solution.py:606
  40.4 6.1 %collective-permute-start.13 = (bf16[272,128]{1,0:T(8,128)(2,1)S(1)}, bf16[272,128]{1,0:T(8,128)(2,1)S(1)}, u32[]{:S(2)}, u32[]{:S(2)}) collective-permute-start(bf16[272,128]{1,0:T(8,128)(2,1)S(1)} %fusion.2), channel_id=1, source_target_pairs={{0,1},{1,0},{2,3},{3,2},{4,5},{5,4},{6,7},{7,6},{8,9},{9,8},{10,11... | collective-permute-start | bytes 208904 | tf_op jit(solution)/shard_map/ppermute | solution.py:606
  46.5 5.1 %collective-permute-start.18 = (bf16[272,128]{1,0:T(8,128)(2,1)S(1)}, bf16[272,128]{1,0:T(8,128)(2,1)S(1)}, u32[]{:S(2)}, u32[]{:S(2)}) collective-permute-start(bf16[272,128]{1,0:T(8,128)(2,1)S(1)} %add_convert_fusion), channel_id=1, source_target_pairs={{0,8},{4,12},{8,0},{12,4},{16,24},{20,28},{24,16},{28,20},{1,9},{5... | collective-permute-start | bytes 208904 | tf_op jit(solution)/shard_map/ppermute | solution.py:600
  47.6 4.3 %collective-permute-start.17 = (bf16[272,128]{1,0:T(8,128)(2,1)S(1)}, bf16[272,128]{1,0:T(8,128)(2,1)S(1)}, u32[]{:S(2)}, u32[]{:S(2)}) collective-permute-start(bf16[272,128]{1,0:T(8,128)(2,1)S(1)} %add_convert_fusion), channel_id=1, source_target_pairs={{0,16},{4,20},{8,24},{12,28},{16,0},{20,4},{24,8},{28,12},{1,17},{... | collective-permute-start | bytes 208904 | tf_op jit(solution)/shard_map/ppermute | solution.py:600
  48.3 5.2 %collective-permute-start.16 = (bf16[272,128]{1,0:T(8,128)(2,1)S(1)}, bf16[272,128]{1,0:T(8,128)(2,1)S(1)}, u32[]{:S(2)}, u32[]{:S(2)}) collective-permute-start(bf16[272,128]{1,0:T(8,128)(2,1)S(1)} %add_convert_fusion), channel_id=1, source_target_pairs={{0,24},{4,28},{8,16},{12,20},{16,8},{20,12},{24,0},{28,4},{1,25},{... | collective-permute-start | bytes 208904 | tf_op jit(solution)/shard_map/ppermute | solution.py:600
  53.5 1.6 %collective-permute-start.19 = (bf16[4,272,128]{2,1,0:T(8,128)(2,1)S(1)}, bf16[4,272,128]{2,1,0:T(8,128)(2,1)S(1)}, u32[]{:S(2)}, u32[]{:S(2)}) collective-permute-start(bf16[4,272,128]{2,1,0:T(8,128)(2,1)S(1)} %pad_maximum_fusion.keep_ref), channel_id=1, source_target_pairs={{0,4},{4,0},{8,12},{12,8},{16,20},{20,16},{24,28},{28,24},{1,5},{5... | collective-permute-start | bytes 835592 | tf_op jit(solution)/shard_map/ppermute | solution.py:603

commit v9 on v8

--- a/solution.py
+++ b/solution.py
@@ -394,18 +394,17 @@
     here, after = pack(plain[:-1]), pack(plain[1:])
     here_up, after_up = pack(moved[:-1]), pack(moved[1:])
 
-    def back(terms):
-        joined = jnp.concatenate([values for values, a, b in terms], axis=1)
-        weights = jnp.concatenate([w2b_ref[3 * a + b] for values, a, b in terms], axis=0)
-        return matmul(joined, weights).reshape(quarter, blocks, 16, LANES)
-
-    rows = [
-        [back([(here, 1, 1)]), back([(here_up, 1, 0), (here, 1, 2)])],
-        [
-            back([(after, 0, 1), (here, 2, 1)]),
-            back([(after_up, 0, 0), (after, 0, 2), (here_up, 2, 0), (here, 2, 2)]),
-        ],
-    ]
+    def back(values, taps):
+        weights = jnp.concatenate([w2b_ref[3 * a + b] for a, b in taps], axis=1)
+        found = matmul(values, weights)
+        found = [found[:, n * LANES : (n + 1) * LANES] for n in range(len(taps))]
+        return [part.reshape(quarter, blocks, 16, LANES) for part in found]
+
+    here_11, here_12, here_21, here_22 = back(here, ((1, 1), (1, 2), (2, 1), (2, 2)))
+    up_10, up_20 = back(here_up, ((1, 0), (2, 0)))
+    after_01, after_02 = back(after, ((0, 1), (0, 2)))
+    (after_00,) = back(after_up, ((0, 0),))
+    rows = [[here_11, up_10 + here_12], [after_01 + here_21, after_00 + after_02 + up_20 + here_22]]
     own_list = []
     for i in range(planes // 2):
         t, parity = i // 2, i % 2
@@ -556,7 +555,6 @@
         route += [((d * rows + i) * cols + c, (d * rows + j) * cols + (c ^ 1 if i == j else c)) for d in (0, 1) for c in range(cols)]
     row_b = lax.ppermute(row_b, ("depth", "row", "col"), route)
     row_a = lax.ppermute(row_a, "row", pairs_on_line(rows, 0))
-    row_a, volume, cotangent = lax.optimization_barrier((row_a, volume, cotangent))
     side_a, side_b = pl.pallas_call(
         pack_sides,
         out_shape=[jax.ShapeDtypeStruct((groups, high, LANES), BF16)] * 2,
@@ -564,6 +562,8 @@
         out_specs=[whole] * 2,
         compiler_params=small,
     )(flags, volume, cotangent)
+    dep, side_a, side_b, first_taps = lax.optimization_barrier((dep, side_a, side_b, first_taps))
+    row_a, side_b = lax.optimization_barrier((row_a, side_b))
     side_a, side_b = to_col(side_a, 0), to_col(side_b, 1)
     low, top = [jnp.concatenate([dep[n : n + 1] for n in (*range(k, 16, 4), 16)], axis=0) for k in (0, 3)]
     even, ends = row % 2 == 0, jnp.logical_or(row == 0, row == rows - 1)

time: 56.9 us -> 56 us (0.984)
  waiting for transfers between devices: 15.3 us -> 14.6 us
    ppermute x1, waiting for transfers between devices: 1.01 us -> 0.34 us  [shards(): dep = lax.ppermute(dep, 'depth', [(0, 1), (1, 0)])]
where the time goes in v9:
time: 56 us; the launch traced here: 55.9 us
  starting transfers between devices  23.7 us (42%)
  Pallas kernels  16.2 us (29%)
  waiting for transfers between devices  14.6 us (26%)
  between operations  0.87 us (2%)
    ppermute x6, starting transfers between devices, to_square(): return lax.ppermute(block, ('depth', 'row'), route)  7.12 us
    ppermute x6, waiting for transfers between devices, to_square(): return lax.ppermute(block, ('depth', 'row'), route)  7.12 us
    pallas_call x1, Pallas kernels, local_grads(): pl.pallas_call(body, out_shape=[jax.ShapeDtypeStruct((squares, rows // (2...  5.86 us
    ppermute x4, starting transfers between devices, to_col(): return lax.ppermute(block, ('row', 'col'), pairs_of_lines(rows, cols, kind))  4.86 us
    ppermute x3, starting transfers between devices, along_col(): return lax.ppermute(block, 'col', [(i, i ^ n) for i in range(cols)])  4.45 us
    ppermute x3, waiting for transfers between devices, along_col(): return lax.ppermute(block, 'col', [(i, i ^ n) for i in range(cols)])  4.36 us
    pallas_call x1, Pallas kernels, local_grads(): pl.pallas_call(own_blocks, out_shape=[jax.ShapeDtypeStruct((3, planes + 9...  3.76 us
    ppermute x1, starting transfers between devices, shards(): dep = lax.ppermute(dep, 'depth', [(0, 1), (1, 0)])  3.03 us
  transfers between devices with their start and end apart: 20, of which 10 were waited for; matrix products, arithmetic and copies ran while one was open for 0% of the time, Pallas kernels for 12%

profile of v9, /device:TPU:0, one launch (start us, length us, event | category | flops | bytes accessed | tf_op | source)
XLA Modules:
  0.0 55.9 jit_solution(14815946256757274432)
XLA Ops:
  0.7 2.0 %shard_map.59 = (bf16[32,16,1024]{2,1,0:T(8,128)(2,1)S(1)}, bf16[8,4,1024]{2,1,0:T(4,128)(2,1)S(1)}, bf16[64,864]{1,0:T(8,128)(2,1)S(1)}, bf16[1728,128]{1,0:T(8,128)(2,1)S(1)}, bf16[17,4,1024]{2,1,0:T(4,128)(2,1)S(1)}) custom-call(s32[5]{0:T(128)S(1)} %stack.58.flag_ref, bf16[32,16,1024]{2,1,0:T(8,128)(2,1)} %vol_hbm.1, bf16[8,4,1024]{2,1,0:T(4,128)(2,1)} %cot_hbm.1, ...), custom_call_target="tpu_custom_call" | custom-call | tf_op jit(solution)/shard_map/pallas_call | solution.py:533
  2.8 3.0 %collective-permute-start.1 = (bf16[17,4,1024]{2,1,0:T(4,128)(2,1)S(1)}, bf16[17,4,1024]{2,1,0:T(4,128)(2,1)S(1)}, u32[]{:S(2)}, u32[]{:S(2)}) collective-permute-start(bf16[17,4,1024]{2,1,0:T(4,128)(2,1)S(1)} %get-tuple-element.38), channel_id=1, source_target_pairs={{0,16},{16,0},{1,17},{17,1},{2,18},{18,2},{3,19},{19,3},{4,20},{20... | collective-permute-start | bytes 417800 | tf_op jit(solution)/shard_map/ppermute | solution.py:552
  5.8 1.0 %shard_map.60 = (bf16[34,4,1024]{2,1,0:T(4,128)(2,1)S(1)}, bf16[34,4,1024]{2,1,0:T(4,128)(2,1)S(1)}) custom-call(s32[5]{0:T(128)S(1)} %stack.58.flag_ref, bf16[32,16,1024]{2,1,0:T(8,128)(2,1)S(1)} %get-tuple-element.54.vol_ref, bf16[8,4,1024]{2,1,0:T(4,128)(2,1)S(1)} %get-tuple-element.36.cot_ref), custom_call_target="tpu_custom_call" | custom-call | tf_op jit(solution)/shard_map/pallas_call | solution.py:541
  6.8 1.6 %collective-permute-start = (bf16[34,4,1024]{2,1,0:T(4,128)(2,1)S(1)}, bf16[34,4,1024]{2,1,0:T(4,128)(2,1)S(1)}, u32[]{:S(2)}, u32[]{:S(2)}) collective-permute-start(bf16[34,4,1024]{2,1,0:T(4,128)(2,1)S(1)} %get-tuple-element.37), channel_id=1, source_target_pairs={{4,8},{5,9},{6,10},{7,11},{20,24},{21,25},{22,26},{23,27},{8,4},{9... | collective-permute-start | bytes 835592 | tf_op jit(solution)/shard_map/ppermute | solution.py:556
  9.7 1.8 %collective-permute-start.4 = (bf16[5,4,1024]{2,1,0:T(4,128)(2,1)S(1)}, bf16[5,4,1024]{2,1,0:T(4,128)(2,1)S(1)}, u32[]{:S(2)}, u32[]{:S(2)}) collective-permute-start(bf16[5,4,1024]{2,1,0:T(4,128)(2,1)S(1)} %get-tuple-element.77), channel_id=1, source_target_pairs={{4,8},{8,4},{0,16},{12,28},{20,24},{24,20},{16,0},{28,12},{5,9},{9... | collective-permute-start | bytes 122888 | tf_op jit(solution)/shard_map/ppermute | solution.py:573
  11.6 1.6 %collective-permute-start.5 = (bf16[34,16,128]{2,1,0:T(8,128)(2,1)S(1)}, bf16[34,16,128]{2,1,0:T(8,128)(2,1)S(1)}, u32[]{:S(2)}, u32[]{:S(2)}) collective-permute-start(bf16[34,16,128]{2,1,0:T(8,128)(2,1)S(1)} %get-tuple-element.58), channel_id=1, source_target_pairs={{0,1},{2,3},{1,0},{3,2},{4,5},{6,7},{5,4},{7,6},{8,9},{10,11},{9,8... | collective-permute-start | bytes 417800 | tf_op jit(solution)/shard_map/ppermute | solution.py:550
  14.8 3.1 %collective-permute-start.7 = (bf16[46,8,128]{2,1,0:T(8,128)(2,1)S(1)}, bf16[46,8,128]{2,1,0:T(8,128)(2,1)S(1)}, u32[]{:S(2)}, u32[]{:S(2)}) collective-permute-start(bf16[46,8,128]{2,1,0:T(8,128)(2,1)S(1)} %get-tuple-element.60), channel_id=1, source_target_pairs={{0,1},{2,3},{1,0},{3,2},{4,5},{6,7},{5,4},{7,6},{8,9},{10,11},{9,8... | collective-permute-start | bytes 282632 | tf_op jit(solution)/shard_map/ppermute | solution.py:550
  17.9 3.8 %shard_map.64 = (bf16[3,41,8,16,128]{4,3,2,1,0:T(8,128)(2,1)S(1)}, f32[20,8,16,256]{3,2,1,0:T(8,128)S(1)}) custom-call(s32[5]{0:T(128)S(1)} %stack.58.flag_ref, bf16[32,16,1024]{2,1,0:T(8,128)(2,1)S(1)} %get-tuple-element.54.vol_ref, bf16[17,4,1024]{2,1,0:T(4,128)(2,1)S(1)} %collective-permute-done.1.dep_ref, ...), custom_call_target="tpu_custom_call" | custom-call | flops 2000000000 | bytes 10000000 | tf_op jit(solution)/shard_map/pallas_call | solution.py:479
  21.7 5.9 %shard_map.65 = (f32[4,272,128]{2,1,0:T(8,128)S(1)}, bf16[4,272,128]{2,1,0:T(8,128)(2,1)S(1)}) custom-call(s32[5]{0:T(128)S(1)} %stack.58.flag_ref, s32[2]{0:T(128)S(1)} %pad_add_fusion.place_ref, bf16[3,41,8,16,128]{4,3,2,1,0:T(8,128)(2,1)S(1)} %get-tuple-element.56.tiles, f32[20,8,16,256]{3,2,1,0:T(8,128)S(1)} %get-tuple-element.57.parts, ...), custom_call_target="tpu_custom_call" | custom-call | flops 4000000000 | bytes 10000000 | tf_op jit(solution)/shard_map/pallas_call | solution.py:504
  28.1 1.2 %collective-permute-done.9 = bf16[4,272,128]{2,1,0:T(8,128)(2,1)S(1)} collective-permute-done((bf16[4,272,128]{2,1,0:T(8,128)(2,1)S(1)}, bf16[4,272,128]{2,1,0:T(8,128)(2,1)S(1)}, u32[]{:S(2)}, u32[]{:S(2)}) %collective-permute-start.9) | collective-permute-done | bytes 278560 | tf_op jit(solution)/shard_map/ppermute | solution.py:603
  29.6 1.5 %collective-permute-start.12 = (bf16[272,128]{1,0:T(8,128)(2,1)S(1)}, bf16[272,128]{1,0:T(8,128)(2,1)S(1)}, u32[]{:S(2)}, u32[]{:S(2)}) collective-permute-start(bf16[272,128]{1,0:T(8,128)(2,1)S(1)} %get-tuple-element.71), channel_id=1, source_target_pairs={{0,16},{4,20},{8,24},{12,28},{16,0},{20,4},{24,8},{28,12},{1,17},{... | collective-permute-start | bytes 208904 | tf_op jit(solution)/shard_map/ppermute | solution.py:600
  31.1 1.9 %collective-permute-start.11 = (bf16[272,128]{1,0:T(8,128)(2,1)S(1)}, bf16[272,128]{1,0:T(8,128)(2,1)S(1)}, u32[]{:S(2)}, u32[]{:S(2)}) collective-permute-start(bf16[272,128]{1,0:T(8,128)(2,1)S(1)} %get-tuple-element.72), channel_id=1, source_target_pairs={{0,24},{4,28},{8,16},{12,20},{16,8},{20,12},{24,0},{28,4},{1,25},{... | collective-permute-start | bytes 208904 | tf_op jit(solution)/shard_map/ppermute | solution.py:600
  33.0 1.2 %collective-permute-done.10 = bf16[272,128]{1,0:T(8,128)(2,1)S(1)} collective-permute-done((bf16[272,128]{1,0:T(8,128)(2,1)S(1)}, bf16[272,128]{1,0:T(8,128)(2,1)S(1)}, u32[]{:S(2)}, u32[]{:S(2)}) %collective-permute-start.10) | collective-permute-done | bytes 69664 | tf_op jit(solution)/shard_map/ppermute | solution.py:600
  34.2 2.2 %collective-permute-done.11 = bf16[272,128]{1,0:T(8,128)(2,1)S(1)} collective-permute-done((bf16[272,128]{1,0:T(8,128)(2,1)S(1)}, bf16[272,128]{1,0:T(8,128)(2,1)S(1)}, u32[]{:S(2)}, u32[]{:S(2)}) %collective-permute-start.11) | collective-permute-done | bytes 69664 | tf_op jit(solution)/shard_map/ppermute | solution.py:600
  36.4 1.9 %collective-permute-start.15 = (bf16[272,128]{1,0:T(8,128)(2,1)S(1)}, bf16[272,128]{1,0:T(8,128)(2,1)S(1)}, u32[]{:S(2)}, u32[]{:S(2)}) collective-permute-start(bf16[272,128]{1,0:T(8,128)(2,1)S(1)} %fusion.2), channel_id=1, source_target_pairs={{0,3},{1,2},{2,1},{3,0},{4,7},{5,6},{6,5},{7,4},{8,11},{9,10},{10,... | collective-permute-start | bytes 208904 | tf_op jit(solution)/shard_map/ppermute | solution.py:606
  38.3 1.8 %collective-permute-start.14 = (bf16[272,128]{1,0:T(8,128)(2,1)S(1)}, bf16[272,128]{1,0:T(8,128)(2,1)S(1)}, u32[]{:S(2)}, u32[]{:S(2)}) collective-permute-start(bf16[272,128]{1,0:T(8,128)(2,1)S(1)} %fusion.2), channel_id=1, source_target_pairs={{0,2},{1,3},{2,0},{3,1},{4,6},{5,7},{6,4},{7,5},{8,10},{9,11},{10,... | collective-permute-start | bytes 208904 | tf_op jit(solution)/shard_map/ppermute | solution.py:606
  40.9 2.5 %collective-permute-done.15 = bf16[272,128]{1,0:T(8,128)(2,1)S(1)} collective-permute-done((bf16[272,128]{1,0:T(8,128)(2,1)S(1)}, bf16[272,128]{1,0:T(8,128)(2,1)S(1)}, u32[]{:S(2)}, u32[]{:S(2)}) %collective-permute-start.15) | collective-permute-done | bytes 69664 | tf_op jit(solution)/shard_map/ppermute | solution.py:606
  43.4 1.9 %collective-permute-done.14 = bf16[272,128]{1,0:T(8,128)(2,1)S(1)} collective-permute-done((bf16[272,128]{1,0:T(8,128)(2,1)S(1)}, bf16[272,128]{1,0:T(8,128)(2,1)S(1)}, u32[]{:S(2)}, u32[]{:S(2)}) %collective-permute-start.14) | collective-permute-done | bytes 69664 | tf_op jit(solution)/shard_map/ppermute | solution.py:606
  45.3 1.2 %collective-permute-start.18 = (bf16[272,128]{1,0:T(8,128)(2,1)S(1)}, bf16[272,128]{1,0:T(8,128)(2,1)S(1)}, u32[]{:S(2)}, u32[]{:S(2)}) collective-permute-start(bf16[272,128]{1,0:T(8,128)(2,1)S(1)} %add_convert_fusion), channel_id=1, source_target_pairs={{0,8},{4,12},{8,0},{12,4},{16,24},{20,28},{24,16},{28,20},{1,9},{5... | collective-permute-start | bytes 208904 | tf_op jit(solution)/shard_map/ppermute | solution.py:600
  47.4 1.5 %collective-permute-start.16 = (bf16[272,128]{1,0:T(8,128)(2,1)S(1)}, bf16[272,128]{1,0:T(8,128)(2,1)S(1)}, u32[]{:S(2)}, u32[]{:S(2)}) collective-permute-start(bf16[272,128]{1,0:T(8,128)(2,1)S(1)} %add_convert_fusion), channel_id=1, source_target_pairs={{0,24},{4,28},{8,16},{12,20},{16,8},{20,12},{24,0},{28,4},{1,25},{... | collective-permute-start | bytes 208904 | tf_op jit(solution)/shard_map/ppermute | solution.py:600
  49.7 1.1 %collective-permute-done.17 = bf16[272,128]{1,0:T(8,128)(2,1)S(1)} collective-permute-done((bf16[272,128]{1,0:T(8,128)(2,1)S(1)}, bf16[272,128]{1,0:T(8,128)(2,1)S(1)}, u32[]{:S(2)}, u32[]{:S(2)}) %collective-permute-start.17) | collective-permute-done | bytes 69664 | tf_op jit(solution)/shard_map/ppermute | solution.py:600
  50.8 1.8 %collective-permute-done.16 = bf16[272,128]{1,0:T(8,128)(2,1)S(1)} collective-permute-done((bf16[272,128]{1,0:T(8,128)(2,1)S(1)}, bf16[272,128]{1,0:T(8,128)(2,1)S(1)}, u32[]{:S(2)}, u32[]{:S(2)}) %collective-permute-start.16) | collective-permute-done | bytes 69664 | tf_op jit(solution)/shard_map/ppermute | solution.py:600
  52.7 1.5 %collective-permute-done.19.got_ref = bf16[4,272,128]{2,1,0:T(8,128)(2,1)S(1)} collective-permute-done((bf16[4,272,128]{2,1,0:T(8,128)(2,1)S(1)}, bf16[4,272,128]{2,1,0:T(8,128)(2,1)S(1)}, u32[]{:S(2)}, u32[]{:S(2)}) %collective-permute-start.19) | collective-permute-done | bytes 278560 | tf_op jit(solution)/shard_map/ppermute | solution.py:603
  54.2 1.6 %shard_map.66 = (f32[64,864]{1,0:T(8,128)}, f32[1728,128]{1,0:T(8,128)}) custom-call(s32[2]{0:T(128)S(1)} %pad_add_fusion.place_ref, bf16[4,272,128]{2,1,0:T(8,128)(2,1)S(1)} %pad_maximum_fusion.keep_ref, bf16[4,272,128]{2,1,0:T(8,128)(2,1)S(1)} %collective-permute-done.19.got_ref), custom_call_target="tpu_custom_call" | custom-call | tf_op jit(solution)/shard_map/pallas_call | solution.py:616
  (38 shorter events, 6.4 us)
Async XLA Ops:
  2.8 6.7 %collective-permute-start.1 = (bf16[17,4,1024]{2,1,0:T(4,128)(2,1)S(1)}, bf16[17,4,1024]{2,1,0:T(4,128)(2,1)S(1)}, u32[]{:S(2)}, u32[]{:S(2)}) collective-permute-start(bf16[17,4,1024]{2,1,0:T(4,128)(2,1)S(1)} %get-tuple-element.38), channel_id=1, source_target_pairs={{0,16},{16,0},{1,17},{17,1},{2,18},{18,2},{3,19},{19,3},{4,20},{20... | collective-permute-start | bytes 417800 | tf_op jit(solution)/shard_map/ppermute | solution.py:552
  6.8 7.3 %collective-permute-start = (bf16[34,4,1024]{2,1,0:T(4,128)(2,1)S(1)}, bf16[34,4,1024]{2,1,0:T(4,128)(2,1)S(1)}, u32[]{:S(2)}, u32[]{:S(2)}) collective-permute-start(bf16[34,4,1024]{2,1,0:T(4,128)(2,1)S(1)} %get-tuple-element.37), channel_id=1, source_target_pairs={{4,8},{5,9},{6,10},{7,11},{20,24},{21,25},{22,26},{23,27},{8,4},{9... | collective-permute-start | bytes 835592 | tf_op jit(solution)/shard_map/ppermute | solution.py:556
  8.5 5.4 %collective-permute-start.2 = (bf16[34,4,1024]{2,1,0:T(4,128)(2,1)S(1)}, bf16[34,4,1024]{2,1,0:T(4,128)(2,1)S(1)}, u32[]{:S(2)}, u32[]{:S(2)}) collective-permute-start(bf16[34,4,1024]{2,1,0:T(4,128)(2,1)S(1)} %get-tuple-element.48), channel_id=1, source_target_pairs={{0,4},{8,12},{4,0},{12,8},{1,5},{9,13},{5,1},{13,9},{2,6},{10,14},... | collective-permute-start | bytes 835592 | tf_op jit(solution)/shard_map/ppermute | solution.py:557
  9.7 4.4 %collective-permute-start.4 = (bf16[5,4,1024]{2,1,0:T(4,128)(2,1)S(1)}, bf16[5,4,1024]{2,1,0:T(4,128)(2,1)S(1)}, u32[]{:S(2)}, u32[]{:S(2)}) collective-permute-start(bf16[5,4,1024]{2,1,0:T(4,128)(2,1)S(1)} %get-tuple-element.77), channel_id=1, source_target_pairs={{4,8},{8,4},{0,16},{12,28},{20,24},{24,20},{16,0},{28,12},{5,9},{9... | collective-permute-start | bytes 122888 | tf_op jit(solution)/shard_map/ppermute | solution.py:573
  11.5 2.6 %collective-permute-start.3 = (bf16[5,4,1024]{2,1,0:T(4,128)(2,1)S(1)}, bf16[5,4,1024]{2,1,0:T(4,128)(2,1)S(1)}, u32[]{:S(2)}, u32[]{:S(2)}) collective-permute-start(bf16[5,4,1024]{2,1,0:T(4,128)(2,1)S(1)} %get-tuple-element.78), channel_id=1, source_target_pairs={{0,4},{8,12},{4,0},{12,8},{1,5},{9,13},{5,1},{13,9},{2,6},{10,14},... | collective-permute-start | bytes 122888 | tf_op jit(solution)/shard_map/ppermute | solution.py:572
  11.6 10.0 %collective-permute-start.5 = (bf16[34,16,128]{2,1,0:T(8,128)(2,1)S(1)}, bf16[34,16,128]{2,1,0:T(8,128)(2,1)S(1)}, u32[]{:S(2)}, u32[]{:S(2)}) collective-permute-start(bf16[34,16,128]{2,1,0:T(8,128)(2,1)S(1)} %get-tuple-element.58), channel_id=1, source_target_pairs={{0,1},{2,3},{1,0},{3,2},{4,5},{6,7},{5,4},{7,6},{8,9},{10,11},{9,8... | collective-permute-start | bytes 417800 | tf_op jit(solution)/shard_map/ppermute | solution.py:550
  13.9 7.8 %collective-permute-start.6 = (bf16[34,16,128]{2,1,0:T(8,128)(2,1)S(1)}, bf16[34,16,128]{2,1,0:T(8,128)(2,1)S(1)}, u32[]{:S(2)}, u32[]{:S(2)}) collective-permute-start(bf16[34,16,128]{2,1,0:T(8,128)(2,1)S(1)} %get-tuple-element.59), channel_id=1, source_target_pairs={{1,2},{2,1},{0,4},{3,7},{5,6},{6,5},{4,0},{7,3},{9,10},{10,9},{8,1... | collective-permute-start | bytes 417800 | tf_op jit(solution)/shard_map/ppermute | solution.py:550
  14.8 6.8 %collective-permute-start.7 = (bf16[46,8,128]{2,1,0:T(8,128)(2,1)S(1)}, bf16[46,8,128]{2,1,0:T(8,128)(2,1)S(1)}, u32[]{:S(2)}, u32[]{:S(2)}) collective-permute-start(bf16[46,8,128]{2,1,0:T(8,128)(2,1)S(1)} %get-tuple-element.60), channel_id=1, source_target_pairs={{0,1},{2,3},{1,0},{3,2},{4,5},{6,7},{5,4},{7,6},{8,9},{10,11},{9,8... | collective-permute-start | bytes 282632 | tf_op jit(solution)/shard_map/ppermute | solution.py:550
  17.9 3.8 %collective-permute-start.8 = (bf16[46,8,128]{2,1,0:T(8,128)(2,1)S(1)}, bf16[46,8,128]{2,1,0:T(8,128)(2,1)S(1)}, u32[]{:S(2)}, u32[]{:S(2)}) collective-permute-start(bf16[46,8,128]{2,1,0:T(8,128)(2,1)S(1)} %get-tuple-element.61), channel_id=1, source_target_pairs={{1,2},{2,1},{0,4},{3,7},{5,6},{6,5},{4,0},{7,3},{9,10},{10,9},{8,1... | collective-permute-start | bytes 282632 | tf_op jit(solution)/shard_map/ppermute | solution.py:550
  27.6 1.8 %collective-permute-start.9 = (bf16[4,272,128]{2,1,0:T(8,128)(2,1)S(1)}, bf16[4,272,128]{2,1,0:T(8,128)(2,1)S(1)}, u32[]{:S(2)}, u32[]{:S(2)}) collective-permute-start(bf16[4,272,128]{2,1,0:T(8,128)(2,1)S(1)} %get-tuple-element.65), channel_id=1, source_target_pairs={{0,4},{4,0},{8,12},{12,8},{16,20},{20,16},{24,28},{28,24},{1,5},{5... | collective-permute-start | bytes 835592 | tf_op jit(solution)/shard_map/ppermute | solution.py:603
  29.4 4.8 %collective-permute-start.10 = (bf16[272,128]{1,0:T(8,128)(2,1)S(1)}, bf16[272,128]{1,0:T(8,128)(2,1)S(1)}, u32[]{:S(2)}, u32[]{:S(2)}) collective-permute-start(bf16[272,128]{1,0:T(8,128)(2,1)S(1)} %get-tuple-element.70), channel_id=1, source_target_pairs={{0,8},{4,12},{8,0},{12,4},{16,24},{20,28},{24,16},{28,20},{1,9},{5... | collective-permute-start | bytes 208904 | tf_op jit(solution)/shard_map/ppermute | solution.py:600
  29.6 4.6 %collective-permute-start.12 = (bf16[272,128]{1,0:T(8,128)(2,1)S(1)}, bf16[272,128]{1,0:T(8,128)(2,1)S(1)}, u32[]{:S(2)}, u32[]{:S(2)}) collective-permute-start(bf16[272,128]{1,0:T(8,128)(2,1)S(1)} %get-tuple-element.71), channel_id=1, source_target_pairs={{0,16},{4,20},{8,24},{12,28},{16,0},{20,4},{24,8},{28,12},{1,17},{... | collective-permute-start | bytes 208904 | tf_op jit(solution)/shard_map/ppermute | solution.py:600
  31.1 5.3 %collective-permute-start.11 = (bf16[272,128]{1,0:T(8,128)(2,1)S(1)}, bf16[272,128]{1,0:T(8,128)(2,1)S(1)}, u32[]{:S(2)}, u32[]{:S(2)}) collective-permute-start(bf16[272,128]{1,0:T(8,128)(2,1)S(1)} %get-tuple-element.72), channel_id=1, source_target_pairs={{0,24},{4,28},{8,16},{12,20},{16,8},{20,12},{24,0},{28,4},{1,25},{... | collective-permute-start | bytes 208904 | tf_op jit(solution)/shard_map/ppermute | solution.py:600
  36.4 7.0 %collective-permute-start.15 = (bf16[272,128]{1,0:T(8,128)(2,1)S(1)}, bf16[272,128]{1,0:T(8,128)(2,1)S(1)}, u32[]{:S(2)}, u32[]{:S(2)}) collective-permute-start(bf16[272,128]{1,0:T(8,128)(2,1)S(1)} %fusion.2), channel_id=1, source_target_pairs={{0,3},{1,2},{2,1},{3,0},{4,7},{5,6},{6,5},{7,4},{8,11},{9,10},{10,... | collective-permute-start | bytes 208904 | tf_op jit(solution)/shard_map/ppermute | solution.py:606
  38.3 6.9 %collective-permute-start.14 = (bf16[272,128]{1,0:T(8,128)(2,1)S(1)}, bf16[272,128]{1,0:T(8,128)(2,1)S(1)}, u32[]{:S(2)}, u32[]{:S(2)}) collective-permute-start(bf16[272,128]{1,0:T(8,128)(2,1)S(1)} %fusion.2), channel_id=1, source_target_pairs={{0,2},{1,3},{2,0},{3,1},{4,6},{5,7},{6,4},{7,5},{8,10},{9,11},{10,... | collective-permute-start | bytes 208904 | tf_op jit(solution)/shard_map/ppermute | solution.py:606
  40.2 5.1 %collective-permute-start.13 = (bf16[272,128]{1,0:T(8,128)(2,1)S(1)}, bf16[272,128]{1,0:T(8,128)(2,1)S(1)}, u32[]{:S(2)}, u32[]{:S(2)}) collective-permute-start(bf16[272,128]{1,0:T(8,128)(2,1)S(1)} %fusion.2), channel_id=1, source_target_pairs={{0,1},{1,0},{2,3},{3,2},{4,5},{5,4},{6,7},{7,6},{8,9},{9,8},{10,11... | collective-permute-start | bytes 208904 | tf_op jit(solution)/shard_map/ppermute | solution.py:606
  45.3 4.4 %collective-permute-start.18 = (bf16[272,128]{1,0:T(8,128)(2,1)S(1)}, bf16[272,128]{1,0:T(8,128)(2,1)S(1)}, u32[]{:S(2)}, u32[]{:S(2)}) collective-permute-start(bf16[272,128]{1,0:T(8,128)(2,1)S(1)} %add_convert_fusion), channel_id=1, source_target_pairs={{0,8},{4,12},{8,0},{12,4},{16,24},{20,28},{24,16},{28,20},{1,9},{5... | collective-permute-start | bytes 208904 | tf_op jit(solution)/shard_map/ppermute | solution.py:600
  46.5 4.3 %collective-permute-start.17 = (bf16[272,128]{1,0:T(8,128)(2,1)S(1)}, bf16[272,128]{1,0:T(8,128)(2,1)S(1)}, u32[]{:S(2)}, u32[]{:S(2)}) collective-permute-start(bf16[272,128]{1,0:T(8,128)(2,1)S(1)} %add_convert_fusion), channel_id=1, source_target_pairs={{0,16},{4,20},{8,24},{12,28},{16,0},{20,4},{24,8},{28,12},{1,17},{... | collective-permute-start | bytes 208904 | tf_op jit(solution)/shard_map/ppermute | solution.py:600
  47.4 5.2 %collective-permute-start.16 = (bf16[272,128]{1,0:T(8,128)(2,1)S(1)}, bf16[272,128]{1,0:T(8,128)(2,1)S(1)}, u32[]{:S(2)}, u32[]{:S(2)}) collective-permute-start(bf16[272,128]{1,0:T(8,128)(2,1)S(1)} %add_convert_fusion), channel_id=1, source_target_pairs={{0,24},{4,28},{8,16},{12,20},{16,8},{20,12},{24,0},{28,4},{1,25},{... | collective-permute-start | bytes 208904 | tf_op jit(solution)/shard_map/ppermute | solution.py:600
  52.6 1.6 %collective-permute-start.19 = (bf16[4,272,128]{2,1,0:T(8,128)(2,1)S(1)}, bf16[4,272,128]{2,1,0:T(8,128)(2,1)S(1)}, u32[]{:S(2)}, u32[]{:S(2)}) collective-permute-start(bf16[4,272,128]{2,1,0:T(8,128)(2,1)S(1)} %pad_maximum_fusion.keep_ref), channel_id=1, source_target_pairs={{0,4},{4,0},{8,12},{12,8},{16,20},{20,16},{24,28},{28,24},{1,5},{5... | collective-permute-start | bytes 835592 | tf_op jit(solution)/shard_map/ppermute | solution.py:603

commit v10 on v9

--- a/solution.py
+++ b/solution.py
@@ -1,3 +1,5 @@
+import functools
+
 import jax
 import jax.numpy as jnp
 from jax import lax
@@ -70,16 +72,24 @@
     planes, high, width = vol_ref.shape
     cots = cot_ref.shape[0]
 
-    def plane(d, carry):
-        for m in range(width // LANES):
-            lanes = slice(m * LANES, (m + 1) * LANES)
-            block = vol_ref[d, :, lanes].astype(F32)
-            low, top = block[:4], block[high - 4 :]
-            row_a_ref[d, :, lanes] = jnp.where(row_even, top, low).astype(BF16)
-            row_b_ref[d, :, lanes] = jnp.where(row_inner, jnp.where(row_even, low, top), 0.0).astype(BF16)
-        return carry
-
-    lax.fori_loop(0, planes, plane, 0, unroll=4)
+    def run(even, inner):
+        def plane(d, carry):
+            for m in range(width // LANES):
+                lanes = slice(m * LANES, (m + 1) * LANES)
+                low, top = vol_ref[d, :4, lanes], vol_ref[d, high - 4 :, lanes]
+                row_a_ref[d, :, lanes] = top if even else low
+                if inner:
+                    row_b_ref[d, :, lanes] = low if even else top
+                else:
+                    row_b_ref[d, :, lanes] = jnp.zeros_like(low)
+            return carry
+
+        lax.fori_loop(0, planes, plane, 0, unroll=4)
+
+    for even in (True, False):
+        for inner in (True, False):
+            here = jnp.logical_and(row_even == even, row_inner == inner)
+            pl.when(here)(functools.partial(run, even, inner))
     for g in range(cots // 4):
         tops = jnp.concatenate([cot_ref[4 * g + n].astype(F32)[:1] for n in range(4)], axis=0)
         row_a_ref[planes + g] = tops.astype(BF16)
@@ -194,38 +204,42 @@
     blocks = vol_ref.shape[2] // LANES
     clear_stage(stage)
 
-    def place(n, target, own, a, b, keep):
-        def kept(values):
-            return values if keep is None else jnp.where(keep, values, 0.0)
-
-        for m in range(blocks):
-            lanes = slice(m * LANES, (m + 1) * LANES)
-            stage[n, m, 8:24, :] = kept(own(lanes).astype(F32))
-            stage[n, m, 4:8, :] = kept(behind(row_even, a(lanes), b(lanes)))
-            stage[n, m, 24:28, :] = kept(ahead(row_even, a(lanes), b(lanes)))
-        split_rows(stage.at[n], tiles, target, range(blocks))
-
-    def place_own(group, carry):
-        for n in range(4):
-            d = 4 * group + n
+    def run(even):
+        def place(n, target, own, a, b, keep):
+            def kept(values):
+                return values if keep is None else jnp.where(keep, values, 0.0)
+
+            for m in range(blocks):
+                lanes = slice(m * LANES, (m + 1) * LANES)
+                stage[n, m, 8:24, :] = kept(own(lanes).astype(F32))
+                stage[n, m, 4:8, :] = kept((b if even else a)(lanes).astype(F32))
+                stage[n, m, 24:28, :] = kept((a if even else b)(lanes).astype(F32))
+            split_rows(stage.at[n], tiles, target, range(blocks))
+
+        def place_own(group, carry):
+            for n in range(4):
+                d = 4 * group + n
+                place(
+                    n, d + 3, lambda lanes: vol_ref[d, :, lanes],
+                    lambda lanes: row_a_ref[d, :, lanes], lambda lanes: row_b_ref[d, :, lanes], None,
+                )
+            return carry
+
+        def place_halo(target, q, keep):
             place(
-                n, d + 3, lambda lanes: vol_ref[d, :, lanes],
-                lambda lanes: row_a_ref[d, :, lanes], lambda lanes: row_b_ref[d, :, lanes], None,
+                target % 4, target,
+                lambda lanes: jnp.concatenate([dep_ref[4 * q + g, :, lanes].astype(F32) for g in range(4)], axis=0),
+                lambda lanes: edge_a_ref[q, :, lanes], lambda lanes: edge_b_ref[q, :, lanes], keep,
             )
-        return carry
-
-    def place_halo(target, q, keep):
-        place(
-            target % 4, target,
-            lambda lanes: jnp.concatenate([dep_ref[4 * q + g, :, lanes].astype(F32) for g in range(4)], axis=0),
-            lambda lanes: edge_a_ref[q, :, lanes], lambda lanes: edge_b_ref[q, :, lanes], keep,
-        )
-
-    lax.fori_loop(0, planes // 4, place_own, 0)
-    for q in range(3):
-        place_halo(q, q + 1, jnp.logical_not(first_plane))
-    for q in range(4):
-        place_halo(planes + 3 + q, q, first_plane)
+
+        lax.fori_loop(0, planes // 4, place_own, 0)
+        for q in range(3):
+            place_halo(q, q + 1, jnp.logical_not(first_plane))
+        for q in range(4):
+            place_halo(planes + 3 + q, q, first_plane)
+
+    for even in (True, False):
+        pl.when(row_even == even)(functools.partial(run, even))
     tiles[:, planes + 7 :] = jnp.zeros((3, 2, blocks, 16, LANES), BF16)
 
     group = 5
@@ -257,34 +271,39 @@
 
     clear_stage(stage)
 
-    def place(n, target, source, side_a, side_b, keep):
-        for m, choose in ((0, behind), (1, ahead)):
-            corners = choose(col_even, col_a_ref[source], col_b_ref[source])
-            own = choose(col_even, side_a, side_b)
-            if keep is not None:
-                corners, own = jnp.where(keep, corners, 0.0), jnp.where(keep, own, 0.0)
-            stage[n, m, 4:8, :] = corners[:4]
-            stage[n, m, 8:24, :] = own
-            stage[n, m, 24:28, :] = corners[4:]
-        split_rows(stage.at[n], rim_tiles, target, range(2))
-
-    def place_own(group, carry):
-        for n in range(4):
-            d = 4 * group + n
-            place(n, d + 3, d, side_a_ref[d], side_b_ref[d], None)
-        return carry
-
-    def place_halo(target, q, keep):
-        start = planes + 4 + 2 * q
-        side_a = jnp.concatenate([col_a_ref[start].astype(F32), col_a_ref[start + 1].astype(F32)], axis=0)
-        side_b = jnp.concatenate([col_b_ref[start].astype(F32), col_b_ref[start + 1].astype(F32)], axis=0)
-        place(target % 4, target, planes + q, side_a, side_b, keep)
-
-    lax.fori_loop(0, planes // 4, place_own, 0, unroll=2)
-    for q in range(3):
-        place_halo(q, q + 1, jnp.logical_not(first_plane))
-    for q in range(4):
-        place_halo(planes + 3 + q, q, first_plane)
+    def run(even):
+        def place(n, target, source, side_a, side_b, keep):
+            for m in range(2):
+                first = even == (m == 1)
+                corners = (col_a_ref if first else col_b_ref)[source].astype(F32)
+                own = (side_a if first else side_b).astype(F32)
+                if keep is not None:
+                    corners, own = jnp.where(keep, corners, 0.0), jnp.where(keep, own, 0.0)
+                stage[n, m, 4:8, :] = corners[:4]
+                stage[n, m, 8:24, :] = own
+                stage[n, m, 24:28, :] = corners[4:]
+            split_rows(stage.at[n], rim_tiles, target, range(2))
+
+        def place_own(group, carry):
+            for n in range(4):
+                d = 4 * group + n
+                place(n, d + 3, d, side_a_ref[d], side_b_ref[d], None)
+            return carry
+
+        def place_halo(target, q, keep):
+            start = planes + 4 + 2 * q
+            side_a = jnp.concatenate([col_a_ref[start].astype(F32), col_a_ref[start + 1].astype(F32)], axis=0)
+            side_b = jnp.concatenate([col_b_ref[start].astype(F32), col_b_ref[start + 1].astype(F32)], axis=0)
+            place(target % 4, target, planes + q, side_a, side_b, keep)
+
+        lax.fori_loop(0, planes // 4, place_own, 0, unroll=2)
+        for q in range(3):
+            place_halo(q, q + 1, jnp.logical_not(first_plane))
+        for q in range(4):
+            place_halo(planes + 3 + q, q, first_plane)
+
+    for even in (True, False):
+        pl.when(col_even == even)(functools.partial(run, even))
 
     taps = []
     for a in range(3):

time: 56 us -> 55.9 us (level)
  no operation moved by 1% of the time
where the time goes in v10:
time: 55.9 us; the launch traced here: 55.8 us
  starting transfers between devices  23.7 us (42%)
  Pallas kernels  16 us (29%)
  waiting for transfers between devices  14.7 us (26%)
  between operations  0.87 us (2%)
    ppermute x6, starting transfers between devices, to_square(): return lax.ppermute(block, ('depth', 'row'), route)  7.12 us
    ppermute x6, waiting for transfers between devices, to_square(): return lax.ppermute(block, ('depth', 'row'), route)  7.11 us
    pallas_call x1, Pallas kernels, local_grads(): pl.pallas_call(body, out_shape=[jax.ShapeDtypeStruct((squares, rows // (2...  5.85 us
    ppermute x4, starting transfers between devices, to_col(): return lax.ppermute(block, ('row', 'col'), pairs_of_lines(rows, cols, kind))  4.86 us
    ppermute x3, starting transfers between devices, along_col(): return lax.ppermute(block, 'col', [(i, i ^ n) for i in range(cols)])  4.45 us
    ppermute x3, waiting for transfers between devices, along_col(): return lax.ppermute(block, 'col', [(i, i ^ n) for i in range(cols)])  4.36 us
    pallas_call x1, Pallas kernels, local_grads(): pl.pallas_call(own_blocks, out_shape=[jax.ShapeDtypeStruct((3, planes + 9...  3.69 us
    ppermute x1, starting transfers between devices, shards(): dep = lax.ppermute(dep, 'depth', [(0, 1), (1, 0)])  3.03 us
  transfers between devices with their start and end apart: 20, of which 10 were waited for; matrix products, arithmetic and copies ran while one was open for 0% of the time, Pallas kernels for 12%

profile of v10, /device:TPU:0, one launch (start us, length us, event | category | flops | bytes accessed | tf_op | source)
XLA Modules:
  0.0 55.8 jit_solution(3069011454461592481)
XLA Ops:
  0.7 2.0 %shard_map.59 = (bf16[32,16,1024]{2,1,0:T(8,128)(2,1)S(1)}, bf16[8,4,1024]{2,1,0:T(4,128)(2,1)S(1)}, bf16[64,864]{1,0:T(8,128)(2,1)S(1)}, bf16[1728,128]{1,0:T(8,128)(2,1)S(1)}, bf16[17,4,1024]{2,1,0:T(4,128)(2,1)S(1)}) custom-call(s32[5]{0:T(128)S(1)} %stack.58.flag_ref, bf16[32,16,1024]{2,1,0:T(8,128)(2,1)} %vol_hbm.1, bf16[8,4,1024]{2,1,0:T(4,128)(2,1)} %cot_hbm.1, ...), custom_call_target="tpu_custom_call" | custom-call | tf_op jit(solution)/shard_map/pallas_call | solution.py:552
  2.8 3.0 %collective-permute-start.1 = (bf16[17,4,1024]{2,1,0:T(4,128)(2,1)S(1)}, bf16[17,4,1024]{2,1,0:T(4,128)(2,1)S(1)}, u32[]{:S(2)}, u32[]{:S(2)}) collective-permute-start(bf16[17,4,1024]{2,1,0:T(4,128)(2,1)S(1)} %get-tuple-element.38), channel_id=1, source_target_pairs={{0,16},{16,0},{1,17},{17,1},{2,18},{18,2},{3,19},{19,3},{4,20},{20... | collective-permute-start | bytes 417800 | tf_op jit(solution)/shard_map/ppermute | solution.py:571
  6.7 1.6 %collective-permute-start = (bf16[34,4,1024]{2,1,0:T(4,128)(2,1)S(1)}, bf16[34,4,1024]{2,1,0:T(4,128)(2,1)S(1)}, u32[]{:S(2)}, u32[]{:S(2)}) collective-permute-start(bf16[34,4,1024]{2,1,0:T(4,128)(2,1)S(1)} %get-tuple-element.37), channel_id=1, source_target_pairs={{4,8},{5,9},{6,10},{7,11},{20,24},{21,25},{22,26},{23,27},{8,4},{9... | collective-permute-start | bytes 835592 | tf_op jit(solution)/shard_map/ppermute | solution.py:575
  9.7 1.8 %collective-permute-start.4 = (bf16[5,4,1024]{2,1,0:T(4,128)(2,1)S(1)}, bf16[5,4,1024]{2,1,0:T(4,128)(2,1)S(1)}, u32[]{:S(2)}, u32[]{:S(2)}) collective-permute-start(bf16[5,4,1024]{2,1,0:T(4,128)(2,1)S(1)} %get-tuple-element.77), channel_id=1, source_target_pairs={{4,8},{8,4},{0,16},{12,28},{20,24},{24,20},{16,0},{28,12},{5,9},{9... | collective-permute-start | bytes 122888 | tf_op jit(solution)/shard_map/ppermute | solution.py:592
  11.6 1.6 %collective-permute-start.5 = (bf16[34,16,128]{2,1,0:T(8,128)(2,1)S(1)}, bf16[34,16,128]{2,1,0:T(8,128)(2,1)S(1)}, u32[]{:S(2)}, u32[]{:S(2)}) collective-permute-start(bf16[34,16,128]{2,1,0:T(8,128)(2,1)S(1)} %get-tuple-element.58), channel_id=1, source_target_pairs={{0,1},{2,3},{1,0},{3,2},{4,5},{6,7},{5,4},{7,6},{8,9},{10,11},{9,8... | collective-permute-start | bytes 417800 | tf_op jit(solution)/shard_map/ppermute | solution.py:569
  14.8 3.1 %collective-permute-start.7 = (bf16[46,8,128]{2,1,0:T(8,128)(2,1)S(1)}, bf16[46,8,128]{2,1,0:T(8,128)(2,1)S(1)}, u32[]{:S(2)}, u32[]{:S(2)}) collective-permute-start(bf16[46,8,128]{2,1,0:T(8,128)(2,1)S(1)} %get-tuple-element.60), channel_id=1, source_target_pairs={{0,1},{2,3},{1,0},{3,2},{4,5},{6,7},{5,4},{7,6},{8,9},{10,11},{9,8... | collective-permute-start | bytes 282632 | tf_op jit(solution)/shard_map/ppermute | solution.py:569
  17.9 3.7 %shard_map.64 = (bf16[3,41,8,16,128]{4,3,2,1,0:T(8,128)(2,1)S(1)}, f32[20,8,16,256]{3,2,1,0:T(8,128)S(1)}) custom-call(s32[5]{0:T(128)S(1)} %stack.58.flag_ref, bf16[32,16,1024]{2,1,0:T(8,128)(2,1)S(1)} %get-tuple-element.54.vol_ref, bf16[17,4,1024]{2,1,0:T(4,128)(2,1)S(1)} %collective-permute-done.1.dep_ref, ...), custom_call_target="tpu_custom_call" | custom-call | flops 2000000000 | bytes 10000000 | tf_op jit(solution)/shard_map/pallas_call | solution.py:498
  21.6 5.8 %shard_map.65 = (f32[4,272,128]{2,1,0:T(8,128)S(1)}, bf16[4,272,128]{2,1,0:T(8,128)(2,1)S(1)}) custom-call(s32[5]{0:T(128)S(1)} %stack.58.flag_ref, s32[2]{0:T(128)S(1)} %pad_add_fusion.place_ref, bf16[3,41,8,16,128]{4,3,2,1,0:T(8,128)(2,1)S(1)} %get-tuple-element.56.tiles, f32[20,8,16,256]{3,2,1,0:T(8,128)S(1)} %get-tuple-element.57.parts, ...), custom_call_target="tpu_custom_call" | custom-call | flops 4000000000 | bytes 10000000 | tf_op jit(solution)/shard_map/pallas_call | solution.py:523
  28.0 1.2 %collective-permute-done.9 = bf16[4,272,128]{2,1,0:T(8,128)(2,1)S(1)} collective-permute-done((bf16[4,272,128]{2,1,0:T(8,128)(2,1)S(1)}, bf16[4,272,128]{2,1,0:T(8,128)(2,1)S(1)}, u32[]{:S(2)}, u32[]{:S(2)}) %collective-permute-start.9) | collective-permute-done | bytes 278560 | tf_op jit(solution)/shard_map/ppermute | solution.py:622
  29.5 1.5 %collective-permute-start.12 = (bf16[272,128]{1,0:T(8,128)(2,1)S(1)}, bf16[272,128]{1,0:T(8,128)(2,1)S(1)}, u32[]{:S(2)}, u32[]{:S(2)}) collective-permute-start(bf16[272,128]{1,0:T(8,128)(2,1)S(1)} %get-tuple-element.71), channel_id=1, source_target_pairs={{0,16},{4,20},{8,24},{12,28},{16,0},{20,4},{24,8},{28,12},{1,17},{... | collective-permute-start | bytes 208904 | tf_op jit(solution)/shard_map/ppermute | solution.py:619
  31.0 1.9 %collective-permute-start.11 = (bf16[272,128]{1,0:T(8,128)(2,1)S(1)}, bf16[272,128]{1,0:T(8,128)(2,1)S(1)}, u32[]{:S(2)}, u32[]{:S(2)}) collective-permute-start(bf16[272,128]{1,0:T(8,128)(2,1)S(1)} %get-tuple-element.72), channel_id=1, source_target_pairs={{0,24},{4,28},{8,16},{12,20},{16,8},{20,12},{24,0},{28,4},{1,25},{... | collective-permute-start | bytes 208904 | tf_op jit(solution)/shard_map/ppermute | solution.py:619
  32.9 1.2 %collective-permute-done.10 = bf16[272,128]{1,0:T(8,128)(2,1)S(1)} collective-permute-done((bf16[272,128]{1,0:T(8,128)(2,1)S(1)}, bf16[272,128]{1,0:T(8,128)(2,1)S(1)}, u32[]{:S(2)}, u32[]{:S(2)}) %collective-permute-start.10) | collective-permute-done | bytes 69664 | tf_op jit(solution)/shard_map/ppermute | solution.py:619
  34.1 2.2 %collective-permute-done.11 = bf16[272,128]{1,0:T(8,128)(2,1)S(1)} collective-permute-done((bf16[272,128]{1,0:T(8,128)(2,1)S(1)}, bf16[272,128]{1,0:T(8,128)(2,1)S(1)}, u32[]{:S(2)}, u32[]{:S(2)}) %collective-permute-start.11) | collective-permute-done | bytes 69664 | tf_op jit(solution)/shard_map/ppermute | solution.py:619
  36.4 2.0 %collective-permute-start.15 = (bf16[272,128]{1,0:T(8,128)(2,1)S(1)}, bf16[272,128]{1,0:T(8,128)(2,1)S(1)}, u32[]{:S(2)}, u32[]{:S(2)}) collective-permute-start(bf16[272,128]{1,0:T(8,128)(2,1)S(1)} %fusion.2), channel_id=1, source_target_pairs={{0,3},{1,2},{2,1},{3,0},{4,7},{5,6},{6,5},{7,4},{8,11},{9,10},{10,... | collective-permute-start | bytes 208904 | tf_op jit(solution)/shard_map/ppermute | solution.py:625
  38.3 1.8 %collective-permute-start.14 = (bf16[272,128]{1,0:T(8,128)(2,1)S(1)}, bf16[272,128]{1,0:T(8,128)(2,1)S(1)}, u32[]{:S(2)}, u32[]{:S(2)}) collective-permute-start(bf16[272,128]{1,0:T(8,128)(2,1)S(1)} %fusion.2), channel_id=1, source_target_pairs={{0,2},{1,3},{2,0},{3,1},{4,6},{5,7},{6,4},{7,5},{8,10},{9,11},{10,... | collective-permute-start | bytes 208904 | tf_op jit(solution)/shard_map/ppermute | solution.py:625
  40.8 2.5 %collective-permute-done.15 = bf16[272,128]{1,0:T(8,128)(2,1)S(1)} collective-permute-done((bf16[272,128]{1,0:T(8,128)(2,1)S(1)}, bf16[272,128]{1,0:T(8,128)(2,1)S(1)}, u32[]{:S(2)}, u32[]{:S(2)}) %collective-permute-start.15) | collective-permute-done | bytes 69664 | tf_op jit(solution)/shard_map/ppermute | solution.py:625
  43.3 1.9 %collective-permute-done.14 = bf16[272,128]{1,0:T(8,128)(2,1)S(1)} collective-permute-done((bf16[272,128]{1,0:T(8,128)(2,1)S(1)}, bf16[272,128]{1,0:T(8,128)(2,1)S(1)}, u32[]{:S(2)}, u32[]{:S(2)}) %collective-permute-start.14) | collective-permute-done | bytes 69664 | tf_op jit(solution)/shard_map/ppermute | solution.py:625
  45.2 1.3 %collective-permute-start.18 = (bf16[272,128]{1,0:T(8,128)(2,1)S(1)}, bf16[272,128]{1,0:T(8,128)(2,1)S(1)}, u32[]{:S(2)}, u32[]{:S(2)}) collective-permute-start(bf16[272,128]{1,0:T(8,128)(2,1)S(1)} %add_convert_fusion), channel_id=1, source_target_pairs={{0,8},{4,12},{8,0},{12,4},{16,24},{20,28},{24,16},{28,20},{1,9},{5... | collective-permute-start | bytes 208904 | tf_op jit(solution)/shard_map/ppermute | solution.py:619
  47.3 1.5 %collective-permute-start.16 = (bf16[272,128]{1,0:T(8,128)(2,1)S(1)}, bf16[272,128]{1,0:T(8,128)(2,1)S(1)}, u32[]{:S(2)}, u32[]{:S(2)}) collective-permute-start(bf16[272,128]{1,0:T(8,128)(2,1)S(1)} %add_convert_fusion), channel_id=1, source_target_pairs={{0,24},{4,28},{8,16},{12,20},{16,8},{20,12},{24,0},{28,4},{1,25},{... | collective-permute-start | bytes 208904 | tf_op jit(solution)/shard_map/ppermute | solution.py:619
  48.8 0.8 %collective-permute-done.18 = bf16[272,128]{1,0:T(8,128)(2,1)S(1)} collective-permute-done((bf16[272,128]{1,0:T(8,128)(2,1)S(1)}, bf16[272,128]{1,0:T(8,128)(2,1)S(1)}, u32[]{:S(2)}, u32[]{:S(2)}) %collective-permute-start.18) | collective-permute-done | bytes 69664 | tf_op jit(solution)/shard_map/ppermute | solution.py:619
  49.6 1.2 %collective-permute-done.17 = bf16[272,128]{1,0:T(8,128)(2,1)S(1)} collective-permute-done((bf16[272,128]{1,0:T(8,128)(2,1)S(1)}, bf16[272,128]{1,0:T(8,128)(2,1)S(1)}, u32[]{:S(2)}, u32[]{:S(2)}) %collective-permute-start.17) | collective-permute-done | bytes 69664 | tf_op jit(solution)/shard_map/ppermute | solution.py:619
  50.8 1.7 %collective-permute-done.16 = bf16[272,128]{1,0:T(8,128)(2,1)S(1)} collective-permute-done((bf16[272,128]{1,0:T(8,128)(2,1)S(1)}, bf16[272,128]{1,0:T(8,128)(2,1)S(1)}, u32[]{:S(2)}, u32[]{:S(2)}) %collective-permute-start.16) | collective-permute-done | bytes 69664 | tf_op jit(solution)/shard_map/ppermute | solution.py:619
  52.6 1.5 %collective-permute-done.19.got_ref = bf16[4,272,128]{2,1,0:T(8,128)(2,1)S(1)} collective-permute-done((bf16[4,272,128]{2,1,0:T(8,128)(2,1)S(1)}, bf16[4,272,128]{2,1,0:T(8,128)(2,1)S(1)}, u32[]{:S(2)}, u32[]{:S(2)}) %collective-permute-start.19) | collective-permute-done | bytes 278560 | tf_op jit(solution)/shard_map/ppermute | solution.py:622
  54.1 1.6 %shard_map.66 = (f32[64,864]{1,0:T(8,128)}, f32[1728,128]{1,0:T(8,128)}) custom-call(s32[2]{0:T(128)S(1)} %pad_add_fusion.place_ref, bf16[4,272,128]{2,1,0:T(8,128)(2,1)S(1)} %pad_maximum_fusion.keep_ref, bf16[4,272,128]{2,1,0:T(8,128)(2,1)S(1)} %collective-permute-done.19.got_ref), custom_call_target="tpu_custom_call" | custom-call | tf_op jit(solution)/shard_map/pallas_call | solution.py:635
  (38 shorter events, 6.5 us)
Async XLA Ops:
  2.8 6.7 %collective-permute-start.1 = (bf16[17,4,1024]{2,1,0:T(4,128)(2,1)S(1)}, bf16[17,4,1024]{2,1,0:T(4,128)(2,1)S(1)}, u32[]{:S(2)}, u32[]{:S(2)}) collective-permute-start(bf16[17,4,1024]{2,1,0:T(4,128)(2,1)S(1)} %get-tuple-element.38), channel_id=1, source_target_pairs={{0,16},{16,0},{1,17},{17,1},{2,18},{18,2},{3,19},{19,3},{4,20},{20... | collective-permute-start | bytes 417800 | tf_op jit(solution)/shard_map/ppermute | solution.py:571
  6.7 7.4 %collective-permute-start = (bf16[34,4,1024]{2,1,0:T(4,128)(2,1)S(1)}, bf16[34,4,1024]{2,1,0:T(4,128)(2,1)S(1)}, u32[]{:S(2)}, u32[]{:S(2)}) collective-permute-start(bf16[34,4,1024]{2,1,0:T(4,128)(2,1)S(1)} %get-tuple-element.37), channel_id=1, source_target_pairs={{4,8},{5,9},{6,10},{7,11},{20,24},{21,25},{22,26},{23,27},{8,4},{9... | collective-permute-start | bytes 835592 | tf_op jit(solution)/shard_map/ppermute | solution.py:575
  8.3 5.6 %collective-permute-start.2 = (bf16[34,4,1024]{2,1,0:T(4,128)(2,1)S(1)}, bf16[34,4,1024]{2,1,0:T(4,128)(2,1)S(1)}, u32[]{:S(2)}, u32[]{:S(2)}) collective-permute-start(bf16[34,4,1024]{2,1,0:T(4,128)(2,1)S(1)} %get-tuple-element.48), channel_id=1, source_target_pairs={{0,4},{8,12},{4,0},{12,8},{1,5},{9,13},{5,1},{13,9},{2,6},{10,14},... | collective-permute-start | bytes 835592 | tf_op jit(solution)/shard_map/ppermute | solution.py:576
  9.7 4.4 %collective-permute-start.4 = (bf16[5,4,1024]{2,1,0:T(4,128)(2,1)S(1)}, bf16[5,4,1024]{2,1,0:T(4,128)(2,1)S(1)}, u32[]{:S(2)}, u32[]{:S(2)}) collective-permute-start(bf16[5,4,1024]{2,1,0:T(4,128)(2,1)S(1)} %get-tuple-element.77), channel_id=1, source_target_pairs={{4,8},{8,4},{0,16},{12,28},{20,24},{24,20},{16,0},{28,12},{5,9},{9... | collective-permute-start | bytes 122888 | tf_op jit(solution)/shard_map/ppermute | solution.py:592
  11.5 2.6 %collective-permute-start.3 = (bf16[5,4,1024]{2,1,0:T(4,128)(2,1)S(1)}, bf16[5,4,1024]{2,1,0:T(4,128)(2,1)S(1)}, u32[]{:S(2)}, u32[]{:S(2)}) collective-permute-start(bf16[5,4,1024]{2,1,0:T(4,128)(2,1)S(1)} %get-tuple-element.78), channel_id=1, source_target_pairs={{0,4},{8,12},{4,0},{12,8},{1,5},{9,13},{5,1},{13,9},{2,6},{10,14},... | collective-permute-start | bytes 122888 | tf_op jit(solution)/shard_map/ppermute | solution.py:591
  11.6 9.9 %collective-permute-start.5 = (bf16[34,16,128]{2,1,0:T(8,128)(2,1)S(1)}, bf16[34,16,128]{2,1,0:T(8,128)(2,1)S(1)}, u32[]{:S(2)}, u32[]{:S(2)}) collective-permute-start(bf16[34,16,128]{2,1,0:T(8,128)(2,1)S(1)} %get-tuple-element.58), channel_id=1, source_target_pairs={{0,1},{2,3},{1,0},{3,2},{4,5},{6,7},{5,4},{7,6},{8,9},{10,11},{9,8... | collective-permute-start | bytes 417800 | tf_op jit(solution)/shard_map/ppermute | solution.py:569
  13.9 7.7 %collective-permute-start.6 = (bf16[34,16,128]{2,1,0:T(8,128)(2,1)S(1)}, bf16[34,16,128]{2,1,0:T(8,128)(2,1)S(1)}, u32[]{:S(2)}, u32[]{:S(2)}) collective-permute-start(bf16[34,16,128]{2,1,0:T(8,128)(2,1)S(1)} %get-tuple-element.59), channel_id=1, source_target_pairs={{1,2},{2,1},{0,4},{3,7},{5,6},{6,5},{4,0},{7,3},{9,10},{10,9},{8,1... | collective-permute-start | bytes 417800 | tf_op jit(solution)/shard_map/ppermute | solution.py:569
  14.8 6.8 %collective-permute-start.7 = (bf16[46,8,128]{2,1,0:T(8,128)(2,1)S(1)}, bf16[46,8,128]{2,1,0:T(8,128)(2,1)S(1)}, u32[]{:S(2)}, u32[]{:S(2)}) collective-permute-start(bf16[46,8,128]{2,1,0:T(8,128)(2,1)S(1)} %get-tuple-element.60), channel_id=1, source_target_pairs={{0,1},{2,3},{1,0},{3,2},{4,5},{6,7},{5,4},{7,6},{8,9},{10,11},{9,8... | collective-permute-start | bytes 282632 | tf_op jit(solution)/shard_map/ppermute | solution.py:569
  17.9 3.7 %collective-permute-start.8 = (bf16[46,8,128]{2,1,0:T(8,128)(2,1)S(1)}, bf16[46,8,128]{2,1,0:T(8,128)(2,1)S(1)}, u32[]{:S(2)}, u32[]{:S(2)}) collective-permute-start(bf16[46,8,128]{2,1,0:T(8,128)(2,1)S(1)} %get-tuple-element.61), channel_id=1, source_target_pairs={{1,2},{2,1},{0,4},{3,7},{5,6},{6,5},{4,0},{7,3},{9,10},{10,9},{8,1... | collective-permute-start | bytes 282632 | tf_op jit(solution)/shard_map/ppermute | solution.py:569
  27.5 1.8 %collective-permute-start.9 = (bf16[4,272,128]{2,1,0:T(8,128)(2,1)S(1)}, bf16[4,272,128]{2,1,0:T(8,128)(2,1)S(1)}, u32[]{:S(2)}, u32[]{:S(2)}) collective-permute-start(bf16[4,272,128]{2,1,0:T(8,128)(2,1)S(1)} %get-tuple-element.65), channel_id=1, source_target_pairs={{0,4},{4,0},{8,12},{12,8},{16,20},{20,16},{24,28},{28,24},{1,5},{5... | collective-permute-start | bytes 835592 | tf_op jit(solution)/shard_map/ppermute | solution.py:622
  29.3 4.8 %collective-permute-start.10 = (bf16[272,128]{1,0:T(8,128)(2,1)S(1)}, bf16[272,128]{1,0:T(8,128)(2,1)S(1)}, u32[]{:S(2)}, u32[]{:S(2)}) collective-permute-start(bf16[272,128]{1,0:T(8,128)(2,1)S(1)} %get-tuple-element.70), channel_id=1, source_target_pairs={{0,8},{4,12},{8,0},{12,4},{16,24},{20,28},{24,16},{28,20},{1,9},{5... | collective-permute-start | bytes 208904 | tf_op jit(solution)/shard_map/ppermute | solution.py:619
  29.5 4.6 %collective-permute-start.12 = (bf16[272,128]{1,0:T(8,128)(2,1)S(1)}, bf16[272,128]{1,0:T(8,128)(2,1)S(1)}, u32[]{:S(2)}, u32[]{:S(2)}) collective-permute-start(bf16[272,128]{1,0:T(8,128)(2,1)S(1)} %get-tuple-element.71), channel_id=1, source_target_pairs={{0,16},{4,20},{8,24},{12,28},{16,0},{20,4},{24,8},{28,12},{1,17},{... | collective-permute-start | bytes 208904 | tf_op jit(solution)/shard_map/ppermute | solution.py:619
  31.0 5.3 %collective-permute-start.11 = (bf16[272,128]{1,0:T(8,128)(2,1)S(1)}, bf16[272,128]{1,0:T(8,128)(2,1)S(1)}, u32[]{:S(2)}, u32[]{:S(2)}) collective-permute-start(bf16[272,128]{1,0:T(8,128)(2,1)S(1)} %get-tuple-element.72), channel_id=1, source_target_pairs={{0,24},{4,28},{8,16},{12,20},{16,8},{20,12},{24,0},{28,4},{1,25},{... | collective-permute-start | bytes 208904 | tf_op jit(solution)/shard_map/ppermute | solution.py:619
  36.4 7.0 %collective-permute-start.15 = (bf16[272,128]{1,0:T(8,128)(2,1)S(1)}, bf16[272,128]{1,0:T(8,128)(2,1)S(1)}, u32[]{:S(2)}, u32[]{:S(2)}) collective-permute-start(bf16[272,128]{1,0:T(8,128)(2,1)S(1)} %fusion.2), channel_id=1, source_target_pairs={{0,3},{1,2},{2,1},{3,0},{4,7},{5,6},{6,5},{7,4},{8,11},{9,10},{10,... | collective-permute-start | bytes 208904 | tf_op jit(solution)/shard_map/ppermute | solution.py:625
  38.3 6.9 %collective-permute-start.14 = (bf16[272,128]{1,0:T(8,128)(2,1)S(1)}, bf16[272,128]{1,0:T(8,128)(2,1)S(1)}, u32[]{:S(2)}, u32[]{:S(2)}) collective-permute-start(bf16[272,128]{1,0:T(8,128)(2,1)S(1)} %fusion.2), channel_id=1, source_target_pairs={{0,2},{1,3},{2,0},{3,1},{4,6},{5,7},{6,4},{7,5},{8,10},{9,11},{10,... | collective-permute-start | bytes 208904 | tf_op jit(solution)/shard_map/ppermute | solution.py:625
  40.1 5.1 %collective-permute-start.13 = (bf16[272,128]{1,0:T(8,128)(2,1)S(1)}, bf16[272,128]{1,0:T(8,128)(2,1)S(1)}, u32[]{:S(2)}, u32[]{:S(2)}) collective-permute-start(bf16[272,128]{1,0:T(8,128)(2,1)S(1)} %fusion.2), channel_id=1, source_target_pairs={{0,1},{1,0},{2,3},{3,2},{4,5},{5,4},{6,7},{7,6},{8,9},{9,8},{10,11... | collective-permute-start | bytes 208904 | tf_op jit(solution)/shard_map/ppermute | solution.py:625
  45.2 4.4 %collective-permute-start.18 = (bf16[272,128]{1,0:T(8,128)(2,1)S(1)}, bf16[272,128]{1,0:T(8,128)(2,1)S(1)}, u32[]{:S(2)}, u32[]{:S(2)}) collective-permute-start(bf16[272,128]{1,0:T(8,128)(2,1)S(1)} %add_convert_fusion), channel_id=1, source_target_pairs={{0,8},{4,12},{8,0},{12,4},{16,24},{20,28},{24,16},{28,20},{1,9},{5... | collective-permute-start | bytes 208904 | tf_op jit(solution)/shard_map/ppermute | solution.py:619
  46.5 4.3 %collective-permute-start.17 = (bf16[272,128]{1,0:T(8,128)(2,1)S(1)}, bf16[272,128]{1,0:T(8,128)(2,1)S(1)}, u32[]{:S(2)}, u32[]{:S(2)}) collective-permute-start(bf16[272,128]{1,0:T(8,128)(2,1)S(1)} %add_convert_fusion), channel_id=1, source_target_pairs={{0,16},{4,20},{8,24},{12,28},{16,0},{20,4},{24,8},{28,12},{1,17},{... | collective-permute-start | bytes 208904 | tf_op jit(solution)/shard_map/ppermute | solution.py:619
  47.3 5.2 %collective-permute-start.16 = (bf16[272,128]{1,0:T(8,128)(2,1)S(1)}, bf16[272,128]{1,0:T(8,128)(2,1)S(1)}, u32[]{:S(2)}, u32[]{:S(2)}) collective-permute-start(bf16[272,128]{1,0:T(8,128)(2,1)S(1)} %add_convert_fusion), channel_id=1, source_target_pairs={{0,24},{4,28},{8,16},{12,20},{16,8},{20,12},{24,0},{28,4},{1,25},{... | collective-permute-start | bytes 208904 | tf_op jit(solution)/shard_map/ppermute | solution.py:619
  52.5 1.6 %collective-permute-start.19 = (bf16[4,272,128]{2,1,0:T(8,128)(2,1)S(1)}, bf16[4,272,128]{2,1,0:T(8,128)(2,1)S(1)}, u32[]{:S(2)}, u32[]{:S(2)}) collective-permute-start(bf16[4,272,128]{2,1,0:T(8,128)(2,1)S(1)} %pad_maximum_fusion.keep_ref), channel_id=1, source_target_pairs={{0,4},{4,0},{8,12},{12,8},{16,20},{20,16},{24,28},{28,24},{1,5},{5... | collective-permute-start | bytes 835592 | tf_op jit(solution)/shard_map/ppermute | solution.py:622

commit v11 on v10

--- a/solution.py
+++ b/solution.py
@@ -232,7 +232,7 @@
                 lambda lanes: edge_a_ref[q, :, lanes], lambda lanes: edge_b_ref[q, :, lanes], keep,
             )
 
-        lax.fori_loop(0, planes // 4, place_own, 0)
+        lax.fori_loop(0, planes // 4, place_own, 0, unroll=2)
         for q in range(3):
             place_halo(q, q + 1, jnp.logical_not(first_plane))
         for q in range(4):
@@ -255,7 +255,7 @@
         parts[pl.ds(group * step, group)] = found.reshape(group, blocks, 16, 2 * LANES)
         return carry
 
-    lax.fori_loop(0, parts.shape[0] // group, product, 0)
+    lax.fori_loop(0, parts.shape[0] // group, product, 0, unroll=True)
 
 
 def body(
@@ -313,22 +313,24 @@
     found = matmul(jnp.concatenate(taps, axis=1), w1_ref[...])
     rim_parts[...] = found.reshape(hidden_planes, 2, 16, 2 * LANES)
 
-    def conv_one(i, carry):
+    def conv_one(i):
         main, prev = parts[i, :, :, :LANES], parts[i, :, :, LANES:]
         rim, rim_prev = rim_parts[i, :, :, :LANES], rim_parts[i, 0:1, :, LANES:]
         blank = jnp.zeros((1, 16, LANES), F32)
         pre = jnp.concatenate([rim[:1], main, rim[1:]], axis=0) + jnp.concatenate([blank, rim_prev, prev], axis=0)
         square = pre * pre + 1.0
         inverse = lax.rsqrt(square)
-        slopes[i] = 0.6 + 0.4 * (pre * inverse)
+        if 1 <= i <= planes // 2:
+            own = slice(1, blocks + 1)
+            slopes[i - 1] = 0.6 + 0.4 * (pre[own] * inverse[own])
         hidden = (0.6 * pre + 0.4 * (square * inverse - 1.0)).astype(BF16).astype(F32)
         odd = hidden[:, 8:, :]
         hid[0, i] = pltpu.roll(odd, 1, 1)
         hid[1, i] = hidden[:, :8, :]
         hid[2, i] = odd
-        return carry
-
-    lax.fori_loop(0, hidden_planes, conv_one, 0, unroll=True)
+
+    for i in range(hidden_planes):
+        conv_one(i)
 
     wide = (blocks + 2) * 16
 
@@ -429,7 +431,7 @@
         t, parity = i // 2, i % 2
         half = slice(0, 8) if t < quarter else slice(8, 16)
         back_one = jnp.concatenate([rows[parity][p][t % quarter, :, half, :] for p in (0, 1)], axis=1)
-        delta = back_one * slopes[i + 1, 1 : blocks + 1]
+        delta = back_one * slopes[i]
         own_list.append(jnp.where(own_rows[0], delta, 0.0).astype(BF16))
     left_one = with_next(jnp.stack(own_list, axis=1).reshape(blocks * (planes // 2) * 16, LANES), 64)
 
@@ -512,7 +514,7 @@
         pltpu.VMEM((4, 2, 40, LANES), F32),
         pltpu.VMEM((3, planes + 7, 2, 16, LANES), BF16),
         pltpu.VMEM((hidden_planes, 2, 16, 2 * LANES), F32),
-        pltpu.VMEM((hidden_planes, blocks + 2, 16, LANES), F32),
+        pltpu.VMEM((planes // 2, blocks, 16, LANES), F32),
         pltpu.VMEM((3, hidden_planes, blocks + 2, 8, LANES), F32),
         pltpu.VMEM((3, out_planes + 3, blocks + 2, 16, LANES), BF16),
         pltpu.VMEM((out_planes + 1, blocks + 1, 8, LANES), F32),

time: 55.9 us -> 55.5 us (level)
  Pallas kernels: 16 us -> 15.4 us
    pallas_call x1, Pallas kernels: 3.69 us -> 3.1 us  [local_grads(): pl.pallas_call(own_blocks, out_shape=[jax.ShapeDtypeStruct((3, planes + 9...]
  transfers between devices with their start and end apart: 20 -> 20, of which waited for: 10 -> 10; matrix products, arithmetic and copies ran while one was open for 0% -> 0% of each run, Pallas kernels for 12% -> 11%
where the time goes in v11:
time: 55.5 us; the launch traced here: 55.4 us
  starting transfers between devices  23.7 us (43%)
  Pallas kernels  15.4 us (28%)
  waiting for transfers between devices  14.9 us (27%)
  between operations  0.86 us (2%)
    ppermute x6, starting transfers between devices, to_square(): return lax.ppermute(block, ('depth', 'row'), route)  7.12 us
    ppermute x6, waiting for transfers between devices, to_square(): return lax.ppermute(block, ('depth', 'row'), route)  6.99 us
    pallas_call x1, Pallas kernels, local_grads(): pl.pallas_call(body, out_shape=[jax.ShapeDtypeStruct((squares, rows // (2...  5.85 us
    ppermute x4, starting transfers between devices, to_col(): return lax.ppermute(block, ('row', 'col'), pairs_of_lines(rows, cols, kind))  4.86 us
    ppermute x3, waiting for transfers between devices, along_col(): return lax.ppermute(block, 'col', [(i, i ^ n) for i in range(cols)])  4.7 us
    ppermute x3, starting transfers between devices, along_col(): return lax.ppermute(block, 'col', [(i, i ^ n) for i in range(cols)])  4.45 us
    pallas_call x1, Pallas kernels, local_grads(): pl.pallas_call(own_blocks, out_shape=[jax.ShapeDtypeStruct((3, planes + 9...  3.1 us
    ppermute x1, starting transfers between devices, shards(): dep = lax.ppermute(dep, 'depth', [(0, 1), (1, 0)])  3.03 us
  transfers between devices with their start and end apart: 20, of which 10 were waited for; matrix products, arithmetic and copies ran while one was open for 0% of the time, Pallas kernels for 11%

profile of v11, /device:TPU:0, one launch (start us, length us, event | category | flops | bytes accessed | tf_op | source)
XLA Modules:
  0.0 55.4 jit_solution(1150465127079933626)
XLA Ops:
  0.7 2.0 %shard_map.59 = (bf16[32,16,1024]{2,1,0:T(8,128)(2,1)S(1)}, bf16[8,4,1024]{2,1,0:T(4,128)(2,1)S(1)}, bf16[64,864]{1,0:T(8,128)(2,1)S(1)}, bf16[1728,128]{1,0:T(8,128)(2,1)S(1)}, bf16[17,4,1024]{2,1,0:T(4,128)(2,1)S(1)}) custom-call(s32[5]{0:T(128)S(1)} %stack.58.flag_ref, bf16[32,16,1024]{2,1,0:T(8,128)(2,1)} %vol_hbm.1, bf16[8,4,1024]{2,1,0:T(4,128)(2,1)} %cot_hbm.1, ...), custom_call_target="tpu_custom_call" | custom-call | tf_op jit(solution)/shard_map/pallas_call | solution.py:554
  2.8 3.0 %collective-permute-start.1 = (bf16[17,4,1024]{2,1,0:T(4,128)(2,1)S(1)}, bf16[17,4,1024]{2,1,0:T(4,128)(2,1)S(1)}, u32[]{:S(2)}, u32[]{:S(2)}) collective-permute-start(bf16[17,4,1024]{2,1,0:T(4,128)(2,1)S(1)} %get-tuple-element.38), channel_id=1, source_target_pairs={{0,16},{16,0},{1,17},{17,1},{2,18},{18,2},{3,19},{19,3},{4,20},{20... | collective-permute-start | bytes 417800 | tf_op jit(solution)/shard_map/ppermute | solution.py:573
  5.8 0.8 %shard_map.60 = (bf16[34,4,1024]{2,1,0:T(4,128)(2,1)S(1)}, bf16[34,4,1024]{2,1,0:T(4,128)(2,1)S(1)}) custom-call(s32[5]{0:T(128)S(1)} %stack.58.flag_ref, bf16[32,16,1024]{2,1,0:T(8,128)(2,1)S(1)} %get-tuple-element.54.vol_ref, bf16[8,4,1024]{2,1,0:T(4,128)(2,1)S(1)} %get-tuple-element.36.cot_ref), custom_call_target="tpu_custom_call" | custom-call | tf_op jit(solution)/shard_map/pallas_call | solution.py:562
  6.7 1.6 %collective-permute-start = (bf16[34,4,1024]{2,1,0:T(4,128)(2,1)S(1)}, bf16[34,4,1024]{2,1,0:T(4,128)(2,1)S(1)}, u32[]{:S(2)}, u32[]{:S(2)}) collective-permute-start(bf16[34,4,1024]{2,1,0:T(4,128)(2,1)S(1)} %get-tuple-element.37), channel_id=1, source_target_pairs={{4,8},{5,9},{6,10},{7,11},{20,24},{21,25},{22,26},{23,27},{8,4},{9... | collective-permute-start | bytes 835592 | tf_op jit(solution)/shard_map/ppermute | solution.py:577
  9.7 1.8 %collective-permute-start.4 = (bf16[5,4,1024]{2,1,0:T(4,128)(2,1)S(1)}, bf16[5,4,1024]{2,1,0:T(4,128)(2,1)S(1)}, u32[]{:S(2)}, u32[]{:S(2)}) collective-permute-start(bf16[5,4,1024]{2,1,0:T(4,128)(2,1)S(1)} %get-tuple-element.77), channel_id=1, source_target_pairs={{4,8},{8,4},{0,16},{12,28},{20,24},{24,20},{16,0},{28,12},{5,9},{9... | collective-permute-start | bytes 122888 | tf_op jit(solution)/shard_map/ppermute | solution.py:594
  11.6 1.6 %collective-permute-start.5 = (bf16[34,16,128]{2,1,0:T(8,128)(2,1)S(1)}, bf16[34,16,128]{2,1,0:T(8,128)(2,1)S(1)}, u32[]{:S(2)}, u32[]{:S(2)}) collective-permute-start(bf16[34,16,128]{2,1,0:T(8,128)(2,1)S(1)} %get-tuple-element.58), channel_id=1, source_target_pairs={{0,1},{2,3},{1,0},{3,2},{4,5},{6,7},{5,4},{7,6},{8,9},{10,11},{9,8... | collective-permute-start | bytes 417800 | tf_op jit(solution)/shard_map/ppermute | solution.py:571
  14.8 3.1 %collective-permute-start.7 = (bf16[46,8,128]{2,1,0:T(8,128)(2,1)S(1)}, bf16[46,8,128]{2,1,0:T(8,128)(2,1)S(1)}, u32[]{:S(2)}, u32[]{:S(2)}) collective-permute-start(bf16[46,8,128]{2,1,0:T(8,128)(2,1)S(1)} %get-tuple-element.60), channel_id=1, source_target_pairs={{0,1},{2,3},{1,0},{3,2},{4,5},{6,7},{5,4},{7,6},{8,9},{10,11},{9,8... | collective-permute-start | bytes 282632 | tf_op jit(solution)/shard_map/ppermute | solution.py:571
  17.9 3.1 %shard_map.64 = (bf16[3,41,8,16,128]{4,3,2,1,0:T(8,128)(2,1)S(1)}, f32[20,8,16,256]{3,2,1,0:T(8,128)S(1)}) custom-call(s32[5]{0:T(128)S(1)} %stack.58.flag_ref, bf16[32,16,1024]{2,1,0:T(8,128)(2,1)S(1)} %get-tuple-element.54.vol_ref, bf16[17,4,1024]{2,1,0:T(4,128)(2,1)S(1)} %collective-permute-done.1.dep_ref, ...), custom_call_target="tpu_custom_call" | custom-call | flops 2000000000 | bytes 10000000 | tf_op jit(solution)/shard_map/pallas_call | solution.py:500
  21.0 5.8 %shard_map.65 = (f32[4,272,128]{2,1,0:T(8,128)S(1)}, bf16[4,272,128]{2,1,0:T(8,128)(2,1)S(1)}) custom-call(s32[5]{0:T(128)S(1)} %stack.58.flag_ref, s32[2]{0:T(128)S(1)} %pad_add_fusion.place_ref, bf16[3,41,8,16,128]{4,3,2,1,0:T(8,128)(2,1)S(1)} %get-tuple-element.56.tiles, f32[20,8,16,256]{3,2,1,0:T(8,128)S(1)} %get-tuple-element.57.parts, ...), custom_call_target="tpu_custom_call" | custom-call | flops 4000000000 | bytes 10000000 | tf_op jit(solution)/shard_map/pallas_call | solution.py:525
  27.5 1.2 %collective-permute-done.9 = bf16[4,272,128]{2,1,0:T(8,128)(2,1)S(1)} collective-permute-done((bf16[4,272,128]{2,1,0:T(8,128)(2,1)S(1)}, bf16[4,272,128]{2,1,0:T(8,128)(2,1)S(1)}, u32[]{:S(2)}, u32[]{:S(2)}) %collective-permute-start.9) | collective-permute-done | bytes 278560 | tf_op jit(solution)/shard_map/ppermute | solution.py:624
  29.0 1.5 %collective-permute-start.12 = (bf16[272,128]{1,0:T(8,128)(2,1)S(1)}, bf16[272,128]{1,0:T(8,128)(2,1)S(1)}, u32[]{:S(2)}, u32[]{:S(2)}) collective-permute-start(bf16[272,128]{1,0:T(8,128)(2,1)S(1)} %get-tuple-element.71), channel_id=1, source_target_pairs={{0,16},{4,20},{8,24},{12,28},{16,0},{20,4},{24,8},{28,12},{1,17},{... | collective-permute-start | bytes 208904 | tf_op jit(solution)/shard_map/ppermute | solution.py:621
  30.4 1.9 %collective-permute-start.11 = (bf16[272,128]{1,0:T(8,128)(2,1)S(1)}, bf16[272,128]{1,0:T(8,128)(2,1)S(1)}, u32[]{:S(2)}, u32[]{:S(2)}) collective-permute-start(bf16[272,128]{1,0:T(8,128)(2,1)S(1)} %get-tuple-element.72), channel_id=1, source_target_pairs={{0,24},{4,28},{8,16},{12,20},{16,8},{20,12},{24,0},{28,4},{1,25},{... | collective-permute-start | bytes 208904 | tf_op jit(solution)/shard_map/ppermute | solution.py:621
  32.3 1.2 %collective-permute-done.10 = bf16[272,128]{1,0:T(8,128)(2,1)S(1)} collective-permute-done((bf16[272,128]{1,0:T(8,128)(2,1)S(1)}, bf16[272,128]{1,0:T(8,128)(2,1)S(1)}, u32[]{:S(2)}, u32[]{:S(2)}) %collective-permute-start.10) | collective-permute-done | bytes 69664 | tf_op jit(solution)/shard_map/ppermute | solution.py:621
  33.6 2.2 %collective-permute-done.11 = bf16[272,128]{1,0:T(8,128)(2,1)S(1)} collective-permute-done((bf16[272,128]{1,0:T(8,128)(2,1)S(1)}, bf16[272,128]{1,0:T(8,128)(2,1)S(1)}, u32[]{:S(2)}, u32[]{:S(2)}) %collective-permute-start.11) | collective-permute-done | bytes 69664 | tf_op jit(solution)/shard_map/ppermute | solution.py:621
  35.8 2.5 %collective-permute-start.15 = (bf16[272,128]{1,0:T(8,128)(2,1)S(1)}, bf16[272,128]{1,0:T(8,128)(2,1)S(1)}, u32[]{:S(2)}, u32[]{:S(2)}) collective-permute-start(bf16[272,128]{1,0:T(8,128)(2,1)S(1)} %fusion.2), channel_id=1, source_target_pairs={{0,3},{1,2},{2,1},{3,0},{4,7},{5,6},{6,5},{7,4},{8,11},{9,10},{10,... | collective-permute-start | bytes 208904 | tf_op jit(solution)/shard_map/ppermute | solution.py:627
  38.3 1.2 %collective-permute-start.14 = (bf16[272,128]{1,0:T(8,128)(2,1)S(1)}, bf16[272,128]{1,0:T(8,128)(2,1)S(1)}, u32[]{:S(2)}, u32[]{:S(2)}) collective-permute-start(bf16[272,128]{1,0:T(8,128)(2,1)S(1)} %fusion.2), channel_id=1, source_target_pairs={{0,2},{1,3},{2,0},{3,1},{4,6},{5,7},{6,4},{7,5},{8,10},{9,11},{10,... | collective-permute-start | bytes 208904 | tf_op jit(solution)/shard_map/ppermute | solution.py:627
  40.2 2.4 %collective-permute-done.15 = bf16[272,128]{1,0:T(8,128)(2,1)S(1)} collective-permute-done((bf16[272,128]{1,0:T(8,128)(2,1)S(1)}, bf16[272,128]{1,0:T(8,128)(2,1)S(1)}, u32[]{:S(2)}, u32[]{:S(2)}) %collective-permute-start.15) | collective-permute-done | bytes 69664 | tf_op jit(solution)/shard_map/ppermute | solution.py:627
  42.6 2.3 %collective-permute-done.14 = bf16[272,128]{1,0:T(8,128)(2,1)S(1)} collective-permute-done((bf16[272,128]{1,0:T(8,128)(2,1)S(1)}, bf16[272,128]{1,0:T(8,128)(2,1)S(1)}, u32[]{:S(2)}, u32[]{:S(2)}) %collective-permute-start.14) | collective-permute-done | bytes 69664 | tf_op jit(solution)/shard_map/ppermute | solution.py:627
  45.0 1.1 %collective-permute-start.18 = (bf16[272,128]{1,0:T(8,128)(2,1)S(1)}, bf16[272,128]{1,0:T(8,128)(2,1)S(1)}, u32[]{:S(2)}, u32[]{:S(2)}) collective-permute-start(bf16[272,128]{1,0:T(8,128)(2,1)S(1)} %add_convert_fusion), channel_id=1, source_target_pairs={{0,8},{4,12},{8,0},{12,4},{16,24},{20,28},{24,16},{28,20},{1,9},{5... | collective-permute-start | bytes 208904 | tf_op jit(solution)/shard_map/ppermute | solution.py:621
  46.9 1.6 %collective-permute-start.16 = (bf16[272,128]{1,0:T(8,128)(2,1)S(1)}, bf16[272,128]{1,0:T(8,128)(2,1)S(1)}, u32[]{:S(2)}, u32[]{:S(2)}) collective-permute-start(bf16[272,128]{1,0:T(8,128)(2,1)S(1)} %add_convert_fusion), channel_id=1, source_target_pairs={{0,24},{4,28},{8,16},{12,20},{16,8},{20,12},{24,0},{28,4},{1,25},{... | collective-permute-start | bytes 208904 | tf_op jit(solution)/shard_map/ppermute | solution.py:621
  49.3 1.0 %collective-permute-done.17 = bf16[272,128]{1,0:T(8,128)(2,1)S(1)} collective-permute-done((bf16[272,128]{1,0:T(8,128)(2,1)S(1)}, bf16[272,128]{1,0:T(8,128)(2,1)S(1)}, u32[]{:S(2)}, u32[]{:S(2)}) %collective-permute-start.17) | collective-permute-done | bytes 69664 | tf_op jit(solution)/shard_map/ppermute | solution.py:621
  50.4 1.7 %collective-permute-done.16 = bf16[272,128]{1,0:T(8,128)(2,1)S(1)} collective-permute-done((bf16[272,128]{1,0:T(8,128)(2,1)S(1)}, bf16[272,128]{1,0:T(8,128)(2,1)S(1)}, u32[]{:S(2)}, u32[]{:S(2)}) %collective-permute-start.16) | collective-permute-done | bytes 69664 | tf_op jit(solution)/shard_map/ppermute | solution.py:621
  52.2 1.5 %collective-permute-done.19.got_ref = bf16[4,272,128]{2,1,0:T(8,128)(2,1)S(1)} collective-permute-done((bf16[4,272,128]{2,1,0:T(8,128)(2,1)S(1)}, bf16[4,272,128]{2,1,0:T(8,128)(2,1)S(1)}, u32[]{:S(2)}, u32[]{:S(2)}) %collective-permute-start.19) | collective-permute-done | bytes 278560 | tf_op jit(solution)/shard_map/ppermute | solution.py:624
  53.8 1.6 %shard_map.66 = (f32[64,864]{1,0:T(8,128)}, f32[1728,128]{1,0:T(8,128)}) custom-call(s32[2]{0:T(128)S(1)} %pad_add_fusion.place_ref, bf16[4,272,128]{2,1,0:T(8,128)(2,1)S(1)} %pad_maximum_fusion.keep_ref, bf16[4,272,128]{2,1,0:T(8,128)(2,1)S(1)} %collective-permute-done.19.got_ref), custom_call_target="tpu_custom_call" | custom-call | tf_op jit(solution)/shard_map/pallas_call | solution.py:637
  (38 shorter events, 6.6 us)
Async XLA Ops:
  2.8 6.7 %collective-permute-start.1 = (bf16[17,4,1024]{2,1,0:T(4,128)(2,1)S(1)}, bf16[17,4,1024]{2,1,0:T(4,128)(2,1)S(1)}, u32[]{:S(2)}, u32[]{:S(2)}) collective-permute-start(bf16[17,4,1024]{2,1,0:T(4,128)(2,1)S(1)} %get-tuple-element.38), channel_id=1, source_target_pairs={{0,16},{16,0},{1,17},{17,1},{2,18},{18,2},{3,19},{19,3},{4,20},{20... | collective-permute-start | bytes 417800 | tf_op jit(solution)/shard_map/ppermute | solution.py:573
  6.7 7.4 %collective-permute-start = (bf16[34,4,1024]{2,1,0:T(4,128)(2,1)S(1)}, bf16[34,4,1024]{2,1,0:T(4,128)(2,1)S(1)}, u32[]{:S(2)}, u32[]{:S(2)}) collective-permute-start(bf16[34,4,1024]{2,1,0:T(4,128)(2,1)S(1)} %get-tuple-element.37), channel_id=1, source_target_pairs={{4,8},{5,9},{6,10},{7,11},{20,24},{21,25},{22,26},{23,27},{8,4},{9... | collective-permute-start | bytes 835592 | tf_op jit(solution)/shard_map/ppermute | solution.py:577
  8.3 5.6 %collective-permute-start.2 = (bf16[34,4,1024]{2,1,0:T(4,128)(2,1)S(1)}, bf16[34,4,1024]{2,1,0:T(4,128)(2,1)S(1)}, u32[]{:S(2)}, u32[]{:S(2)}) collective-permute-start(bf16[34,4,1024]{2,1,0:T(4,128)(2,1)S(1)} %get-tuple-element.48), channel_id=1, source_target_pairs={{0,4},{8,12},{4,0},{12,8},{1,5},{9,13},{5,1},{13,9},{2,6},{10,14},... | collective-permute-start | bytes 835592 | tf_op jit(solution)/shard_map/ppermute | solution.py:578
  9.7 4.4 %collective-permute-start.4 = (bf16[5,4,1024]{2,1,0:T(4,128)(2,1)S(1)}, bf16[5,4,1024]{2,1,0:T(4,128)(2,1)S(1)}, u32[]{:S(2)}, u32[]{:S(2)}) collective-permute-start(bf16[5,4,1024]{2,1,0:T(4,128)(2,1)S(1)} %get-tuple-element.77), channel_id=1, source_target_pairs={{4,8},{8,4},{0,16},{12,28},{20,24},{24,20},{16,0},{28,12},{5,9},{9... | collective-permute-start | bytes 122888 | tf_op jit(solution)/shard_map/ppermute | solution.py:594
  11.5 2.6 %collective-permute-start.3 = (bf16[5,4,1024]{2,1,0:T(4,128)(2,1)S(1)}, bf16[5,4,1024]{2,1,0:T(4,128)(2,1)S(1)}, u32[]{:S(2)}, u32[]{:S(2)}) collective-permute-start(bf16[5,4,1024]{2,1,0:T(4,128)(2,1)S(1)} %get-tuple-element.78), channel_id=1, source_target_pairs={{0,4},{8,12},{4,0},{12,8},{1,5},{9,13},{5,1},{13,9},{2,6},{10,14},... | collective-permute-start | bytes 122888 | tf_op jit(solution)/shard_map/ppermute | solution.py:593
  11.6 9.3 %collective-permute-start.5 = (bf16[34,16,128]{2,1,0:T(8,128)(2,1)S(1)}, bf16[34,16,128]{2,1,0:T(8,128)(2,1)S(1)}, u32[]{:S(2)}, u32[]{:S(2)}) collective-permute-start(bf16[34,16,128]{2,1,0:T(8,128)(2,1)S(1)} %get-tuple-element.58), channel_id=1, source_target_pairs={{0,1},{2,3},{1,0},{3,2},{4,5},{6,7},{5,4},{7,6},{8,9},{10,11},{9,8... | collective-permute-start | bytes 417800 | tf_op jit(solution)/shard_map/ppermute | solution.py:571
  13.9 7.1 %collective-permute-start.6 = (bf16[34,16,128]{2,1,0:T(8,128)(2,1)S(1)}, bf16[34,16,128]{2,1,0:T(8,128)(2,1)S(1)}, u32[]{:S(2)}, u32[]{:S(2)}) collective-permute-start(bf16[34,16,128]{2,1,0:T(8,128)(2,1)S(1)} %get-tuple-element.59), channel_id=1, source_target_pairs={{1,2},{2,1},{0,4},{3,7},{5,6},{6,5},{4,0},{7,3},{9,10},{10,9},{8,1... | collective-permute-start | bytes 417800 | tf_op jit(solution)/shard_map/ppermute | solution.py:571
  14.8 6.2 %collective-permute-start.7 = (bf16[46,8,128]{2,1,0:T(8,128)(2,1)S(1)}, bf16[46,8,128]{2,1,0:T(8,128)(2,1)S(1)}, u32[]{:S(2)}, u32[]{:S(2)}) collective-permute-start(bf16[46,8,128]{2,1,0:T(8,128)(2,1)S(1)} %get-tuple-element.60), channel_id=1, source_target_pairs={{0,1},{2,3},{1,0},{3,2},{4,5},{6,7},{5,4},{7,6},{8,9},{10,11},{9,8... | collective-permute-start | bytes 282632 | tf_op jit(solution)/shard_map/ppermute | solution.py:571
  17.9 3.1 %collective-permute-start.8 = (bf16[46,8,128]{2,1,0:T(8,128)(2,1)S(1)}, bf16[46,8,128]{2,1,0:T(8,128)(2,1)S(1)}, u32[]{:S(2)}, u32[]{:S(2)}) collective-permute-start(bf16[46,8,128]{2,1,0:T(8,128)(2,1)S(1)} %get-tuple-element.61), channel_id=1, source_target_pairs={{1,2},{2,1},{0,4},{3,7},{5,6},{6,5},{4,0},{7,3},{9,10},{10,9},{8,1... | collective-permute-start | bytes 282632 | tf_op jit(solution)/shard_map/ppermute | solution.py:571
  26.9 1.8 %collective-permute-start.9 = (bf16[4,272,128]{2,1,0:T(8,128)(2,1)S(1)}, bf16[4,272,128]{2,1,0:T(8,128)(2,1)S(1)}, u32[]{:S(2)}, u32[]{:S(2)}) collective-permute-start(bf16[4,272,128]{2,1,0:T(8,128)(2,1)S(1)} %get-tuple-element.65), channel_id=1, source_target_pairs={{0,4},{4,0},{8,12},{12,8},{16,20},{20,16},{24,28},{28,24},{1,5},{5... | collective-permute-start | bytes 835592 | tf_op jit(solution)/shard_map/ppermute | solution.py:624
  28.8 4.8 %collective-permute-start.10 = (bf16[272,128]{1,0:T(8,128)(2,1)S(1)}, bf16[272,128]{1,0:T(8,128)(2,1)S(1)}, u32[]{:S(2)}, u32[]{:S(2)}) collective-permute-start(bf16[272,128]{1,0:T(8,128)(2,1)S(1)} %get-tuple-element.70), channel_id=1, source_target_pairs={{0,8},{4,12},{8,0},{12,4},{16,24},{20,28},{24,16},{28,20},{1,9},{5... | collective-permute-start | bytes 208904 | tf_op jit(solution)/shard_map/ppermute | solution.py:621
  29.0 4.6 %collective-permute-start.12 = (bf16[272,128]{1,0:T(8,128)(2,1)S(1)}, bf16[272,128]{1,0:T(8,128)(2,1)S(1)}, u32[]{:S(2)}, u32[]{:S(2)}) collective-permute-start(bf16[272,128]{1,0:T(8,128)(2,1)S(1)} %get-tuple-element.71), channel_id=1, source_target_pairs={{0,16},{4,20},{8,24},{12,28},{16,0},{20,4},{24,8},{28,12},{1,17},{... | collective-permute-start | bytes 208904 | tf_op jit(solution)/shard_map/ppermute | solution.py:621
  30.4 5.3 %collective-permute-start.11 = (bf16[272,128]{1,0:T(8,128)(2,1)S(1)}, bf16[272,128]{1,0:T(8,128)(2,1)S(1)}, u32[]{:S(2)}, u32[]{:S(2)}) collective-permute-start(bf16[272,128]{1,0:T(8,128)(2,1)S(1)} %get-tuple-element.72), channel_id=1, source_target_pairs={{0,24},{4,28},{8,16},{12,20},{16,8},{20,12},{24,0},{28,4},{1,25},{... | collective-permute-start | bytes 208904 | tf_op jit(solution)/shard_map/ppermute | solution.py:621
  35.8 6.9 %collective-permute-start.15 = (bf16[272,128]{1,0:T(8,128)(2,1)S(1)}, bf16[272,128]{1,0:T(8,128)(2,1)S(1)}, u32[]{:S(2)}, u32[]{:S(2)}) collective-permute-start(bf16[272,128]{1,0:T(8,128)(2,1)S(1)} %fusion.2), channel_id=1, source_target_pairs={{0,3},{1,2},{2,1},{3,0},{4,7},{5,6},{6,5},{7,4},{8,11},{9,10},{10,... | collective-permute-start | bytes 208904 | tf_op jit(solution)/shard_map/ppermute | solution.py:627
  38.3 6.6 %collective-permute-start.14 = (bf16[272,128]{1,0:T(8,128)(2,1)S(1)}, bf16[272,128]{1,0:T(8,128)(2,1)S(1)}, u32[]{:S(2)}, u32[]{:S(2)}) collective-permute-start(bf16[272,128]{1,0:T(8,128)(2,1)S(1)} %fusion.2), channel_id=1, source_target_pairs={{0,2},{1,3},{2,0},{3,1},{4,6},{5,7},{6,4},{7,5},{8,10},{9,11},{10,... | collective-permute-start | bytes 208904 | tf_op jit(solution)/shard_map/ppermute | solution.py:627
  39.5 5.4 %collective-permute-start.13 = (bf16[272,128]{1,0:T(8,128)(2,1)S(1)}, bf16[272,128]{1,0:T(8,128)(2,1)S(1)}, u32[]{:S(2)}, u32[]{:S(2)}) collective-permute-start(bf16[272,128]{1,0:T(8,128)(2,1)S(1)} %fusion.2), channel_id=1, source_target_pairs={{0,1},{1,0},{2,3},{3,2},{4,5},{5,4},{6,7},{7,6},{8,9},{9,8},{10,11... | collective-permute-start | bytes 208904 | tf_op jit(solution)/shard_map/ppermute | solution.py:627
  45.0 4.4 %collective-permute-start.18 = (bf16[272,128]{1,0:T(8,128)(2,1)S(1)}, bf16[272,128]{1,0:T(8,128)(2,1)S(1)}, u32[]{:S(2)}, u32[]{:S(2)}) collective-permute-start(bf16[272,128]{1,0:T(8,128)(2,1)S(1)} %add_convert_fusion), channel_id=1, source_target_pairs={{0,8},{4,12},{8,0},{12,4},{16,24},{20,28},{24,16},{28,20},{1,9},{5... | collective-permute-start | bytes 208904 | tf_op jit(solution)/shard_map/ppermute | solution.py:621
  46.1 4.3 %collective-permute-start.17 = (bf16[272,128]{1,0:T(8,128)(2,1)S(1)}, bf16[272,128]{1,0:T(8,128)(2,1)S(1)}, u32[]{:S(2)}, u32[]{:S(2)}) collective-permute-start(bf16[272,128]{1,0:T(8,128)(2,1)S(1)} %add_convert_fusion), channel_id=1, source_target_pairs={{0,16},{4,20},{8,24},{12,28},{16,0},{20,4},{24,8},{28,12},{1,17},{... | collective-permute-start | bytes 208904 | tf_op jit(solution)/shard_map/ppermute | solution.py:621
  46.9 5.2 %collective-permute-start.16 = (bf16[272,128]{1,0:T(8,128)(2,1)S(1)}, bf16[272,128]{1,0:T(8,128)(2,1)S(1)}, u32[]{:S(2)}, u32[]{:S(2)}) collective-permute-start(bf16[272,128]{1,0:T(8,128)(2,1)S(1)} %add_convert_fusion), channel_id=1, source_target_pairs={{0,24},{4,28},{8,16},{12,20},{16,8},{20,12},{24,0},{28,4},{1,25},{... | collective-permute-start | bytes 208904 | tf_op jit(solution)/shard_map/ppermute | solution.py:621
  52.1 1.6 %collective-permute-start.19 = (bf16[4,272,128]{2,1,0:T(8,128)(2,1)S(1)}, bf16[4,272,128]{2,1,0:T(8,128)(2,1)S(1)}, u32[]{:S(2)}, u32[]{:S(2)}) collective-permute-start(bf16[4,272,128]{2,1,0:T(8,128)(2,1)S(1)} %pad_maximum_fusion.keep_ref), channel_id=1, source_target_pairs={{0,4},{4,0},{8,12},{12,8},{16,20},{20,16},{24,28},{28,24},{1,5},{5... | collective-permute-start | bytes 835592 | tf_op jit(solution)/shard_map/ppermute | solution.py:624

commit v12 on v11

--- a/solution.py
+++ b/solution.py
@@ -196,8 +196,17 @@
     return jnp.where(even, b.astype(F32), a.astype(F32))
 
 
+def first_values(pre):
+    square = pre * pre + 1.0
+    inverse = lax.rsqrt(square)
+    hidden = (0.6 * pre + 0.4 * (square * inverse - 1.0)).astype(BF16).astype(F32)
+    odd = hidden[:, 8:, :]
+    return 0.6 + 0.4 * (pre * inverse), (pltpu.roll(odd, 1, 1), hidden[:, :8, :], odd)
+
+
 def own_blocks(
-    flag_ref, vol_ref, dep_ref, row_a_ref, row_b_ref, edge_a_ref, edge_b_ref, w1_ref, tiles, parts, stage
+    flag_ref, vol_ref, dep_ref, row_a_ref, row_b_ref, edge_a_ref, edge_b_ref, w1_ref,
+    tiles, parts, hid, slopes, stage,
 ):
     first_plane, row_even = flag_ref[0] == 0, flag_ref[1] == 0
     planes = vol_ref.shape[0]
@@ -257,9 +266,16 @@
 
     lax.fori_loop(0, parts.shape[0] // group, product, 0, unroll=True)
 
+    for i in range(planes // 2 + 3):
+        slope, rows = first_values(parts[i, 1:, :, :LANES] + parts[i, :-1, :, LANES:])
+        for b in range(3):
+            hid[b, i] = rows[b]
+        if 1 <= i <= planes // 2:
+            slopes[i - 1] = slope
+
 
 def body(
-    flag_ref, place_ref, tiles, parts, dep_ref, row_a_ref, row_b_ref, edge_a_ref, edge_b_ref,
+    flag_ref, place_ref, tiles, parts, inner_hid, inner_slopes, dep_ref, row_a_ref, row_b_ref, edge_a_ref, edge_b_ref,
     side_a_ref, side_b_ref, col_a_ref, col_b_ref, cot_ref, w1_ref, w2_ref, w2b_ref, keep_ref, give_ref,
     out_ref, stage, rim_tiles, rim_parts, slopes, hid, pairs, ups, deltas, shifted,
 ):
@@ -313,30 +329,24 @@
     found = matmul(jnp.concatenate(taps, axis=1), w1_ref[...])
     rim_parts[...] = found.reshape(hidden_planes, 2, 16, 2 * LANES)
 
-    def conv_one(i):
-        main, prev = parts[i, :, :, :LANES], parts[i, :, :, LANES:]
+    for i in range(hidden_planes):
         rim, rim_prev = rim_parts[i, :, :, :LANES], rim_parts[i, 0:1, :, LANES:]
-        blank = jnp.zeros((1, 16, LANES), F32)
-        pre = jnp.concatenate([rim[:1], main, rim[1:]], axis=0) + jnp.concatenate([blank, rim_prev, prev], axis=0)
-        square = pre * pre + 1.0
-        inverse = lax.rsqrt(square)
+        first = parts[i, 0:1, :, :LANES] + rim_prev
+        last = rim[1:] + parts[i, blocks - 1 :, :, LANES:]
+        slope, rows = first_values(jnp.concatenate([rim[:1], first, last], axis=0))
+        for b in range(3):
+            hid[b, i] = rows[b]
         if 1 <= i <= planes // 2:
-            own = slice(1, blocks + 1)
-            slopes[i - 1] = 0.6 + 0.4 * (pre[own] * inverse[own])
-        hidden = (0.6 * pre + 0.4 * (square * inverse - 1.0)).astype(BF16).astype(F32)
-        odd = hidden[:, 8:, :]
-        hid[0, i] = pltpu.roll(odd, 1, 1)
-        hid[1, i] = hidden[:, :8, :]
-        hid[2, i] = odd
-
-    for i in range(hidden_planes):
-        conv_one(i)
+            slopes[i - 1] = slope[1:2]
 
     wide = (blocks + 2) * 16
 
     def pair(i, carry):
         for b in range(3):
-            pairs[b, i] = jnp.concatenate([hid[b, i], hid[b, i + half_planes]], axis=1).astype(BF16)
+            both = [
+                jnp.concatenate([hid[b, n, 0:2], inner_hid[b, n], hid[b, n, 2:3]], axis=0) for n in (i, i + half_planes)
+            ]
+            pairs[b, i] = jnp.concatenate(both, axis=1).astype(BF16)
         return carry
 
     lax.fori_loop(0, half_planes + 3, pair, 0, unroll=True)
@@ -431,7 +441,7 @@
         t, parity = i // 2, i % 2
         half = slice(0, 8) if t < quarter else slice(8, 16)
         back_one = jnp.concatenate([rows[parity][p][t % quarter, :, half, :] for p in (0, 1)], axis=1)
-        delta = back_one * slopes[i]
+        delta = back_one * jnp.concatenate([slopes[i], inner_slopes[i]], axis=0)
         own_list.append(jnp.where(own_rows[0], delta, 0.0).astype(BF16))
     left_one = with_next(jnp.stack(own_list, axis=1).reshape(blocks * (planes // 2) * 16, LANES), 64)
 
@@ -497,14 +507,16 @@
     whole = pl.BlockSpec(memory_space=pltpu.VMEM)
     smem = pl.BlockSpec(memory_space=pltpu.SMEM)
     dep, row_a, row_b, edge_a, edge_b = faces
-    tiles, parts = pl.pallas_call(
+    tiles, parts, inner_hid, inner_slopes = pl.pallas_call(
         own_blocks,
         out_shape=[
             jax.ShapeDtypeStruct((3, planes + 9, blocks, 16, LANES), BF16),
             jax.ShapeDtypeStruct((hidden_planes + 1, blocks, 16, 2 * LANES), F32),
+            jax.ShapeDtypeStruct((3, hidden_planes, blocks - 1, 8, LANES), F32),
+            jax.ShapeDtypeStruct((planes // 2, blocks - 1, 16, LANES), F32),
         ],
         in_specs=[smem] + [whole] * 7,
-        out_specs=[whole] * 2,
+        out_specs=[whole] * 4,
         scratch_shapes=[pltpu.VMEM((4, blocks, 40, LANES), F32)],
         compiler_params=pltpu.CompilerParams(vmem_limit_bytes=16 * 1024 * 1024),
         cost_estimate=pl.CostEstimate(flops=2 * 10**9, bytes_accessed=10**7, transcendentals=0),
@@ -514,14 +526,14 @@
         pltpu.VMEM((4, 2, 40, LANES), F32),
         pltpu.VMEM((3, planes + 7, 2, 16, LANES), BF16),
         pltpu.VMEM((hidden_planes, 2, 16, 2 * LANES), F32),
-        pltpu.VMEM((planes // 2, blocks, 16, LANES), F32),
-        pltpu.VMEM((3, hidden_planes, blocks + 2, 8, LANES), F32),
+        pltpu.VMEM((planes // 2, 1, 16, LANES), F32),
+        pltpu.VMEM((3, hidden_planes, 3, 8, LANES), F32),
         pltpu.VMEM((3, out_planes + 3, blocks + 2, 16, LANES), BF16),
         pltpu.VMEM((out_planes + 1, blocks + 1, 8, LANES), F32),
         pltpu.VMEM((out_planes // 2 + 1, blocks + 1, 16, LANES), F32),
         pltpu.VMEM((out_planes // 2 + 1, blocks + 1, 16, LANES), BF16),
     ]
-    operands = (tiles, parts, *faces, *corners, cotangent, *weights)
+    operands = (tiles, parts, inner_hid, inner_slopes, *faces, *corners, cotangent, *weights)
     return pl.pallas_call(
         body,
         out_shape=[jax.ShapeDtypeStruct((squares, rows // (2 * squares), LANES), dtype) for dtype in (F32, BF16)],

time: 55.5 us -> 55.4 us (level)
  no operation moved by 1% of the time
where the time goes in v12:
time: 55.4 us; the launch traced here: 55.3 us
  starting transfers between devices  23.7 us (43%)
  Pallas kernels  15.5 us (28%)
  waiting for transfers between devices  14.8 us (27%)
  between operations  0.86 us (2%)
    ppermute x6, starting transfers between devices, to_square(): return lax.ppermute(block, ('depth', 'row'), route)  7.12 us
    ppermute x6, waiting for transfers between devices, to_square(): return lax.ppermute(block, ('depth', 'row'), route)  6.83 us
    pallas_call x1, Pallas kernels, local_grads(): pl.pallas_call(body, out_shape=[jax.ShapeDtypeStruct((squares, rows // (2...  5.75 us
    ppermute x4, starting transfers between devices, to_col(): return lax.ppermute(block, ('row', 'col'), pairs_of_lines(rows, cols, kind))  4.86 us
    ppermute x3, waiting for transfers between devices, along_col(): return lax.ppermute(block, 'col', [(i, i ^ n) for i in range(cols)])  4.7 us
    ppermute x3, starting transfers between devices, along_col(): return lax.ppermute(block, 'col', [(i, i ^ n) for i in range(cols)])  4.45 us
    pallas_call x1, Pallas kernels, local_grads(): pl.pallas_call(own_blocks, out_shape=[jax.ShapeDtypeStruct((3, planes + 9...  3.26 us
    ppermute x1, starting transfers between devices, shards(): dep = lax.ppermute(dep, 'depth', [(0, 1), (1, 0)])  3.03 us
  transfers between devices with their start and end apart: 20, of which 10 were waited for; matrix products, arithmetic and copies ran while one was open for 0% of the time, Pallas kernels for 11%

profile of v12, /device:TPU:0, one launch (start us, length us, event | category | flops | bytes accessed | tf_op | source)
XLA Modules:
  0.0 55.3 jit_solution(8455920863158775719)
XLA Ops:
  0.7 2.0 %shard_map.59 = (bf16[32,16,1024]{2,1,0:T(8,128)(2,1)S(1)}, bf16[8,4,1024]{2,1,0:T(4,128)(2,1)S(1)}, bf16[64,864]{1,0:T(8,128)(2,1)S(1)}, bf16[1728,128]{1,0:T(8,128)(2,1)S(1)}, bf16[17,4,1024]{2,1,0:T(4,128)(2,1)S(1)}) custom-call(s32[5]{0:T(128)S(1)} %stack.58.flag_ref, bf16[32,16,1024]{2,1,0:T(8,128)(2,1)} %vol_hbm.1, bf16[8,4,1024]{2,1,0:T(4,128)(2,1)} %cot_hbm.1, ...), custom_call_target="tpu_custom_call" | custom-call | tf_op jit(solution)/shard_map/pallas_call | solution.py:566
  2.8 3.0 %collective-permute-start.1 = (bf16[17,4,1024]{2,1,0:T(4,128)(2,1)S(1)}, bf16[17,4,1024]{2,1,0:T(4,128)(2,1)S(1)}, u32[]{:S(2)}, u32[]{:S(2)}) collective-permute-start(bf16[17,4,1024]{2,1,0:T(4,128)(2,1)S(1)} %get-tuple-element.40), channel_id=1, source_target_pairs={{0,16},{16,0},{1,17},{17,1},{2,18},{18,2},{3,19},{19,3},{4,20},{20... | collective-permute-start | bytes 417800 | tf_op jit(solution)/shard_map/ppermute | solution.py:585
  6.7 1.6 %collective-permute-start = (bf16[34,4,1024]{2,1,0:T(4,128)(2,1)S(1)}, bf16[34,4,1024]{2,1,0:T(4,128)(2,1)S(1)}, u32[]{:S(2)}, u32[]{:S(2)}) collective-permute-start(bf16[34,4,1024]{2,1,0:T(4,128)(2,1)S(1)} %get-tuple-element.39), channel_id=1, source_target_pairs={{4,8},{5,9},{6,10},{7,11},{20,24},{21,25},{22,26},{23,27},{8,4},{9... | collective-permute-start | bytes 835592 | tf_op jit(solution)/shard_map/ppermute | solution.py:589
  9.7 1.8 %collective-permute-start.4 = (bf16[5,4,1024]{2,1,0:T(4,128)(2,1)S(1)}, bf16[5,4,1024]{2,1,0:T(4,128)(2,1)S(1)}, u32[]{:S(2)}, u32[]{:S(2)}) collective-permute-start(bf16[5,4,1024]{2,1,0:T(4,128)(2,1)S(1)} %get-tuple-element.81), channel_id=1, source_target_pairs={{4,8},{8,4},{0,16},{12,28},{20,24},{24,20},{16,0},{28,12},{5,9},{9... | collective-permute-start | bytes 122888 | tf_op jit(solution)/shard_map/ppermute | solution.py:606
  11.6 1.6 %collective-permute-start.5 = (bf16[34,16,128]{2,1,0:T(8,128)(2,1)S(1)}, bf16[34,16,128]{2,1,0:T(8,128)(2,1)S(1)}, u32[]{:S(2)}, u32[]{:S(2)}) collective-permute-start(bf16[34,16,128]{2,1,0:T(8,128)(2,1)S(1)} %get-tuple-element.62), channel_id=1, source_target_pairs={{0,1},{2,3},{1,0},{3,2},{4,5},{6,7},{5,4},{7,6},{8,9},{10,11},{9,8... | collective-permute-start | bytes 417800 | tf_op jit(solution)/shard_map/ppermute | solution.py:583
  14.8 3.1 %collective-permute-start.7 = (bf16[46,8,128]{2,1,0:T(8,128)(2,1)S(1)}, bf16[46,8,128]{2,1,0:T(8,128)(2,1)S(1)}, u32[]{:S(2)}, u32[]{:S(2)}) collective-permute-start(bf16[46,8,128]{2,1,0:T(8,128)(2,1)S(1)} %get-tuple-element.64), channel_id=1, source_target_pairs={{0,1},{2,3},{1,0},{3,2},{4,5},{6,7},{5,4},{7,6},{8,9},{10,11},{9,8... | collective-permute-start | bytes 282632 | tf_op jit(solution)/shard_map/ppermute | solution.py:583
  17.9 3.3 %shard_map.64 = (bf16[3,41,8,16,128]{4,3,2,1,0:T(8,128)(2,1)S(1)}, f32[20,8,16,256]{3,2,1,0:T(8,128)S(1)}, f32[3,19,7,8,128]{4,3,2,1,0:T(8,128)S(1)}, f32[16,7,16,128]{3,2,1,0:T(8,128)S(1)}) custom-call(s32[5]{0:T(128)S(1)} %stack.58.flag_ref, bf16[32,16,1024]{2,1,0:T(8,128)(2,1)S(1)} %get-tuple-element.56.vol_ref, ...), custom_call_target="tpu_custom_call" | custom-call | flops 2000000000 | bytes 10000000 | tf_op jit(solution)/shard_map/pallas_call | solution.py:510
  21.2 5.7 %shard_map.65 = (f32[4,272,128]{2,1,0:T(8,128)S(1)}, bf16[4,272,128]{2,1,0:T(8,128)(2,1)S(1)}) custom-call(s32[5]{0:T(128)S(1)} %stack.58.flag_ref, s32[2]{0:T(128)S(1)} %pad_add_fusion.place_ref, bf16[3,41,8,16,128]{4,3,2,1,0:T(8,128)(2,1)S(1)} %get-tuple-element.58.tiles, f32[20,8,16,256]{3,2,1,0:T(8,128)S(1)} %get-tuple-element.59.parts, ...), custom_call_target="tpu_custom_call" | custom-call | flops 4000000000 | bytes 10000000 | tf_op jit(solution)/shard_map/pallas_call | solution.py:537
  27.5 1.2 %collective-permute-done.9 = bf16[4,272,128]{2,1,0:T(8,128)(2,1)S(1)} collective-permute-done((bf16[4,272,128]{2,1,0:T(8,128)(2,1)S(1)}, bf16[4,272,128]{2,1,0:T(8,128)(2,1)S(1)}, u32[]{:S(2)}, u32[]{:S(2)}) %collective-permute-start.9) | collective-permute-done | bytes 278560 | tf_op jit(solution)/shard_map/ppermute | solution.py:636
  29.0 1.5 %collective-permute-start.12 = (bf16[272,128]{1,0:T(8,128)(2,1)S(1)}, bf16[272,128]{1,0:T(8,128)(2,1)S(1)}, u32[]{:S(2)}, u32[]{:S(2)}) collective-permute-start(bf16[272,128]{1,0:T(8,128)(2,1)S(1)} %get-tuple-element.75), channel_id=1, source_target_pairs={{0,16},{4,20},{8,24},{12,28},{16,0},{20,4},{24,8},{28,12},{1,17},{... | collective-permute-start | bytes 208904 | tf_op jit(solution)/shard_map/ppermute | solution.py:633
  30.5 1.9 %collective-permute-start.11 = (bf16[272,128]{1,0:T(8,128)(2,1)S(1)}, bf16[272,128]{1,0:T(8,128)(2,1)S(1)}, u32[]{:S(2)}, u32[]{:S(2)}) collective-permute-start(bf16[272,128]{1,0:T(8,128)(2,1)S(1)} %get-tuple-element.76), channel_id=1, source_target_pairs={{0,24},{4,28},{8,16},{12,20},{16,8},{20,12},{24,0},{28,4},{1,25},{... | collective-permute-start | bytes 208904 | tf_op jit(solution)/shard_map/ppermute | solution.py:633
  32.4 1.2 %collective-permute-done.10 = bf16[272,128]{1,0:T(8,128)(2,1)S(1)} collective-permute-done((bf16[272,128]{1,0:T(8,128)(2,1)S(1)}, bf16[272,128]{1,0:T(8,128)(2,1)S(1)}, u32[]{:S(2)}, u32[]{:S(2)}) %collective-permute-start.10) | collective-permute-done | bytes 69664 | tf_op jit(solution)/shard_map/ppermute | solution.py:633
  33.6 2.2 %collective-permute-done.11 = bf16[272,128]{1,0:T(8,128)(2,1)S(1)} collective-permute-done((bf16[272,128]{1,0:T(8,128)(2,1)S(1)}, bf16[272,128]{1,0:T(8,128)(2,1)S(1)}, u32[]{:S(2)}, u32[]{:S(2)}) %collective-permute-start.11) | collective-permute-done | bytes 69664 | tf_op jit(solution)/shard_map/ppermute | solution.py:633
  35.8 2.4 %collective-permute-start.15 = (bf16[272,128]{1,0:T(8,128)(2,1)S(1)}, bf16[272,128]{1,0:T(8,128)(2,1)S(1)}, u32[]{:S(2)}, u32[]{:S(2)}) collective-permute-start(bf16[272,128]{1,0:T(8,128)(2,1)S(1)} %fusion.2), channel_id=1, source_target_pairs={{0,3},{1,2},{2,1},{3,0},{4,7},{5,6},{6,5},{7,4},{8,11},{9,10},{10,... | collective-permute-start | bytes 208904 | tf_op jit(solution)/shard_map/ppermute | solution.py:639
  38.2 1.3 %collective-permute-start.14 = (bf16[272,128]{1,0:T(8,128)(2,1)S(1)}, bf16[272,128]{1,0:T(8,128)(2,1)S(1)}, u32[]{:S(2)}, u32[]{:S(2)}) collective-permute-start(bf16[272,128]{1,0:T(8,128)(2,1)S(1)} %fusion.2), channel_id=1, source_target_pairs={{0,2},{1,3},{2,0},{3,1},{4,6},{5,7},{6,4},{7,5},{8,10},{9,11},{10,... | collective-permute-start | bytes 208904 | tf_op jit(solution)/shard_map/ppermute | solution.py:639
  40.2 2.4 %collective-permute-done.15 = bf16[272,128]{1,0:T(8,128)(2,1)S(1)} collective-permute-done((bf16[272,128]{1,0:T(8,128)(2,1)S(1)}, bf16[272,128]{1,0:T(8,128)(2,1)S(1)}, u32[]{:S(2)}, u32[]{:S(2)}) %collective-permute-start.15) | collective-permute-done | bytes 69664 | tf_op jit(solution)/shard_map/ppermute | solution.py:639
  42.7 2.3 %collective-permute-done.14 = bf16[272,128]{1,0:T(8,128)(2,1)S(1)} collective-permute-done((bf16[272,128]{1,0:T(8,128)(2,1)S(1)}, bf16[272,128]{1,0:T(8,128)(2,1)S(1)}, u32[]{:S(2)}, u32[]{:S(2)}) %collective-permute-start.14) | collective-permute-done | bytes 69664 | tf_op jit(solution)/shard_map/ppermute | solution.py:639
  45.0 1.1 %collective-permute-start.18 = (bf16[272,128]{1,0:T(8,128)(2,1)S(1)}, bf16[272,128]{1,0:T(8,128)(2,1)S(1)}, u32[]{:S(2)}, u32[]{:S(2)}) collective-permute-start(bf16[272,128]{1,0:T(8,128)(2,1)S(1)} %add_convert_fusion), channel_id=1, source_target_pairs={{0,8},{4,12},{8,0},{12,4},{16,24},{20,28},{24,16},{28,20},{1,9},{5... | collective-permute-start | bytes 208904 | tf_op jit(solution)/shard_map/ppermute | solution.py:633
  46.8 1.8 %collective-permute-start.16 = (bf16[272,128]{1,0:T(8,128)(2,1)S(1)}, bf16[272,128]{1,0:T(8,128)(2,1)S(1)}, u32[]{:S(2)}, u32[]{:S(2)}) collective-permute-start(bf16[272,128]{1,0:T(8,128)(2,1)S(1)} %add_convert_fusion), channel_id=1, source_target_pairs={{0,24},{4,28},{8,16},{12,20},{16,8},{20,12},{24,0},{28,4},{1,25},{... | collective-permute-start | bytes 208904 | tf_op jit(solution)/shard_map/ppermute | solution.py:633
  48.5 0.8 %collective-permute-done.18 = bf16[272,128]{1,0:T(8,128)(2,1)S(1)} collective-permute-done((bf16[272,128]{1,0:T(8,128)(2,1)S(1)}, bf16[272,128]{1,0:T(8,128)(2,1)S(1)}, u32[]{:S(2)}, u32[]{:S(2)}) %collective-permute-start.18) | collective-permute-done | bytes 69664 | tf_op jit(solution)/shard_map/ppermute | solution.py:633
  49.4 1.0 %collective-permute-done.17 = bf16[272,128]{1,0:T(8,128)(2,1)S(1)} collective-permute-done((bf16[272,128]{1,0:T(8,128)(2,1)S(1)}, bf16[272,128]{1,0:T(8,128)(2,1)S(1)}, u32[]{:S(2)}, u32[]{:S(2)}) %collective-permute-start.17) | collective-permute-done | bytes 69664 | tf_op jit(solution)/shard_map/ppermute | solution.py:633
  50.4 1.6 %collective-permute-done.16 = bf16[272,128]{1,0:T(8,128)(2,1)S(1)} collective-permute-done((bf16[272,128]{1,0:T(8,128)(2,1)S(1)}, bf16[272,128]{1,0:T(8,128)(2,1)S(1)}, u32[]{:S(2)}, u32[]{:S(2)}) %collective-permute-start.16) | collective-permute-done | bytes 69664 | tf_op jit(solution)/shard_map/ppermute | solution.py:633
  52.1 1.5 %collective-permute-done.19.got_ref = bf16[4,272,128]{2,1,0:T(8,128)(2,1)S(1)} collective-permute-done((bf16[4,272,128]{2,1,0:T(8,128)(2,1)S(1)}, bf16[4,272,128]{2,1,0:T(8,128)(2,1)S(1)}, u32[]{:S(2)}, u32[]{:S(2)}) %collective-permute-start.19) | collective-permute-done | bytes 278560 | tf_op jit(solution)/shard_map/ppermute | solution.py:636
  53.6 1.6 %shard_map.66 = (f32[64,864]{1,0:T(8,128)}, f32[1728,128]{1,0:T(8,128)}) custom-call(s32[2]{0:T(128)S(1)} %pad_add_fusion.place_ref, bf16[4,272,128]{2,1,0:T(8,128)(2,1)S(1)} %pad_maximum_fusion.keep_ref, bf16[4,272,128]{2,1,0:T(8,128)(2,1)S(1)} %collective-permute-done.19.got_ref), custom_call_target="tpu_custom_call" | custom-call | tf_op jit(solution)/shard_map/pallas_call | solution.py:649
  (38 shorter events, 6.4 us)
Async XLA Ops:
  2.8 6.7 %collective-permute-start.1 = (bf16[17,4,1024]{2,1,0:T(4,128)(2,1)S(1)}, bf16[17,4,1024]{2,1,0:T(4,128)(2,1)S(1)}, u32[]{:S(2)}, u32[]{:S(2)}) collective-permute-start(bf16[17,4,1024]{2,1,0:T(4,128)(2,1)S(1)} %get-tuple-element.40), channel_id=1, source_target_pairs={{0,16},{16,0},{1,17},{17,1},{2,18},{18,2},{3,19},{19,3},{4,20},{20... | collective-permute-start | bytes 417800 | tf_op jit(solution)/shard_map/ppermute | solution.py:585
  6.7 7.4 %collective-permute-start = (bf16[34,4,1024]{2,1,0:T(4,128)(2,1)S(1)}, bf16[34,4,1024]{2,1,0:T(4,128)(2,1)S(1)}, u32[]{:S(2)}, u32[]{:S(2)}) collective-permute-start(bf16[34,4,1024]{2,1,0:T(4,128)(2,1)S(1)} %get-tuple-element.39), channel_id=1, source_target_pairs={{4,8},{5,9},{6,10},{7,11},{20,24},{21,25},{22,26},{23,27},{8,4},{9... | collective-permute-start | bytes 835592 | tf_op jit(solution)/shard_map/ppermute | solution.py:589
  8.3 5.6 %collective-permute-start.2 = (bf16[34,4,1024]{2,1,0:T(4,128)(2,1)S(1)}, bf16[34,4,1024]{2,1,0:T(4,128)(2,1)S(1)}, u32[]{:S(2)}, u32[]{:S(2)}) collective-permute-start(bf16[34,4,1024]{2,1,0:T(4,128)(2,1)S(1)} %get-tuple-element.50), channel_id=1, source_target_pairs={{0,4},{8,12},{4,0},{12,8},{1,5},{9,13},{5,1},{13,9},{2,6},{10,14},... | collective-permute-start | bytes 835592 | tf_op jit(solution)/shard_map/ppermute | solution.py:590
  9.7 4.4 %collective-permute-start.4 = (bf16[5,4,1024]{2,1,0:T(4,128)(2,1)S(1)}, bf16[5,4,1024]{2,1,0:T(4,128)(2,1)S(1)}, u32[]{:S(2)}, u32[]{:S(2)}) collective-permute-start(bf16[5,4,1024]{2,1,0:T(4,128)(2,1)S(1)} %get-tuple-element.81), channel_id=1, source_target_pairs={{4,8},{8,4},{0,16},{12,28},{20,24},{24,20},{16,0},{28,12},{5,9},{9... | collective-permute-start | bytes 122888 | tf_op jit(solution)/shard_map/ppermute | solution.py:606
  11.5 2.6 %collective-permute-start.3 = (bf16[5,4,1024]{2,1,0:T(4,128)(2,1)S(1)}, bf16[5,4,1024]{2,1,0:T(4,128)(2,1)S(1)}, u32[]{:S(2)}, u32[]{:S(2)}) collective-permute-start(bf16[5,4,1024]{2,1,0:T(4,128)(2,1)S(1)} %get-tuple-element.82), channel_id=1, source_target_pairs={{0,4},{8,12},{4,0},{12,8},{1,5},{9,13},{5,1},{13,9},{2,6},{10,14},... | collective-permute-start | bytes 122888 | tf_op jit(solution)/shard_map/ppermute | solution.py:605
  11.6 9.5 %collective-permute-start.5 = (bf16[34,16,128]{2,1,0:T(8,128)(2,1)S(1)}, bf16[34,16,128]{2,1,0:T(8,128)(2,1)S(1)}, u32[]{:S(2)}, u32[]{:S(2)}) collective-permute-start(bf16[34,16,128]{2,1,0:T(8,128)(2,1)S(1)} %get-tuple-element.62), channel_id=1, source_target_pairs={{0,1},{2,3},{1,0},{3,2},{4,5},{6,7},{5,4},{7,6},{8,9},{10,11},{9,8... | collective-permute-start | bytes 417800 | tf_op jit(solution)/shard_map/ppermute | solution.py:583
  13.9 7.3 %collective-permute-start.6 = (bf16[34,16,128]{2,1,0:T(8,128)(2,1)S(1)}, bf16[34,16,128]{2,1,0:T(8,128)(2,1)S(1)}, u32[]{:S(2)}, u32[]{:S(2)}) collective-permute-start(bf16[34,16,128]{2,1,0:T(8,128)(2,1)S(1)} %get-tuple-element.63), channel_id=1, source_target_pairs={{1,2},{2,1},{0,4},{3,7},{5,6},{6,5},{4,0},{7,3},{9,10},{10,9},{8,1... | collective-permute-start | bytes 417800 | tf_op jit(solution)/shard_map/ppermute | solution.py:583
  14.8 6.3 %collective-permute-start.7 = (bf16[46,8,128]{2,1,0:T(8,128)(2,1)S(1)}, bf16[46,8,128]{2,1,0:T(8,128)(2,1)S(1)}, u32[]{:S(2)}, u32[]{:S(2)}) collective-permute-start(bf16[46,8,128]{2,1,0:T(8,128)(2,1)S(1)} %get-tuple-element.64), channel_id=1, source_target_pairs={{0,1},{2,3},{1,0},{3,2},{4,5},{6,7},{5,4},{7,6},{8,9},{10,11},{9,8... | collective-permute-start | bytes 282632 | tf_op jit(solution)/shard_map/ppermute | solution.py:583
  17.9 3.3 %collective-permute-start.8 = (bf16[46,8,128]{2,1,0:T(8,128)(2,1)S(1)}, bf16[46,8,128]{2,1,0:T(8,128)(2,1)S(1)}, u32[]{:S(2)}, u32[]{:S(2)}) collective-permute-start(bf16[46,8,128]{2,1,0:T(8,128)(2,1)S(1)} %get-tuple-element.65), channel_id=1, source_target_pairs={{1,2},{2,1},{0,4},{3,7},{5,6},{6,5},{4,0},{7,3},{9,10},{10,9},{8,1... | collective-permute-start | bytes 282632 | tf_op jit(solution)/shard_map/ppermute | solution.py:583
  26.9 1.7 %collective-permute-start.9 = (bf16[4,272,128]{2,1,0:T(8,128)(2,1)S(1)}, bf16[4,272,128]{2,1,0:T(8,128)(2,1)S(1)}, u32[]{:S(2)}, u32[]{:S(2)}) collective-permute-start(bf16[4,272,128]{2,1,0:T(8,128)(2,1)S(1)} %get-tuple-element.69), channel_id=1, source_target_pairs={{0,4},{4,0},{8,12},{12,8},{16,20},{20,16},{24,28},{28,24},{1,5},{5... | collective-permute-start | bytes 835592 | tf_op jit(solution)/shard_map/ppermute | solution.py:636
  28.8 4.8 %collective-permute-start.10 = (bf16[272,128]{1,0:T(8,128)(2,1)S(1)}, bf16[272,128]{1,0:T(8,128)(2,1)S(1)}, u32[]{:S(2)}, u32[]{:S(2)}) collective-permute-start(bf16[272,128]{1,0:T(8,128)(2,1)S(1)} %get-tuple-element.74), channel_id=1, source_target_pairs={{0,8},{4,12},{8,0},{12,4},{16,24},{20,28},{24,16},{28,20},{1,9},{5... | collective-permute-start | bytes 208904 | tf_op jit(solution)/shard_map/ppermute | solution.py:633
  29.0 4.6 %collective-permute-start.12 = (bf16[272,128]{1,0:T(8,128)(2,1)S(1)}, bf16[272,128]{1,0:T(8,128)(2,1)S(1)}, u32[]{:S(2)}, u32[]{:S(2)}) collective-permute-start(bf16[272,128]{1,0:T(8,128)(2,1)S(1)} %get-tuple-element.75), channel_id=1, source_target_pairs={{0,16},{4,20},{8,24},{12,28},{16,0},{20,4},{24,8},{28,12},{1,17},{... | collective-permute-start | bytes 208904 | tf_op jit(solution)/shard_map/ppermute | solution.py:633
  30.5 5.3 %collective-permute-start.11 = (bf16[272,128]{1,0:T(8,128)(2,1)S(1)}, bf16[272,128]{1,0:T(8,128)(2,1)S(1)}, u32[]{:S(2)}, u32[]{:S(2)}) collective-permute-start(bf16[272,128]{1,0:T(8,128)(2,1)S(1)} %get-tuple-element.76), channel_id=1, source_target_pairs={{0,24},{4,28},{8,16},{12,20},{16,8},{20,12},{24,0},{28,4},{1,25},{... | collective-permute-start | bytes 208904 | tf_op jit(solution)/shard_map/ppermute | solution.py:633
  35.8 6.9 %collective-permute-start.15 = (bf16[272,128]{1,0:T(8,128)(2,1)S(1)}, bf16[272,128]{1,0:T(8,128)(2,1)S(1)}, u32[]{:S(2)}, u32[]{:S(2)}) collective-permute-start(bf16[272,128]{1,0:T(8,128)(2,1)S(1)} %fusion.2), channel_id=1, source_target_pairs={{0,3},{1,2},{2,1},{3,0},{4,7},{5,6},{6,5},{7,4},{8,11},{9,10},{10,... | collective-permute-start | bytes 208904 | tf_op jit(solution)/shard_map/ppermute | solution.py:639
  38.2 6.7 %collective-permute-start.14 = (bf16[272,128]{1,0:T(8,128)(2,1)S(1)}, bf16[272,128]{1,0:T(8,128)(2,1)S(1)}, u32[]{:S(2)}, u32[]{:S(2)}) collective-permute-start(bf16[272,128]{1,0:T(8,128)(2,1)S(1)} %fusion.2), channel_id=1, source_target_pairs={{0,2},{1,3},{2,0},{3,1},{4,6},{5,7},{6,4},{7,5},{8,10},{9,11},{10,... | collective-permute-start | bytes 208904 | tf_op jit(solution)/shard_map/ppermute | solution.py:639
  39.5 5.5 %collective-permute-start.13 = (bf16[272,128]{1,0:T(8,128)(2,1)S(1)}, bf16[272,128]{1,0:T(8,128)(2,1)S(1)}, u32[]{:S(2)}, u32[]{:S(2)}) collective-permute-start(bf16[272,128]{1,0:T(8,128)(2,1)S(1)} %fusion.2), channel_id=1, source_target_pairs={{0,1},{1,0},{2,3},{3,2},{4,5},{5,4},{6,7},{7,6},{8,9},{9,8},{10,11... | collective-permute-start | bytes 208904 | tf_op jit(solution)/shard_map/ppermute | solution.py:639
  45.0 4.4 %collective-permute-start.18 = (bf16[272,128]{1,0:T(8,128)(2,1)S(1)}, bf16[272,128]{1,0:T(8,128)(2,1)S(1)}, u32[]{:S(2)}, u32[]{:S(2)}) collective-permute-start(bf16[272,128]{1,0:T(8,128)(2,1)S(1)} %add_convert_fusion), channel_id=1, source_target_pairs={{0,8},{4,12},{8,0},{12,4},{16,24},{20,28},{24,16},{28,20},{1,9},{5... | collective-permute-start | bytes 208904 | tf_op jit(solution)/shard_map/ppermute | solution.py:633
  46.1 4.3 %collective-permute-start.17 = (bf16[272,128]{1,0:T(8,128)(2,1)S(1)}, bf16[272,128]{1,0:T(8,128)(2,1)S(1)}, u32[]{:S(2)}, u32[]{:S(2)}) collective-permute-start(bf16[272,128]{1,0:T(8,128)(2,1)S(1)} %add_convert_fusion), channel_id=1, source_target_pairs={{0,16},{4,20},{8,24},{12,28},{16,0},{20,4},{24,8},{28,12},{1,17},{... | collective-permute-start | bytes 208904 | tf_op jit(solution)/shard_map/ppermute | solution.py:633
  46.8 5.2 %collective-permute-start.16 = (bf16[272,128]{1,0:T(8,128)(2,1)S(1)}, bf16[272,128]{1,0:T(8,128)(2,1)S(1)}, u32[]{:S(2)}, u32[]{:S(2)}) collective-permute-start(bf16[272,128]{1,0:T(8,128)(2,1)S(1)} %add_convert_fusion), channel_id=1, source_target_pairs={{0,24},{4,28},{8,16},{12,20},{16,8},{20,12},{24,0},{28,4},{1,25},{... | collective-permute-start | bytes 208904 | tf_op jit(solution)/shard_map/ppermute | solution.py:633
  52.0 1.6 %collective-permute-start.19 = (bf16[4,272,128]{2,1,0:T(8,128)(2,1)S(1)}, bf16[4,272,128]{2,1,0:T(8,128)(2,1)S(1)}, u32[]{:S(2)}, u32[]{:S(2)}) collective-permute-start(bf16[4,272,128]{2,1,0:T(8,128)(2,1)S(1)} %pad_maximum_fusion.keep_ref), channel_id=1, source_target_pairs={{0,4},{4,0},{8,12},{12,8},{16,20},{20,16},{24,28},{28,24},{1,5},{5... | collective-permute-start | bytes 835592 | tf_op jit(solution)/shard_map/ppermute | solution.py:636

commit v13 on v12

--- a/solution.py
+++ b/solution.py
@@ -116,46 +116,56 @@
 
 
 def pack_corners(flag_ref, row_b_ref, row_a_ref, dep_ref, edge_a_ref, edge_b_ref, col_a_ref, col_b_ref):
-    row_even, col_even, col_inner = flag_ref[1] == 0, flag_ref[2] == 0, flag_ref[4] != 0
-    width = dep_ref.shape[2]
-    groups = row_a_ref.shape[0]
-    planes = (groups * 16) // 17
-    faces = (slice(0, LANES), slice(width - LANES, width))
-
-    def store(n, left, right):
-        col_a_ref[n] = jnp.where(col_even, right, left).astype(BF16)
-        col_b_ref[n] = jnp.where(col_inner, jnp.where(col_even, left, right), 0.0).astype(BF16)
-
-    def lower_upper(a_ref, b_ref, source, target):
-        values = []
-        for lanes in faces:
-            a, b = a_ref[source, :, lanes].astype(F32), b_ref[source, :, lanes].astype(F32)
-            values.append(jnp.concatenate([jnp.where(row_even, b, a), jnp.where(row_even, a, b)], axis=0))
-        store(target, *values)
-
-    def plane(d, carry):
-        lower_upper(row_a_ref, row_b_ref, d, d)
-        return carry
-
-    lax.fori_loop(0, planes, plane, 0, unroll=4)
-    for q in range(4):
-        lower_upper(edge_a_ref, edge_b_ref, q, planes + q)
-        for n in range(2):
-            units = range(4 * q + 2 * n, 4 * q + 2 * n + 2)
-            store(
-                planes + 4 + 2 * q + n,
-                *[jnp.concatenate([dep_ref[u, :, lanes].astype(F32) for u in units], axis=0) for lanes in faces],
-            )
-    lanes = faces[0]
-    tops = [
-        jnp.where(row_even, row_a_ref[g, :, lanes].astype(F32), row_b_ref[g, :, lanes].astype(F32))
-        for g in range(planes, groups)
-    ]
-    corner = jnp.where(row_even, edge_a_ref[4, :, lanes].astype(F32), edge_b_ref[4, :, lanes].astype(F32))
-    own = dep_ref[16, :, lanes].astype(F32)
-    for n, values in enumerate((jnp.concatenate(tops, axis=0), jnp.concatenate([own, corner], axis=0))):
-        col_a_ref[planes + 12 + n] = values.astype(BF16)
-        col_b_ref[planes + 12 + n] = jnp.where(col_inner, values, 0.0).astype(BF16)
+    col_inner = flag_ref[4] != 0
+
+    def pick(even, a, b):
+        return a if even else b
+
+    def run(row_even, col_even):
+        width = dep_ref.shape[2]
+        groups = row_a_ref.shape[0]
+        planes = (groups * 16) // 17
+        faces = (slice(0, LANES), slice(width - LANES, width))
+
+        def store(n, left, right):
+            col_a_ref[n] = pick(col_even, right, left).astype(BF16)
+            col_b_ref[n] = jnp.where(col_inner, pick(col_even, left, right), 0.0).astype(BF16)
+
+        def lower_upper(a_ref, b_ref, source, target):
+            values = []
+            for lanes in faces:
+                a, b = a_ref[source, :, lanes].astype(F32), b_ref[source, :, lanes].astype(F32)
+                values.append(jnp.concatenate([pick(row_even, b, a), pick(row_even, a, b)], axis=0))
+            store(target, *values)
+
+        def plane(d, carry):
+            lower_upper(row_a_ref, row_b_ref, d, d)
+            return carry
+
+        lax.fori_loop(0, planes, plane, 0, unroll=4)
+        for q in range(4):
+            lower_upper(edge_a_ref, edge_b_ref, q, planes + q)
+            for n in range(2):
+                units = range(4 * q + 2 * n, 4 * q + 2 * n + 2)
+                store(
+                    planes + 4 + 2 * q + n,
+                    *[jnp.concatenate([dep_ref[u, :, lanes].astype(F32) for u in units], axis=0) for lanes in faces],
+                )
+        lanes = faces[0]
+        tops = [
+            pick(row_even, row_a_ref[g, :, lanes].astype(F32), row_b_ref[g, :, lanes].astype(F32))
+            for g in range(planes, groups)
+        ]
+        corner = pick(row_even, edge_a_ref[4, :, lanes].astype(F32), edge_b_ref[4, :, lanes].astype(F32))
+        own = dep_ref[16, :, lanes].astype(F32)
+        for n, values in enumerate((jnp.concatenate(tops, axis=0), jnp.concatenate([own, corner], axis=0))):
+            col_a_ref[planes + 12 + n] = values.astype(BF16)
+            col_b_ref[planes + 12 + n] = jnp.where(col_inner, values, 0.0).astype(BF16)
+
+    for rows in (True, False):
+        for cols in (True, False):
+            here = jnp.logical_and((flag_ref[1] == 0) == rows, (flag_ref[2] == 0) == cols)
+            pl.when(here)(functools.partial(run, rows, cols))
 
 
 def bands(first_ref, second_ref, w1_ref, w2_ref, w2b_ref):

time: 55.4 us -> 55.4 us (level)
  no operation moved by 1% of the time
where the time goes in v13:
time: 55.4 us; the launch traced here: 55.3 us
  starting transfers between devices  23.7 us (43%)
  Pallas kernels  15.4 us (28%)
  waiting for transfers between devices  14.8 us (27%)
  between operations  0.86 us (2%)
    ppermute x6, starting transfers between devices, to_square(): return lax.ppermute(block, ('depth', 'row'), route)  7.12 us
    ppermute x6, waiting for transfers between devices, to_square(): return lax.ppermute(block, ('depth', 'row'), route)  6.83 us
    pallas_call x1, Pallas kernels, local_grads(): pl.pallas_call(body, out_shape=[jax.ShapeDtypeStruct((squares, rows // (2...  5.73 us
    ppermute x4, starting transfers between devices, to_col(): return lax.ppermute(block, ('row', 'col'), pairs_of_lines(rows, cols, kind))  4.86 us
    ppermute x3, waiting for transfers between devices, along_col(): return lax.ppermute(block, 'col', [(i, i ^ n) for i in range(cols)])  4.7 us
    ppermute x3, starting transfers between devices, along_col(): return lax.ppermute(block, 'col', [(i, i ^ n) for i in range(cols)])  4.45 us
    pallas_call x1, Pallas kernels, local_grads(): pl.pallas_call(own_blocks, out_shape=[jax.ShapeDtypeStruct((3, planes + 9...  3.26 us
    ppermute x1, starting transfers between devices, shards(): dep = lax.ppermute(dep, 'depth', [(0, 1), (1, 0)])  3.03 us
  transfers between devices with their start and end apart: 20, of which 10 were waited for; matrix products, arithmetic and copies ran while one was open for 0% of the time, Pallas kernels for 11%

profile of v13, /device:TPU:0, one launch (start us, length us, event | category | flops | bytes accessed | tf_op | source)
XLA Modules:
  0.0 55.3 jit_solution(10967771834176480694)
XLA Ops:
  0.7 2.0 %shard_map.59 = (bf16[32,16,1024]{2,1,0:T(8,128)(2,1)S(1)}, bf16[8,4,1024]{2,1,0:T(4,128)(2,1)S(1)}, bf16[64,864]{1,0:T(8,128)(2,1)S(1)}, bf16[1728,128]{1,0:T(8,128)(2,1)S(1)}, bf16[17,4,1024]{2,1,0:T(4,128)(2,1)S(1)}) custom-call(s32[5]{0:T(128)S(1)} %stack.58.flag_ref, bf16[32,16,1024]{2,1,0:T(8,128)(2,1)} %vol_hbm.1, bf16[8,4,1024]{2,1,0:T(4,128)(2,1)} %cot_hbm.1, ...), custom_call_target="tpu_custom_call" | custom-call | tf_op jit(solution)/shard_map/pallas_call | solution.py:576
  2.8 3.0 %collective-permute-start.1 = (bf16[17,4,1024]{2,1,0:T(4,128)(2,1)S(1)}, bf16[17,4,1024]{2,1,0:T(4,128)(2,1)S(1)}, u32[]{:S(2)}, u32[]{:S(2)}) collective-permute-start(bf16[17,4,1024]{2,1,0:T(4,128)(2,1)S(1)} %get-tuple-element.40), channel_id=1, source_target_pairs={{0,16},{16,0},{1,17},{17,1},{2,18},{18,2},{3,19},{19,3},{4,20},{20... | collective-permute-start | bytes 417800 | tf_op jit(solution)/shard_map/ppermute | solution.py:595
  5.8 0.8 %shard_map.60 = (bf16[34,4,1024]{2,1,0:T(4,128)(2,1)S(1)}, bf16[34,4,1024]{2,1,0:T(4,128)(2,1)S(1)}) custom-call(s32[5]{0:T(128)S(1)} %stack.58.flag_ref, bf16[32,16,1024]{2,1,0:T(8,128)(2,1)S(1)} %get-tuple-element.56.vol_ref, bf16[8,4,1024]{2,1,0:T(4,128)(2,1)S(1)} %get-tuple-element.38.cot_ref), custom_call_target="tpu_custom_call" | custom-call | tf_op jit(solution)/shard_map/pallas_call | solution.py:584
  6.7 1.6 %collective-permute-start = (bf16[34,4,1024]{2,1,0:T(4,128)(2,1)S(1)}, bf16[34,4,1024]{2,1,0:T(4,128)(2,1)S(1)}, u32[]{:S(2)}, u32[]{:S(2)}) collective-permute-start(bf16[34,4,1024]{2,1,0:T(4,128)(2,1)S(1)} %get-tuple-element.39), channel_id=1, source_target_pairs={{4,8},{5,9},{6,10},{7,11},{20,24},{21,25},{22,26},{23,27},{8,4},{9... | collective-permute-start | bytes 835592 | tf_op jit(solution)/shard_map/ppermute | solution.py:599
  9.7 1.8 %collective-permute-start.4 = (bf16[5,4,1024]{2,1,0:T(4,128)(2,1)S(1)}, bf16[5,4,1024]{2,1,0:T(4,128)(2,1)S(1)}, u32[]{:S(2)}, u32[]{:S(2)}) collective-permute-start(bf16[5,4,1024]{2,1,0:T(4,128)(2,1)S(1)} %get-tuple-element.81), channel_id=1, source_target_pairs={{4,8},{8,4},{0,16},{12,28},{20,24},{24,20},{16,0},{28,12},{5,9},{9... | collective-permute-start | bytes 122888 | tf_op jit(solution)/shard_map/ppermute | solution.py:616
  11.6 1.6 %collective-permute-start.5 = (bf16[34,16,128]{2,1,0:T(8,128)(2,1)S(1)}, bf16[34,16,128]{2,1,0:T(8,128)(2,1)S(1)}, u32[]{:S(2)}, u32[]{:S(2)}) collective-permute-start(bf16[34,16,128]{2,1,0:T(8,128)(2,1)S(1)} %get-tuple-element.62), channel_id=1, source_target_pairs={{0,1},{2,3},{1,0},{3,2},{4,5},{6,7},{5,4},{7,6},{8,9},{10,11},{9,8... | collective-permute-start | bytes 417800 | tf_op jit(solution)/shard_map/ppermute | solution.py:593
  14.8 3.1 %collective-permute-start.7 = (bf16[46,8,128]{2,1,0:T(8,128)(2,1)S(1)}, bf16[46,8,128]{2,1,0:T(8,128)(2,1)S(1)}, u32[]{:S(2)}, u32[]{:S(2)}) collective-permute-start(bf16[46,8,128]{2,1,0:T(8,128)(2,1)S(1)} %get-tuple-element.64), channel_id=1, source_target_pairs={{0,1},{2,3},{1,0},{3,2},{4,5},{6,7},{5,4},{7,6},{8,9},{10,11},{9,8... | collective-permute-start | bytes 282632 | tf_op jit(solution)/shard_map/ppermute | solution.py:593
  17.9 3.3 %shard_map.64 = (bf16[3,41,8,16,128]{4,3,2,1,0:T(8,128)(2,1)S(1)}, f32[20,8,16,256]{3,2,1,0:T(8,128)S(1)}, f32[3,19,7,8,128]{4,3,2,1,0:T(8,128)S(1)}, f32[16,7,16,128]{3,2,1,0:T(8,128)S(1)}) custom-call(s32[5]{0:T(128)S(1)} %stack.58.flag_ref, bf16[32,16,1024]{2,1,0:T(8,128)(2,1)S(1)} %get-tuple-element.56.vol_ref, ...), custom_call_target="tpu_custom_call" | custom-call | flops 2000000000 | bytes 10000000 | tf_op jit(solution)/shard_map/pallas_call | solution.py:520
  21.2 5.7 %shard_map.65 = (f32[4,272,128]{2,1,0:T(8,128)S(1)}, bf16[4,272,128]{2,1,0:T(8,128)(2,1)S(1)}) custom-call(s32[5]{0:T(128)S(1)} %stack.58.flag_ref, s32[2]{0:T(128)S(1)} %pad_add_fusion.place_ref, bf16[3,41,8,16,128]{4,3,2,1,0:T(8,128)(2,1)S(1)} %get-tuple-element.58.tiles, f32[20,8,16,256]{3,2,1,0:T(8,128)S(1)} %get-tuple-element.59.parts, ...), custom_call_target="tpu_custom_call" | custom-call | flops 4000000000 | bytes 10000000 | tf_op jit(solution)/shard_map/pallas_call | solution.py:547
  27.5 1.2 %collective-permute-done.9 = bf16[4,272,128]{2,1,0:T(8,128)(2,1)S(1)} collective-permute-done((bf16[4,272,128]{2,1,0:T(8,128)(2,1)S(1)}, bf16[4,272,128]{2,1,0:T(8,128)(2,1)S(1)}, u32[]{:S(2)}, u32[]{:S(2)}) %collective-permute-start.9) | collective-permute-done | bytes 278560 | tf_op jit(solution)/shard_map/ppermute | solution.py:646
  29.0 1.4 %collective-permute-start.12 = (bf16[272,128]{1,0:T(8,128)(2,1)S(1)}, bf16[272,128]{1,0:T(8,128)(2,1)S(1)}, u32[]{:S(2)}, u32[]{:S(2)}) collective-permute-start(bf16[272,128]{1,0:T(8,128)(2,1)S(1)} %get-tuple-element.75), channel_id=1, source_target_pairs={{0,16},{4,20},{8,24},{12,28},{16,0},{20,4},{24,8},{28,12},{1,17},{... | collective-permute-start | bytes 208904 | tf_op jit(solution)/shard_map/ppermute | solution.py:643
  30.4 1.9 %collective-permute-start.11 = (bf16[272,128]{1,0:T(8,128)(2,1)S(1)}, bf16[272,128]{1,0:T(8,128)(2,1)S(1)}, u32[]{:S(2)}, u32[]{:S(2)}) collective-permute-start(bf16[272,128]{1,0:T(8,128)(2,1)S(1)} %get-tuple-element.76), channel_id=1, source_target_pairs={{0,24},{4,28},{8,16},{12,20},{16,8},{20,12},{24,0},{28,4},{1,25},{... | collective-permute-start | bytes 208904 | tf_op jit(solution)/shard_map/ppermute | solution.py:643
  32.4 1.2 %collective-permute-done.10 = bf16[272,128]{1,0:T(8,128)(2,1)S(1)} collective-permute-done((bf16[272,128]{1,0:T(8,128)(2,1)S(1)}, bf16[272,128]{1,0:T(8,128)(2,1)S(1)}, u32[]{:S(2)}, u32[]{:S(2)}) %collective-permute-start.10) | collective-permute-done | bytes 69664 | tf_op jit(solution)/shard_map/ppermute | solution.py:643
  33.6 2.1 %collective-permute-done.11 = bf16[272,128]{1,0:T(8,128)(2,1)S(1)} collective-permute-done((bf16[272,128]{1,0:T(8,128)(2,1)S(1)}, bf16[272,128]{1,0:T(8,128)(2,1)S(1)}, u32[]{:S(2)}, u32[]{:S(2)}) %collective-permute-start.11) | collective-permute-done | bytes 69664 | tf_op jit(solution)/shard_map/ppermute | solution.py:643
  35.8 2.4 %collective-permute-start.15 = (bf16[272,128]{1,0:T(8,128)(2,1)S(1)}, bf16[272,128]{1,0:T(8,128)(2,1)S(1)}, u32[]{:S(2)}, u32[]{:S(2)}) collective-permute-start(bf16[272,128]{1,0:T(8,128)(2,1)S(1)} %fusion.2), channel_id=1, source_target_pairs={{0,3},{1,2},{2,1},{3,0},{4,7},{5,6},{6,5},{7,4},{8,11},{9,10},{10,... | collective-permute-start | bytes 208904 | tf_op jit(solution)/shard_map/ppermute | solution.py:649
  38.2 1.3 %collective-permute-start.14 = (bf16[272,128]{1,0:T(8,128)(2,1)S(1)}, bf16[272,128]{1,0:T(8,128)(2,1)S(1)}, u32[]{:S(2)}, u32[]{:S(2)}) collective-permute-start(bf16[272,128]{1,0:T(8,128)(2,1)S(1)} %fusion.2), channel_id=1, source_target_pairs={{0,2},{1,3},{2,0},{3,1},{4,6},{5,7},{6,4},{7,5},{8,10},{9,11},{10,... | collective-permute-start | bytes 208904 | tf_op jit(solution)/shard_map/ppermute | solution.py:649
  40.2 2.4 %collective-permute-done.15 = bf16[272,128]{1,0:T(8,128)(2,1)S(1)} collective-permute-done((bf16[272,128]{1,0:T(8,128)(2,1)S(1)}, bf16[272,128]{1,0:T(8,128)(2,1)S(1)}, u32[]{:S(2)}, u32[]{:S(2)}) %collective-permute-start.15) | collective-permute-done | bytes 69664 | tf_op jit(solution)/shard_map/ppermute | solution.py:649
  42.6 2.3 %collective-permute-done.14 = bf16[272,128]{1,0:T(8,128)(2,1)S(1)} collective-permute-done((bf16[272,128]{1,0:T(8,128)(2,1)S(1)}, bf16[272,128]{1,0:T(8,128)(2,1)S(1)}, u32[]{:S(2)}, u32[]{:S(2)}) %collective-permute-start.14) | collective-permute-done | bytes 69664 | tf_op jit(solution)/shard_map/ppermute | solution.py:649
  45.0 1.1 %collective-permute-start.18 = (bf16[272,128]{1,0:T(8,128)(2,1)S(1)}, bf16[272,128]{1,0:T(8,128)(2,1)S(1)}, u32[]{:S(2)}, u32[]{:S(2)}) collective-permute-start(bf16[272,128]{1,0:T(8,128)(2,1)S(1)} %add_convert_fusion), channel_id=1, source_target_pairs={{0,8},{4,12},{8,0},{12,4},{16,24},{20,28},{24,16},{28,20},{1,9},{5... | collective-permute-start | bytes 208904 | tf_op jit(solution)/shard_map/ppermute | solution.py:643
  46.8 1.8 %collective-permute-start.16 = (bf16[272,128]{1,0:T(8,128)(2,1)S(1)}, bf16[272,128]{1,0:T(8,128)(2,1)S(1)}, u32[]{:S(2)}, u32[]{:S(2)}) collective-permute-start(bf16[272,128]{1,0:T(8,128)(2,1)S(1)} %add_convert_fusion), channel_id=1, source_target_pairs={{0,24},{4,28},{8,16},{12,20},{16,8},{20,12},{24,0},{28,4},{1,25},{... | collective-permute-start | bytes 208904 | tf_op jit(solution)/shard_map/ppermute | solution.py:643
  49.4 1.0 %collective-permute-done.17 = bf16[272,128]{1,0:T(8,128)(2,1)S(1)} collective-permute-done((bf16[272,128]{1,0:T(8,128)(2,1)S(1)}, bf16[272,128]{1,0:T(8,128)(2,1)S(1)}, u32[]{:S(2)}, u32[]{:S(2)}) %collective-permute-start.17) | collective-permute-done | bytes 69664 | tf_op jit(solution)/shard_map/ppermute | solution.py:643
  50.4 1.6 %collective-permute-done.16 = bf16[272,128]{1,0:T(8,128)(2,1)S(1)} collective-permute-done((bf16[272,128]{1,0:T(8,128)(2,1)S(1)}, bf16[272,128]{1,0:T(8,128)(2,1)S(1)}, u32[]{:S(2)}, u32[]{:S(2)}) %collective-permute-start.16) | collective-permute-done | bytes 69664 | tf_op jit(solution)/shard_map/ppermute | solution.py:643
  52.1 1.5 %collective-permute-done.19.got_ref = bf16[4,272,128]{2,1,0:T(8,128)(2,1)S(1)} collective-permute-done((bf16[4,272,128]{2,1,0:T(8,128)(2,1)S(1)}, bf16[4,272,128]{2,1,0:T(8,128)(2,1)S(1)}, u32[]{:S(2)}, u32[]{:S(2)}) %collective-permute-start.19) | collective-permute-done | bytes 278560 | tf_op jit(solution)/shard_map/ppermute | solution.py:646
  53.6 1.6 %shard_map.66 = (f32[64,864]{1,0:T(8,128)}, f32[1728,128]{1,0:T(8,128)}) custom-call(s32[2]{0:T(128)S(1)} %pad_add_fusion.place_ref, bf16[4,272,128]{2,1,0:T(8,128)(2,1)S(1)} %pad_maximum_fusion.keep_ref, bf16[4,272,128]{2,1,0:T(8,128)(2,1)S(1)} %collective-permute-done.19.got_ref), custom_call_target="tpu_custom_call" | custom-call | tf_op jit(solution)/shard_map/pallas_call | solution.py:659
  (38 shorter events, 6.5 us)
Async XLA Ops:
  2.8 6.7 %collective-permute-start.1 = (bf16[17,4,1024]{2,1,0:T(4,128)(2,1)S(1)}, bf16[17,4,1024]{2,1,0:T(4,128)(2,1)S(1)}, u32[]{:S(2)}, u32[]{:S(2)}) collective-permute-start(bf16[17,4,1024]{2,1,0:T(4,128)(2,1)S(1)} %get-tuple-element.40), channel_id=1, source_target_pairs={{0,16},{16,0},{1,17},{17,1},{2,18},{18,2},{3,19},{19,3},{4,20},{20... | collective-permute-start | bytes 417800 | tf_op jit(solution)/shard_map/ppermute | solution.py:595
  6.7 7.4 %collective-permute-start = (bf16[34,4,1024]{2,1,0:T(4,128)(2,1)S(1)}, bf16[34,4,1024]{2,1,0:T(4,128)(2,1)S(1)}, u32[]{:S(2)}, u32[]{:S(2)}) collective-permute-start(bf16[34,4,1024]{2,1,0:T(4,128)(2,1)S(1)} %get-tuple-element.39), channel_id=1, source_target_pairs={{4,8},{5,9},{6,10},{7,11},{20,24},{21,25},{22,26},{23,27},{8,4},{9... | collective-permute-start | bytes 835592 | tf_op jit(solution)/shard_map/ppermute | solution.py:599
  8.3 5.6 %collective-permute-start.2 = (bf16[34,4,1024]{2,1,0:T(4,128)(2,1)S(1)}, bf16[34,4,1024]{2,1,0:T(4,128)(2,1)S(1)}, u32[]{:S(2)}, u32[]{:S(2)}) collective-permute-start(bf16[34,4,1024]{2,1,0:T(4,128)(2,1)S(1)} %get-tuple-element.50), channel_id=1, source_target_pairs={{0,4},{8,12},{4,0},{12,8},{1,5},{9,13},{5,1},{13,9},{2,6},{10,14},... | collective-permute-start | bytes 835592 | tf_op jit(solution)/shard_map/ppermute | solution.py:600
  9.7 4.4 %collective-permute-start.4 = (bf16[5,4,1024]{2,1,0:T(4,128)(2,1)S(1)}, bf16[5,4,1024]{2,1,0:T(4,128)(2,1)S(1)}, u32[]{:S(2)}, u32[]{:S(2)}) collective-permute-start(bf16[5,4,1024]{2,1,0:T(4,128)(2,1)S(1)} %get-tuple-element.81), channel_id=1, source_target_pairs={{4,8},{8,4},{0,16},{12,28},{20,24},{24,20},{16,0},{28,12},{5,9},{9... | collective-permute-start | bytes 122888 | tf_op jit(solution)/shard_map/ppermute | solution.py:616
  11.5 2.6 %collective-permute-start.3 = (bf16[5,4,1024]{2,1,0:T(4,128)(2,1)S(1)}, bf16[5,4,1024]{2,1,0:T(4,128)(2,1)S(1)}, u32[]{:S(2)}, u32[]{:S(2)}) collective-permute-start(bf16[5,4,1024]{2,1,0:T(4,128)(2,1)S(1)} %get-tuple-element.82), channel_id=1, source_target_pairs={{0,4},{8,12},{4,0},{12,8},{1,5},{9,13},{5,1},{13,9},{2,6},{10,14},... | collective-permute-start | bytes 122888 | tf_op jit(solution)/shard_map/ppermute | solution.py:615
  11.6 9.5 %collective-permute-start.5 = (bf16[34,16,128]{2,1,0:T(8,128)(2,1)S(1)}, bf16[34,16,128]{2,1,0:T(8,128)(2,1)S(1)}, u32[]{:S(2)}, u32[]{:S(2)}) collective-permute-start(bf16[34,16,128]{2,1,0:T(8,128)(2,1)S(1)} %get-tuple-element.62), channel_id=1, source_target_pairs={{0,1},{2,3},{1,0},{3,2},{4,5},{6,7},{5,4},{7,6},{8,9},{10,11},{9,8... | collective-permute-start | bytes 417800 | tf_op jit(solution)/shard_map/ppermute | solution.py:593
  13.9 7.3 %collective-permute-start.6 = (bf16[34,16,128]{2,1,0:T(8,128)(2,1)S(1)}, bf16[34,16,128]{2,1,0:T(8,128)(2,1)S(1)}, u32[]{:S(2)}, u32[]{:S(2)}) collective-permute-start(bf16[34,16,128]{2,1,0:T(8,128)(2,1)S(1)} %get-tuple-element.63), channel_id=1, source_target_pairs={{1,2},{2,1},{0,4},{3,7},{5,6},{6,5},{4,0},{7,3},{9,10},{10,9},{8,1... | collective-permute-start | bytes 417800 | tf_op jit(solution)/shard_map/ppermute | solution.py:593
  14.8 6.3 %collective-permute-start.7 = (bf16[46,8,128]{2,1,0:T(8,128)(2,1)S(1)}, bf16[46,8,128]{2,1,0:T(8,128)(2,1)S(1)}, u32[]{:S(2)}, u32[]{:S(2)}) collective-permute-start(bf16[46,8,128]{2,1,0:T(8,128)(2,1)S(1)} %get-tuple-element.64), channel_id=1, source_target_pairs={{0,1},{2,3},{1,0},{3,2},{4,5},{6,7},{5,4},{7,6},{8,9},{10,11},{9,8... | collective-permute-start | bytes 282632 | tf_op jit(solution)/shard_map/ppermute | solution.py:593
  17.9 3.3 %collective-permute-start.8 = (bf16[46,8,128]{2,1,0:T(8,128)(2,1)S(1)}, bf16[46,8,128]{2,1,0:T(8,128)(2,1)S(1)}, u32[]{:S(2)}, u32[]{:S(2)}) collective-permute-start(bf16[46,8,128]{2,1,0:T(8,128)(2,1)S(1)} %get-tuple-element.65), channel_id=1, source_target_pairs={{1,2},{2,1},{0,4},{3,7},{5,6},{6,5},{4,0},{7,3},{9,10},{10,9},{8,1... | collective-permute-start | bytes 282632 | tf_op jit(solution)/shard_map/ppermute | solution.py:593
  26.9 1.8 %collective-permute-start.9 = (bf16[4,272,128]{2,1,0:T(8,128)(2,1)S(1)}, bf16[4,272,128]{2,1,0:T(8,128)(2,1)S(1)}, u32[]{:S(2)}, u32[]{:S(2)}) collective-permute-start(bf16[4,272,128]{2,1,0:T(8,128)(2,1)S(1)} %get-tuple-element.69), channel_id=1, source_target_pairs={{0,4},{4,0},{8,12},{12,8},{16,20},{20,16},{24,28},{28,24},{1,5},{5... | collective-permute-start | bytes 835592 | tf_op jit(solution)/shard_map/ppermute | solution.py:646
  28.8 4.8 %collective-permute-start.10 = (bf16[272,128]{1,0:T(8,128)(2,1)S(1)}, bf16[272,128]{1,0:T(8,128)(2,1)S(1)}, u32[]{:S(2)}, u32[]{:S(2)}) collective-permute-start(bf16[272,128]{1,0:T(8,128)(2,1)S(1)} %get-tuple-element.74), channel_id=1, source_target_pairs={{0,8},{4,12},{8,0},{12,4},{16,24},{20,28},{24,16},{28,20},{1,9},{5... | collective-permute-start | bytes 208904 | tf_op jit(solution)/shard_map/ppermute | solution.py:643
  29.0 4.6 %collective-permute-start.12 = (bf16[272,128]{1,0:T(8,128)(2,1)S(1)}, bf16[272,128]{1,0:T(8,128)(2,1)S(1)}, u32[]{:S(2)}, u32[]{:S(2)}) collective-permute-start(bf16[272,128]{1,0:T(8,128)(2,1)S(1)} %get-tuple-element.75), channel_id=1, source_target_pairs={{0,16},{4,20},{8,24},{12,28},{16,0},{20,4},{24,8},{28,12},{1,17},{... | collective-permute-start | bytes 208904 | tf_op jit(solution)/shard_map/ppermute | solution.py:643
  30.4 5.3 %collective-permute-start.11 = (bf16[272,128]{1,0:T(8,128)(2,1)S(1)}, bf16[272,128]{1,0:T(8,128)(2,1)S(1)}, u32[]{:S(2)}, u32[]{:S(2)}) collective-permute-start(bf16[272,128]{1,0:T(8,128)(2,1)S(1)} %get-tuple-element.76), channel_id=1, source_target_pairs={{0,24},{4,28},{8,16},{12,20},{16,8},{20,12},{24,0},{28,4},{1,25},{... | collective-permute-start | bytes 208904 | tf_op jit(solution)/shard_map/ppermute | solution.py:643
  35.8 6.9 %collective-permute-start.15 = (bf16[272,128]{1,0:T(8,128)(2,1)S(1)}, bf16[272,128]{1,0:T(8,128)(2,1)S(1)}, u32[]{:S(2)}, u32[]{:S(2)}) collective-permute-start(bf16[272,128]{1,0:T(8,128)(2,1)S(1)} %fusion.2), channel_id=1, source_target_pairs={{0,3},{1,2},{2,1},{3,0},{4,7},{5,6},{6,5},{7,4},{8,11},{9,10},{10,... | collective-permute-start | bytes 208904 | tf_op jit(solution)/shard_map/ppermute | solution.py:649
  38.2 6.8 %collective-permute-start.14 = (bf16[272,128]{1,0:T(8,128)(2,1)S(1)}, bf16[272,128]{1,0:T(8,128)(2,1)S(1)}, u32[]{:S(2)}, u32[]{:S(2)}) collective-permute-start(bf16[272,128]{1,0:T(8,128)(2,1)S(1)} %fusion.2), channel_id=1, source_target_pairs={{0,2},{1,3},{2,0},{3,1},{4,6},{5,7},{6,4},{7,5},{8,10},{9,11},{10,... | collective-permute-start | bytes 208904 | tf_op jit(solution)/shard_map/ppermute | solution.py:649
  39.5 5.4 %collective-permute-start.13 = (bf16[272,128]{1,0:T(8,128)(2,1)S(1)}, bf16[272,128]{1,0:T(8,128)(2,1)S(1)}, u32[]{:S(2)}, u32[]{:S(2)}) collective-permute-start(bf16[272,128]{1,0:T(8,128)(2,1)S(1)} %fusion.2), channel_id=1, source_target_pairs={{0,1},{1,0},{2,3},{3,2},{4,5},{5,4},{6,7},{7,6},{8,9},{9,8},{10,11... | collective-permute-start | bytes 208904 | tf_op jit(solution)/shard_map/ppermute | solution.py:649
  45.0 4.4 %collective-permute-start.18 = (bf16[272,128]{1,0:T(8,128)(2,1)S(1)}, bf16[272,128]{1,0:T(8,128)(2,1)S(1)}, u32[]{:S(2)}, u32[]{:S(2)}) collective-permute-start(bf16[272,128]{1,0:T(8,128)(2,1)S(1)} %add_convert_fusion), channel_id=1, source_target_pairs={{0,8},{4,12},{8,0},{12,4},{16,24},{20,28},{24,16},{28,20},{1,9},{5... | collective-permute-start | bytes 208904 | tf_op jit(solution)/shard_map/ppermute | solution.py:643
  46.1 4.3 %collective-permute-start.17 = (bf16[272,128]{1,0:T(8,128)(2,1)S(1)}, bf16[272,128]{1,0:T(8,128)(2,1)S(1)}, u32[]{:S(2)}, u32[]{:S(2)}) collective-permute-start(bf16[272,128]{1,0:T(8,128)(2,1)S(1)} %add_convert_fusion), channel_id=1, source_target_pairs={{0,16},{4,20},{8,24},{12,28},{16,0},{20,4},{24,8},{28,12},{1,17},{... | collective-permute-start | bytes 208904 | tf_op jit(solution)/shard_map/ppermute | solution.py:643
  46.8 5.2 %collective-permute-start.16 = (bf16[272,128]{1,0:T(8,128)(2,1)S(1)}, bf16[272,128]{1,0:T(8,128)(2,1)S(1)}, u32[]{:S(2)}, u32[]{:S(2)}) collective-permute-start(bf16[272,128]{1,0:T(8,128)(2,1)S(1)} %add_convert_fusion), channel_id=1, source_target_pairs={{0,24},{4,28},{8,16},{12,20},{16,8},{20,12},{24,0},{28,4},{1,25},{... | collective-permute-start | bytes 208904 | tf_op jit(solution)/shard_map/ppermute | solution.py:643
  52.0 1.6 %collective-permute-start.19 = (bf16[4,272,128]{2,1,0:T(8,128)(2,1)S(1)}, bf16[4,272,128]{2,1,0:T(8,128)(2,1)S(1)}, u32[]{:S(2)}, u32[]{:S(2)}) collective-permute-start(bf16[4,272,128]{2,1,0:T(8,128)(2,1)S(1)} %pad_maximum_fusion.keep_ref), channel_id=1, source_target_pairs={{0,4},{4,0},{8,12},{12,8},{16,20},{20,16},{24,28},{28,24},{1,5},{5... | collective-permute-start | bytes 835592 | tf_op jit(solution)/shard_map/ppermute | solution.py:646
